TPU v7x, 32 devices: a whole 2x2x4 slice. The times are simulated.
32 devices in a mesh: lon: 8 (over z, y), lat: 4 (over x, core).
Axes of the slice: x: 2, y: 2, z: 4, core: 2. Of those that a mesh axis runs over, the one named last changes fastest.
Arguments:
- tokens: bfloat16 [2, 48, 192, 192], P(None, 'lat', 'lon'), may hold values from -6 to 6
- mask_ids: int32 [2, 48, 192], P(None, 'lat', 'lon'), may hold values from 0 to 1
- fine_qkv: bfloat16 [192, 576], replicated, may hold values from -0.4375 to 0.4375
- fine_proj: bfloat16 [192, 192], replicated, may hold values from -0.4375 to 0.4375
- fine_up: bfloat16 [192, 768], replicated, may hold values from -0.4375 to 0.4375
- fine_down: bfloat16 [768, 192], replicated, may hold values from -0.21875 to 0.21875
- fine_bias: float32 [8, 6, 3312], P('lat'), may hold values from -10 to 260
- reduce_weight: bfloat16 [768, 384], replicated, may hold values from -0.21875 to 0.21875
- coarse_qkv: bfloat16 [384, 1152], replicated, may hold values from -0.3125 to 0.3125
- coarse_proj: bfloat16 [384, 384], replicated, may hold values from -0.3125 to 0.3125
- coarse_up: bfloat16 [384, 1536], replicated, may hold values from -0.3125 to 0.3125
- coarse_down: bfloat16 [1536, 384], replicated, may hold values from -0.15625 to 0.15625
- coarse_bias: float32 [4, 12, 3312], P('lat'), may hold values from -10 to 260
- out_grad: bfloat16 [2, 24, 96, 384], P(None, 'lat', 'lon'), may hold values from -6 to 6
Outputs:
- coarse_result: bfloat16 [2, 24, 96, 384], P(None, 'lat', 'lon')
- d_tokens: bfloat16 [2, 48, 192, 192], P(None, 'lat', 'lon')
- fine_bias_grad: float32 [8, 6, 3312], P('lat')
- coarse_bias_grad: float32 [4, 12, 3312], P('lat')
All inputs are finite; a program needn't handle non-finite values.
Results may differ from a plain program's by a relative error of at most 0.024.
Values may be sent and summed in bfloat16 or wider, within the bound.
No kernel may reach another device: no remote copies, remote signals or barrier semaphores. Data moves between devices by JAX's collectives and lax.ppermute only.
A program may use at most 128 MiB of HBM per device.

v0:
```python
import math

import jax
import jax.numpy as jnp
import numpy as np
from jax import lax
from jax.experimental import pallas as pl
from jax.experimental.pallas import tpu as pltpu
from jax.sharding import PartitionSpec as P

HEADS_F = 6
HEADS_C = 12
HEAD = 32
WIN = 144
QUAD = 36
SPAN = 23
ENTRIES = 276
LOG2E = math.log2(math.e)
VMEM = 32 * 1024 * 1024
f32 = jnp.float32
bf16 = jnp.bfloat16


def spot(z, i, j):
    quadrant = (i % 6) // 3 * 2 + (j % 12) // 6
    return quadrant * QUAD + z * 18 + i % 3 * 6 + j % 6


def fine_spot(z, i, j):
    return (i // 6 * 2 + j // 12) * WIN + spot(z, i, j)


def in_quad(z, i, j):
    return z * 18 + i % 3 * 6 + j % 6


def index_maps():
    arrive = np.zeros(576, np.int32)
    merge = np.zeros(576, np.int32)
    split = np.full(608, -1, np.int32)
    back = np.zeros(576, np.int32)
    leave = np.zeros(576, np.int32)
    for z in range(2):
        for i in range(12):
            for j in range(24):
                here = fine_spot(z, i, j)
                if i >= 3 and j >= 6:
                    arrive[here] = z * 288 + (i - 3) * 24 + j - 6
                    came = fine_spot(z, i - 3, j - 6)
                elif i >= 3:
                    arrive[here] = 576 + z * 72 + (i - 3) * 8 + 2 + j
                    came = 576 + (i - 3) // 3 * QUAD + in_quad(z, i, j)
                elif j >= 6:
                    arrive[here] = 720 + z * 72 + i * 24 + j - 6
                    came = 688 + (j - 6) // 6 * QUAD + in_quad(z, i, j)
                else:
                    arrive[here] = 864 + z * 24 + i * 8 + 2 + j
                    came = 800 + in_quad(z, i, j)
                part = (i % 2 + j % 2 * 2) * WIN + spot(z, i // 2, j // 2)
                merge[part] = came
                if i >= 3 and j >= 6:
                    slot = 272 + z * 162 + (i - 3) * 18 + j - 6
                    back[fine_spot(z, i - 3, j - 6)] = slot
                elif i >= 3:
                    slot = z * 54 + (i - 3) * 6 + j
                    back[fine_spot(z, i - 3, j + 18)] = slot
                elif j >= 6:
                    slot = 112 + z * 54 + i * 18 + j - 6
                    back[fine_spot(z, i + 9, j - 6)] = slot
                else:
                    slot = 224 + z * 18 + i * 6 + j
                    back[fine_spot(z, i + 9, j + 18)] = slot
                split[slot] = part
                natural = z * 288 + i * 24 + j
                if i < 9 and j < 18:
                    leave[natural] = fine_spot(z, i + 3, j + 6)
                elif i < 9:
                    leave[natural] = 576 + i // 3 * QUAD + in_quad(z, i, j)
                elif j < 18:
                    leave[natural] = 688 + j // 6 * QUAD + in_quad(z, i, j)
                else:
                    leave[natural] = 800 + in_quad(z, i, j)
    result = np.zeros(WIN, np.int32)
    base = np.zeros(WIN, np.int32)
    row_slot = np.zeros(WIN, np.int32)
    for z in range(2):
        for i in range(6):
            for j in range(12):
                result[z * 72 + i * 12 + j] = (i // 3 * 2 + j // 6) * 48 + in_quad(z, i, j)
                here = spot(z, i, j)
                base[here] = (z * 6 + i) * SPAN + 11 - j
                row_slot[here] = j * 16 + z * 6 + i
    return arrive, merge, split, back, leave, result, base, row_slot


ARRIVE, MERGE, SPLIT, BACK, LEAVE, RESULT, BASE, ROW_SLOT = index_maps()


def one_hot(column, width):
    spots = lax.broadcasted_iota(jnp.int32, (column.shape[0], width), 1)
    return jnp.where(spots == column, 1.0, 0.0).astype(bf16)


def mm(left, right):
    return jnp.dot(left, right, preferred_element_type=f32)


def mm_nt(left, right):
    return lax.dot_general(left, right, (((1,), (1,)), ((), ())), preferred_element_type=f32)


def mm_tn(left, right):
    return lax.dot_general(left, right, (((0,), (0,)), ((), ())), preferred_element_type=f32)


def norm(values):
    centred = values - jnp.mean(values, axis=-1, keepdims=True)
    scale = lax.rsqrt(jnp.mean(centred * centred, axis=-1, keepdims=True) + 1e-5)
    return centred * scale, scale


def norm_back(grad, normed, scale):
    along = jnp.mean(grad * normed, axis=-1, keepdims=True)
    return (grad - jnp.mean(grad, axis=-1, keepdims=True) - normed * along) * scale


def gelu_pair(x):
    u = jnp.abs(x) * math.sqrt(0.5)
    t = 1.0 / (1.0 + 0.3275911 * u)
    e = jnp.exp(-u * u)
    poly = 1.421413741 + t * (-1.453152027 + t * 1.061405429)
    tail = 0.5 * (t * (0.254829592 + t * (-0.284496736 + t * poly))) * e
    below = jnp.where(x >= 0, 1.0 - tail, tail)
    return x * below, below + x * (e * (1.0 / math.sqrt(2 * math.pi)))


def groups(channels):
    return [(start, min(start + 128, channels)) for start in range(0, channels, 128)]


def head_lanes(rows, width):
    return lax.broadcasted_iota(jnp.int32, (rows, width), 1) // HEAD


def stack_heads(part):
    lanes = head_lanes(part.shape[0], part.shape[1])
    count = part.shape[1] // HEAD
    zero = jnp.zeros_like(part)
    return jnp.concatenate([jnp.where(lanes == h, part, zero) for h in range(count)], axis=0)


def pick_heads(stacked):
    width = stacked.shape[1]
    lanes = head_lanes(WIN, width)
    total = stacked[:WIN]
    for h in range(1, width // HEAD):
        total = jnp.where(lanes == h, stacked[h * WIN : (h + 1) * WIN], total)
    return total


def attend(queries, keys, values, bias_ref, bias_row, mask, probs_ref, probs_row):
    mixed = []
    for start, stop in groups(queries.shape[1]):
        count = (stop - start) // HEAD
        scores = mm_nt(stack_heads(queries[:, start:stop]), keys[:, start:stop])
        row = start // HEAD * WIN
        for h in range(count):
            here = row + h * WIN
            logits = (
                scores[h * WIN : (h + 1) * WIN] * (HEAD**-0.5 * LOG2E)
                + bias_ref[pl.ds(bias_row + here, WIN), :]
                + mask
            )
            raised = jnp.exp2(logits - jnp.max(logits, axis=-1, keepdims=True))
            probs = raised * (1.0 / jnp.sum(raised, axis=-1, keepdims=True))
            probs_ref[pl.ds(probs_row + here, WIN), :] = probs.astype(bf16)
        stacked = mm(probs_ref[pl.ds(probs_row + row, count * WIN), :], values[:, start:stop])
        mixed.append(pick_heads(stacked))
    return jnp.concatenate(mixed, axis=1)


def attend_back(queries, keys, values, mix_grad, probs_ref, probs_row, score_ref, add):
    query_grad, key_grad, value_grad = [], [], []
    for start, stop in groups(queries.shape[1]):
        count = (stop - start) // HEAD
        row = start // HEAD * WIN
        probs_all = probs_ref[pl.ds(probs_row + row, count * WIN), :]
        grads = stack_heads(mix_grad[:, start:stop])
        value_grad.append(mm_tn(probs_all, grads))
        probs_grad = mm_nt(grads, values[:, start:stop])
        pieces = []
        for h in range(count):
            probs = probs_all[h * WIN : (h + 1) * WIN].astype(f32)
            grad = probs_grad[h * WIN : (h + 1) * WIN]
            weighted = grad * probs
            score_grad = weighted - probs * jnp.sum(weighted, axis=-1, keepdims=True)
            place = pl.ds(row + h * WIN, WIN)
            if add:
                score_ref[place, :] += score_grad
            else:
                score_ref[place, :] = score_grad
            pieces.append(score_grad.astype(bf16))
        score_all = jnp.concatenate(pieces, axis=0)
        query_grad.append(pick_heads(mm(score_all, keys[:, start:stop])))
        key_grad.append(mm_tn(score_all, stack_heads(queries[:, start:stop])))
    scale = HEAD**-0.5
    return (
        jnp.concatenate(query_grad, axis=1) * scale,
        jnp.concatenate(key_grad, axis=1) * scale,
        jnp.concatenate(value_grad, axis=1),
    )


def table_grad(score_ref, base_ref, slot_ref, rows_ref):
    regroup = jnp.where(
        lax.broadcasted_iota(jnp.int32, (192, WIN), 0) == slot_ref[...], 1.0, 0.0
    ).astype(bf16)
    for h in range(12):
        moved = mm(regroup, score_ref[pl.ds(h * WIN, WIN), :].astype(bf16)).astype(bf16)
        rows_ref[:, pl.ds(h * 16, 16), :] = moved.reshape(12, 16, WIN)
    total = jnp.zeros((192, ENTRIES), f32)
    for column in range(12):
        total += mm(rows_ref[column], one_hot(base_ref[...] + column, ENTRIES))
    return total


def pack(pieces, rows):
    count = sum(piece.shape[0] for piece in pieces)
    if rows > count:
        pieces = pieces + [jnp.zeros((rows - count, pieces[0].shape[1]), f32)]
    return jnp.concatenate(pieces, axis=0).astype(bf16)


def quadrant(windows, qi, qj):
    part = (qi % 2 * 2 + qj % 2) * QUAD
    return windows[qi // 2 * 2 + qj // 2][part : part + QUAD]


def bias_kernel(table_ref, base_ref, slot_ref, grad_ref, fine_ref, coarse_ref, g0, g1, g2, g3, held):
    table = table_ref[...]
    high = table.astype(bf16)
    low = (table - high.astype(f32)).astype(bf16)
    entry = lax.broadcasted_iota(jnp.int32, (ENTRIES, WIN), 0)
    for column in range(12):
        picker = jnp.where(entry == base_ref[...] + column, 1.0, 0.0).astype(bf16)
        held[:, 0, column] = mm(high, picker).astype(bf16).reshape(24, 16, WIN)
        held[:, 1, column] = mm(low, picker).astype(bf16).reshape(24, 16, WIN)
    once = one_hot(slot_ref[...], 192)
    for h in range(24):
        place = pl.ds(h % 12 * WIN, WIN)
        target = fine_ref if h < 12 else coarse_ref
        target[place, :] = (
            mm(once, held[h, 0].reshape(192, WIN)) + mm(once, held[h, 1].reshape(192, WIN))
        ) * LOG2E
    for index, out in enumerate((g0, g1, g2, g3)):
        hi, hj = index // 2, index % 2
        pieces = [
            grad_ref[z, hi * 3 + row].astype(f32)[hj * 6 : hj * 6 + 6]
            for z in range(2)
            for row in range(3)
        ]
        out[...] = pack(pieces, 48)


def fine_kernel(
    tokens_ref, lon_ref, lat_ref, diag_ref, arrive_ref, bias_ref, mask_ref,
    qkv_ref, proj_ref, up_ref, down_ref,
    res_ref, slon_ref, slat_ref, sdiag_ref,
    q_ref, k_ref, v_ref, probs_ref, n1_ref, r1_ref, n2_ref, r2_ref, slope_ref,
    source,
):
    source[0:576] = tokens_ref[...]
    source[576:720] = lon_ref[...]
    source[720:864] = lat_ref[...]
    source[864:912] = diag_ref[...]
    everything = source[...]
    w_qkv = qkv_ref[...]
    bases = []
    for w in range(4):
        rows = pl.ds(w * WIN, WIN)
        base = mm(one_hot(arrive_ref[rows, :], 912), everything)
        normed, scale = norm(base)
        normed = normed.astype(bf16)
        n1_ref[rows, :] = normed
        r1_ref[rows, :] = scale
        q_ref[rows, :] = mm(normed, w_qkv[:, 0:192]).astype(bf16)
        k_ref[rows, :] = mm(normed, w_qkv[:, 192:384]).astype(bf16)
        v_ref[rows, :] = mm(normed, w_qkv[:, 384:576]).astype(bf16)
        bases.append(base)
    windows = []
    for w in range(4):
        rows = pl.ds(w * WIN, WIN)
        mixture = attend(
            q_ref[rows, :], k_ref[rows, :], v_ref[rows, :],
            bias_ref, w // 2 * 6 * WIN, mask_ref[w], probs_ref, w * 6 * WIN,
        ).astype(bf16)
        first = bases[w] + mm(mixture, proj_ref[...])
        renormed, scale = norm(first)
        renormed = renormed.astype(bf16)
        n2_ref[rows, :] = renormed
        r2_ref[rows, :] = scale
        active, slope = gelu_pair(mm(renormed, up_ref[...]))
        slope_ref[rows, :] = slope.astype(bf16)
        result = first + mm(active.astype(bf16), down_ref[...])
        res_ref[rows, :] = result.astype(bf16)
        windows.append(result)
    slon_ref[...] = pack([quadrant(windows, q, 3) for q in range(3)], 112)
    slat_ref[...] = pack([quadrant(windows, 3, q) for q in range(3)], 112)
    sdiag_ref[...] = pack([quadrant(windows, 3, 3)], 48)


def coarse_kernel(
    res_ref, lon_ref, lat_ref, diag_ref, merge_ref, split_ref, bias_ref, mask_ref,
    gloc_ref, glon_ref, glat_ref, gdiag_ref,
    reduce_ref, qkv_ref, proj_ref, up_ref, down_ref, base_ref, slot_ref,
    c0, c1, c2, c3, dlon_ref, dlat_ref, ddiag_ref, dloc_ref, table_ref,
    source, probs_ref, score_ref, rows_ref, parts_ref,
):
    source[0:576] = res_ref[...]
    source[576:688] = lon_ref[...]
    source[688:800] = lat_ref[...]
    source[800:848] = diag_ref[...]
    everything = source[...]
    parts = [mm(one_hot(merge_ref[pl.ds(k * WIN, WIN), :], 848), everything) for k in range(4)]
    mean = sum(jnp.sum(part, axis=-1, keepdims=True) for part in parts) * (1.0 / 768)
    parts = [part - mean for part in parts]
    square = sum(jnp.sum(part * part, axis=-1, keepdims=True) for part in parts)
    merge_scale = lax.rsqrt(square * (1.0 / 768) + 1e-5)
    parts = [(part * merge_scale).astype(bf16) for part in parts]
    base = sum(mm(parts[k], reduce_ref[k * 192 : (k + 1) * 192]) for k in range(4))
    base = base.astype(bf16).astype(f32)
    normed, scale1 = norm(base)
    normed = normed.astype(bf16)
    queries = mm(normed, qkv_ref[:, 0:384]).astype(bf16)
    keys = mm(normed, qkv_ref[:, 384:768]).astype(bf16)
    values = mm(normed, qkv_ref[:, 768:1152]).astype(bf16)
    mixture = attend(queries, keys, values, bias_ref, 0, mask_ref[...], probs_ref, 0).astype(bf16)
    first = base + mm(mixture, proj_ref[...])
    renormed, scale2 = norm(first)
    renormed = renormed.astype(bf16)
    active, slope = gelu_pair(mm(renormed, up_ref[...]))
    result = first + mm(active.astype(bf16), down_ref[...])
    for index, out in enumerate((c0, c1, c2, c3)):
        out[...] = pack([result[index * QUAD : (index + 1) * QUAD]], 48)

    grad = jnp.concatenate(
        [ref[...].astype(f32)[:QUAD] for ref in (gdiag_ref, glat_ref, glon_ref, gloc_ref)], axis=0
    )
    inner = mm_nt(grad.astype(bf16), down_ref[...]) * slope
    grad = grad + norm_back(mm_nt(inner.astype(bf16), up_ref[...]), renormed.astype(f32), scale2)
    mix_grad = mm_nt(grad.astype(bf16), proj_ref[...]).astype(bf16)
    dq, dk, dv = attend_back(queries, keys, values, mix_grad, probs_ref, 0, score_ref, False)
    normed_grad = (
        mm_nt(dq.astype(bf16), qkv_ref[:, 0:384])
        + mm_nt(dk.astype(bf16), qkv_ref[:, 384:768])
        + mm_nt(dv.astype(bf16), qkv_ref[:, 768:1152])
    )
    grad = grad + norm_back(normed_grad, normed.astype(f32), scale1)
    grad = grad.astype(bf16)
    grads = [mm_nt(grad, reduce_ref[k * 192 : (k + 1) * 192]) for k in range(4)]
    mean = sum(jnp.sum(g, axis=-1, keepdims=True) for g in grads) * (1.0 / 768)
    along = sum(
        jnp.sum(g * p.astype(f32), axis=-1, keepdims=True) for g, p in zip(grads, parts)
    ) * (1.0 / 768)
    for k in range(4):
        part = (grads[k] - mean - parts[k].astype(f32) * along) * merge_scale
        parts_ref[pl.ds(k * WIN, WIN), :] = part.astype(bf16)
    everything = parts_ref[...]
    moved = mm(one_hot(split_ref[...], 576), everything).astype(bf16)
    dlon_ref[...] = moved[0:112]
    dlat_ref[...] = moved[112:224]
    ddiag_ref[...] = moved[224:272]
    dloc_ref[...] = moved[272:608]
    table_ref[...] = table_grad(score_ref, base_ref, slot_ref, rows_ref).astype(bf16)


def fine_back_kernel(
    dlon_ref, dlat_ref, ddiag_ref, dloc_ref, back_ref,
    q_ref, k_ref, v_ref, probs_ref, n1_ref, r1_ref, n2_ref, r2_ref, slope_ref,
    qkv_ref, proj_ref, up_ref, down_ref, base_ref, slot_ref,
    res_ref, slon_ref, slat_ref, sdiag_ref, table_ref,
    source, score_ref, rows_ref,
):
    source[0:112] = dlon_ref[...]
    source[112:224] = dlat_ref[...]
    source[224:272] = ddiag_ref[...]
    source[272:608] = dloc_ref[...]
    everything = source[...]
    w_qkv = qkv_ref[...]
    windows = []
    for w in range(4):
        rows = pl.ds(w * WIN, WIN)
        grad = mm(one_hot(back_ref[rows, :], 608), everything)
        inner = mm_nt(grad.astype(bf16), down_ref[...]) * slope_ref[rows, :].astype(f32)
        grad = grad + norm_back(
            mm_nt(inner.astype(bf16), up_ref[...]), n2_ref[rows, :].astype(f32), r2_ref[rows, :]
        )
        mix_grad = mm_nt(grad.astype(bf16), proj_ref[...]).astype(bf16)
        dq, dk, dv = attend_back(
            q_ref[rows, :], k_ref[rows, :], v_ref[rows, :], mix_grad,
            probs_ref, w * 6 * WIN,
            score_ref.at[pl.ds(w // 2 * 6 * WIN, 6 * WIN)], w % 2 == 1,
        )
        normed_grad = (
            mm_nt(dq.astype(bf16), w_qkv[:, 0:192])
            + mm_nt(dk.astype(bf16), w_qkv[:, 192:384])
            + mm_nt(dv.astype(bf16), w_qkv[:, 384:576])
        )
        result = grad + norm_back(normed_grad, n1_ref[rows, :].astype(f32), r1_ref[rows, :])
        res_ref[rows, :] = result.astype(bf16)
        windows.append(result)
    slon_ref[...] = pack([quadrant(windows, q, 0) for q in range(1, 4)], 112)
    slat_ref[...] = pack([quadrant(windows, 0, q) for q in range(1, 4)], 112)
    sdiag_ref[...] = pack([quadrant(windows, 0, 0)], 48)
    table_ref[...] = table_grad(score_ref, base_ref, slot_ref, rows_ref).astype(bf16)


def last_kernel(
    res_ref, lon_ref, lat_ref, diag_ref, leave_ref, cloc, clon, clat, cdiag, result_ref,
    tokens_ref, coarse_ref, source, coarse_source,
):
    source[0:576] = res_ref[...]
    source[576:688] = lon_ref[...]
    source[688:800] = lat_ref[...]
    source[800:848] = diag_ref[...]
    everything = source[...]
    for w in range(4):
        rows = pl.ds(w * WIN, WIN)
        tokens_ref[rows, :] = mm(one_hot(leave_ref[rows, :], 848), everything).astype(bf16)
    coarse_source[0:48] = cloc[...]
    coarse_source[48:96] = clon[...]
    coarse_source[96:144] = clat[...]
    coarse_source[144:192] = cdiag[...]
    moved = mm(one_hot(result_ref[...], 192), coarse_source[...])
    for z in range(2):
        for row in range(6):
            start = z * 72 + row * 12
            coarse_ref[z, row] = moved[start : start + 12].astype(bf16)


def run(kernel, outs, scratch, flops, inputs):
    shapes = [jax.ShapeDtypeStruct(shape, kind) for shape, kind in outs]
    size = sum(math.prod(s.shape) * s.dtype.itemsize for s in shapes)
    size += sum(x.size * x.dtype.itemsize for x in inputs)
    return pl.pallas_call(
        kernel,
        out_shape=shapes,
        scratch_shapes=[pltpu.VMEM(shape, kind) for shape, kind in scratch],
        compiler_params=pltpu.CompilerParams(vmem_limit_bytes=VMEM),
        cost_estimate=pl.CostEstimate(flops=flops, bytes_accessed=size, transcendentals=0),
    )(*inputs)


def move(value, lon_steps, lat_steps):
    lon, lat = lax.axis_size("lon"), lax.axis_size("lat")
    if lat_steps == 0:
        pairs = [(s, (s + lon_steps) % lon) for s in range(lon)]
        return lax.ppermute(value, "lon", pairs)
    if lon_steps == 0:
        pairs = [(s, (s + lat_steps) % lat) for s in range(lat)]
        return lax.ppermute(value, "lat", pairs)
    pairs = [
        (b * lat + a, (b + lon_steps) % lon * lat + (a + lat_steps) % lat)
        for b in range(lon)
        for a in range(lat)
    ]
    return lax.ppermute(value, ("lon", "lat"), pairs)


def send(pieces, steps):
    on_lon, on_lat, on_both = pieces
    return move(on_lon, steps, 0), move(on_lat, 0, steps), move(on_both, steps, steps)


def lon_total(value):
    count = lax.axis_size("lon")
    if count & (count - 1):
        return lax.psum(value, "lon").astype(f32)
    step = 1
    total = value
    while step < count:
        kept = total.astype(bf16)
        other = lax.ppermute(kept, "lon", [(s, s ^ step) for s in range(count)])
        total = kept.astype(f32) + other.astype(f32)
        step *= 2
    return total.astype(f32)


def to_table(grad, bands, heads):
    return grad.reshape(12, 16, ENTRIES)[:, :12].reshape(bands, heads, 12 * ENTRIES)


def body(
    tokens, mask_ids, fine_qkv, fine_proj, fine_up, fine_down, fine_bias, reduce_weight,
    coarse_qkv, coarse_proj, coarse_up, coarse_down, coarse_bias, out_grad,
):
    lat_index = lax.axis_index("lat")
    flat = tokens.reshape(576, 192)
    arrived = send(
        (
            tokens[:, 0:9, 16:24].reshape(144, 192),
            tokens[:, 9:12].reshape(144, 192),
            tokens[:, 9:12, 16:24].reshape(48, 192),
        ),
        1,
    )
    column = lambda index: jnp.asarray(index).reshape(-1, 1)
    line = lambda index: jnp.asarray(index).reshape(1, -1)

    tables = jnp.concatenate(
        [fine_bias.reshape(12, 12, ENTRIES), coarse_bias.reshape(12, 12, ENTRIES)], axis=0
    )
    tables = jnp.pad(tables, ((0, 0), (0, 4), (0, 0))).reshape(384, ENTRIES)
    expanded = run(
        bias_kernel,
        [((12 * WIN, WIN), f32)] * 2 + [((48, 384), bf16)] * 4,
        [((24, 2, 12, 16, WIN), bf16)],
        4_000_000_000,
        (tables, line(BASE), column(ROW_SLOT), out_grad),
    )
    fine_table, coarse_table, g00, g01, g10, g11 = expanded
    grads = (g00, *send((g01, g10, g11), 1))

    labels = mask_ids.reshape(2, 2, 2, 3, 2, 2, 6)
    top = jnp.zeros((2, 2, 1, 1, 1, 1), jnp.int32).at[0, 0].set(1)[None]
    labels = labels * 2 + jnp.where(lat_index == 0, top, 0)
    labels = labels.transpose(1, 4, 2, 5, 0, 3, 6).reshape(4, WIN)
    fine_mask = jnp.where(labels[:, :, None] == labels[:, None, :], 0.0, -1e30).astype(f32)
    low_half = jnp.arange(WIN) < WIN // 2
    coarse_mask = jnp.where(
        (low_half[:, None] == low_half[None, :]) | (lat_index != 0), 0.0, -1e30
    ).astype(f32)

    tok = ((576, 192), bf16)
    edges = [((112, 192), bf16), ((112, 192), bf16), ((48, 192), bf16)]
    fine = run(
        fine_kernel,
        [tok] + edges
        + [tok] * 3
        + [((24 * WIN, WIN), bf16), tok, ((576, 1), f32), tok, ((576, 1), f32), ((576, 768), bf16)],
        [((912, 192), bf16)],
        2_000_000_000,
        (flat, *arrived, column(ARRIVE), fine_table, fine_mask, fine_qkv, fine_proj, fine_up, fine_down),
    )
    saved = fine[4:]
    arrived = send(fine[1:4], 1)
    coarse = run(
        coarse_kernel,
        [((48, 384), bf16)] * 4 + edges + [((336, 192), bf16), ((192, ENTRIES), bf16)],
        [
            ((848, 192), bf16),
            ((12 * WIN, WIN), bf16),
            ((12 * WIN, WIN), f32),
            ((12, 192, WIN), bf16),
            ((576, 192), bf16),
        ],
        3_000_000_000,
        (
            fine[0], *arrived, column(MERGE), column(SPLIT), coarse_table, coarse_mask, *grads,
            reduce_weight, coarse_qkv, coarse_proj, coarse_up, coarse_down,
            column(BASE), line(ROW_SLOT),
        ),
    )
    c00, c01, c10, c11 = coarse[:4]
    arrived = send(coarse[4:7], -1)
    results = (c11, *send((c10, c01, c00), -1))
    coarse_total = lon_total(coarse[8])
    fine_back = run(
        fine_back_kernel,
        [tok] + edges + [((192, ENTRIES), bf16)],
        [((608, 192), bf16), ((12 * WIN, WIN), f32), ((12, 192, WIN), bf16)],
        3_000_000_000,
        (
            *arrived, coarse[7], column(BACK), *saved,
            fine_qkv, fine_proj, fine_up, fine_down, column(BASE), line(ROW_SLOT),
        ),
    )
    arrived = send(fine_back[1:4], -1)
    fine_total = lon_total(fine_back[4])
    d_tokens, coarse_result = run(
        last_kernel,
        [tok, ((2, 6, 12, 384), bf16)],
        [((848, 192), bf16), ((192, 384), bf16)],
        300_000_000,
        (fine_back[0], *arrived, column(LEAVE), *results, column(RESULT)),
    )
    return (
        coarse_result,
        d_tokens.reshape(tokens.shape),
        to_table(fine_total, 2, HEADS_F),
        to_table(coarse_total, 1, HEADS_C),
    )


def solution(mesh):
    grid = P(None, "lat", "lon", None)
    bands = P("lat", None, None)
    in_specs = (
        grid, P(None, "lat", "lon"), P(), P(), P(), P(), bands,
        P(), P(), P(), P(), P(), bands, grid,
    )
    out_specs = (grid, grid, bands, bands)
    return jax.shard_map(body, mesh=mesh, in_specs=in_specs, out_specs=out_specs, check_vma=False)
```

profile of v0, /device:TPU:0, one launch (start us, length us, event | category | flops | bytes accessed | tf_op | source)
XLA Modules:
  0.0 97.9 jit_solution(16637943895365014669)
XLA Ops:
  0.7 1.0 slice.51
  1.6 3.0 %collective-permute-start = (bf16[144,192]{1,0:T(8,128)(2,1)S(1)}, bf16[144,192]{1,0:T(8,128)(2,1)S(1)}, u32[]{:S(2)}, u32[]{:S(2)}) collective-permute-start(bf16[144,192]{1,0:T(8,128)(2,1)S(1)} %bitcast.18), channel_id=1, source_target_pairs={{0,4},{4,8},{8,12},{12,16},{16,20},{20,24},{24,28},{28,0},{1,5},{5... | collective-permute-start | bytes 165896 | tf_op jit(solution)/shard_map/ppermute | solution.py:458
  4.6 0.9 slice.52
  5.5 0.7 slice.53
  6.2 2.7 %collective-permute-start.2 = (bf16[48,192]{1,0:T(8,128)(2,1)S(1)}, bf16[48,192]{1,0:T(8,128)(2,1)S(1)}, u32[]{:S(2)}, u32[]{:S(2)}) collective-permute-start(bf16[48,192]{1,0:T(8,128)(2,1)S(1)} %bitcast.20), channel_id=1, source_target_pairs={{0,5},{1,6},{2,7},{3,4},{4,9},{5,10},{6,11},{7,8},{8,13},{9,14},{1... | collective-permute-start | bytes 55304 | tf_op jit(solution)/shard_map/ppermute | solution.py:467
  9.0 0.9 copy.31
  9.9 0.2 reshape.147
  10.1 1.3 %reduce.2 = f32[12,3312]{1,0:T(8,128)S(1)} reduce(f32[1,12,3312]{2,0,1:T(1,128)} %param.36, f32[]{:T(128)} %constant.95), dimensions={0}, to_apply=%param.36.reduce_sub_computation | reduce | bytes 317956 | tf_op args[12]
  11.4 0.2 reshape.148
  11.8 3.6 %shard_map.237 = (f32[1728,144]{1,0:T(8,128)S(1)}, f32[1728,144]{1,0:T(8,128)S(1)}, bf16[48,384]{1,0:T(8,128)(2,1)S(1)}, bf16[48,384]{1,0:T(8,128)(2,1)S(1)}, bf...) custom-call(f32[384,276]{1,0:T(8,128)S(1)} %bitcast.14, s32[1,144]{1,0:T(1,128)S(1)} %copy-done.18, ...), custom_call_target="tpu_custom_call" | custom-call | flops 4000000000 | bytes 2673792 | tf_op jit(solution)/shard_map/pallas_call | solution.py:445
  15.4 1.2 %copy-done.19 = f32[1728,144]{1,0:T(8,128)} copy-done((f32[1728,144]{1,0:T(8,128)}, f32[1728,144]{1,0:T(8,128)S(1)}, u32[]{:S(2)}) %copy-start.19) | copy-done | bytes 995352
  16.6 1.2 %copy-done.21 = f32[1728,144]{1,0:T(8,128)} copy-done((f32[1728,144]{1,0:T(8,128)}, f32[1728,144]{1,0:T(8,128)S(1)}, u32[]{:S(2)}) %copy-start.21) | copy-done | bytes 995352
  17.8 1.5 %collective-permute-start.6 = (bf16[48,384]{1,0:T(8,128)(2,1)S(1)}, bf16[48,384]{1,0:T(8,128)(2,1)S(1)}, u32[]{:S(2)}, u32[]{:S(2)}) collective-permute-start(bf16[48,384]{1,0:T(8,128)(2,1)S(1)} %get-tuple-element.58), channel_id=1, source_target_pairs={{0,4},{4,8},{8,12},{12,16},{16,20},{20,24},{24,28},{28,0},{1,5},{5... | collective-permute-start | bytes 110600 | tf_op jit(solution)/shard_map/ppermute | solution.py:458
  19.6 0.1 eq.32
  19.7 0.1 compare_select_fusion.mask_ref
  19.9 0.2 copy.34.down_ref
  20.1 1.8 %collective-permute-start.8 = (bf16[48,384]{1,0:T(8,128)(2,1)S(1)}, bf16[48,384]{1,0:T(8,128)(2,1)S(1)}, u32[]{:S(2)}, u32[]{:S(2)}) collective-permute-start(bf16[48,384]{1,0:T(8,128)(2,1)S(1)} %get-tuple-element.60), channel_id=1, source_target_pairs={{0,5},{1,6},{2,7},{3,4},{4,9},{5,10},{6,11},{7,8},{8,13},{9,14},{1... | collective-permute-start | bytes 110600 | tf_op jit(solution)/shard_map/ppermute | solution.py:467
  22.0 1.5 %copy-done.20 = f32[1728,144]{1,0:T(8,128)S(1)} copy-done((f32[1728,144]{1,0:T(8,128)S(1)}, f32[1728,144]{1,0:T(8,128)}, u32[]{:S(2)}) %copy-start.20) | copy-done | bytes 995352
  23.5 7.8 %shard_map.238 = (bf16[576,192]{1,0:T(8,128)(2,1)S(1)}, bf16[112,192]{1,0:T(8,128)(2,1)S(1)}, bf16[112,192]{1,0:T(8,128)(2,1)S(1)}, bf16[48,192]{1,0:T(8,128)(2,...) custom-call(bf16[576,192]{1,0:T(8,128)(2,1)S(1)} %bitcast.15, ...), custom_call_target="tpu_custom_call" | custom-call | flops 2000000000 | bytes 5880576 | tf_op jit(solution)/shard_map/pallas_call | solution.py:445
  31.3 1.6 %collective-permute-start.3 = (bf16[112,192]{1,0:T(8,128)(2,1)S(1)}, bf16[112,192]{1,0:T(8,128)(2,1)S(1)}, u32[]{:S(2)}, u32[]{:S(2)}) collective-permute-start(bf16[112,192]{1,0:T(8,128)(2,1)S(1)} %get-tuple-element.53), channel_id=1, source_target_pairs={{0,4},{4,8},{8,12},{12,16},{16,20},{20,24},{24,28},{28,0},{1,5},{5... | collective-permute-start | bytes 129032 | tf_op jit(solution)/shard_map/ppermute | solution.py:458
  32.9 2.7 %collective-permute-start.5 = (bf16[48,192]{1,0:T(8,128)(2,1)S(1)}, bf16[48,192]{1,0:T(8,128)(2,1)S(1)}, u32[]{:S(2)}, u32[]{:S(2)}) collective-permute-start(bf16[48,192]{1,0:T(8,128)(2,1)S(1)} %get-tuple-element.55), channel_id=1, source_target_pairs={{0,5},{1,6},{2,7},{3,4},{4,9},{5,10},{6,11},{7,8},{8,13},{9,14},{1... | collective-permute-start | bytes 55304 | tf_op jit(solution)/shard_map/ppermute | solution.py:467
  35.8 4.0 %collective-permute-done.5.diag_ref = bf16[48,192]{1,0:T(8,128)(2,1)S(1)} collective-permute-done((bf16[48,192]{1,0:T(8,128)(2,1)S(1)}, bf16[48,192]{1,0:T(8,128)(2,1)S(1)}, u32[]{:S(2)}, u32[]{:S(2)}) %collective-permute-start.5) | collective-permute-done | bytes 18464 | tf_op jit(solution)/shard_map/ppermute | solution.py:467
  39.9 9.4 %shard_map.239 = (bf16[48,384]{1,0:T(8,128)(2,1)S(1)}, bf16[48,384]{1,0:T(8,128)(2,1)S(1)}, bf16[48,384]{1,0:T(8,128)(2,1)S(1)}, bf16[48,384]{1,0:T(8,128)(2,1)S...) custom-call(bf16[576,192]{1,0:T(8,128)(2,1)S(1)} %get-tuple-element., ...), custom_call_target="tpu_custom_call" | custom-call | flops 3000000000 | bytes 6172928 | tf_op jit(solution)/shard_map/pallas_call | solution.py:445
  49.2 1.2 %collective-permute-start.10 = (bf16[112,192]{1,0:T(8,128)(2,1)S(1)}, bf16[112,192]{1,0:T(8,128)(2,1)S(1)}, u32[]{:S(2)}, u32[]{:S(2)}) collective-permute-start(bf16[112,192]{1,0:T(8,128)(2,1)S(1)} %get-tuple-element.62), channel_id=1, source_target_pairs={{0,3},{1,0},{2,1},{3,2},{4,7},{5,4},{6,5},{7,6},{8,11},{9,8},{10,9... | collective-permute-start | bytes 129032 | tf_op jit(solution)/shard_map/ppermute | solution.py:461
  50.5 0.6 collective-permute-start.9
  51.0 1.2 %collective-permute-start.11 = (bf16[48,192]{1,0:T(8,128)(2,1)S(1)}, bf16[48,192]{1,0:T(8,128)(2,1)S(1)}, u32[]{:S(2)}, u32[]{:S(2)}) collective-permute-start(bf16[48,192]{1,0:T(8,128)(2,1)S(1)} %get-tuple-element.63), channel_id=1, source_target_pairs={{0,31},{1,28},{2,29},{3,30},{4,3},{5,0},{6,1},{7,2},{8,7},{9,4},{1... | collective-permute-start | bytes 55304 | tf_op jit(solution)/shard_map/ppermute | solution.py:467
  52.2 0.5 collective-permute-start.21
  52.7 1.4 %collective-permute-start.15 = (bf16[48,384]{1,0:T(8,128)(2,1)S(1)}, bf16[48,384]{1,0:T(8,128)(2,1)S(1)}, u32[]{:S(2)}, u32[]{:S(2)}) collective-permute-start(bf16[48,384]{1,0:T(8,128)(2,1)S(1)} %get-tuple-element.79), channel_id=1, source_target_pairs={{0,28},{4,0},{8,4},{12,8},{16,12},{20,16},{24,20},{28,24},{1,29},{... | collective-permute-start | bytes 110600 | tf_op jit(solution)/shard_map/ppermute | solution.py:458
  54.1 0.4 collective-permute-done.11.ddiag_ref
  54.5 1.0 %collective-permute-start.16 = (bf16[48,384]{1,0:T(8,128)(2,1)S(1)}, bf16[48,384]{1,0:T(8,128)(2,1)S(1)}, u32[]{:S(2)}, u32[]{:S(2)}) collective-permute-start(bf16[48,384]{1,0:T(8,128)(2,1)S(1)} %get-tuple-element.80), channel_id=1, source_target_pairs={{0,3},{1,0},{2,1},{3,2},{4,7},{5,4},{6,5},{7,6},{8,11},{9,8},{10,9... | collective-permute-start | bytes 110600 | tf_op jit(solution)/shard_map/ppermute | solution.py:461
  55.5 8.4 %shard_map.240 = (bf16[576,192]{1,0:T(8,128)(2,1)S(1)}, bf16[112,192]{1,0:T(8,128)(2,1)S(1)}, bf16[112,192]{1,0:T(8,128)(2,1)S(1)}, bf16[48,192]{1,0:T(8,128)(2,1)S(1)}, bf16[192,276]{1,0:T(8,128)(2,1)S(1)}) custom-call(bf16[112,192]{1,0:T(8,128)(2,1)S(1)} %collective-permute-done.9.dlon_ref, bf16[112,192]{1,0:T(8,128)(2,1)S(1)} %collective-permute-done.10.dlat_ref, ...), custom_call_target="tpu_custom_call" | custom-call | flops 3000000000 | bytes 4543872 | tf_op jit(solution)/shard_map/pallas_call | solution.py:445
  64.0 4.2 %collective-permute-start.12 = (bf16[112,192]{1,0:T(8,128)(2,1)S(1)}, bf16[112,192]{1,0:T(8,128)(2,1)S(1)}, u32[]{:S(2)}, u32[]{:S(2)}) collective-permute-start(bf16[112,192]{1,0:T(8,128)(2,1)S(1)} %get-tuple-element.75), channel_id=1, source_target_pairs={{0,28},{4,0},{8,4},{12,8},{16,12},{20,16},{24,20},{28,24},{1,29},{... | collective-permute-start | bytes 129032 | tf_op jit(solution)/shard_map/ppermute | solution.py:458
  68.1 0.2 collective-permute-start.17
  68.4 3.1 %collective-permute-done.17.cdiag = bf16[48,384]{1,0:T(8,128)(2,1)S(1)} collective-permute-done((bf16[48,384]{1,0:T(8,128)(2,1)S(1)}, bf16[48,384]{1,0:T(8,128)(2,1)S(1)}, u32[]{:S(2)}, u32[]{:S(2)}) %collective-permute-start.17) | collective-permute-done | bytes 36896 | tf_op jit(solution)/shard_map/ppermute | solution.py:467
  71.5 0.4 collective-permute-start.18
  72.0 1.3 %shard_map.241 = (bf16[576,192]{1,0:T(8,128)(2,1)}, bf16[2,6,12,384]{3,2,1,0:T(8,128)(2,1)S(1)}) custom-call(bf16[576,192]{1,0:T(8,128)(2,1)S(1)} %get-tuple-element.74.res_ref, bf16[112,192]{1,0:T(8,128)(2,1)S(1)} %collective-permute-done.12.lon_ref, bf16[112,192]{1,0:T(8,128)(2,1)S(1)} %collective-permute-done.13.lat_ref, ...), custom_call_target="tpu_custom_call" | custom-call | flops 300000000 | bytes 807744 | tf_op jit(solution)/shard_map/pallas_call | solution.py:445
  73.3 0.7 copy.36
  74.1 1.0 %collective-permute-start.22 = (bf16[192,276]{1,0:T(8,128)(2,1)S(1)}, bf16[192,276]{1,0:T(8,128)(2,1)S(1)}, u32[]{:S(2)}, u32[]{:S(2)}) collective-permute-start(bf16[192,276]{1,0:T(8,128)(2,1)S(1)} %add_convert_fusion.1), channel_id=1, source_target_pairs={{0,8},{4,12},{8,0},{12,4},{16,24},{20,28},{24,16},{28,20},{1,9},{5... | collective-permute-start | bytes 317960 | tf_op jit(solution)/shard_map/ppermute | solution.py:483
  75.1 2.8 %collective-permute-done.18 = bf16[192,276]{1,0:T(8,128)(2,1)S(1)} collective-permute-done((bf16[192,276]{1,0:T(8,128)(2,1)S(1)}, bf16[192,276]{1,0:T(8,128)(2,1)S(1)}, u32[]{:S(2)}, u32[]{:S(2)}) %collective-permute-start.18) | collective-permute-done | bytes 106016 | tf_op jit(solution)/shard_map/ppermute | solution.py:483
  78.0 2.6 %collective-permute-done.22 = bf16[192,276]{1,0:T(8,128)(2,1)S(1)} collective-permute-done((bf16[192,276]{1,0:T(8,128)(2,1)S(1)}, bf16[192,276]{1,0:T(8,128)(2,1)S(1)}, u32[]{:S(2)}, u32[]{:S(2)}) %collective-permute-start.22) | collective-permute-done | bytes 106016 | tf_op jit(solution)/shard_map/ppermute | solution.py:483
  80.7 2.3 %collective-permute-start.23 = (bf16[192,276]{1,0:T(8,128)(2,1)S(1)}, bf16[192,276]{1,0:T(8,128)(2,1)S(1)}, u32[]{:S(2)}, u32[]{:S(2)}) collective-permute-start(bf16[192,276]{1,0:T(8,128)(2,1)S(1)} %add_convert_fusion), channel_id=1, source_target_pairs={{0,16},{4,20},{8,24},{12,28},{16,0},{20,4},{24,8},{28,12},{1,17},{... | collective-permute-start | bytes 317960 | tf_op jit(solution)/shard_map/ppermute | solution.py:483
  83.0 1.3 %collective-permute-done.19 = bf16[192,276]{1,0:T(8,128)(2,1)S(1)} collective-permute-done((bf16[192,276]{1,0:T(8,128)(2,1)S(1)}, bf16[192,276]{1,0:T(8,128)(2,1)S(1)}, u32[]{:S(2)}, u32[]{:S(2)}) %collective-permute-start.19) | collective-permute-done | bytes 106016 | tf_op jit(solution)/shard_map/ppermute | solution.py:483
  84.3 1.8 %collective-permute-start.20 = (bf16[192,276]{1,0:T(8,128)(2,1)S(1)}, bf16[192,276]{1,0:T(8,128)(2,1)S(1)}, u32[]{:S(2)}, u32[]{:S(2)}) collective-permute-start(bf16[192,276]{1,0:T(8,128)(2,1)S(1)} %add_convert_fusion.2), channel_id=1, source_target_pairs={{0,16},{4,20},{8,24},{12,28},{16,0},{20,4},{24,8},{28,12},{1,17},{... | collective-permute-start | bytes 317960 | tf_op jit(solution)/shard_map/ppermute | solution.py:483
  86.1 8.5 %collective-permute-done.23 = bf16[192,276]{1,0:T(8,128)(2,1)S(1)} collective-permute-done((bf16[192,276]{1,0:T(8,128)(2,1)S(1)}, bf16[192,276]{1,0:T(8,128)(2,1)S(1)}, u32[]{:S(2)}, u32[]{:S(2)}) %collective-permute-start.23) | collective-permute-done | bytes 106016 | tf_op jit(solution)/shard_map/ppermute | solution.py:483
  94.7 1.0 %reshape.163 = f32[1,12,3312]{2,0,1:T(1,128)} reshape(f32[12,12,276]{2,1,0:T(8,128)S(1)} %bitcast.16) | data formatting | bytes 317952 | tf_op jit(solution)/shard_map/reshape | solution.py:490
  95.7 1.3 %collective-permute-done.20 = bf16[192,276]{1,0:T(8,128)(2,1)S(1)} collective-permute-done((bf16[192,276]{1,0:T(8,128)(2,1)S(1)}, bf16[192,276]{1,0:T(8,128)(2,1)S(1)}, u32[]{:S(2)}, u32[]{:S(2)}) %collective-permute-start.20) | collective-permute-done | bytes 106016 | tf_op jit(solution)/shard_map/ppermute | solution.py:483
  97.0 0.2 reshape.161
  97.2 0.7 copy.37
  (87 shorter events, 0.9 us)
Async XLA Ops:
  0.6 11.0 %copy-start.16 = (s32[144,1]{1,0:T(8,128)S(1)}, s32[144,1]{1,0:T(8,128)}, u32[]{:S(2)}) copy-start(s32[144,1]{1,0:T(8,128)} %constant.87.slot_ref) | copy-start | bytes 1732
  0.6 11.0 %copy-start.18 = (s32[1,144]{1,0:T(1,128)S(1)}, s32[1,144]{1,0:T(1,128)}, u32[]{:S(2)}) copy-start(s32[1,144]{1,0:T(1,128)} %constant.86.base_ref) | copy-start | bytes 1732
  0.7 10.9 %copy-start.24 = (bf16[2,6,12,384]{3,0,2,1:T(2,128)(2,1)S(1)}, bf16[2,6,12,384]{3,0,2,1:T(2,128)(2,1)}, u32[]{:S(2)}) copy-start(bf16[2,6,12,384]{3,0,2,1:T(2,128)(2,1)} %param.37) | copy-start | bytes 331780
  1.6 20.3 %collective-permute-start = (bf16[144,192]{1,0:T(8,128)(2,1)S(1)}, bf16[144,192]{1,0:T(8,128)(2,1)S(1)}, u32[]{:S(2)}, u32[]{:S(2)}) collective-permute-start(bf16[144,192]{1,0:T(8,128)(2,1)S(1)} %bitcast.18), channel_id=1, source_target_pairs={{0,4},{4,8},{8,12},{12,16},{16,20},{20,24},{24,28},{28,0},{1,5},{5... | collective-permute-start | bytes 165896 | tf_op jit(solution)/shard_map/ppermute | solution.py:458
  5.5 16.4 %collective-permute-start.1 = (bf16[144,192]{1,0:T(8,128)(2,1)S(1)}, bf16[144,192]{1,0:T(8,128)(2,1)S(1)}, u32[]{:S(2)}, u32[]{:S(2)}) collective-permute-start(bf16[144,192]{1,0:T(8,128)(2,1)S(1)} %bitcast.19), channel_id=1, source_target_pairs={{0,1},{1,2},{2,3},{3,0},{4,5},{5,6},{6,7},{7,4},{8,9},{9,10},{10,1... | collective-permute-start | bytes 165896 | tf_op jit(solution)/shard_map/ppermute | solution.py:461
  6.2 13.8 %collective-permute-start.2 = (bf16[48,192]{1,0:T(8,128)(2,1)S(1)}, bf16[48,192]{1,0:T(8,128)(2,1)S(1)}, u32[]{:S(2)}, u32[]{:S(2)}) collective-permute-start(bf16[48,192]{1,0:T(8,128)(2,1)S(1)} %bitcast.20), channel_id=1, source_target_pairs={{0,5},{1,6},{2,7},{3,4},{4,9},{5,10},{6,11},{7,8},{8,13},{9,14},{1... | collective-permute-start | bytes 55304 | tf_op jit(solution)/shard_map/ppermute | solution.py:467
  11.7 7.7 %copy-start.25 = (s32[2,12,24]{2,0,1:T(2,128)S(1)}, s32[2,12,24]{2,0,1:T(2,128)}, u32[]{:S(2)}) copy-start(s32[2,12,24]{2,0,1:T(2,128)} %param.25) | copy-start | bytes 6916
  11.7 7.8 %copy-start.26 = (s32[2,2]{1,0:T(2,128)S(1)}, s32[2,2]{1,0:T(2,128)}, u32[]{:S(2)}) copy-start(s32[2,2]{1,0:T(2,128)} %constant.69.clone.1) | copy-start | bytes 52
  11.7 8.2 %copy-start.23 = (bf16[768,192]{0,1:T(8,128)(2,1)S(1)}, bf16[768,192]{0,1:T(8,128)(2,1)}, u32[]{:S(2)}) copy-start(bf16[768,192]{0,1:T(8,128)(2,1)} %param.29) | copy-start | bytes 884740
  11.7 10.2 %copy-start = (bf16[2,12,24,192]{3,2,1,0:T(8,128)(2,1)S(1)}, bf16[2,12,24,192]{3,2,1,0:T(8,128)(2,1)}, u32[]{:S(2)}) copy-start(bf16[2,12,24,192]{3,2,1,0:T(8,128)(2,1)} %param.24) | copy-start | bytes 663556
  11.7 10.2 %copy-start.6 = (bf16[192,768]{1,0:T(8,128)(2,1)S(1)}, bf16[192,768]{1,0:T(8,128)(2,1)}, u32[]{:S(2)}) copy-start(bf16[192,768]{1,0:T(8,128)(2,1)} %up_ref.5) | copy-start | bytes 884740
  11.7 10.2 %copy-start.7 = (bf16[192,576]{1,0:T(8,128)(2,1)S(1)}, bf16[192,576]{1,0:T(8,128)(2,1)}, u32[]{:S(2)}) copy-start(bf16[192,576]{1,0:T(8,128)(2,1)} %qkv_ref.5) | copy-start | bytes 663556
  11.7 10.2 %copy-start.8 = (bf16[192,192]{1,0:T(8,128)(2,1)S(1)}, bf16[192,192]{1,0:T(8,128)(2,1)}, u32[]{:S(2)}) copy-start(bf16[192,192]{1,0:T(8,128)(2,1)} %proj_ref.5) | copy-start | bytes 221188
  11.8 10.2 %copy-start.13 = (s32[576,1]{1,0:T(8,128)S(1)}, s32[576,1]{1,0:T(8,128)}, u32[]{:S(2)}) copy-start(s32[576,1]{1,0:T(8,128)} %constant.85.arrive_ref) | copy-start | bytes 6916
  17.8 15.1 %collective-permute-start.6 = (bf16[48,384]{1,0:T(8,128)(2,1)S(1)}, bf16[48,384]{1,0:T(8,128)(2,1)S(1)}, u32[]{:S(2)}, u32[]{:S(2)}) collective-permute-start(bf16[48,384]{1,0:T(8,128)(2,1)S(1)} %get-tuple-element.58), channel_id=1, source_target_pairs={{0,4},{4,8},{8,12},{12,16},{16,20},{20,24},{24,28},{28,0},{1,5},{5... | collective-permute-start | bytes 110600 | tf_op jit(solution)/shard_map/ppermute | solution.py:458
  19.4 16.4 %collective-permute-start.7 = (bf16[48,384]{1,0:T(8,128)(2,1)S(1)}, bf16[48,384]{1,0:T(8,128)(2,1)S(1)}, u32[]{:S(2)}, u32[]{:S(2)}) collective-permute-start(bf16[48,384]{1,0:T(8,128)(2,1)S(1)} %get-tuple-element.59), channel_id=1, source_target_pairs={{0,1},{1,2},{2,3},{3,0},{4,5},{5,6},{6,7},{7,4},{8,9},{9,10},{10,1... | collective-permute-start | bytes 110600 | tf_op jit(solution)/shard_map/ppermute | solution.py:461
  20.1 15.7 %collective-permute-start.8 = (bf16[48,384]{1,0:T(8,128)(2,1)S(1)}, bf16[48,384]{1,0:T(8,128)(2,1)S(1)}, u32[]{:S(2)}, u32[]{:S(2)}) collective-permute-start(bf16[48,384]{1,0:T(8,128)(2,1)S(1)} %get-tuple-element.60), channel_id=1, source_target_pairs={{0,5},{1,6},{2,7},{3,4},{4,9},{5,10},{6,11},{7,8},{8,13},{9,14},{1... | collective-permute-start | bytes 110600 | tf_op jit(solution)/shard_map/ppermute | solution.py:467
  23.4 16.3 %copy-start.1 = (bf16[384,1536]{1,0:T(8,128)(2,1)S(1)}, bf16[384,1536]{1,0:T(8,128)(2,1)}, u32[]{:S(2)}) copy-start(bf16[384,1536]{1,0:T(8,128)(2,1)} %up_ref.4) | copy-start | bytes 3538948
  23.4 16.3 %copy-start.2 = (bf16[1536,384]{1,0:T(8,128)(2,1)S(1)}, bf16[1536,384]{1,0:T(8,128)(2,1)}, u32[]{:S(2)}) copy-start(bf16[1536,384]{1,0:T(8,128)(2,1)} %down_ref.3) | copy-start | bytes 3538948
  23.4 16.3 %copy-start.3 = (bf16[384,1152]{1,0:T(8,128)(2,1)S(1)}, bf16[384,1152]{1,0:T(8,128)(2,1)}, u32[]{:S(2)}) copy-start(bf16[384,1152]{1,0:T(8,128)(2,1)} %qkv_ref.4) | copy-start | bytes 2654212
  23.4 16.4 %copy-start.4 = (bf16[768,384]{1,0:T(8,128)(2,1)S(1)}, bf16[768,384]{1,0:T(8,128)(2,1)}, u32[]{:S(2)}) copy-start(bf16[768,384]{1,0:T(8,128)(2,1)} %reduce_ref.1) | copy-start | bytes 1769476
  23.5 16.4 %copy-start.5 = (bf16[384,384]{1,0:T(8,128)(2,1)S(1)}, bf16[384,384]{1,0:T(8,128)(2,1)}, u32[]{:S(2)}) copy-start(bf16[384,384]{1,0:T(8,128)(2,1)} %proj_ref.4) | copy-start | bytes 884740
  23.5 16.4 %copy-start.9 = (s32[608,1]{1,0:T(8,128)S(1)}, s32[608,1]{1,0:T(8,128)}, u32[]{:S(2)}) copy-start(s32[608,1]{1,0:T(8,128)} %constant.89.split_ref) | copy-start | bytes 7300
  23.5 16.4 %copy-start.12 = (s32[576,1]{1,0:T(8,128)S(1)}, s32[576,1]{1,0:T(8,128)}, u32[]{:S(2)}) copy-start(s32[576,1]{1,0:T(8,128)} %constant.88.merge_ref) | copy-start | bytes 6916
  23.5 16.3 %copy-start.15 = (s32[144,1]{1,0:T(8,128)S(1)}, s32[144,1]{1,0:T(8,128)}, u32[]{:S(2)}) copy-start(s32[144,1]{1,0:T(8,128)} %constant.90.base_ref) | copy-start | bytes 1732
  23.5 16.3 %copy-start.17 = (s32[1,144]{1,0:T(1,128)S(1)}, s32[1,144]{1,0:T(1,128)}, u32[]{:S(2)}) copy-start(s32[1,144]{1,0:T(1,128)} %constant.91.slot_ref) | copy-start | bytes 1732
  23.5 16.3 %copy-start.22 = (f32[1728,144]{1,0:T(8,128)S(1)}, f32[1728,144]{1,0:T(8,128)}, u32[]{:S(2)}) copy-start(f32[1728,144]{1,0:T(8,128)} %copy-done.21) | copy-start | bytes 2985988
  31.3 8.4 %collective-permute-start.3 = (bf16[112,192]{1,0:T(8,128)(2,1)S(1)}, bf16[112,192]{1,0:T(8,128)(2,1)S(1)}, u32[]{:S(2)}, u32[]{:S(2)}) collective-permute-start(bf16[112,192]{1,0:T(8,128)(2,1)S(1)} %get-tuple-element.53), channel_id=1, source_target_pairs={{0,4},{4,8},{8,12},{12,16},{16,20},{20,24},{24,28},{28,0},{1,5},{5... | collective-permute-start | bytes 129032 | tf_op jit(solution)/shard_map/ppermute | solution.py:458
  32.9 6.9 %collective-permute-start.4 = (bf16[112,192]{1,0:T(8,128)(2,1)S(1)}, bf16[112,192]{1,0:T(8,128)(2,1)S(1)}, u32[]{:S(2)}, u32[]{:S(2)}) collective-permute-start(bf16[112,192]{1,0:T(8,128)(2,1)S(1)} %get-tuple-element.54), channel_id=1, source_target_pairs={{0,1},{1,2},{2,3},{3,0},{4,5},{5,6},{6,7},{7,4},{8,9},{9,10},{10,1... | collective-permute-start | bytes 129032 | tf_op jit(solution)/shard_map/ppermute | solution.py:461
  32.9 6.8 %collective-permute-start.5 = (bf16[48,192]{1,0:T(8,128)(2,1)S(1)}, bf16[48,192]{1,0:T(8,128)(2,1)S(1)}, u32[]{:S(2)}, u32[]{:S(2)}) collective-permute-start(bf16[48,192]{1,0:T(8,128)(2,1)S(1)} %get-tuple-element.55), channel_id=1, source_target_pairs={{0,5},{1,6},{2,7},{3,4},{4,9},{5,10},{6,11},{7,8},{8,13},{9,14},{1... | collective-permute-start | bytes 55304 | tf_op jit(solution)/shard_map/ppermute | solution.py:467
  39.9 15.7 %copy-start.11 = (s32[576,1]{1,0:T(8,128)S(1)}, s32[576,1]{1,0:T(8,128)}, u32[]{:S(2)}) copy-start(s32[576,1]{1,0:T(8,128)} %constant.92.back_ref) | copy-start | bytes 6916
  49.2 6.3 %collective-permute-start.10 = (bf16[112,192]{1,0:T(8,128)(2,1)S(1)}, bf16[112,192]{1,0:T(8,128)(2,1)S(1)}, u32[]{:S(2)}, u32[]{:S(2)}) collective-permute-start(bf16[112,192]{1,0:T(8,128)(2,1)S(1)} %get-tuple-element.62), channel_id=1, source_target_pairs={{0,3},{1,0},{2,1},{3,2},{4,7},{5,4},{6,5},{7,6},{8,11},{9,8},{10,9... | collective-permute-start | bytes 129032 | tf_op jit(solution)/shard_map/ppermute | solution.py:461
  50.5 5.1 %collective-permute-start.9 = (bf16[112,192]{1,0:T(8,128)(2,1)S(1)}, bf16[112,192]{1,0:T(8,128)(2,1)S(1)}, u32[]{:S(2)}, u32[]{:S(2)}) collective-permute-start(bf16[112,192]{1,0:T(8,128)(2,1)S(1)} %get-tuple-element.61), channel_id=1, source_target_pairs={{0,28},{4,0},{8,4},{12,8},{16,12},{20,16},{24,20},{28,24},{1,29},{... | collective-permute-start | bytes 129032 | tf_op jit(solution)/shard_map/ppermute | solution.py:458
  51.0 3.5 %collective-permute-start.11 = (bf16[48,192]{1,0:T(8,128)(2,1)S(1)}, bf16[48,192]{1,0:T(8,128)(2,1)S(1)}, u32[]{:S(2)}, u32[]{:S(2)}) collective-permute-start(bf16[48,192]{1,0:T(8,128)(2,1)S(1)} %get-tuple-element.63), channel_id=1, source_target_pairs={{0,31},{1,28},{2,29},{3,30},{4,3},{5,0},{6,1},{7,2},{8,7},{9,4},{1... | collective-permute-start | bytes 55304 | tf_op jit(solution)/shard_map/ppermute | solution.py:467
  52.2 21.9 %collective-permute-start.21 = (bf16[192,276]{1,0:T(8,128)(2,1)S(1)}, bf16[192,276]{1,0:T(8,128)(2,1)S(1)}, u32[]{:S(2)}, u32[]{:S(2)}) collective-permute-start(bf16[192,276]{1,0:T(8,128)(2,1)S(1)} %get-tuple-element.85), channel_id=1, source_target_pairs={{0,4},{4,0},{8,12},{12,8},{16,20},{20,16},{24,28},{28,24},{1,5},{5... | collective-permute-start | bytes 317960 | tf_op jit(solution)/shard_map/ppermute | solution.py:483
  52.7 15.4 %collective-permute-start.15 = (bf16[48,384]{1,0:T(8,128)(2,1)S(1)}, bf16[48,384]{1,0:T(8,128)(2,1)S(1)}, u32[]{:S(2)}, u32[]{:S(2)}) collective-permute-start(bf16[48,384]{1,0:T(8,128)(2,1)S(1)} %get-tuple-element.79), channel_id=1, source_target_pairs={{0,28},{4,0},{8,4},{12,8},{16,12},{20,16},{24,20},{28,24},{1,29},{... | collective-permute-start | bytes 110600 | tf_op jit(solution)/shard_map/ppermute | solution.py:458
  54.5 13.8 %collective-permute-start.16 = (bf16[48,384]{1,0:T(8,128)(2,1)S(1)}, bf16[48,384]{1,0:T(8,128)(2,1)S(1)}, u32[]{:S(2)}, u32[]{:S(2)}) collective-permute-start(bf16[48,384]{1,0:T(8,128)(2,1)S(1)} %get-tuple-element.80), channel_id=1, source_target_pairs={{0,3},{1,0},{2,1},{3,2},{4,7},{5,4},{6,5},{7,6},{8,11},{9,8},{10,9... | collective-permute-start | bytes 110600 | tf_op jit(solution)/shard_map/ppermute | solution.py:461
  55.5 16.5 %copy-start.10 = (s32[576,1]{1,0:T(8,128)S(1)}, s32[576,1]{1,0:T(8,128)}, u32[]{:S(2)}) copy-start(s32[576,1]{1,0:T(8,128)} %constant.93.leave_ref) | copy-start | bytes 6916
  55.5 16.5 %copy-start.14 = (s32[144,1]{1,0:T(8,128)S(1)}, s32[144,1]{1,0:T(8,128)}, u32[]{:S(2)}) copy-start(s32[144,1]{1,0:T(8,128)} %constant.94.result_ref) | copy-start | bytes 1732
  64.0 8.0 %collective-permute-start.12 = (bf16[112,192]{1,0:T(8,128)(2,1)S(1)}, bf16[112,192]{1,0:T(8,128)(2,1)S(1)}, u32[]{:S(2)}, u32[]{:S(2)}) collective-permute-start(bf16[112,192]{1,0:T(8,128)(2,1)S(1)} %get-tuple-element.75), channel_id=1, source_target_pairs={{0,28},{4,0},{8,4},{12,8},{16,12},{20,16},{24,20},{28,24},{1,29},{... | collective-permute-start | bytes 129032 | tf_op jit(solution)/shard_map/ppermute | solution.py:458
  68.1 3.8 %collective-permute-start.13 = (bf16[112,192]{1,0:T(8,128)(2,1)S(1)}, bf16[112,192]{1,0:T(8,128)(2,1)S(1)}, u32[]{:S(2)}, u32[]{:S(2)}) collective-permute-start(bf16[112,192]{1,0:T(8,128)(2,1)S(1)} %get-tuple-element.76), channel_id=1, source_target_pairs={{0,3},{1,0},{2,1},{3,2},{4,7},{5,4},{6,5},{7,6},{8,11},{9,8},{10,9... | collective-permute-start | bytes 129032 | tf_op jit(solution)/shard_map/ppermute | solution.py:461
  68.1 3.4 %collective-permute-start.17 = (bf16[48,384]{1,0:T(8,128)(2,1)S(1)}, bf16[48,384]{1,0:T(8,128)(2,1)S(1)}, u32[]{:S(2)}, u32[]{:S(2)}) collective-permute-start(bf16[48,384]{1,0:T(8,128)(2,1)S(1)} %get-tuple-element.81), channel_id=1, source_target_pairs={{0,31},{1,28},{2,29},{3,30},{4,3},{5,0},{6,1},{7,2},{8,7},{9,4},{1... | collective-permute-start | bytes 110600 | tf_op jit(solution)/shard_map/ppermute | solution.py:467
  68.4 3.6 %collective-permute-start.14 = (bf16[48,192]{1,0:T(8,128)(2,1)S(1)}, bf16[48,192]{1,0:T(8,128)(2,1)S(1)}, u32[]{:S(2)}, u32[]{:S(2)}) collective-permute-start(bf16[48,192]{1,0:T(8,128)(2,1)S(1)} %get-tuple-element.77), channel_id=1, source_target_pairs={{0,31},{1,28},{2,29},{3,30},{4,3},{5,0},{6,1},{7,2},{8,7},{9,4},{1... | collective-permute-start | bytes 55304 | tf_op jit(solution)/shard_map/ppermute | solution.py:467
  71.5 6.4 %collective-permute-start.18 = (bf16[192,276]{1,0:T(8,128)(2,1)S(1)}, bf16[192,276]{1,0:T(8,128)(2,1)S(1)}, u32[]{:S(2)}, u32[]{:S(2)}) collective-permute-start(bf16[192,276]{1,0:T(8,128)(2,1)S(1)} %get-tuple-element.84), channel_id=1, source_target_pairs={{0,4},{4,0},{8,12},{12,8},{16,20},{20,16},{24,28},{28,24},{1,5},{5... | collective-permute-start | bytes 317960 | tf_op jit(solution)/shard_map/ppermute | solution.py:483
  74.1 6.5 %collective-permute-start.22 = (bf16[192,276]{1,0:T(8,128)(2,1)S(1)}, bf16[192,276]{1,0:T(8,128)(2,1)S(1)}, u32[]{:S(2)}, u32[]{:S(2)}) collective-permute-start(bf16[192,276]{1,0:T(8,128)(2,1)S(1)} %add_convert_fusion.1), channel_id=1, source_target_pairs={{0,8},{4,12},{8,0},{12,4},{16,24},{20,28},{24,16},{28,20},{1,9},{5... | collective-permute-start | bytes 317960 | tf_op jit(solution)/shard_map/ppermute | solution.py:483
  77.9 6.3 %collective-permute-start.19 = (bf16[192,276]{1,0:T(8,128)(2,1)S(1)}, bf16[192,276]{1,0:T(8,128)(2,1)S(1)}, u32[]{:S(2)}, u32[]{:S(2)}) collective-permute-start(bf16[192,276]{1,0:T(8,128)(2,1)S(1)} %add_convert_fusion.3), channel_id=1, source_target_pairs={{0,8},{4,12},{8,0},{12,4},{16,24},{20,28},{24,16},{28,20},{1,9},{5... | collective-permute-start | bytes 317960 | tf_op jit(solution)/shard_map/ppermute | solution.py:483
  80.7 14.0 %collective-permute-start.23 = (bf16[192,276]{1,0:T(8,128)(2,1)S(1)}, bf16[192,276]{1,0:T(8,128)(2,1)S(1)}, u32[]{:S(2)}, u32[]{:S(2)}) collective-permute-start(bf16[192,276]{1,0:T(8,128)(2,1)S(1)} %add_convert_fusion), channel_id=1, source_target_pairs={{0,16},{4,20},{8,24},{12,28},{16,0},{20,4},{24,8},{28,12},{1,17},{... | collective-permute-start | bytes 317960 | tf_op jit(solution)/shard_map/ppermute | solution.py:483
  84.3 12.7 %collective-permute-start.20 = (bf16[192,276]{1,0:T(8,128)(2,1)S(1)}, bf16[192,276]{1,0:T(8,128)(2,1)S(1)}, u32[]{:S(2)}, u32[]{:S(2)}) collective-permute-start(bf16[192,276]{1,0:T(8,128)(2,1)S(1)} %add_convert_fusion.2), channel_id=1, source_target_pairs={{0,16},{4,20},{8,24},{12,28},{16,0},{20,4},{24,8},{28,12},{1,17},{... | collective-permute-start | bytes 317960 | tf_op jit(solution)/shard_map/ppermute | solution.py:483
  (3 other events, 3.9 us)
where the time goes:
time: 98.3 us; the launch traced here: 97.9 us
  Pallas kernels  30.5 us (31%)
  starting transfers between devices  29.3 us (30%)
  waiting for transfers between devices  24 us (24%)
  local copies, waits for them, and re-layouts  11 us (11%)
  other arithmetic  1.91 us (2%)
  between operations  1.19 us (1%)
    pallas_call x5, Pallas kernels, run(): pl.pallas_call(kernel, out_shape=shapes, scratch_shapes=[pltpu.VMEM(shape...  30.5 us
    ppermute x6, waiting for transfers between devices, lon_total(): other = lax.ppermute(kept, 'lon', [(s, s ^ step) for s in range(count)])  16.5 us
    ppermute x6, starting transfers between devices, move(): return lax.ppermute(value, 'lon', pairs)  12.2 us
    ppermute x6, starting transfers between devices, move(): return lax.ppermute(value, ('lon', 'lat'), pairs)  8.73 us
    ppermute x6, waiting for transfers between devices, move(): return lax.ppermute(value, ('lon', 'lat'), pairs)  7.52 us
    unnamed x59, local copies, waits for them, and re-layouts  6.68 us
    ppermute x6, starting transfers between devices, lon_total(): other = lax.ppermute(kept, 'lon', [(s, s ^ step) for s in range(count)])  6.2 us
    ppermute x6, starting transfers between devices, move(): return lax.ppermute(value, 'lat', pairs)  2.19 us
  transfers between devices with their start and end apart: 24, of which 8 were waited for; matrix products, arithmetic and copies ran while one was open for 7% of the time, Pallas kernels for 22%

commit v1 on v0

--- a/solution.py
+++ b/solution.py
@@ -16,7 +16,7 @@
 SPAN = 23
 ENTRIES = 276
 LOG2E = math.log2(math.e)
-VMEM = 32 * 1024 * 1024
+VMEM = 20 * 1024 * 1024
 f32 = jnp.float32
 bf16 = jnp.bfloat16
 
@@ -36,6 +36,7 @@
 
 def index_maps():
     arrive = np.zeros(576, np.int32)
+    edge = np.full(272, -1, np.int32)
     merge = np.zeros(576, np.int32)
     split = np.full(608, -1, np.int32)
     back = np.zeros(576, np.int32)
@@ -48,14 +49,16 @@
                     arrive[here] = z * 288 + (i - 3) * 24 + j - 6
                     came = fine_spot(z, i - 3, j - 6)
                 elif i >= 3:
-                    arrive[here] = 576 + z * 72 + (i - 3) * 8 + 2 + j
                     came = 576 + (i - 3) // 3 * QUAD + in_quad(z, i, j)
+                    edge[came - 576] = z * 288 + (i - 3) * 24 + 18 + j
                 elif j >= 6:
-                    arrive[here] = 720 + z * 72 + i * 24 + j - 6
                     came = 688 + (j - 6) // 6 * QUAD + in_quad(z, i, j)
+                    edge[came - 576] = z * 288 + (i + 9) * 24 + j - 6
                 else:
-                    arrive[here] = 864 + z * 24 + i * 8 + 2 + j
                     came = 800 + in_quad(z, i, j)
+                    edge[came - 576] = z * 288 + (i + 9) * 24 + 18 + j
+                if came >= 576:
+                    arrive[here] = came
                 part = (i % 2 + j % 2 * 2) * WIN + spot(z, i // 2, j // 2)
                 merge[part] = came
                 if i >= 3 and j >= 6:
@@ -90,10 +93,10 @@
                 here = spot(z, i, j)
                 base[here] = (z * 6 + i) * SPAN + 11 - j
                 row_slot[here] = j * 16 + z * 6 + i
-    return arrive, merge, split, back, leave, result, base, row_slot
-
-
-ARRIVE, MERGE, SPLIT, BACK, LEAVE, RESULT, BASE, ROW_SLOT = index_maps()
+    return arrive, edge, merge, split, back, leave, result, base, row_slot
+
+
+ARRIVE, EDGE, MERGE, SPLIT, BACK, LEAVE, RESULT, BASE, ROW_SLOT = index_maps()
 
 
 def one_hot(column, width):
@@ -211,6 +214,13 @@
     )
 
 
+def swap_rows():
+    row = lax.broadcasted_iota(jnp.int32, (192, 192), 0)
+    return jnp.where(
+        lax.broadcasted_iota(jnp.int32, (192, 192), 1) == row % 16 * 16 + row // 16, 1.0, 0.0
+    ).astype(bf16)
+
+
 def table_grad(score_ref, base_ref, slot_ref, rows_ref):
     regroup = jnp.where(
         lax.broadcasted_iota(jnp.int32, (192, WIN), 0) == slot_ref[...], 1.0, 0.0
@@ -221,7 +231,12 @@
     total = jnp.zeros((192, ENTRIES), f32)
     for column in range(12):
         total += mm(rows_ref[column], one_hot(base_ref[...] + column, ENTRIES))
-    return total
+    swapped = mm(swap_rows(), total.astype(bf16))
+    halves = [
+        jnp.concatenate([swapped[a * 16 : a * 16 + 12] for a in range(start, start + 6)], axis=1)
+        for start in (0, 6)
+    ]
+    return jnp.concatenate(halves, axis=0).astype(bf16)
 
 
 def pack(pieces, rows):
@@ -236,22 +251,37 @@
     return windows[qi // 2 * 2 + qj // 2][part : part + QUAD]
 
 
-def bias_kernel(table_ref, base_ref, slot_ref, grad_ref, fine_ref, coarse_ref, g0, g1, g2, g3, held):
-    table = table_ref[...]
+def edge_kernel(tokens_ref, edge_ref, slon_ref, slat_ref, sdiag_ref):
+    moved = mm(one_hot(edge_ref[...], 576), tokens_ref[...]).astype(bf16)
+    slon_ref[...] = moved[0:112]
+    slat_ref[...] = moved[112:224]
+    sdiag_ref[...] = moved[224:272]
+
+
+def expand(table_ref, base_ref, slot_ref, out_ref, held):
+    table = jnp.concatenate([table_ref[:, b, :] for b in range(table_ref.shape[1])], axis=0)
+    filler = jnp.zeros((4, ENTRIES), f32)
+    pieces = []
+    for a in range(12):
+        pieces += [table[:, a * ENTRIES : (a + 1) * ENTRIES], filler]
+    table = jnp.concatenate(pieces, axis=0)
     high = table.astype(bf16)
     low = (table - high.astype(f32)).astype(bf16)
+    swap = swap_rows()
+    high, low = mm(swap, high).astype(bf16), mm(swap, low).astype(bf16)
     entry = lax.broadcasted_iota(jnp.int32, (ENTRIES, WIN), 0)
     for column in range(12):
         picker = jnp.where(entry == base_ref[...] + column, 1.0, 0.0).astype(bf16)
-        held[:, 0, column] = mm(high, picker).astype(bf16).reshape(24, 16, WIN)
-        held[:, 1, column] = mm(low, picker).astype(bf16).reshape(24, 16, WIN)
+        held[:, 0, column] = mm(high, picker).astype(bf16).reshape(12, 16, WIN)
+        held[:, 1, column] = mm(low, picker).astype(bf16).reshape(12, 16, WIN)
     once = one_hot(slot_ref[...], 192)
-    for h in range(24):
-        place = pl.ds(h % 12 * WIN, WIN)
-        target = fine_ref if h < 12 else coarse_ref
-        target[place, :] = (
+    for h in range(12):
+        out_ref[pl.ds(h * WIN, WIN), :] = (
             mm(once, held[h, 0].reshape(192, WIN)) + mm(once, held[h, 1].reshape(192, WIN))
         ) * LOG2E
+
+
+def fine_bias_kernel(table_ref, base_ref, slot_ref, grad_ref, out_ref, g0, g1, g2, g3, held):
     for index, out in enumerate((g0, g1, g2, g3)):
         hi, hj = index // 2, index % 2
         pieces = [
@@ -260,6 +290,23 @@
             for row in range(3)
         ]
         out[...] = pack(pieces, 48)
+    expand(table_ref, base_ref, slot_ref, out_ref, held)
+
+
+def coarse_bias_kernel(table_ref, base_ref, slot_ref, out_ref, held):
+    expand(table_ref, base_ref, slot_ref, out_ref, held)
+
+
+def coarse_table_kernel(score_ref, base_ref, slot_ref, table_ref, rows_ref):
+    table_ref[...] = table_grad(score_ref, base_ref, slot_ref, rows_ref)
+
+
+def table_sum_kernel(kept_ref, other_ref, out_ref):
+    total = kept_ref[...].astype(f32) + other_ref[...].astype(f32)
+    total = jnp.concatenate([total[0:12], total[12:24]], axis=1)
+    heads = out_ref.shape[0]
+    for b in range(out_ref.shape[1]):
+        out_ref[:, b, :] = total[b * heads : (b + 1) * heads]
 
 
 def fine_kernel(
@@ -270,15 +317,15 @@
     source,
 ):
     source[0:576] = tokens_ref[...]
-    source[576:720] = lon_ref[...]
-    source[720:864] = lat_ref[...]
-    source[864:912] = diag_ref[...]
+    source[576:688] = lon_ref[...]
+    source[688:800] = lat_ref[...]
+    source[800:848] = diag_ref[...]
     everything = source[...]
     w_qkv = qkv_ref[...]
     bases = []
     for w in range(4):
         rows = pl.ds(w * WIN, WIN)
-        base = mm(one_hot(arrive_ref[rows, :], 912), everything)
+        base = mm(one_hot(arrive_ref[rows, :], 848), everything)
         normed, scale = norm(base)
         normed = normed.astype(bf16)
         n1_ref[rows, :] = normed
@@ -312,9 +359,9 @@
 def coarse_kernel(
     res_ref, lon_ref, lat_ref, diag_ref, merge_ref, split_ref, bias_ref, mask_ref,
     gloc_ref, glon_ref, glat_ref, gdiag_ref,
-    reduce_ref, qkv_ref, proj_ref, up_ref, down_ref, base_ref, slot_ref,
-    c0, c1, c2, c3, dlon_ref, dlat_ref, ddiag_ref, dloc_ref, table_ref,
-    source, probs_ref, score_ref, rows_ref, parts_ref,
+    reduce_ref, qkv_ref, proj_ref, up_ref, down_ref,
+    c0, c1, c2, c3, dlon_ref, dlat_ref, ddiag_ref, dloc_ref, score_ref,
+    source, probs_ref, parts_ref,
 ):
     source[0:576] = res_ref[...]
     source[576:688] = lon_ref[...]
@@ -371,14 +418,13 @@
     dlat_ref[...] = moved[112:224]
     ddiag_ref[...] = moved[224:272]
     dloc_ref[...] = moved[272:608]
-    table_ref[...] = table_grad(score_ref, base_ref, slot_ref, rows_ref).astype(bf16)
 
 
 def fine_back_kernel(
     dlon_ref, dlat_ref, ddiag_ref, dloc_ref, back_ref,
-    q_ref, k_ref, v_ref, probs_ref, n1_ref, r1_ref, n2_ref, r2_ref, slope_ref,
-    qkv_ref, proj_ref, up_ref, down_ref, base_ref, slot_ref,
-    res_ref, slon_ref, slat_ref, sdiag_ref, table_ref,
+    q_ref, k_ref, v_ref, probs_ref, n2_ref, r2_ref, slope_ref,
+    proj_ref, up_ref, down_ref, base_ref, slot_ref,
+    grad_ref, dq_ref, dk_ref, dv_ref, table_ref,
     source, score_ref, rows_ref,
 ):
     source[0:112] = dlon_ref[...]
@@ -386,8 +432,6 @@
     source[224:272] = ddiag_ref[...]
     source[272:608] = dloc_ref[...]
     everything = source[...]
-    w_qkv = qkv_ref[...]
-    windows = []
     for w in range(4):
         rows = pl.ds(w * WIN, WIN)
         grad = mm(one_hot(back_ref[rows, :], 608), everything)
@@ -395,24 +439,40 @@
         grad = grad + norm_back(
             mm_nt(inner.astype(bf16), up_ref[...]), n2_ref[rows, :].astype(f32), r2_ref[rows, :]
         )
+        grad_ref[rows, :] = grad
         mix_grad = mm_nt(grad.astype(bf16), proj_ref[...]).astype(bf16)
         dq, dk, dv = attend_back(
             q_ref[rows, :], k_ref[rows, :], v_ref[rows, :], mix_grad,
             probs_ref, w * 6 * WIN,
             score_ref.at[pl.ds(w // 2 * 6 * WIN, 6 * WIN)], w % 2 == 1,
         )
+        dq_ref[rows, :] = dq.astype(bf16)
+        dk_ref[rows, :] = dk.astype(bf16)
+        dv_ref[rows, :] = dv.astype(bf16)
+    table_ref[...] = table_grad(score_ref, base_ref, slot_ref, rows_ref)
+
+
+def qkv_back_kernel(
+    grad_ref, dq_ref, dk_ref, dv_ref, n1_ref, r1_ref, qkv_ref,
+    res_ref, slon_ref, slat_ref, sdiag_ref,
+):
+    w_qkv = qkv_ref[...]
+    windows = []
+    for w in range(4):
+        rows = pl.ds(w * WIN, WIN)
         normed_grad = (
-            mm_nt(dq.astype(bf16), w_qkv[:, 0:192])
-            + mm_nt(dk.astype(bf16), w_qkv[:, 192:384])
-            + mm_nt(dv.astype(bf16), w_qkv[:, 384:576])
+            mm_nt(dq_ref[rows, :], w_qkv[:, 0:192])
+            + mm_nt(dk_ref[rows, :], w_qkv[:, 192:384])
+            + mm_nt(dv_ref[rows, :], w_qkv[:, 384:576])
         )
-        result = grad + norm_back(normed_grad, n1_ref[rows, :].astype(f32), r1_ref[rows, :])
+        result = grad_ref[rows, :] + norm_back(
+            normed_grad, n1_ref[rows, :].astype(f32), r1_ref[rows, :]
+        )
         res_ref[rows, :] = result.astype(bf16)
         windows.append(result)
     slon_ref[...] = pack([quadrant(windows, q, 0) for q in range(1, 4)], 112)
     slat_ref[...] = pack([quadrant(windows, 0, q) for q in range(1, 4)], 112)
     sdiag_ref[...] = pack([quadrant(windows, 0, 0)], 48)
-    table_ref[...] = table_grad(score_ref, base_ref, slot_ref, rows_ref).astype(bf16)
 
 
 def last_kernel(
@@ -438,7 +498,7 @@
             coarse_ref[z, row] = moved[start : start + 12].astype(bf16)
 
 
-def run(kernel, outs, scratch, flops, inputs):
+def run(kernel, outs, scratch, weight, inputs):
     shapes = [jax.ShapeDtypeStruct(shape, kind) for shape, kind in outs]
     size = sum(math.prod(s.shape) * s.dtype.itemsize for s in shapes)
     size += sum(x.size * x.dtype.itemsize for x in inputs)
@@ -447,7 +507,9 @@
         out_shape=shapes,
         scratch_shapes=[pltpu.VMEM(shape, kind) for shape, kind in scratch],
         compiler_params=pltpu.CompilerParams(vmem_limit_bytes=VMEM),
-        cost_estimate=pl.CostEstimate(flops=flops, bytes_accessed=size, transcendentals=0),
+        cost_estimate=pl.CostEstimate(
+            flops=weight * 1_000_000_000, bytes_accessed=size, transcendentals=0
+        ),
     )(*inputs)
 
 
@@ -474,8 +536,6 @@
 
 def lon_total(value):
     count = lax.axis_size("lon")
-    if count & (count - 1):
-        return lax.psum(value, "lon").astype(f32)
     step = 1
     total = value
     while step < count:
@@ -483,11 +543,7 @@
         other = lax.ppermute(kept, "lon", [(s, s ^ step) for s in range(count)])
         total = kept.astype(f32) + other.astype(f32)
         step *= 2
-    return total.astype(f32)
-
-
-def to_table(grad, bands, heads):
-    return grad.reshape(12, 16, ENTRIES)[:, :12].reshape(bands, heads, 12 * ENTRIES)
+    return kept, other
 
 
 def body(
@@ -496,29 +552,23 @@
 ):
     lat_index = lax.axis_index("lat")
     flat = tokens.reshape(576, 192)
-    arrived = send(
-        (
-            tokens[:, 0:9, 16:24].reshape(144, 192),
-            tokens[:, 9:12].reshape(144, 192),
-            tokens[:, 9:12, 16:24].reshape(48, 192),
-        ),
-        1,
-    )
     column = lambda index: jnp.asarray(index).reshape(-1, 1)
     line = lambda index: jnp.asarray(index).reshape(1, -1)
-
-    tables = jnp.concatenate(
-        [fine_bias.reshape(12, 12, ENTRIES), coarse_bias.reshape(12, 12, ENTRIES)], axis=0
-    )
-    tables = jnp.pad(tables, ((0, 0), (0, 4), (0, 0))).reshape(384, ENTRIES)
-    expanded = run(
-        bias_kernel,
-        [((12 * WIN, WIN), f32)] * 2 + [((48, 384), bf16)] * 4,
-        [((24, 2, 12, 16, WIN), bf16)],
-        4_000_000_000,
-        (tables, line(BASE), column(ROW_SLOT), out_grad),
-    )
-    fine_table, coarse_table, g00, g01, g10, g11 = expanded
+    tok = ((576, 192), bf16)
+    edges = [((112, 192), bf16), ((112, 192), bf16), ((48, 192), bf16)]
+    scores = ((12 * WIN, WIN), f32)
+    table = ((24, 6 * ENTRIES), bf16)
+    table_rows = ((12, 192, WIN), bf16)
+
+    arrived = send(run(edge_kernel, edges, [], 1, (flat, column(EDGE))), 1)
+    held = ((12, 2, 12, 16, WIN), bf16)
+    fine_table, g00, g01, g10, g11 = run(
+        fine_bias_kernel,
+        [scores] + [((48, 384), bf16)] * 4,
+        [held],
+        2,
+        (fine_bias.transpose(1, 0, 2), line(BASE), column(ROW_SLOT), out_grad),
+    )
     grads = (g00, *send((g01, g10, g11), 1))
 
     labels = mask_ids.reshape(2, 2, 2, 3, 2, 2, 6)
@@ -531,64 +581,69 @@
         (low_half[:, None] == low_half[None, :]) | (lat_index != 0), 0.0, -1e30
     ).astype(f32)
 
-    tok = ((576, 192), bf16)
-    edges = [((112, 192), bf16), ((112, 192), bf16), ((48, 192), bf16)]
     fine = run(
         fine_kernel,
         [tok] + edges
         + [tok] * 3
         + [((24 * WIN, WIN), bf16), tok, ((576, 1), f32), tok, ((576, 1), f32), ((576, 768), bf16)],
-        [((912, 192), bf16)],
-        2_000_000_000,
+        [((848, 192), bf16)],
+        8,
         (flat, *arrived, column(ARRIVE), fine_table, fine_mask, fine_qkv, fine_proj, fine_up, fine_down),
     )
-    saved = fine[4:]
+    q, k, v, probs, n1, r1, n2, r2, slope = fine[4:]
     arrived = send(fine[1:4], 1)
+    late_table, _ = lax.optimization_barrier((coarse_bias.transpose(1, 0, 2), fine[1]))
+    (coarse_table,) = run(
+        coarse_bias_kernel, [scores], [held], 2, (late_table, line(BASE), column(ROW_SLOT))
+    )
     coarse = run(
         coarse_kernel,
-        [((48, 384), bf16)] * 4 + edges + [((336, 192), bf16), ((192, ENTRIES), bf16)],
-        [
-            ((848, 192), bf16),
-            ((12 * WIN, WIN), bf16),
-            ((12 * WIN, WIN), f32),
-            ((12, 192, WIN), bf16),
-            ((576, 192), bf16),
-        ],
-        3_000_000_000,
+        [((48, 384), bf16)] * 4 + edges + [((336, 192), bf16), scores],
+        [((848, 192), bf16), ((12 * WIN, WIN), bf16), ((576, 192), bf16)],
+        9,
         (
             fine[0], *arrived, column(MERGE), column(SPLIT), coarse_table, coarse_mask, *grads,
             reduce_weight, coarse_qkv, coarse_proj, coarse_up, coarse_down,
-            column(BASE), line(ROW_SLOT),
         ),
     )
     c00, c01, c10, c11 = coarse[:4]
     arrived = send(coarse[4:7], -1)
+    (coarse_grad,) = run(
+        coarse_table_kernel, [table], [table_rows], 2, (coarse[8], column(BASE), line(ROW_SLOT))
+    )
     results = (c11, *send((c10, c01, c00), -1))
-    coarse_total = lon_total(coarse[8])
+    coarse_total = lon_total(coarse_grad)
+    *passed, fine_grad = run(
+        fine_back_kernel,
+        [((576, 192), f32)] + [tok] * 3 + [table],
+        [((608, 192), bf16), scores, table_rows],
+        7,
+        (
+            *arrived, coarse[7], column(BACK), q, k, v, probs, n2, r2, slope,
+            fine_proj, fine_up, fine_down, column(BASE), line(ROW_SLOT),
+        ),
+    )
+    fine_total = lon_total(fine_grad)
     fine_back = run(
-        fine_back_kernel,
-        [tok] + edges + [((192, ENTRIES), bf16)],
-        [((608, 192), bf16), ((12 * WIN, WIN), f32), ((12, 192, WIN), bf16)],
-        3_000_000_000,
-        (
-            *arrived, coarse[7], column(BACK), *saved,
-            fine_qkv, fine_proj, fine_up, fine_down, column(BASE), line(ROW_SLOT),
-        ),
+        qkv_back_kernel, [tok] + edges, [], 2, (*passed, n1, r1, fine_qkv)
     )
     arrived = send(fine_back[1:4], -1)
-    fine_total = lon_total(fine_back[4])
     d_tokens, coarse_result = run(
         last_kernel,
         [tok, ((2, 6, 12, 384), bf16)],
         [((848, 192), bf16), ((192, 384), bf16)],
-        300_000_000,
+        1,
         (fine_back[0], *arrived, column(LEAVE), *results, column(RESULT)),
     )
+    (coarse_out,) = run(
+        table_sum_kernel, [((HEADS_C, 1, 12 * ENTRIES), f32)], [], 1, coarse_total
+    )
+    (fine_out,) = run(table_sum_kernel, [((HEADS_F, 2, 12 * ENTRIES), f32)], [], 1, fine_total)
     return (
         coarse_result,
         d_tokens.reshape(tokens.shape),
-        to_table(fine_total, 2, HEADS_F),
-        to_table(coarse_total, 1, HEADS_C),
+        fine_out.transpose(1, 0, 2),
+        coarse_out.transpose(1, 0, 2),
     )
 
 

time: 98.3 us -> 83 us (0.84)
  waiting for transfers between devices: 24 us -> 12.7 us
  local copies, waits for them, and re-layouts: 11 us -> 5.86 us
  Pallas kernels: 30.5 us -> 34.9 us
  starting transfers between devices: 29.3 us -> 27.8 us
  other arithmetic: 1.91 us -> 0.43 us
    ppermute x6, waiting for transfers between devices: 16.5 us -> 10.7 us  [lon_total(): other = lax.ppermute(kept, 'lon', [(s, s ^ step) for s in range(count)])]
    ppermute x6, waiting for transfers between devices: 7.52 us -> 1.77 us  [move(): return lax.ppermute(value, ('lon', 'lat'), pairs)]
    ppermute x6, starting transfers between devices: 2.19 us -> 6.68 us  [move(): return lax.ppermute(value, 'lat', pairs)]
    pallas_call x5 -> x11, Pallas kernels: 30.5 us -> 34.9 us  [run(): pl.pallas_call(kernel, out_shape=shapes, scratch_shapes=[pltpu.VMEM(shape...]
    ppermute x6, starting transfers between devices: 12.2 us -> 8.05 us  [move(): return lax.ppermute(value, 'lon', pairs)]
    slice x3 -> x0, local copies, waits for them, and re-layouts: 2.59 us -> none  [the longest x1 0.96 us: body(): tokens[:, 0:9, 16:24].reshape(144, 192)]
    ppermute x6, starting transfers between devices: 6.2 us -> 3.96 us  [lon_total(): other = lax.ppermute(kept, 'lon', [(s, s ^ step) for s in range(count)])]
    reshape x4 -> x0, local copies, waits for them, and re-layouts: 1.51 us -> none  [the longest x2 1.18 us: to_table(): grad.reshape(12, 16, ENTRIES)[:, :12].reshape(bands, heads, 12 * ENTRIES)]
  transfers between devices with their start and end apart: 24 -> 24, of which waited for: 8 -> 6; matrix products, arithmetic and copies ran while one was open for 7% -> 2% of each run, Pallas kernels for 22% -> 30%
where the time goes in v1:
time: 83 us; the launch traced here: 82.8 us
  Pallas kernels  34.9 us (42%)
  starting transfers between devices  27.8 us (33%)
  waiting for transfers between devices  12.7 us (15%)
  local copies, waits for them, and re-layouts  5.86 us (7%)
  between operations  1.12 us (1%)
    pallas_call x11, Pallas kernels, run(): pl.pallas_call(kernel, out_shape=shapes, scratch_shapes=[pltpu.VMEM(shape...  34.9 us
    ppermute x6, waiting for transfers between devices, lon_total(): other = lax.ppermute(kept, 'lon', [(s, s ^ step) for s in range(count)])  10.7 us
    ppermute x6, starting transfers between devices, move(): return lax.ppermute(value, ('lon', 'lat'), pairs)  9.13 us
    ppermute x6, starting transfers between devices, move(): return lax.ppermute(value, 'lon', pairs)  8.05 us
    ppermute x6, starting transfers between devices, move(): return lax.ppermute(value, 'lat', pairs)  6.68 us
    unnamed x61, local copies, waits for them, and re-layouts  5.65 us
    ppermute x6, starting transfers between devices, lon_total(): other = lax.ppermute(kept, 'lon', [(s, s ^ step) for s in range(count)])  3.96 us
    ppermute x6, waiting for transfers between devices, move(): return lax.ppermute(value, ('lon', 'lat'), pairs)  1.77 us
  transfers between devices with their start and end apart: 24, of which 6 were waited for; matrix products, arithmetic and copies ran while one was open for 2% of the time, Pallas kernels for 30%

profile of v1, /device:TPU:0, one launch (start us, length us, event | category | flops | bytes accessed | tf_op | source)
XLA Modules:
  0.0 82.8 jit_solution(9721616581720536416)
XLA Ops:
  0.6 1.0 %copy-done.4 = bf16[2,12,24,192]{3,2,1,0:T(8,128)(2,1)S(1)} copy-done((bf16[2,12,24,192]{3,2,1,0:T(8,128)(2,1)S(1)}, bf16[2,12,24,192]{3,2,1,0:T(8,128)(2,1)}, u32[]{:S(2)}) %copy-start.4) | copy-done | bytes 221208
  1.6 0.9 %copy-done.17 = s32[272,1]{1,0:T(8,128)S(1)} copy-done((s32[272,1]{1,0:T(8,128)S(1)}, s32[272,1]{1,0:T(8,128)}, u32[]{:S(2)}) %copy-start.17) | copy-done | bytes 1112
  2.5 0.3 shard_map.246
  2.9 2.5 %collective-permute-start.2 = (bf16[48,192]{1,0:T(8,128)(2,1)S(1)}, bf16[48,192]{1,0:T(8,128)(2,1)S(1)}, u32[]{:S(2)}, u32[]{:S(2)}) collective-permute-start(bf16[48,192]{1,0:T(8,128)(2,1)S(1)} %get-tuple-element.60), channel_id=1, source_target_pairs={{0,5},{1,6},{2,7},{3,4},{4,9},{5,10},{6,11},{7,8},{8,13},{9,14},{1... | collective-permute-start | bytes 55304 | tf_op jit(solution)/shard_map/ppermute | solution.py:529
  5.3 1.5 %collective-permute-start = (bf16[112,192]{1,0:T(8,128)(2,1)S(1)}, bf16[112,192]{1,0:T(8,128)(2,1)S(1)}, u32[]{:S(2)}, u32[]{:S(2)}) collective-permute-start(bf16[112,192]{1,0:T(8,128)(2,1)S(1)} %get-tuple-element.58), channel_id=1, source_target_pairs={{0,4},{4,8},{8,12},{12,16},{16,20},{20,24},{24,28},{28,0},{1,5},{5... | collective-permute-start | bytes 129032 | tf_op jit(solution)/shard_map/ppermute | solution.py:520
  6.8 1.3 %collective-permute-start.1 = (bf16[112,192]{1,0:T(8,128)(2,1)S(1)}, bf16[112,192]{1,0:T(8,128)(2,1)S(1)}, u32[]{:S(2)}, u32[]{:S(2)}) collective-permute-start(bf16[112,192]{1,0:T(8,128)(2,1)S(1)} %get-tuple-element.59), channel_id=1, source_target_pairs={{0,1},{1,2},{2,3},{3,0},{4,5},{5,6},{6,7},{7,4},{8,9},{9,10},{10,1... | collective-permute-start | bytes 129032 | tf_op jit(solution)/shard_map/ppermute | solution.py:523
  8.3 2.3 %shard_map.247 = (f32[1728,144]{1,0:T(8,128)S(1)}, bf16[48,384]{1,0:T(8,128)(2,1)S(1)}, bf16[48,384]{1,0:T(8,128)(2,1)S(1)}, bf16[48,384]{1,0:T(8,128)(2,1)S(1)}, bf16[48,384]{1,0:T(8,128)(2,1)S(1)}) custom-call(f32[6,2,3312]{2,1,0:T(2,128)S(1)} %bitcast.12, s32[1,144]{1,0:T(1,128)S(1)} %copy-done.22, s32[144,1]{1,0:T(8,128)S(1)} %copy-done.20, ...), custom_call_target="tpu_custom_call" | custom-call | flops 2000000000 | bytes 1413504 | tf_op jit(solution)/shard_map/pallas_call | solution.py:505
  10.6 1.3 %copy-done.23 = f32[1728,144]{1,0:T(8,128)} copy-done((f32[1728,144]{1,0:T(8,128)}, f32[1728,144]{1,0:T(8,128)S(1)}, u32[]{:S(2)}) %copy-start.23) | copy-done | bytes 995352
  11.9 1.5 %collective-permute-start.6 = (bf16[48,384]{1,0:T(8,128)(2,1)S(1)}, bf16[48,384]{1,0:T(8,128)(2,1)S(1)}, u32[]{:S(2)}, u32[]{:S(2)}) collective-permute-start(bf16[48,384]{1,0:T(8,128)(2,1)S(1)} %get-tuple-element.68), channel_id=1, source_target_pairs={{0,4},{4,8},{8,12},{12,16},{16,20},{20,24},{24,28},{28,0},{1,5},{5... | collective-permute-start | bytes 110600 | tf_op jit(solution)/shard_map/ppermute | solution.py:520
  13.4 0.1 mul.11
  13.6 0.1 eq.32
  13.8 0.1 compare_select_fusion.mask_ref
  14.0 0.2 copy.34.down_ref
  14.2 1.8 %collective-permute-start.8 = (bf16[48,384]{1,0:T(8,128)(2,1)S(1)}, bf16[48,384]{1,0:T(8,128)(2,1)S(1)}, u32[]{:S(2)}, u32[]{:S(2)}) collective-permute-start(bf16[48,384]{1,0:T(8,128)(2,1)S(1)} %get-tuple-element.70), channel_id=1, source_target_pairs={{0,5},{1,6},{2,7},{3,4},{4,9},{5,10},{6,11},{7,8},{8,13},{9,14},{1... | collective-permute-start | bytes 110600 | tf_op jit(solution)/shard_map/ppermute | solution.py:529
  16.1 1.5 %copy-done.24 = f32[1728,144]{1,0:T(8,128)S(1)} copy-done((f32[1728,144]{1,0:T(8,128)S(1)}, f32[1728,144]{1,0:T(8,128)}, u32[]{:S(2)}) %copy-start.24) | copy-done | bytes 995352
  17.5 7.9 %shard_map.248 = (bf16[576,192]{1,0:T(8,128)(2,1)S(1)}, bf16[112,192]{1,0:T(8,128)(2,1)S(1)}, bf16[112,192]{1,0:T(8,128)(2,1)S(1)}, bf16[48,192]{1,0:T(8,128)(2,...) custom-call(bf16[576,192]{1,0:T(8,128)(2,1)S(1)} %bitcast.11, ...), custom_call_target="tpu_custom_call" | custom-call | flops 8000000000 | bytes 5856000 | tf_op jit(solution)/shard_map/pallas_call | solution.py:505
  25.5 1.6 %collective-permute-start.3 = (bf16[112,192]{1,0:T(8,128)(2,1)S(1)}, bf16[112,192]{1,0:T(8,128)(2,1)S(1)}, u32[]{:S(2)}, u32[]{:S(2)}) collective-permute-start(bf16[112,192]{1,0:T(8,128)(2,1)S(1)} %get-tuple-element.63), channel_id=1, source_target_pairs={{0,4},{4,8},{8,12},{12,16},{16,20},{20,24},{24,28},{28,0},{1,5},{5... | collective-permute-start | bytes 129032 | tf_op jit(solution)/shard_map/ppermute | solution.py:520
  27.0 0.7 collective-permute-start.5
  27.8 2.1 %collective-permute-start.4 = (bf16[112,192]{1,0:T(8,128)(2,1)S(1)}, bf16[112,192]{1,0:T(8,128)(2,1)S(1)}, u32[]{:S(2)}, u32[]{:S(2)}) collective-permute-start(bf16[112,192]{1,0:T(8,128)(2,1)S(1)} %get-tuple-element.64), channel_id=1, source_target_pairs={{0,1},{1,2},{2,3},{3,0},{4,5},{5,6},{6,7},{7,4},{8,9},{9,10},{10,1... | collective-permute-start | bytes 129032 | tf_op jit(solution)/shard_map/ppermute | solution.py:523
  29.9 2.2 %shard_map.249.bias_ref = f32[1728,144]{1,0:T(8,128)S(1)} custom-call(f32[12,1,3312]{2,1,0:T(1,128)S(1)} %bitcast.13, s32[1,144]{1,0:T(1,128)S(1)} %copy-done.22, s32[144,1]{1,0:T(8,128)S(1)} %copy-done.20), custom_call_target="tpu_custom_call" | custom-call | flops 2000000000 | bytes 1155456 | tf_op jit(solution)/shard_map/pallas_call | solution.py:505
  32.2 1.8 %collective-permute-done.5.diag_ref = bf16[48,192]{1,0:T(8,128)(2,1)S(1)} collective-permute-done((bf16[48,192]{1,0:T(8,128)(2,1)S(1)}, bf16[48,192]{1,0:T(8,128)(2,1)S(1)}, u32[]{:S(2)}, u32[]{:S(2)}) %collective-permute-start.5) | collective-permute-done | bytes 18464 | tf_op jit(solution)/shard_map/ppermute | solution.py:529
  34.0 8.5 %shard_map.250 = (bf16[48,384]{1,0:T(8,128)(2,1)S(1)}, bf16[48,384]{1,0:T(8,128)(2,1)S(1)}, bf16[48,384]{1,0:T(8,128)(2,1)S(1)}, bf16[48,384]{1,0:T(8,128)(2,1)S...) custom-call(bf16[576,192]{1,0:T(8,128)(2,1)S(1)} %get-tuple-element., ...), custom_call_target="tpu_custom_call" | custom-call | flops 8999999488 | bytes 7061120 | tf_op jit(solution)/shard_map/pallas_call | solution.py:505
  42.6 1.1 %collective-permute-start.11 = (bf16[48,192]{1,0:T(8,128)(2,1)S(1)}, bf16[48,192]{1,0:T(8,128)(2,1)S(1)}, u32[]{:S(2)}, u32[]{:S(2)}) collective-permute-start(bf16[48,192]{1,0:T(8,128)(2,1)S(1)} %get-tuple-element.73), channel_id=1, source_target_pairs={{0,31},{1,28},{2,29},{3,30},{4,3},{5,0},{6,1},{7,2},{8,7},{9,4},{1... | collective-permute-start | bytes 55304 | tf_op jit(solution)/shard_map/ppermute | solution.py:529
  43.7 0.5 collective-permute-start.15
  44.2 1.3 %collective-permute-start.16 = (bf16[48,384]{1,0:T(8,128)(2,1)S(1)}, bf16[48,384]{1,0:T(8,128)(2,1)S(1)}, u32[]{:S(2)}, u32[]{:S(2)}) collective-permute-start(bf16[48,384]{1,0:T(8,128)(2,1)S(1)} %get-tuple-element.94), channel_id=1, source_target_pairs={{0,3},{1,0},{2,1},{3,2},{4,7},{5,4},{6,5},{7,6},{8,11},{9,8},{10,9... | collective-permute-start | bytes 110600 | tf_op jit(solution)/shard_map/ppermute | solution.py:523
  45.5 1.2 %collective-permute-start.9 = (bf16[112,192]{1,0:T(8,128)(2,1)S(1)}, bf16[112,192]{1,0:T(8,128)(2,1)S(1)}, u32[]{:S(2)}, u32[]{:S(2)}) collective-permute-start(bf16[112,192]{1,0:T(8,128)(2,1)S(1)} %get-tuple-element.71), channel_id=1, source_target_pairs={{0,28},{4,0},{8,4},{12,8},{16,12},{20,16},{24,20},{28,24},{1,29},{... | collective-permute-start | bytes 129032 | tf_op jit(solution)/shard_map/ppermute | solution.py:520
  46.6 0.3 collective-permute-start.10
  47.0 1.4 %shard_map.255 = bf16[24,1656]{1,0:T(8,128)(2,1)S(1)} custom-call(f32[1728,144]{1,0:T(8,128)S(1)} %get-tuple-element.99.score_ref, s32[144,1]{1,0:T(8,128)S(1)} %copy-done.19, s32[1,144]{1,0:T(1,128)S(1)} %copy-done.21), custom_call_target="tpu_custom_call" | custom-call | flops 2000000000 | bytes 1075968 | tf_op jit(solution)/shard_map/pallas_call | solution.py:505
  48.4 2.5 %collective-permute-start.17 = (bf16[48,384]{1,0:T(8,128)(2,1)S(1)}, bf16[48,384]{1,0:T(8,128)(2,1)S(1)}, u32[]{:S(2)}, u32[]{:S(2)}) collective-permute-start(bf16[48,384]{1,0:T(8,128)(2,1)S(1)} %get-tuple-element.95), channel_id=1, source_target_pairs={{0,31},{1,28},{2,29},{3,30},{4,3},{5,0},{6,1},{7,2},{8,7},{9,4},{1... | collective-permute-start | bytes 110600 | tf_op jit(solution)/shard_map/ppermute | solution.py:529
  50.8 1.0 %collective-permute-start.21 = (bf16[24,1656]{1,0:T(8,128)(2,1)S(1)}, bf16[24,1656]{1,0:T(8,128)(2,1)S(1)}, u32[]{:S(2)}, u32[]{:S(2)}) collective-permute-start(bf16[24,1656]{1,0:T(8,128)(2,1)S(1)} %shard_map.255), channel_id=1, source_target_pairs={{0,4},{4,0},{8,12},{12,8},{16,20},{20,16},{24,28},{28,24},{1,5},{5... | collective-permute-start | bytes 238472 | tf_op jit(solution)/shard_map/ppermute | solution.py:543
  51.8 8.5 %shard_map.251 = (f32[576,192]{1,0:T(8,128)S(1)}, bf16[576,192]{1,0:T(8,128)(2,1)S(1)}, bf16[576,192]{1,0:T(8,128)(2,1)S(1)}, bf16[576,192]{1,0:T(8,128)(2,1)S(1)}, bf16[24,1656]{1,0:T(8,128)(2,1)S(1)}) custom-call(bf16[112,192]{1,0:T(8,128)(2,1)S(1)} %collective-permute-done.9.dlon_ref, bf16[112,192]{1,0:T(8,128)(2,1)S(1)} %collective-permute-done.10.dlat_ref, ...), custom_call_target="tpu_custom_call" | custom-call | flops 7000000000 | bytes 4852992 | tf_op jit(solution)/shard_map/pallas_call | solution.py:505
  60.4 0.8 shard_map.252
  61.1 0.6 collective-permute-start.14
  61.8 1.8 %collective-permute-start.12 = (bf16[112,192]{1,0:T(8,128)(2,1)S(1)}, bf16[112,192]{1,0:T(8,128)(2,1)S(1)}, u32[]{:S(2)}, u32[]{:S(2)}) collective-permute-start(bf16[112,192]{1,0:T(8,128)(2,1)S(1)} %get-tuple-element.89), channel_id=1, source_target_pairs={{0,28},{4,0},{8,4},{12,8},{16,12},{20,16},{24,20},{28,24},{1,29},{... | collective-permute-start | bytes 129032 | tf_op jit(solution)/shard_map/ppermute | solution.py:520
  63.5 1.7 %collective-permute-start.13 = (bf16[112,192]{1,0:T(8,128)(2,1)S(1)}, bf16[112,192]{1,0:T(8,128)(2,1)S(1)}, u32[]{:S(2)}, u32[]{:S(2)}) collective-permute-start(bf16[112,192]{1,0:T(8,128)(2,1)S(1)} %get-tuple-element.90), channel_id=1, source_target_pairs={{0,3},{1,0},{2,1},{3,2},{4,7},{5,4},{6,5},{7,6},{8,11},{9,8},{10,9... | collective-permute-start | bytes 129032 | tf_op jit(solution)/shard_map/ppermute | solution.py:523
  65.2 0.1 collective-permute-start.18
  65.3 1.4 %collective-permute-start.22 = (bf16[24,1656]{1,0:T(8,128)(2,1)S(1)}, bf16[24,1656]{1,0:T(8,128)(2,1)S(1)}, u32[]{:S(2)}, u32[]{:S(2)}) collective-permute-start(bf16[24,1656]{1,0:T(8,128)(2,1)S(1)} %add_convert_fusion.1), channel_id=1, source_target_pairs={{0,8},{4,12},{8,0},{12,4},{16,24},{20,28},{24,16},{28,20},{1,9},{5... | collective-permute-start | bytes 238472 | tf_op jit(solution)/shard_map/ppermute | solution.py:543
  66.8 0.2 collective-permute-done.13.lat_ref
  67.0 1.3 %shard_map.253 = (bf16[576,192]{1,0:T(8,128)(2,1)}, bf16[2,6,12,384]{3,2,1,0:T(8,128)(2,1)S(1)}) custom-call(bf16[576,192]{1,0:T(8,128)(2,1)S(1)} %get-tuple-element.88.res_ref, bf16[112,192]{1,0:T(8,128)(2,1)S(1)} %collective-permute-done.12.lon_ref, bf16[112,192]{1,0:T(8,128)(2,1)S(1)} %collective-permute-done.13.lat_ref, ...), custom_call_target="tpu_custom_call" | custom-call | flops 1000000000 | bytes 807744 | tf_op jit(solution)/shard_map/pallas_call | solution.py:505
  68.3 0.7 copy.36
  69.1 0.7 collective-permute-done.18
  69.7 0.2 collective-permute-start.19
  69.9 1.2 %collective-permute-start.23 = (bf16[24,1656]{1,0:T(8,128)(2,1)S(1)}, bf16[24,1656]{1,0:T(8,128)(2,1)S(1)}, u32[]{:S(2)}, u32[]{:S(2)}) collective-permute-start(bf16[24,1656]{1,0:T(8,128)(2,1)S(1)} %add_convert_fusion.kept_ref), channel_id=1, source_target_pairs={{0,16},{4,20},{8,24},{12,28},{16,0},{20,4},{24,8},{28,12},{1,17},{... | collective-permute-start | bytes 238472 | tf_op jit(solution)/shard_map/ppermute | solution.py:543
  71.1 4.9 %collective-permute-done.19 = bf16[24,1656]{1,0:T(8,128)(2,1)S(1)} collective-permute-done((bf16[24,1656]{1,0:T(8,128)(2,1)S(1)}, bf16[24,1656]{1,0:T(8,128)(2,1)S(1)}, u32[]{:S(2)}, u32[]{:S(2)}) %collective-permute-start.19) | collective-permute-done | bytes 79520 | tf_op jit(solution)/shard_map/ppermute | solution.py:543
  76.1 1.4 %collective-permute-done.23.other_ref = bf16[24,1656]{1,0:T(8,128)(2,1)S(1)} collective-permute-done((bf16[24,1656]{1,0:T(8,128)(2,1)S(1)}, bf16[24,1656]{1,0:T(8,128)(2,1)S(1)}, u32[]{:S(2)}, u32[]{:S(2)}) %collective-permute-start.23) | collective-permute-done | bytes 79520 | tf_op jit(solution)/shard_map/ppermute | solution.py:543
  77.6 0.8 shard_map.256
  78.3 3.7 %collective-permute-done.20.other_ref = bf16[24,1656]{1,0:T(8,128)(2,1)S(1)} collective-permute-done((bf16[24,1656]{1,0:T(8,128)(2,1)S(1)}, bf16[24,1656]{1,0:T(8,128)(2,1)S(1)}, u32[]{:S(2)}, u32[]{:S(2)}) %collective-permute-start.20) | collective-permute-done | bytes 79520 | tf_op jit(solution)/shard_map/ppermute | solution.py:543
  82.0 0.8 shard_map.254
  (84 shorter events, 0.6 us)
Async XLA Ops:
  2.5 5.7 %copy-start.26 = (bf16[2,6,12,384]{3,0,2,1:T(2,128)(2,1)S(1)}, bf16[2,6,12,384]{3,0,2,1:T(2,128)(2,1)}, u32[]{:S(2)}) copy-start(bf16[2,6,12,384]{3,0,2,1:T(2,128)(2,1)} %param.38) | copy-start | bytes 331780
  2.5 5.7 %copy-start.9 = (f32[2,6,3312]{2,0,1:T(2,128)S(1)}, f32[2,6,3312]{2,0,1:T(2,128)}, u32[]{:S(2)}) copy-start(f32[2,6,3312]{2,0,1:T(2,128)} %param.31) | copy-start | bytes 476932
  2.5 5.7 %copy-start.20 = (s32[144,1]{1,0:T(8,128)S(1)}, s32[144,1]{1,0:T(8,128)}, u32[]{:S(2)}) copy-start(s32[144,1]{1,0:T(8,128)} %constant.88.slot_ref) | copy-start | bytes 1732
  2.5 5.7 %copy-start.22 = (s32[1,144]{1,0:T(1,128)S(1)}, s32[1,144]{1,0:T(1,128)}, u32[]{:S(2)}) copy-start(s32[1,144]{1,0:T(1,128)} %constant.87.base_ref) | copy-start | bytes 1732
  2.9 11.3 %collective-permute-start.2 = (bf16[48,192]{1,0:T(8,128)(2,1)S(1)}, bf16[48,192]{1,0:T(8,128)(2,1)S(1)}, u32[]{:S(2)}, u32[]{:S(2)}) collective-permute-start(bf16[48,192]{1,0:T(8,128)(2,1)S(1)} %get-tuple-element.60), channel_id=1, source_target_pairs={{0,5},{1,6},{2,7},{3,4},{4,9},{5,10},{6,11},{7,8},{8,13},{9,14},{1... | collective-permute-start | bytes 55304 | tf_op jit(solution)/shard_map/ppermute | solution.py:529
  5.3 10.7 %collective-permute-start = (bf16[112,192]{1,0:T(8,128)(2,1)S(1)}, bf16[112,192]{1,0:T(8,128)(2,1)S(1)}, u32[]{:S(2)}, u32[]{:S(2)}) collective-permute-start(bf16[112,192]{1,0:T(8,128)(2,1)S(1)} %get-tuple-element.58), channel_id=1, source_target_pairs={{0,4},{4,8},{8,12},{12,16},{16,20},{20,24},{24,28},{28,0},{1,5},{5... | collective-permute-start | bytes 129032 | tf_op jit(solution)/shard_map/ppermute | solution.py:520
  6.8 9.2 %collective-permute-start.1 = (bf16[112,192]{1,0:T(8,128)(2,1)S(1)}, bf16[112,192]{1,0:T(8,128)(2,1)S(1)}, u32[]{:S(2)}, u32[]{:S(2)}) collective-permute-start(bf16[112,192]{1,0:T(8,128)(2,1)S(1)} %get-tuple-element.59), channel_id=1, source_target_pairs={{0,1},{1,2},{2,3},{3,0},{4,5},{5,6},{6,7},{7,4},{8,9},{9,10},{10,1... | collective-permute-start | bytes 129032 | tf_op jit(solution)/shard_map/ppermute | solution.py:523
  8.2 5.2 %copy-start.27 = (s32[2,12,24]{2,0,1:T(2,128)S(1)}, s32[2,12,24]{2,0,1:T(2,128)}, u32[]{:S(2)}) copy-start(s32[2,12,24]{2,0,1:T(2,128)} %param.26) | copy-start | bytes 6916
  8.2 5.3 %copy-start.28 = (s32[2,2]{1,0:T(2,128)S(1)}, s32[2,2]{1,0:T(2,128)}, u32[]{:S(2)}) copy-start(s32[2,2]{1,0:T(2,128)} %constant.69.clone.1) | copy-start | bytes 52
  8.2 5.8 %copy-start.25 = (bf16[768,192]{0,1:T(8,128)(2,1)S(1)}, bf16[768,192]{0,1:T(8,128)(2,1)}, u32[]{:S(2)}) copy-start(bf16[768,192]{0,1:T(8,128)(2,1)} %param.30) | copy-start | bytes 884740
  8.2 7.8 %copy-start.5 = (bf16[2,12,24,192]{3,2,1,0:T(8,128)(2,1)S(1)}, bf16[2,12,24,192]{3,2,1,0:T(8,128)(2,1)}, u32[]{:S(2)}) copy-start(bf16[2,12,24,192]{3,2,1,0:T(8,128)(2,1)} %param.25) | copy-start | bytes 663556
  8.3 7.8 %copy-start.7 = (bf16[192,768]{1,0:T(8,128)(2,1)S(1)}, bf16[192,768]{1,0:T(8,128)(2,1)}, u32[]{:S(2)}) copy-start(bf16[192,768]{1,0:T(8,128)(2,1)} %up_ref.5) | copy-start | bytes 884740
  8.3 7.8 %copy-start.8 = (bf16[192,576]{1,0:T(8,128)(2,1)S(1)}, bf16[192,576]{1,0:T(8,128)(2,1)}, u32[]{:S(2)}) copy-start(bf16[192,576]{1,0:T(8,128)(2,1)} %qkv_ref.5) | copy-start | bytes 663556
  8.3 7.8 %copy-start.11 = (bf16[192,192]{1,0:T(8,128)(2,1)S(1)}, bf16[192,192]{1,0:T(8,128)(2,1)}, u32[]{:S(2)}) copy-start(bf16[192,192]{1,0:T(8,128)(2,1)} %proj_ref.5) | copy-start | bytes 221188
  8.3 7.8 %copy-start.16 = (s32[576,1]{1,0:T(8,128)S(1)}, s32[576,1]{1,0:T(8,128)}, u32[]{:S(2)}) copy-start(s32[576,1]{1,0:T(8,128)} %constant.86.arrive_ref) | copy-start | bytes 6916
  11.9 15.9 %collective-permute-start.6 = (bf16[48,384]{1,0:T(8,128)(2,1)S(1)}, bf16[48,384]{1,0:T(8,128)(2,1)S(1)}, u32[]{:S(2)}, u32[]{:S(2)}) collective-permute-start(bf16[48,384]{1,0:T(8,128)(2,1)S(1)} %get-tuple-element.68), channel_id=1, source_target_pairs={{0,4},{4,8},{8,12},{12,16},{16,20},{20,24},{24,28},{28,0},{1,5},{5... | collective-permute-start | bytes 110600 | tf_op jit(solution)/shard_map/ppermute | solution.py:520
  13.4 18.8 %collective-permute-start.7 = (bf16[48,384]{1,0:T(8,128)(2,1)S(1)}, bf16[48,384]{1,0:T(8,128)(2,1)S(1)}, u32[]{:S(2)}, u32[]{:S(2)}) collective-permute-start(bf16[48,384]{1,0:T(8,128)(2,1)S(1)} %get-tuple-element.69), channel_id=1, source_target_pairs={{0,1},{1,2},{2,3},{3,0},{4,5},{5,6},{6,7},{7,4},{8,9},{9,10},{10,1... | collective-permute-start | bytes 110600 | tf_op jit(solution)/shard_map/ppermute | solution.py:523
  14.2 18.0 %collective-permute-start.8 = (bf16[48,384]{1,0:T(8,128)(2,1)S(1)}, bf16[48,384]{1,0:T(8,128)(2,1)S(1)}, u32[]{:S(2)}, u32[]{:S(2)}) collective-permute-start(bf16[48,384]{1,0:T(8,128)(2,1)S(1)} %get-tuple-element.70), channel_id=1, source_target_pairs={{0,5},{1,6},{2,7},{3,4},{4,9},{5,10},{6,11},{7,8},{8,13},{9,14},{1... | collective-permute-start | bytes 110600 | tf_op jit(solution)/shard_map/ppermute | solution.py:529
  17.5 12.4 %copy-start.10 = (f32[1,12,3312]{2,0,1:T(1,128)S(1)}, f32[1,12,3312]{2,0,1:T(1,128)}, u32[]{:S(2)}) copy-start(f32[1,12,3312]{2,0,1:T(1,128)} %param.37) | copy-start | bytes 476932
  25.5 8.5 %collective-permute-start.3 = (bf16[112,192]{1,0:T(8,128)(2,1)S(1)}, bf16[112,192]{1,0:T(8,128)(2,1)S(1)}, u32[]{:S(2)}, u32[]{:S(2)}) collective-permute-start(bf16[112,192]{1,0:T(8,128)(2,1)S(1)} %get-tuple-element.63), channel_id=1, source_target_pairs={{0,4},{4,8},{8,12},{12,16},{16,20},{20,24},{24,28},{28,0},{1,5},{5... | collective-permute-start | bytes 129032 | tf_op jit(solution)/shard_map/ppermute | solution.py:520
  27.0 6.9 %collective-permute-start.5 = (bf16[48,192]{1,0:T(8,128)(2,1)S(1)}, bf16[48,192]{1,0:T(8,128)(2,1)S(1)}, u32[]{:S(2)}, u32[]{:S(2)}) collective-permute-start(bf16[48,192]{1,0:T(8,128)(2,1)S(1)} %get-tuple-element.65), channel_id=1, source_target_pairs={{0,5},{1,6},{2,7},{3,4},{4,9},{5,10},{6,11},{7,8},{8,13},{9,14},{1... | collective-permute-start | bytes 55304 | tf_op jit(solution)/shard_map/ppermute | solution.py:529
  27.7 6.2 %copy-start = (bf16[384,1536]{1,0:T(8,128)(2,1)S(1)}, bf16[384,1536]{1,0:T(8,128)(2,1)}, u32[]{:S(2)}) copy-start(bf16[384,1536]{1,0:T(8,128)(2,1)} %up_ref.4) | copy-start | bytes 3538948
  27.7 6.2 %copy-start.1 = (bf16[1536,384]{1,0:T(8,128)(2,1)S(1)}, bf16[1536,384]{1,0:T(8,128)(2,1)}, u32[]{:S(2)}) copy-start(bf16[1536,384]{1,0:T(8,128)(2,1)} %down_ref.3) | copy-start | bytes 3538948
  27.7 6.2 %copy-start.2 = (bf16[384,1152]{1,0:T(8,128)(2,1)S(1)}, bf16[384,1152]{1,0:T(8,128)(2,1)}, u32[]{:S(2)}) copy-start(bf16[384,1152]{1,0:T(8,128)(2,1)} %qkv_ref.4) | copy-start | bytes 2654212
  27.7 6.2 %copy-start.3 = (bf16[768,384]{1,0:T(8,128)(2,1)S(1)}, bf16[768,384]{1,0:T(8,128)(2,1)}, u32[]{:S(2)}) copy-start(bf16[768,384]{1,0:T(8,128)(2,1)} %reduce_ref.1) | copy-start | bytes 1769476
  27.8 6.2 %copy-start.6 = (bf16[384,384]{1,0:T(8,128)(2,1)S(1)}, bf16[384,384]{1,0:T(8,128)(2,1)}, u32[]{:S(2)}) copy-start(bf16[384,384]{1,0:T(8,128)(2,1)} %proj_ref.4) | copy-start | bytes 884740
  27.8 6.2 %copy-start.12 = (s32[608,1]{1,0:T(8,128)S(1)}, s32[608,1]{1,0:T(8,128)}, u32[]{:S(2)}) copy-start(s32[608,1]{1,0:T(8,128)} %constant.90.split_ref) | copy-start | bytes 7300
  27.8 6.2 %copy-start.15 = (s32[576,1]{1,0:T(8,128)S(1)}, s32[576,1]{1,0:T(8,128)}, u32[]{:S(2)}) copy-start(s32[576,1]{1,0:T(8,128)} %constant.89.merge_ref) | copy-start | bytes 6916
  27.8 6.1 %collective-permute-start.4 = (bf16[112,192]{1,0:T(8,128)(2,1)S(1)}, bf16[112,192]{1,0:T(8,128)(2,1)S(1)}, u32[]{:S(2)}, u32[]{:S(2)}) collective-permute-start(bf16[112,192]{1,0:T(8,128)(2,1)S(1)} %get-tuple-element.64), channel_id=1, source_target_pairs={{0,1},{1,2},{2,3},{3,0},{4,5},{5,6},{6,7},{7,4},{8,9},{9,10},{10,1... | collective-permute-start | bytes 129032 | tf_op jit(solution)/shard_map/ppermute | solution.py:523
  34.0 12.9 %copy-start.19 = (s32[144,1]{1,0:T(8,128)S(1)}, s32[144,1]{1,0:T(8,128)}, u32[]{:S(2)}) copy-start(s32[144,1]{1,0:T(8,128)} %constant.92.base_ref) | copy-start | bytes 1732
  34.0 12.9 %copy-start.21 = (s32[1,144]{1,0:T(1,128)S(1)}, s32[1,144]{1,0:T(1,128)}, u32[]{:S(2)}) copy-start(s32[1,144]{1,0:T(1,128)} %constant.93.slot_ref) | copy-start | bytes 1732
  42.6 5.8 %collective-permute-start.11 = (bf16[48,192]{1,0:T(8,128)(2,1)S(1)}, bf16[48,192]{1,0:T(8,128)(2,1)S(1)}, u32[]{:S(2)}, u32[]{:S(2)}) collective-permute-start(bf16[48,192]{1,0:T(8,128)(2,1)S(1)} %get-tuple-element.73), channel_id=1, source_target_pairs={{0,31},{1,28},{2,29},{3,30},{4,3},{5,0},{6,1},{7,2},{8,7},{9,4},{1... | collective-permute-start | bytes 55304 | tf_op jit(solution)/shard_map/ppermute | solution.py:529
  43.7 18.1 %collective-permute-start.15 = (bf16[48,384]{1,0:T(8,128)(2,1)S(1)}, bf16[48,384]{1,0:T(8,128)(2,1)S(1)}, u32[]{:S(2)}, u32[]{:S(2)}) collective-permute-start(bf16[48,384]{1,0:T(8,128)(2,1)S(1)} %get-tuple-element.93), channel_id=1, source_target_pairs={{0,28},{4,0},{8,4},{12,8},{16,12},{20,16},{24,20},{28,24},{1,29},{... | collective-permute-start | bytes 110600 | tf_op jit(solution)/shard_map/ppermute | solution.py:520
  44.2 21.0 %collective-permute-start.16 = (bf16[48,384]{1,0:T(8,128)(2,1)S(1)}, bf16[48,384]{1,0:T(8,128)(2,1)S(1)}, u32[]{:S(2)}, u32[]{:S(2)}) collective-permute-start(bf16[48,384]{1,0:T(8,128)(2,1)S(1)} %get-tuple-element.94), channel_id=1, source_target_pairs={{0,3},{1,0},{2,1},{3,2},{4,7},{5,4},{6,5},{7,6},{8,11},{9,8},{10,9... | collective-permute-start | bytes 110600 | tf_op jit(solution)/shard_map/ppermute | solution.py:523
  45.5 5.4 %collective-permute-start.9 = (bf16[112,192]{1,0:T(8,128)(2,1)S(1)}, bf16[112,192]{1,0:T(8,128)(2,1)S(1)}, u32[]{:S(2)}, u32[]{:S(2)}) collective-permute-start(bf16[112,192]{1,0:T(8,128)(2,1)S(1)} %get-tuple-element.71), channel_id=1, source_target_pairs={{0,28},{4,0},{8,4},{12,8},{16,12},{20,16},{24,20},{28,24},{1,29},{... | collective-permute-start | bytes 129032 | tf_op jit(solution)/shard_map/ppermute | solution.py:520
  46.6 5.2 %collective-permute-start.10 = (bf16[112,192]{1,0:T(8,128)(2,1)S(1)}, bf16[112,192]{1,0:T(8,128)(2,1)S(1)}, u32[]{:S(2)}, u32[]{:S(2)}) collective-permute-start(bf16[112,192]{1,0:T(8,128)(2,1)S(1)} %get-tuple-element.72), channel_id=1, source_target_pairs={{0,3},{1,0},{2,1},{3,2},{4,7},{5,4},{6,5},{7,6},{8,11},{9,8},{10,9... | collective-permute-start | bytes 129032 | tf_op jit(solution)/shard_map/ppermute | solution.py:523
  48.4 17.0 %collective-permute-start.17 = (bf16[48,384]{1,0:T(8,128)(2,1)S(1)}, bf16[48,384]{1,0:T(8,128)(2,1)S(1)}, u32[]{:S(2)}, u32[]{:S(2)}) collective-permute-start(bf16[48,384]{1,0:T(8,128)(2,1)S(1)} %get-tuple-element.95), channel_id=1, source_target_pairs={{0,31},{1,28},{2,29},{3,30},{4,3},{5,0},{6,1},{7,2},{8,7},{9,4},{1... | collective-permute-start | bytes 110600 | tf_op jit(solution)/shard_map/ppermute | solution.py:529
  50.8 12.7 %collective-permute-start.21 = (bf16[24,1656]{1,0:T(8,128)(2,1)S(1)}, bf16[24,1656]{1,0:T(8,128)(2,1)S(1)}, u32[]{:S(2)}, u32[]{:S(2)}) collective-permute-start(bf16[24,1656]{1,0:T(8,128)(2,1)S(1)} %shard_map.255), channel_id=1, source_target_pairs={{0,4},{4,0},{8,12},{12,8},{16,20},{20,16},{24,28},{28,24},{1,5},{5... | collective-permute-start | bytes 238472 | tf_op jit(solution)/shard_map/ppermute | solution.py:543
  60.3 6.7 %copy-start.13 = (s32[576,1]{1,0:T(8,128)S(1)}, s32[576,1]{1,0:T(8,128)}, u32[]{:S(2)}) copy-start(s32[576,1]{1,0:T(8,128)} %constant.94.leave_ref) | copy-start | bytes 6916
  60.3 6.7 %copy-start.18 = (s32[144,1]{1,0:T(8,128)S(1)}, s32[144,1]{1,0:T(8,128)}, u32[]{:S(2)}) copy-start(s32[144,1]{1,0:T(8,128)} %constant.95.result_ref) | copy-start | bytes 1732
  61.1 5.6 %collective-permute-start.14 = (bf16[48,192]{1,0:T(8,128)(2,1)S(1)}, bf16[48,192]{1,0:T(8,128)(2,1)S(1)}, u32[]{:S(2)}, u32[]{:S(2)}) collective-permute-start(bf16[48,192]{1,0:T(8,128)(2,1)S(1)} %get-tuple-element.91), channel_id=1, source_target_pairs={{0,31},{1,28},{2,29},{3,30},{4,3},{5,0},{6,1},{7,2},{8,7},{9,4},{1... | collective-permute-start | bytes 55304 | tf_op jit(solution)/shard_map/ppermute | solution.py:529
  61.8 5.0 %collective-permute-start.12 = (bf16[112,192]{1,0:T(8,128)(2,1)S(1)}, bf16[112,192]{1,0:T(8,128)(2,1)S(1)}, u32[]{:S(2)}, u32[]{:S(2)}) collective-permute-start(bf16[112,192]{1,0:T(8,128)(2,1)S(1)} %get-tuple-element.89), channel_id=1, source_target_pairs={{0,28},{4,0},{8,4},{12,8},{16,12},{20,16},{24,20},{28,24},{1,29},{... | collective-permute-start | bytes 129032 | tf_op jit(solution)/shard_map/ppermute | solution.py:520
  63.5 3.5 %collective-permute-start.13 = (bf16[112,192]{1,0:T(8,128)(2,1)S(1)}, bf16[112,192]{1,0:T(8,128)(2,1)S(1)}, u32[]{:S(2)}, u32[]{:S(2)}) collective-permute-start(bf16[112,192]{1,0:T(8,128)(2,1)S(1)} %get-tuple-element.90), channel_id=1, source_target_pairs={{0,3},{1,0},{2,1},{3,2},{4,7},{5,4},{6,5},{7,6},{8,11},{9,8},{10,9... | collective-permute-start | bytes 129032 | tf_op jit(solution)/shard_map/ppermute | solution.py:523
  65.2 4.5 %collective-permute-start.18 = (bf16[24,1656]{1,0:T(8,128)(2,1)S(1)}, bf16[24,1656]{1,0:T(8,128)(2,1)S(1)}, u32[]{:S(2)}, u32[]{:S(2)}) collective-permute-start(bf16[24,1656]{1,0:T(8,128)(2,1)S(1)} %get-tuple-element.98), channel_id=1, source_target_pairs={{0,4},{4,0},{8,12},{12,8},{16,20},{20,16},{24,28},{28,24},{1,5},{5... | collective-permute-start | bytes 238472 | tf_op jit(solution)/shard_map/ppermute | solution.py:543
  65.3 4.6 %collective-permute-start.22 = (bf16[24,1656]{1,0:T(8,128)(2,1)S(1)}, bf16[24,1656]{1,0:T(8,128)(2,1)S(1)}, u32[]{:S(2)}, u32[]{:S(2)}) collective-permute-start(bf16[24,1656]{1,0:T(8,128)(2,1)S(1)} %add_convert_fusion.1), channel_id=1, source_target_pairs={{0,8},{4,12},{8,0},{12,4},{16,24},{20,28},{24,16},{28,20},{1,9},{5... | collective-permute-start | bytes 238472 | tf_op jit(solution)/shard_map/ppermute | solution.py:543
  69.7 6.3 %collective-permute-start.19 = (bf16[24,1656]{1,0:T(8,128)(2,1)S(1)}, bf16[24,1656]{1,0:T(8,128)(2,1)S(1)}, u32[]{:S(2)}, u32[]{:S(2)}) collective-permute-start(bf16[24,1656]{1,0:T(8,128)(2,1)S(1)} %add_convert_fusion.3), channel_id=1, source_target_pairs={{0,8},{4,12},{8,0},{12,4},{16,24},{20,28},{24,16},{28,20},{1,9},{5... | collective-permute-start | bytes 238472 | tf_op jit(solution)/shard_map/ppermute | solution.py:543
  69.9 7.6 %collective-permute-start.23 = (bf16[24,1656]{1,0:T(8,128)(2,1)S(1)}, bf16[24,1656]{1,0:T(8,128)(2,1)S(1)}, u32[]{:S(2)}, u32[]{:S(2)}) collective-permute-start(bf16[24,1656]{1,0:T(8,128)(2,1)S(1)} %add_convert_fusion.kept_ref), channel_id=1, source_target_pairs={{0,16},{4,20},{8,24},{12,28},{16,0},{20,4},{24,8},{28,12},{1,17},{... | collective-permute-start | bytes 238472 | tf_op jit(solution)/shard_map/ppermute | solution.py:543
  76.1 6.0 %collective-permute-start.20 = (bf16[24,1656]{1,0:T(8,128)(2,1)S(1)}, bf16[24,1656]{1,0:T(8,128)(2,1)S(1)}, u32[]{:S(2)}, u32[]{:S(2)}) collective-permute-start(bf16[24,1656]{1,0:T(8,128)(2,1)S(1)} %add_convert_fusion.2.kept_ref), channel_id=1, source_target_pairs={{0,16},{4,20},{8,24},{12,28},{16,0},{20,4},{24,8},{28,12},{1,17},{... | collective-permute-start | bytes 238472 | tf_op jit(solution)/shard_map/ppermute | solution.py:543
  (5 other events, 9.5 us)

commit v2 on v1

--- a/solution.py
+++ b/solution.py
@@ -36,7 +36,6 @@
 
 def index_maps():
     arrive = np.zeros(576, np.int32)
-    edge = np.full(272, -1, np.int32)
     merge = np.zeros(576, np.int32)
     split = np.full(608, -1, np.int32)
     back = np.zeros(576, np.int32)
@@ -50,13 +49,10 @@
                     came = fine_spot(z, i - 3, j - 6)
                 elif i >= 3:
                     came = 576 + (i - 3) // 3 * QUAD + in_quad(z, i, j)
-                    edge[came - 576] = z * 288 + (i - 3) * 24 + 18 + j
                 elif j >= 6:
                     came = 688 + (j - 6) // 6 * QUAD + in_quad(z, i, j)
-                    edge[came - 576] = z * 288 + (i + 9) * 24 + j - 6
                 else:
                     came = 800 + in_quad(z, i, j)
-                    edge[came - 576] = z * 288 + (i + 9) * 24 + 18 + j
                 if came >= 576:
                     arrive[here] = came
                 part = (i % 2 + j % 2 * 2) * WIN + spot(z, i // 2, j // 2)
@@ -93,10 +89,10 @@
                 here = spot(z, i, j)
                 base[here] = (z * 6 + i) * SPAN + 11 - j
                 row_slot[here] = j * 16 + z * 6 + i
-    return arrive, edge, merge, split, back, leave, result, base, row_slot
-
-
-ARRIVE, EDGE, MERGE, SPLIT, BACK, LEAVE, RESULT, BASE, ROW_SLOT = index_maps()
+    return arrive, merge, split, back, leave, result, base, row_slot
+
+
+ARRIVE, MERGE, SPLIT, BACK, LEAVE, RESULT, BASE, ROW_SLOT = index_maps()
 
 
 def one_hot(column, width):
@@ -251,11 +247,36 @@
     return windows[qi // 2 * 2 + qj // 2][part : part + QUAD]
 
 
-def edge_kernel(tokens_ref, edge_ref, slon_ref, slat_ref, sdiag_ref):
-    moved = mm(one_hot(edge_ref[...], 576), tokens_ref[...]).astype(bf16)
-    slon_ref[...] = moved[0:112]
-    slat_ref[...] = moved[112:224]
-    sdiag_ref[...] = moved[224:272]
+def halves(values):
+    return [values[:, 0:192], values[:, 192:384]]
+
+
+def edge_kernel(tokens_ref, grad_ref, slon_ref, slat_ref, sdiag_ref, gloc_ref):
+    tokens = tokens_ref[...].astype(f32)
+
+    def token_quadrant(row, start):
+        pieces = []
+        for z in range(2):
+            for i in range(row, row + 3):
+                place = (z * 12 + i) * 24 + start
+                pieces.append(tokens[place : place + 6])
+        return jnp.concatenate(pieces, axis=0)
+
+    def grad_quadrant(hi, hj):
+        pieces = [
+            grad_ref[z, hi * 3 + row].astype(f32)[hj * 6 : hj * 6 + 6]
+            for z in range(2)
+            for row in range(3)
+        ]
+        return pack(pieces, 48)
+
+    slon_ref[0:112] = pack([token_quadrant(q * 3, 18) for q in range(3)], 112)
+    slat_ref[0:112] = pack([token_quadrant(9, q * 6) for q in range(3)], 112)
+    sdiag_ref[0:48] = pack([token_quadrant(9, 18)], 48)
+    gloc_ref[0:48], gloc_ref[48:96] = halves(grad_quadrant(0, 0))
+    slon_ref[112:160], slon_ref[160:208] = halves(grad_quadrant(0, 1))
+    slat_ref[112:160], slat_ref[160:208] = halves(grad_quadrant(1, 0))
+    sdiag_ref[48:96], sdiag_ref[96:144] = halves(grad_quadrant(1, 1))
 
 
 def expand(table_ref, base_ref, slot_ref, out_ref, held):
@@ -281,19 +302,7 @@
         ) * LOG2E
 
 
-def fine_bias_kernel(table_ref, base_ref, slot_ref, grad_ref, out_ref, g0, g1, g2, g3, held):
-    for index, out in enumerate((g0, g1, g2, g3)):
-        hi, hj = index // 2, index % 2
-        pieces = [
-            grad_ref[z, hi * 3 + row].astype(f32)[hj * 6 : hj * 6 + 6]
-            for z in range(2)
-            for row in range(3)
-        ]
-        out[...] = pack(pieces, 48)
-    expand(table_ref, base_ref, slot_ref, out_ref, held)
-
-
-def coarse_bias_kernel(table_ref, base_ref, slot_ref, out_ref, held):
+def bias_kernel(table_ref, base_ref, slot_ref, out_ref, held):
     expand(table_ref, base_ref, slot_ref, out_ref, held)
 
 
@@ -301,12 +310,13 @@
     table_ref[...] = table_grad(score_ref, base_ref, slot_ref, rows_ref)
 
 
-def table_sum_kernel(kept_ref, other_ref, out_ref):
-    total = kept_ref[...].astype(f32) + other_ref[...].astype(f32)
-    total = jnp.concatenate([total[0:12], total[12:24]], axis=1)
-    heads = out_ref.shape[0]
-    for b in range(out_ref.shape[1]):
-        out_ref[:, b, :] = total[b * heads : (b + 1) * heads]
+def table_sum_kernel(sums_ref, fine_ref, coarse_ref):
+    rows = jnp.concatenate([sums_ref[c].astype(f32) for c in range(sums_ref.shape[0])], axis=0)
+    for start, out in ((0, fine_ref), (24, coarse_ref)):
+        total = jnp.concatenate([rows[start : start + 12], rows[start + 12 : start + 24]], axis=1)
+        heads = out.shape[0]
+        for b in range(out.shape[1]):
+            out[:, b, :] = total[b * heads : (b + 1) * heads]
 
 
 def fine_kernel(
@@ -317,9 +327,9 @@
     source,
 ):
     source[0:576] = tokens_ref[...]
-    source[576:688] = lon_ref[...]
-    source[688:800] = lat_ref[...]
-    source[800:848] = diag_ref[...]
+    source[576:688] = lon_ref[0:112]
+    source[688:800] = lat_ref[0:112]
+    source[800:848] = diag_ref[0:48]
     everything = source[...]
     w_qkv = qkv_ref[...]
     bases = []
@@ -388,11 +398,14 @@
     active, slope = gelu_pair(mm(renormed, up_ref[...]))
     result = first + mm(active.astype(bf16), down_ref[...])
     for index, out in enumerate((c0, c1, c2, c3)):
-        out[...] = pack([result[index * QUAD : (index + 1) * QUAD]], 48)
-
-    grad = jnp.concatenate(
-        [ref[...].astype(f32)[:QUAD] for ref in (gdiag_ref, glat_ref, glon_ref, gloc_ref)], axis=0
-    )
+        piece = pack([result[index * QUAD : (index + 1) * QUAD]], 48)
+        out[0:48], out[48:96] = halves(piece)
+
+    pieces = []
+    for ref, start in ((gdiag_ref, 48), (glat_ref, 112), (glon_ref, 112), (gloc_ref, 0)):
+        both = [ref[start : start + 48], ref[start + 48 : start + 96]]
+        pieces.append(jnp.concatenate([half.astype(f32)[:QUAD] for half in both], axis=1))
+    grad = jnp.concatenate(pieces, axis=0)
     inner = mm_nt(grad.astype(bf16), down_ref[...]) * slope
     grad = grad + norm_back(mm_nt(inner.astype(bf16), up_ref[...]), renormed.astype(f32), scale2)
     mix_grad = mm_nt(grad.astype(bf16), proj_ref[...]).astype(bf16)
@@ -423,7 +436,7 @@
 def fine_back_kernel(
     dlon_ref, dlat_ref, ddiag_ref, dloc_ref, back_ref,
     q_ref, k_ref, v_ref, probs_ref, n2_ref, r2_ref, slope_ref,
-    proj_ref, up_ref, down_ref, base_ref, slot_ref,
+    proj_ref, up_ref, down_ref, base_ref, slot_ref, coarse_table_ref,
     grad_ref, dq_ref, dk_ref, dv_ref, table_ref,
     source, score_ref, rows_ref,
 ):
@@ -449,11 +462,15 @@
         dq_ref[rows, :] = dq.astype(bf16)
         dk_ref[rows, :] = dk.astype(bf16)
         dv_ref[rows, :] = dv.astype(bf16)
-    table_ref[...] = table_grad(score_ref, base_ref, slot_ref, rows_ref)
+    tables = [table_grad(score_ref, base_ref, slot_ref, rows_ref), coarse_table_ref[...]]
+    rows = jnp.concatenate([part.astype(f32) for part in tables], axis=0)
+    count = table_ref.shape[1]
+    for chunk in range(table_ref.shape[0]):
+        table_ref[chunk] = rows[chunk * count : (chunk + 1) * count].astype(bf16)
 
 
 def qkv_back_kernel(
-    grad_ref, dq_ref, dk_ref, dv_ref, n1_ref, r1_ref, qkv_ref,
+    grad_ref, dq_ref, dk_ref, dv_ref, n1_ref, r1_ref, qkv_ref, clon_ref, clat_ref, cdiag_ref,
     res_ref, slon_ref, slat_ref, sdiag_ref,
 ):
     w_qkv = qkv_ref[...]
@@ -470,28 +487,35 @@
         )
         res_ref[rows, :] = result.astype(bf16)
         windows.append(result)
-    slon_ref[...] = pack([quadrant(windows, q, 0) for q in range(1, 4)], 112)
-    slat_ref[...] = pack([quadrant(windows, 0, q) for q in range(1, 4)], 112)
-    sdiag_ref[...] = pack([quadrant(windows, 0, 0)], 48)
+    slon_ref[0:112] = pack([quadrant(windows, q, 0) for q in range(1, 4)], 112)
+    slat_ref[0:112] = pack([quadrant(windows, 0, q) for q in range(1, 4)], 112)
+    sdiag_ref[0:48] = pack([quadrant(windows, 0, 0)], 48)
+    slon_ref[112:208] = clon_ref[...]
+    slat_ref[112:208] = clat_ref[...]
+    sdiag_ref[48:144] = cdiag_ref[...]
 
 
 def last_kernel(
-    res_ref, lon_ref, lat_ref, diag_ref, leave_ref, cloc, clon, clat, cdiag, result_ref,
+    res_ref, lon_ref, lat_ref, diag_ref, leave_ref, cloc_ref, result_ref,
     tokens_ref, coarse_ref, source, coarse_source,
 ):
     source[0:576] = res_ref[...]
-    source[576:688] = lon_ref[...]
-    source[688:800] = lat_ref[...]
-    source[800:848] = diag_ref[...]
+    source[576:688] = lon_ref[0:112]
+    source[688:800] = lat_ref[0:112]
+    source[800:848] = diag_ref[0:48]
     everything = source[...]
     for w in range(4):
         rows = pl.ds(w * WIN, WIN)
         tokens_ref[rows, :] = mm(one_hot(leave_ref[rows, :], 848), everything).astype(bf16)
-    coarse_source[0:48] = cloc[...]
-    coarse_source[48:96] = clon[...]
-    coarse_source[96:144] = clat[...]
-    coarse_source[144:192] = cdiag[...]
-    moved = mm(one_hot(result_ref[...], 192), coarse_source[...])
+    picks = one_hot(result_ref[...], 192)
+    moved = []
+    for half in (0, 48):
+        coarse_source[0:48] = cloc_ref[half : half + 48]
+        coarse_source[48:96] = lon_ref[112 + half : 160 + half]
+        coarse_source[96:144] = lat_ref[112 + half : 160 + half]
+        coarse_source[144:192] = diag_ref[48 + half : 96 + half]
+        moved.append(mm(picks, coarse_source[...]))
+    moved = jnp.concatenate(moved, axis=1)
     for z in range(2):
         for row in range(6):
             start = z * 72 + row * 12
@@ -536,14 +560,16 @@
 
 def lon_total(value):
     count = lax.axis_size("lon")
+    if value.shape[0] == count:
+        parts = lax.all_to_all(value, "lon", 0, 0)
+        total = jnp.sum(parts.astype(f32), axis=0, keepdims=True).astype(bf16)
+        return lax.all_to_all(jnp.broadcast_to(total, value.shape), "lon", 0, 0)
     step = 1
-    total = value
     while step < count:
-        kept = total.astype(bf16)
-        other = lax.ppermute(kept, "lon", [(s, s ^ step) for s in range(count)])
-        total = kept.astype(f32) + other.astype(f32)
+        other = lax.ppermute(value, "lon", [(s, s ^ step) for s in range(count)])
+        value = (value.astype(f32) + other.astype(f32)).astype(bf16)
         step *= 2
-    return kept, other
+    return value
 
 
 def body(
@@ -556,20 +582,18 @@
     line = lambda index: jnp.asarray(index).reshape(1, -1)
     tok = ((576, 192), bf16)
     edges = [((112, 192), bf16), ((112, 192), bf16), ((48, 192), bf16)]
+    wide_edges = [((208, 192), bf16), ((208, 192), bf16), ((144, 192), bf16)]
+    quad = ((96, 192), bf16)
     scores = ((12 * WIN, WIN), f32)
-    table = ((24, 6 * ENTRIES), bf16)
     table_rows = ((12, 192, WIN), bf16)
-
-    arrived = send(run(edge_kernel, edges, [], 1, (flat, column(EDGE))), 1)
     held = ((12, 2, 12, 16, WIN), bf16)
-    fine_table, g00, g01, g10, g11 = run(
-        fine_bias_kernel,
-        [scores] + [((48, 384), bf16)] * 4,
-        [held],
-        2,
-        (fine_bias.transpose(1, 0, 2), line(BASE), column(ROW_SLOT), out_grad),
-    )
-    grads = (g00, *send((g01, g10, g11), 1))
+
+    *sent, grad_here = run(edge_kernel, wide_edges + [quad], [], 1, (flat, out_grad))
+    first = send(sent, 1)
+    (fine_table,) = run(
+        bias_kernel, [scores], [held], 2,
+        (fine_bias.transpose(1, 0, 2), line(BASE), column(ROW_SLOT)),
+    )
 
     labels = mask_ids.reshape(2, 2, 2, 3, 2, 2, 6)
     top = jnp.zeros((2, 2, 1, 1, 1, 1), jnp.int32).at[0, 0].set(1)[None]
@@ -588,57 +612,59 @@
         + [((24 * WIN, WIN), bf16), tok, ((576, 1), f32), tok, ((576, 1), f32), ((576, 768), bf16)],
         [((848, 192), bf16)],
         8,
-        (flat, *arrived, column(ARRIVE), fine_table, fine_mask, fine_qkv, fine_proj, fine_up, fine_down),
+        (flat, *first, column(ARRIVE), fine_table, fine_mask, fine_qkv, fine_proj, fine_up, fine_down),
     )
     q, k, v, probs, n1, r1, n2, r2, slope = fine[4:]
     arrived = send(fine[1:4], 1)
     late_table, _ = lax.optimization_barrier((coarse_bias.transpose(1, 0, 2), fine[1]))
     (coarse_table,) = run(
-        coarse_bias_kernel, [scores], [held], 2, (late_table, line(BASE), column(ROW_SLOT))
+        bias_kernel, [scores], [held], 2, (late_table, line(BASE), column(ROW_SLOT))
     )
     coarse = run(
         coarse_kernel,
-        [((48, 384), bf16)] * 4 + edges + [((336, 192), bf16), scores],
+        [quad] * 4 + edges + [((336, 192), bf16), scores],
         [((848, 192), bf16), ((12 * WIN, WIN), bf16), ((576, 192), bf16)],
         9,
         (
-            fine[0], *arrived, column(MERGE), column(SPLIT), coarse_table, coarse_mask, *grads,
+            fine[0], *arrived, column(MERGE), column(SPLIT), coarse_table, coarse_mask, grad_here, *first,
             reduce_weight, coarse_qkv, coarse_proj, coarse_up, coarse_down,
         ),
     )
     c00, c01, c10, c11 = coarse[:4]
     arrived = send(coarse[4:7], -1)
     (coarse_grad,) = run(
-        coarse_table_kernel, [table], [table_rows], 2, (coarse[8], column(BASE), line(ROW_SLOT))
-    )
-    results = (c11, *send((c10, c01, c00), -1))
-    coarse_total = lon_total(coarse_grad)
-    *passed, fine_grad = run(
+        coarse_table_kernel, [((24, 6 * ENTRIES), bf16)], [table_rows], 2,
+        (coarse[8], column(BASE), line(ROW_SLOT)),
+    )
+    chunks = 8 if lax.axis_size("lon") == 8 else 1
+    *passed, tables = run(
         fine_back_kernel,
-        [((576, 192), f32)] + [tok] * 3 + [table],
+        [((576, 192), f32)] + [tok] * 3 + [((chunks, 48 // chunks, 6 * ENTRIES), bf16)],
         [((608, 192), bf16), scores, table_rows],
         7,
         (
             *arrived, coarse[7], column(BACK), q, k, v, probs, n2, r2, slope,
-            fine_proj, fine_up, fine_down, column(BASE), line(ROW_SLOT),
+            fine_proj, fine_up, fine_down, column(BASE), line(ROW_SLOT), coarse_grad,
         ),
     )
-    fine_total = lon_total(fine_grad)
+    sums = lon_total(tables)
     fine_back = run(
-        qkv_back_kernel, [tok] + edges, [], 2, (*passed, n1, r1, fine_qkv)
+        qkv_back_kernel, [tok] + wide_edges, [], 2,
+        (*passed, n1, r1, fine_qkv, c10, c01, c00),
     )
     arrived = send(fine_back[1:4], -1)
     d_tokens, coarse_result = run(
         last_kernel,
         [tok, ((2, 6, 12, 384), bf16)],
-        [((848, 192), bf16), ((192, 384), bf16)],
+        [((848, 192), bf16), ((192, 192), bf16)],
         1,
-        (fine_back[0], *arrived, column(LEAVE), *results, column(RESULT)),
-    )
-    (coarse_out,) = run(
-        table_sum_kernel, [((HEADS_C, 1, 12 * ENTRIES), f32)], [], 1, coarse_total
-    )
-    (fine_out,) = run(table_sum_kernel, [((HEADS_F, 2, 12 * ENTRIES), f32)], [], 1, fine_total)
+        (fine_back[0], *arrived, column(LEAVE), c11, column(RESULT)),
+    )
+    fine_out, coarse_out = run(
+        table_sum_kernel,
+        [((HEADS_F, 2, 12 * ENTRIES), f32), ((HEADS_C, 1, 12 * ENTRIES), f32)],
+        [], 1, (sums,),
+    )
     return (
         coarse_result,
         d_tokens.reshape(tokens.shape),

time: 83 us -> 88.9 us (1.071); the launches traced: 82.8 us -> 87.5 us
  blocking collectives: 0 us -> 13.6 us
  starting transfers between devices: 27.8 us -> 21.6 us
  waiting for transfers between devices: 12.7 us -> 6.55 us
  local copies, waits for them, and re-layouts: 5.86 us -> 10.6 us
  Pallas kernels: 34.9 us -> 33.8 us
    all_to_all x0 -> x1, blocking collectives: none -> 13.6 us  [lon_total(): parts = lax.all_to_all(value, 'lon', 0, 0)]
    ppermute x6 -> x0, waiting for transfers between devices: 10.7 us -> none  [lon_total(): other = lax.ppermute(kept, 'lon', [(s, s ^ step) for s in range(count)])]
    unnamed x61 -> x69, local copies, waits for them, and re-layouts: 5.65 us -> 9.66 us
    ppermute x6 -> x0, starting transfers between devices: 3.96 us -> none  [lon_total(): other = lax.ppermute(kept, 'lon', [(s, s ^ step) for s in range(count)])]
    all_to_all x0 -> x1, starting transfers between devices: none -> 3.4 us  [lon_total(): return lax.all_to_all(jnp.broadcast_to(total, value.shape), 'lon', 0, 0)]
    ppermute x6 -> x4, starting transfers between devices: 9.13 us -> 5.78 us  [move(): return lax.ppermute(value, ('lon', 'lat'), pairs)]
    ppermute x6 -> x4, waiting for transfers between devices: 1.77 us -> 4.83 us  [move(): return lax.ppermute(value, ('lon', 'lat'), pairs)]
    ppermute x6 -> x4, starting transfers between devices: 6.68 us -> 4.31 us  [move(): return lax.ppermute(value, 'lat', pairs)]
  transfers between devices with their start and end apart: 24 -> 13, of which waited for: 6 -> 4; matrix products, arithmetic and copies ran while one was open for 2% -> 2% of each run, Pallas kernels for 30% -> 9%
where the time goes in v2:
time: 88.9 us; the launch traced here: 87.5 us
  Pallas kernels  33.8 us (38%)
  starting transfers between devices  21.6 us (24%)
  blocking collectives  13.6 us (15%)
  local copies, waits for them, and re-layouts  10.6 us (12%)
  waiting for transfers between devices  6.55 us (7%)
  between operations  1.08 us (1%)
    pallas_call x10, Pallas kernels, run(): pl.pallas_call(kernel, out_shape=shapes, scratch_shapes=[pltpu.VMEM(shape...  33.8 us
    all_to_all x1, blocking collectives, lon_total(): parts = lax.all_to_all(value, 'lon', 0, 0)  13.6 us
    unnamed x69, local copies, waits for them, and re-layouts  9.66 us
    ppermute x4, starting transfers between devices, move(): return lax.ppermute(value, 'lon', pairs)  8.07 us
    ppermute x4, starting transfers between devices, move(): return lax.ppermute(value, ('lon', 'lat'), pairs)  5.78 us
    ppermute x4, waiting for transfers between devices, move(): return lax.ppermute(value, ('lon', 'lat'), pairs)  4.83 us
    ppermute x4, starting transfers between devices, move(): return lax.ppermute(value, 'lat', pairs)  4.31 us
    all_to_all x1, starting transfers between devices, lon_total(): return lax.all_to_all(jnp.broadcast_to(total, value.shape), 'lon', 0, 0)  3.4 us
  transfers between devices with their start and end apart: 13, of which 4 were waited for; matrix products, arithmetic and copies ran while one was open for 2% of the time, Pallas kernels for 9%

profile of v2, /device:TPU:0, one launch (start us, length us, event | category | flops | bytes accessed | tf_op | source)
XLA Modules:
  0.0 87.5 jit_solution(17540641879782681058)
XLA Ops:
  0.6 0.9 %copy.31.grad_ref = bf16[2,6,12,384]{3,2,1,0:T(8,128)(2,1)S(1)} copy(bf16[2,6,12,384]{3,0,2,1:T(2,128)(2,1)} %param.37) | data formatting | bytes 221184 | tf_op args[13]
  1.6 1.0 %copy-done.4 = bf16[2,12,24,192]{3,2,1,0:T(8,128)(2,1)S(1)} copy-done((bf16[2,12,24,192]{3,2,1,0:T(8,128)(2,1)S(1)}, bf16[2,12,24,192]{3,2,1,0:T(8,128)(2,1)}, u32[]{:S(2)}) %copy-start.4) | copy-done | bytes 221208
  2.5 0.0 copy-start.21
  2.5 0.2 shard_map.237
  2.7 2.5 %collective-permute-start.2 = (bf16[144,192]{1,0:T(8,128)(2,1)S(1)}, bf16[144,192]{1,0:T(8,128)(2,1)S(1)}, u32[]{:S(2)}, u32[]{:S(2)}) collective-permute-start(bf16[144,192]{1,0:T(8,128)(2,1)S(1)} %get-tuple-element.58), channel_id=1, source_target_pairs={{0,5},{1,6},{2,7},{3,4},{4,9},{5,10},{6,11},{7,8},{8,13},{9,14},{1... | collective-permute-start | bytes 165896 | tf_op jit(solution)/shard_map/ppermute | solution.py:553
  5.2 1.5 %collective-permute-start = (bf16[208,192]{1,0:T(8,128)(2,1)S(1)}, bf16[208,192]{1,0:T(8,128)(2,1)S(1)}, u32[]{:S(2)}, u32[]{:S(2)}) collective-permute-start(bf16[208,192]{1,0:T(8,128)(2,1)S(1)} %get-tuple-element.56), channel_id=1, source_target_pairs={{0,4},{4,8},{8,12},{12,16},{16,20},{20,24},{24,28},{28,0},{1,5},{5... | collective-permute-start | bytes 239624 | tf_op jit(solution)/shard_map/ppermute | solution.py:544
  6.7 1.3 %collective-permute-start.1 = (bf16[208,192]{1,0:T(8,128)(2,1)S(1)}, bf16[208,192]{1,0:T(8,128)(2,1)S(1)}, u32[]{:S(2)}, u32[]{:S(2)}) collective-permute-start(bf16[208,192]{1,0:T(8,128)(2,1)S(1)} %get-tuple-element.57), channel_id=1, source_target_pairs={{0,1},{1,2},{2,3},{3,0},{4,5},{5,6},{6,7},{7,4},{8,9},{9,10},{10,1... | collective-permute-start | bytes 239624 | tf_op jit(solution)/shard_map/ppermute | solution.py:547
  8.0 0.1 mul.11
  8.2 0.1 fusion
  8.2 0.1 eq.32
  8.3 0.1 compare_select_fusion.mask_ref
  8.5 0.1 or_select_fusion.mask_ref
  8.7 0.0 copy-start.16
  8.7 2.2 %shard_map.238.bias_ref = f32[1728,144]{1,0:T(8,128)S(1)} custom-call(f32[6,2,3312]{2,1,0:T(2,128)S(1)} %bitcast.12, s32[1,144]{1,0:T(1,128)S(1)} %copy-done.21, s32[144,1]{1,0:T(8,128)S(1)} %copy-done.19), custom_call_target="tpu_custom_call" | custom-call | flops 2000000000 | bytes 1155456 | tf_op jit(solution)/shard_map/pallas_call | solution.py:529
  11.0 1.2 %copy-done.22 = f32[1728,144]{1,0:T(8,128)} copy-done((f32[1728,144]{1,0:T(8,128)}, f32[1728,144]{1,0:T(8,128)S(1)}, u32[]{:S(2)}) %copy-start.22) | copy-done | bytes 995352
  12.2 0.2 copy.33.down_ref
  12.4 1.3 %collective-permute-done.lon_ref.glon_ref = bf16[208,192]{1,0:T(8,128)(2,1)S(1)} collective-permute-done((bf16[208,192]{1,0:T(8,128)(2,1)S(1)}, bf16[208,192]{1,0:T(8,128)(2,1)S(1)}, u32[]{:S(2)}, u32[]{:S(2)}) %collective-permute-start) | collective-permute-done | bytes 79904 | tf_op jit(solution)/shard_map/ppermute | solution.py:544
  13.8 1.5 %copy-done.23 = f32[1728,144]{1,0:T(8,128)S(1)} copy-done((f32[1728,144]{1,0:T(8,128)S(1)}, f32[1728,144]{1,0:T(8,128)}, u32[]{:S(2)}) %copy-start.23) | copy-done | bytes 995352
  15.2 7.9 %shard_map.239 = (bf16[576,192]{1,0:T(8,128)(2,1)S(1)}, bf16[112,192]{1,0:T(8,128)(2,1)S(1)}, bf16[112,192]{1,0:T(8,128)(2,1)S(1)}, bf16[48,192]{1,0:T(8,128)(2,...) custom-call(bf16[576,192]{1,0:T(8,128)(2,1)S(1)} %bitcast.11, ...), custom_call_target="tpu_custom_call" | custom-call | flops 8000000000 | bytes 5966592 | tf_op jit(solution)/shard_map/pallas_call | solution.py:529
  23.1 0.7 copy-done.24
  23.9 0.2 collective-permute-start.3
  24.1 1.1 %collective-permute-start.5 = (bf16[48,192]{1,0:T(8,128)(2,1)S(1)}, bf16[48,192]{1,0:T(8,128)(2,1)S(1)}, u32[]{:S(2)}, u32[]{:S(2)}) collective-permute-start(bf16[48,192]{1,0:T(8,128)(2,1)S(1)} %get-tuple-element.62), channel_id=1, source_target_pairs={{0,5},{1,6},{2,7},{3,4},{4,9},{5,10},{6,11},{7,8},{8,13},{9,14},{1... | collective-permute-start | bytes 55304 | tf_op jit(solution)/shard_map/ppermute | solution.py:553
  25.3 0.0 copy-start.15
  25.3 1.6 %collective-permute-start.4 = (bf16[112,192]{1,0:T(8,128)(2,1)S(1)}, bf16[112,192]{1,0:T(8,128)(2,1)S(1)}, u32[]{:S(2)}, u32[]{:S(2)}) collective-permute-start(bf16[112,192]{1,0:T(8,128)(2,1)S(1)} %get-tuple-element.61), channel_id=1, source_target_pairs={{0,1},{1,2},{2,3},{3,0},{4,5},{5,6},{6,7},{7,4},{8,9},{9,10},{10,1... | collective-permute-start | bytes 129032 | tf_op jit(solution)/shard_map/ppermute | solution.py:547
  26.9 2.3 %shard_map.240.bias_ref = f32[1728,144]{1,0:T(8,128)S(1)} custom-call(f32[12,1,3312]{2,1,0:T(1,128)S(1)} %bitcast.13, s32[1,144]{1,0:T(1,128)S(1)} %copy-done.21, s32[144,1]{1,0:T(8,128)S(1)} %copy-done.19), custom_call_target="tpu_custom_call" | custom-call | flops 2000000000 | bytes 1155456 | tf_op jit(solution)/shard_map/pallas_call | solution.py:529
  29.2 2.0 %collective-permute-done.5.diag_ref = bf16[48,192]{1,0:T(8,128)(2,1)S(1)} collective-permute-done((bf16[48,192]{1,0:T(8,128)(2,1)S(1)}, bf16[48,192]{1,0:T(8,128)(2,1)S(1)}, u32[]{:S(2)}, u32[]{:S(2)}) %collective-permute-start.5) | collective-permute-done | bytes 18464 | tf_op jit(solution)/shard_map/ppermute | solution.py:553
  31.2 0.0 copy-start.18
  31.3 8.5 %shard_map.241 = (bf16[96,192]{1,0:T(8,128)(2,1)S(1)}, bf16[96,192]{1,0:T(8,128)(2,1)S(1)}, bf16[96,192]{1,0:T(8,128)(2,1)S(1)}, bf16[96,192]{1,0:T(8,128)(2,1)S...) custom-call(bf16[576,192]{1,0:T(8,128)(2,1)S(1)} %get-tuple-element., ...), custom_call_target="tpu_custom_call" | custom-call | flops 8999999488 | bytes 7165568 | tf_op jit(solution)/shard_map/pallas_call | solution.py:529
  39.7 1.2 %collective-permute-start.8 = (bf16[48,192]{1,0:T(8,128)(2,1)S(1)}, bf16[48,192]{1,0:T(8,128)(2,1)S(1)}, u32[]{:S(2)}, u32[]{:S(2)}) collective-permute-start(bf16[48,192]{1,0:T(8,128)(2,1)S(1)} %get-tuple-element.67), channel_id=1, source_target_pairs={{0,31},{1,28},{2,29},{3,30},{4,3},{5,0},{6,1},{7,2},{8,7},{9,4},{1... | collective-permute-start | bytes 55304 | tf_op jit(solution)/shard_map/ppermute | solution.py:553
  41.0 1.6 %collective-permute-start.6 = (bf16[112,192]{1,0:T(8,128)(2,1)S(1)}, bf16[112,192]{1,0:T(8,128)(2,1)S(1)}, u32[]{:S(2)}, u32[]{:S(2)}) collective-permute-start(bf16[112,192]{1,0:T(8,128)(2,1)S(1)} %get-tuple-element.65), channel_id=1, source_target_pairs={{0,28},{4,0},{8,4},{12,8},{16,12},{20,16},{24,20},{28,24},{1,29},{... | collective-permute-start | bytes 129032 | tf_op jit(solution)/shard_map/ppermute | solution.py:544
  42.6 1.4 %collective-permute-start.7 = (bf16[112,192]{1,0:T(8,128)(2,1)S(1)}, bf16[112,192]{1,0:T(8,128)(2,1)S(1)}, u32[]{:S(2)}, u32[]{:S(2)}) collective-permute-start(bf16[112,192]{1,0:T(8,128)(2,1)S(1)} %get-tuple-element.66), channel_id=1, source_target_pairs={{0,3},{1,0},{2,1},{3,2},{4,7},{5,4},{6,5},{7,6},{8,11},{9,8},{10,9... | collective-permute-start | bytes 129032 | tf_op jit(solution)/shard_map/ppermute | solution.py:547
  43.9 1.4 %shard_map.242.coarse_table_ref = bf16[24,1656]{1,0:T(8,128)(2,1)S(1)} custom-call(f32[1728,144]{1,0:T(8,128)S(1)} %get-tuple-element.76.score_ref, s32[144,1]{1,0:T(8,128)S(1)} %copy-done.18, s32[1,144]{1,0:T(1,128)S(1)} %copy-done.20), custom_call_target="tpu_custom_call" | custom-call | flops 2000000000 | bytes 1075968 | tf_op jit(solution)/shard_map/pallas_call | solution.py:529
  45.3 0.4 collective-permute-done.7.dlat_ref
  45.7 8.5 %shard_map.243 = (f32[576,192]{1,0:T(8,128)S(1)}, bf16[576,192]{1,0:T(8,128)(2,1)S(1)}, bf16[576,192]{1,0:T(8,128)(2,1)S(1)}, bf16[576,192]{1,0:T(8,128)(2,1)S(1)}, bf16[8,6,1656]{2,1,0:T(8,128)(2,1)S(1)}) custom-call(bf16[112,192]{1,0:T(8,128)(2,1)S(1)} %collective-permute-done.6.dlon_ref, bf16[112,192]{1,0:T(8,128)(2,1)S(1)} %collective-permute-done.7.dlat_ref, ...), custom_call_target="tpu_custom_call" | custom-call | flops 7000000000 | bytes 5011968 | tf_op jit(solution)/shard_map/pallas_call | solution.py:529
  54.2 0.7 copy-done.26
  54.9 0.7 copy-done.28
  55.7 13.6 %all_to_all.10 = bf16[8,6,1656]{2,1,0:T(8,128)(2,1)S(1)} all-to-all(bf16[8,6,1656]{2,1,0:T(8,128)(2,1)S(1)} %get-tuple-element.93), channel_id=1, replica_groups=mesh['lon'=8,'lat'=4] {'lon'}, dimensions={0} | all-to-all | bytes 317952 | tf_op jit(solution)/shard_map/all_to_all | solution.py:564
  69.3 0.7 broadcast_in_dim.34
  70.0 3.4 %all-to-all-start.1 = ((bf16[8,6,1656]{2,1,0:T(8,128)(2,1)}), bf16[8,6,1656]{2,1,0:T(8,128)(2,1)S(1)}, u32[]{:S(2)}, u32[]{:S(2)}) async-start(bf16[8,6,1656]{2,1,0:T(8,128)(2,1)} %broadcast_in_dim.34), calls=%async_computation.1 | async-start | bytes 425984 | tf_op jit(solution)/shard_map/all_to_all | solution.py:566
  73.4 1.0 %copy-done.27 = bf16[576,192]{1,0:T(8,128)(2,1)S(1)} copy-done((bf16[576,192]{1,0:T(8,128)(2,1)S(1)}, bf16[576,192]{1,0:T(8,128)(2,1)}, u32[]{:S(2)}) %copy-start.27) | copy-done | bytes 221208
  74.4 1.0 %copy-done.29 = bf16[576,192]{1,0:T(8,128)(2,1)S(1)} copy-done((bf16[576,192]{1,0:T(8,128)(2,1)S(1)}, bf16[576,192]{1,0:T(8,128)(2,1)}, u32[]{:S(2)}) %copy-start.29) | copy-done | bytes 221208
  75.3 0.8 shard_map.244
  76.1 4.7 %collective-permute-start.9 = (bf16[208,192]{1,0:T(8,128)(2,1)S(1)}, bf16[208,192]{1,0:T(8,128)(2,1)S(1)}, u32[]{:S(2)}, u32[]{:S(2)}) collective-permute-start(bf16[208,192]{1,0:T(8,128)(2,1)S(1)} %get-tuple-element.87), channel_id=1, source_target_pairs={{0,28},{4,0},{8,4},{12,8},{16,12},{20,16},{24,20},{28,24},{1,29},{... | collective-permute-start | bytes 239624 | tf_op jit(solution)/shard_map/ppermute | solution.py:544
  80.8 1.0 %collective-permute-start.11 = (bf16[144,192]{1,0:T(8,128)(2,1)S(1)}, bf16[144,192]{1,0:T(8,128)(2,1)S(1)}, u32[]{:S(2)}, u32[]{:S(2)}) collective-permute-start(bf16[144,192]{1,0:T(8,128)(2,1)S(1)} %get-tuple-element.89), channel_id=1, source_target_pairs={{0,31},{1,28},{2,29},{3,30},{4,3},{5,0},{6,1},{7,2},{8,7},{9,4},{1... | collective-permute-start | bytes 165896 | tf_op jit(solution)/shard_map/ppermute | solution.py:553
  81.8 2.8 %collective-permute-done.11.diag_ref = bf16[144,192]{1,0:T(8,128)(2,1)S(1)} collective-permute-done((bf16[144,192]{1,0:T(8,128)(2,1)S(1)}, bf16[144,192]{1,0:T(8,128)(2,1)S(1)}, u32[]{:S(2)}, u32[]{:S(2)}) %collective-permute-start.11) | collective-permute-done | bytes 55328 | tf_op jit(solution)/shard_map/ppermute | solution.py:553
  84.6 1.3 %shard_map.245 = (bf16[576,192]{1,0:T(8,128)(2,1)}, bf16[2,6,12,384]{3,2,1,0:T(8,128)(2,1)S(1)}) custom-call(bf16[576,192]{1,0:T(8,128)(2,1)S(1)} %get-tuple-element.86.res_ref, bf16[208,192]{1,0:T(8,128)(2,1)S(1)} %collective-permute-done.9.lon_ref, bf16[208,192]{1,0:T(8,128)(2,1)S(1)} %collective-permute-done.10.lat_ref, ...), custom_call_target="tpu_custom_call" | custom-call | flops 1000000000 | bytes 807744 | tf_op jit(solution)/shard_map/pallas_call | solution.py:529
  85.9 0.7 copy.35
  86.7 0.8 shard_map.246
  (68 shorter events, 0.2 us)
Async XLA Ops:
  1.6 1.0 %copy-start.4 = (bf16[2,12,24,192]{3,2,1,0:T(8,128)(2,1)S(1)}, bf16[2,12,24,192]{3,2,1,0:T(8,128)(2,1)}, u32[]{:S(2)}) copy-start(bf16[2,12,24,192]{3,2,1,0:T(8,128)(2,1)} %param.24) | copy-start | bytes 663556
  2.5 5.5 %copy-start.31 = (s32[2,12,24]{2,0,1:T(2,128)S(1)}, s32[2,12,24]{2,0,1:T(2,128)}, u32[]{:S(2)}) copy-start(s32[2,12,24]{2,0,1:T(2,128)} %param.25) | copy-start | bytes 6916
  2.5 5.6 %copy-start.32 = (s32[2,2]{1,0:T(2,128)S(1)}, s32[2,2]{1,0:T(2,128)}, u32[]{:S(2)}) copy-start(s32[2,2]{1,0:T(2,128)} %constant.68.clone.1) | copy-start | bytes 52
  2.5 6.1 %copy-start.9 = (f32[2,6,3312]{2,0,1:T(2,128)S(1)}, f32[2,6,3312]{2,0,1:T(2,128)}, u32[]{:S(2)}) copy-start(f32[2,6,3312]{2,0,1:T(2,128)} %param.30) | copy-start | bytes 476932
  2.5 6.1 %copy-start.19 = (s32[144,1]{1,0:T(8,128)S(1)}, s32[144,1]{1,0:T(8,128)}, u32[]{:S(2)}) copy-start(s32[144,1]{1,0:T(8,128)} %constant.86.slot_ref) | copy-start | bytes 1732
  2.5 6.1 %copy-start.21 = (s32[1,144]{1,0:T(1,128)S(1)}, s32[1,144]{1,0:T(1,128)}, u32[]{:S(2)}) copy-start(s32[1,144]{1,0:T(1,128)} %constant.85.base_ref) | copy-start | bytes 1732
  2.7 9.7 %collective-permute-start.2 = (bf16[144,192]{1,0:T(8,128)(2,1)S(1)}, bf16[144,192]{1,0:T(8,128)(2,1)S(1)}, u32[]{:S(2)}, u32[]{:S(2)}) collective-permute-start(bf16[144,192]{1,0:T(8,128)(2,1)S(1)} %get-tuple-element.58), channel_id=1, source_target_pairs={{0,5},{1,6},{2,7},{3,4},{4,9},{5,10},{6,11},{7,8},{8,13},{9,14},{1... | collective-permute-start | bytes 165896 | tf_op jit(solution)/shard_map/ppermute | solution.py:553
  5.2 8.6 %collective-permute-start = (bf16[208,192]{1,0:T(8,128)(2,1)S(1)}, bf16[208,192]{1,0:T(8,128)(2,1)S(1)}, u32[]{:S(2)}, u32[]{:S(2)}) collective-permute-start(bf16[208,192]{1,0:T(8,128)(2,1)S(1)} %get-tuple-element.56), channel_id=1, source_target_pairs={{0,4},{4,8},{8,12},{12,16},{16,20},{20,24},{24,28},{28,0},{1,5},{5... | collective-permute-start | bytes 239624 | tf_op jit(solution)/shard_map/ppermute | solution.py:544
  6.7 7.0 %collective-permute-start.1 = (bf16[208,192]{1,0:T(8,128)(2,1)S(1)}, bf16[208,192]{1,0:T(8,128)(2,1)S(1)}, u32[]{:S(2)}, u32[]{:S(2)}) collective-permute-start(bf16[208,192]{1,0:T(8,128)(2,1)S(1)} %get-tuple-element.57), channel_id=1, source_target_pairs={{0,1},{1,2},{2,3},{3,0},{4,5},{5,6},{6,7},{7,4},{8,9},{9,10},{10,1... | collective-permute-start | bytes 239624 | tf_op jit(solution)/shard_map/ppermute | solution.py:547
  8.6 3.6 %copy-start.30 = (bf16[768,192]{0,1:T(8,128)(2,1)S(1)}, bf16[768,192]{0,1:T(8,128)(2,1)}, u32[]{:S(2)}) copy-start(bf16[768,192]{0,1:T(8,128)(2,1)} %param.29) | copy-start | bytes 884740
  8.6 5.1 %copy-start.5 = (bf16[2,12,24,192]{3,2,1,0:T(8,128)(2,1)S(1)}, bf16[2,12,24,192]{3,2,1,0:T(8,128)(2,1)}, u32[]{:S(2)}) copy-start(bf16[2,12,24,192]{3,2,1,0:T(8,128)(2,1)} %param.24) | copy-start | bytes 663556
  8.7 5.1 %copy-start.7 = (bf16[192,768]{1,0:T(8,128)(2,1)S(1)}, bf16[192,768]{1,0:T(8,128)(2,1)}, u32[]{:S(2)}) copy-start(bf16[192,768]{1,0:T(8,128)(2,1)} %up_ref.5) | copy-start | bytes 884740
  8.7 5.1 %copy-start.8 = (bf16[192,576]{1,0:T(8,128)(2,1)S(1)}, bf16[192,576]{1,0:T(8,128)(2,1)}, u32[]{:S(2)}) copy-start(bf16[192,576]{1,0:T(8,128)(2,1)} %qkv_ref.5) | copy-start | bytes 663556
  8.7 5.1 %copy-start.11 = (bf16[192,192]{1,0:T(8,128)(2,1)S(1)}, bf16[192,192]{1,0:T(8,128)(2,1)}, u32[]{:S(2)}) copy-start(bf16[192,192]{1,0:T(8,128)(2,1)} %proj_ref.5) | copy-start | bytes 221188
  8.7 5.1 %copy-start.16 = (s32[576,1]{1,0:T(8,128)S(1)}, s32[576,1]{1,0:T(8,128)}, u32[]{:S(2)}) copy-start(s32[576,1]{1,0:T(8,128)} %constant.84.arrive_ref) | copy-start | bytes 6916
  11.0 1.3 %copy-start.22 = (f32[1728,144]{1,0:T(8,128)}, f32[1728,144]{1,0:T(8,128)S(1)}, u32[]{:S(2)}) copy-start(f32[1728,144]{1,0:T(8,128)S(1)} %shard_map.238.bias_ref) | copy-start | bytes 2985988
  12.4 14.5 %copy-start.10 = (f32[1,12,3312]{2,0,1:T(1,128)S(1)}, f32[1,12,3312]{2,0,1:T(1,128)}, u32[]{:S(2)}) copy-start(f32[1,12,3312]{2,0,1:T(1,128)} %param.36) | copy-start | bytes 476932
  13.8 1.5 %copy-start.23 = (f32[1728,144]{1,0:T(8,128)S(1)}, f32[1728,144]{1,0:T(8,128)}, u32[]{:S(2)}) copy-start(f32[1728,144]{1,0:T(8,128)} %copy-done.22) | copy-start | bytes 2985988
  23.1 0.7 copy-start.24
  23.9 7.3 %collective-permute-start.3 = (bf16[112,192]{1,0:T(8,128)(2,1)S(1)}, bf16[112,192]{1,0:T(8,128)(2,1)S(1)}, u32[]{:S(2)}, u32[]{:S(2)}) collective-permute-start(bf16[112,192]{1,0:T(8,128)(2,1)S(1)} %get-tuple-element.60), channel_id=1, source_target_pairs={{0,4},{4,8},{8,12},{12,16},{16,20},{20,24},{24,28},{28,0},{1,5},{5... | collective-permute-start | bytes 129032 | tf_op jit(solution)/shard_map/ppermute | solution.py:544
  24.1 7.1 %collective-permute-start.5 = (bf16[48,192]{1,0:T(8,128)(2,1)S(1)}, bf16[48,192]{1,0:T(8,128)(2,1)S(1)}, u32[]{:S(2)}, u32[]{:S(2)}) collective-permute-start(bf16[48,192]{1,0:T(8,128)(2,1)S(1)} %get-tuple-element.62), channel_id=1, source_target_pairs={{0,5},{1,6},{2,7},{3,4},{4,9},{5,10},{6,11},{7,8},{8,13},{9,14},{1... | collective-permute-start | bytes 55304 | tf_op jit(solution)/shard_map/ppermute | solution.py:553
  25.2 6.0 %copy-start = (bf16[384,1536]{1,0:T(8,128)(2,1)S(1)}, bf16[384,1536]{1,0:T(8,128)(2,1)}, u32[]{:S(2)}) copy-start(bf16[384,1536]{1,0:T(8,128)(2,1)} %up_ref.4) | copy-start | bytes 3538948
  25.2 6.0 %copy-start.1 = (bf16[1536,384]{1,0:T(8,128)(2,1)S(1)}, bf16[1536,384]{1,0:T(8,128)(2,1)}, u32[]{:S(2)}) copy-start(bf16[1536,384]{1,0:T(8,128)(2,1)} %down_ref.3) | copy-start | bytes 3538948
  25.2 6.0 %copy-start.2 = (bf16[384,1152]{1,0:T(8,128)(2,1)S(1)}, bf16[384,1152]{1,0:T(8,128)(2,1)}, u32[]{:S(2)}) copy-start(bf16[384,1152]{1,0:T(8,128)(2,1)} %qkv_ref.4) | copy-start | bytes 2654212
  25.2 6.0 %copy-start.3 = (bf16[768,384]{1,0:T(8,128)(2,1)S(1)}, bf16[768,384]{1,0:T(8,128)(2,1)}, u32[]{:S(2)}) copy-start(bf16[768,384]{1,0:T(8,128)(2,1)} %reduce_ref.1) | copy-start | bytes 1769476
  25.2 6.0 %copy-start.6 = (bf16[384,384]{1,0:T(8,128)(2,1)S(1)}, bf16[384,384]{1,0:T(8,128)(2,1)}, u32[]{:S(2)}) copy-start(bf16[384,384]{1,0:T(8,128)(2,1)} %proj_ref.4) | copy-start | bytes 884740
  25.2 6.0 %copy-start.12 = (s32[608,1]{1,0:T(8,128)S(1)}, s32[608,1]{1,0:T(8,128)}, u32[]{:S(2)}) copy-start(s32[608,1]{1,0:T(8,128)} %constant.88.split_ref) | copy-start | bytes 7300
  25.3 6.0 %copy-start.15 = (s32[576,1]{1,0:T(8,128)S(1)}, s32[576,1]{1,0:T(8,128)}, u32[]{:S(2)}) copy-start(s32[576,1]{1,0:T(8,128)} %constant.87.merge_ref) | copy-start | bytes 6916
  25.3 5.9 %collective-permute-start.4 = (bf16[112,192]{1,0:T(8,128)(2,1)S(1)}, bf16[112,192]{1,0:T(8,128)(2,1)S(1)}, u32[]{:S(2)}, u32[]{:S(2)}) collective-permute-start(bf16[112,192]{1,0:T(8,128)(2,1)S(1)} %get-tuple-element.61), channel_id=1, source_target_pairs={{0,1},{1,2},{2,3},{3,0},{4,5},{5,6},{6,7},{7,4},{8,9},{9,10},{10,1... | collective-permute-start | bytes 129032 | tf_op jit(solution)/shard_map/ppermute | solution.py:547
  31.2 12.7 %copy-start.18 = (s32[144,1]{1,0:T(8,128)S(1)}, s32[144,1]{1,0:T(8,128)}, u32[]{:S(2)}) copy-start(s32[144,1]{1,0:T(8,128)} %constant.90.base_ref) | copy-start | bytes 1732
  31.3 12.7 %copy-start.20 = (s32[1,144]{1,0:T(1,128)S(1)}, s32[1,144]{1,0:T(1,128)}, u32[]{:S(2)}) copy-start(s32[1,144]{1,0:T(1,128)} %constant.91.slot_ref) | copy-start | bytes 1732
  39.7 5.6 %collective-permute-start.8 = (bf16[48,192]{1,0:T(8,128)(2,1)S(1)}, bf16[48,192]{1,0:T(8,128)(2,1)S(1)}, u32[]{:S(2)}, u32[]{:S(2)}) collective-permute-start(bf16[48,192]{1,0:T(8,128)(2,1)S(1)} %get-tuple-element.67), channel_id=1, source_target_pairs={{0,31},{1,28},{2,29},{3,30},{4,3},{5,0},{6,1},{7,2},{8,7},{9,4},{1... | collective-permute-start | bytes 55304 | tf_op jit(solution)/shard_map/ppermute | solution.py:553
  41.0 4.4 %collective-permute-start.6 = (bf16[112,192]{1,0:T(8,128)(2,1)S(1)}, bf16[112,192]{1,0:T(8,128)(2,1)S(1)}, u32[]{:S(2)}, u32[]{:S(2)}) collective-permute-start(bf16[112,192]{1,0:T(8,128)(2,1)S(1)} %get-tuple-element.65), channel_id=1, source_target_pairs={{0,28},{4,0},{8,4},{12,8},{16,12},{20,16},{24,20},{28,24},{1,29},{... | collective-permute-start | bytes 129032 | tf_op jit(solution)/shard_map/ppermute | solution.py:544
  42.6 3.2 %collective-permute-start.7 = (bf16[112,192]{1,0:T(8,128)(2,1)S(1)}, bf16[112,192]{1,0:T(8,128)(2,1)S(1)}, u32[]{:S(2)}, u32[]{:S(2)}) collective-permute-start(bf16[112,192]{1,0:T(8,128)(2,1)S(1)} %get-tuple-element.66), channel_id=1, source_target_pairs={{0,3},{1,0},{2,1},{3,2},{4,7},{5,4},{6,5},{7,6},{8,11},{9,8},{10,9... | collective-permute-start | bytes 129032 | tf_op jit(solution)/shard_map/ppermute | solution.py:547
  43.9 1.8 %copy-start.14 = (s32[576,1]{1,0:T(8,128)S(1)}, s32[576,1]{1,0:T(8,128)}, u32[]{:S(2)}) copy-start(s32[576,1]{1,0:T(8,128)} %constant.89.back_ref) | copy-start | bytes 6916
  45.7 27.6 %copy-start.25 = (f32[576,1]{1,0:T(8,128)S(1)}, f32[576,1]{1,0:T(8,128)}, u32[]{:S(2)}) copy-start(f32[576,1]{1,0:T(8,128)} %copy-done.24) | copy-start | bytes 6916
  54.2 0.7 copy-start.26
  54.9 0.7 copy-start.28
  70.0 16.7 %all-to-all-start.1 = ((bf16[8,6,1656]{2,1,0:T(8,128)(2,1)}), bf16[8,6,1656]{2,1,0:T(8,128)(2,1)S(1)}, u32[]{:S(2)}, u32[]{:S(2)}) async-start(bf16[8,6,1656]{2,1,0:T(8,128)(2,1)} %broadcast_in_dim.34), calls=%async_computation.1 | async-start | bytes 425984 | tf_op jit(solution)/shard_map/all_to_all | solution.py:566
  73.4 1.0 %copy-start.27 = (bf16[576,192]{1,0:T(8,128)(2,1)S(1)}, bf16[576,192]{1,0:T(8,128)(2,1)}, u32[]{:S(2)}) copy-start(bf16[576,192]{1,0:T(8,128)(2,1)} %copy-done.26) | copy-start | bytes 663556
  74.4 1.0 %copy-start.29 = (bf16[576,192]{1,0:T(8,128)(2,1)S(1)}, bf16[576,192]{1,0:T(8,128)(2,1)}, u32[]{:S(2)}) copy-start(bf16[576,192]{1,0:T(8,128)(2,1)} %copy-done.28) | copy-start | bytes 663556
  75.3 9.3 %copy-start.13 = (s32[576,1]{1,0:T(8,128)S(1)}, s32[576,1]{1,0:T(8,128)}, u32[]{:S(2)}) copy-start(s32[576,1]{1,0:T(8,128)} %constant.92.leave_ref) | copy-start | bytes 6916
  75.3 9.3 %copy-start.17 = (s32[144,1]{1,0:T(8,128)S(1)}, s32[144,1]{1,0:T(8,128)}, u32[]{:S(2)}) copy-start(s32[144,1]{1,0:T(8,128)} %constant.93.result_ref) | copy-start | bytes 1732
  76.1 8.5 %collective-permute-start.9 = (bf16[208,192]{1,0:T(8,128)(2,1)S(1)}, bf16[208,192]{1,0:T(8,128)(2,1)S(1)}, u32[]{:S(2)}, u32[]{:S(2)}) collective-permute-start(bf16[208,192]{1,0:T(8,128)(2,1)S(1)} %get-tuple-element.87), channel_id=1, source_target_pairs={{0,28},{4,0},{8,4},{12,8},{16,12},{20,16},{24,20},{28,24},{1,29},{... | collective-permute-start | bytes 239624 | tf_op jit(solution)/shard_map/ppermute | solution.py:544
  80.8 3.8 %collective-permute-start.10 = (bf16[208,192]{1,0:T(8,128)(2,1)S(1)}, bf16[208,192]{1,0:T(8,128)(2,1)S(1)}, u32[]{:S(2)}, u32[]{:S(2)}) collective-permute-start(bf16[208,192]{1,0:T(8,128)(2,1)S(1)} %get-tuple-element.88), channel_id=1, source_target_pairs={{0,3},{1,0},{2,1},{3,2},{4,7},{5,4},{6,5},{7,6},{8,11},{9,8},{10,9... | collective-permute-start | bytes 239624 | tf_op jit(solution)/shard_map/ppermute | solution.py:547
  80.8 3.8 %collective-permute-start.11 = (bf16[144,192]{1,0:T(8,128)(2,1)S(1)}, bf16[144,192]{1,0:T(8,128)(2,1)S(1)}, u32[]{:S(2)}, u32[]{:S(2)}) collective-permute-start(bf16[144,192]{1,0:T(8,128)(2,1)S(1)} %get-tuple-element.89), channel_id=1, source_target_pairs={{0,31},{1,28},{2,29},{3,30},{4,3},{5,0},{6,1},{7,2},{8,7},{9,4},{1... | collective-permute-start | bytes 165896 | tf_op jit(solution)/shard_map/ppermute | solution.py:553

commit v3 on v2

--- a/solution.py
+++ b/solution.py
@@ -58,16 +58,16 @@
                 part = (i % 2 + j % 2 * 2) * WIN + spot(z, i // 2, j // 2)
                 merge[part] = came
                 if i >= 3 and j >= 6:
-                    slot = 272 + z * 162 + (i - 3) * 18 + j - 6
+                    slot = 112 + z * 162 + (i - 3) * 18 + j - 6
                     back[fine_spot(z, i - 3, j - 6)] = slot
                 elif i >= 3:
                     slot = z * 54 + (i - 3) * 6 + j
                     back[fine_spot(z, i - 3, j + 18)] = slot
                 elif j >= 6:
-                    slot = 112 + z * 54 + i * 18 + j - 6
+                    slot = 448 + z * 54 + i * 18 + j - 6
                     back[fine_spot(z, i + 9, j - 6)] = slot
                 else:
-                    slot = 224 + z * 18 + i * 6 + j
+                    slot = 560 + z * 18 + i * 6 + j
                     back[fine_spot(z, i + 9, j + 18)] = slot
                 split[slot] = part
                 natural = z * 288 + i * 24 + j
@@ -251,8 +251,19 @@
     return [values[:, 0:192], values[:, 192:384]]
 
 
-def edge_kernel(tokens_ref, grad_ref, slon_ref, slat_ref, sdiag_ref, gloc_ref):
+def edge_kernel(
+    tokens_hbm, grad_hbm, slon_ref, slat_ref, sdiag_ref, gloc_ref, tokens_ref, grad_ref, done
+):
+    copies = [
+        pltpu.make_async_copy(tokens_hbm, tokens_ref, done.at[0]),
+        pltpu.make_async_copy(grad_hbm, grad_ref, done.at[1]),
+    ]
+    for copy in copies:
+        copy.start()
+    for copy in copies:
+        copy.wait()
     tokens = tokens_ref[...].astype(f32)
+    grads = grad_ref[...].astype(f32)
 
     def token_quadrant(row, start):
         pieces = []
@@ -264,7 +275,7 @@
 
     def grad_quadrant(hi, hj):
         pieces = [
-            grad_ref[z, hi * 3 + row].astype(f32)[hj * 6 : hj * 6 + 6]
+            grads[hi * 3 + row, hj * 6 : hj * 6 + 6, z]
             for z in range(2)
             for row in range(3)
         ]
@@ -289,17 +300,20 @@
     high = table.astype(bf16)
     low = (table - high.astype(f32)).astype(bf16)
     swap = swap_rows()
-    high, low = mm(swap, high).astype(bf16), mm(swap, low).astype(bf16)
+    table = jnp.concatenate(
+        [mm(swap, high).astype(bf16), mm(swap, low).astype(bf16)], axis=0
+    )
     entry = lax.broadcasted_iota(jnp.int32, (ENTRIES, WIN), 0)
     for column in range(12):
         picker = jnp.where(entry == base_ref[...] + column, 1.0, 0.0).astype(bf16)
-        held[:, 0, column] = mm(high, picker).astype(bf16).reshape(12, 16, WIN)
-        held[:, 1, column] = mm(low, picker).astype(bf16).reshape(12, 16, WIN)
-    once = one_hot(slot_ref[...], 192)
+        picked = mm(table, picker).astype(bf16)
+        held[:, 0, column] = picked[0:192].reshape(12, 16, WIN)
+        held[:, 1, column] = picked[192:384].reshape(12, 16, WIN)
+    spots = lax.broadcasted_iota(jnp.int32, (WIN, 384), 1)
+    spots = jnp.where(spots >= 192, spots - 192, spots)
+    twice = jnp.where(spots == slot_ref[...], 1.0, 0.0).astype(bf16)
     for h in range(12):
-        out_ref[pl.ds(h * WIN, WIN), :] = (
-            mm(once, held[h, 0].reshape(192, WIN)) + mm(once, held[h, 1].reshape(192, WIN))
-        ) * LOG2E
+        out_ref[pl.ds(h * WIN, WIN), :] = mm(twice, held[h].reshape(384, WIN)) * LOG2E
 
 
 def bias_kernel(table_ref, base_ref, slot_ref, out_ref, held):
@@ -310,13 +324,12 @@
     table_ref[...] = table_grad(score_ref, base_ref, slot_ref, rows_ref)
 
 
-def table_sum_kernel(sums_ref, fine_ref, coarse_ref):
-    rows = jnp.concatenate([sums_ref[c].astype(f32) for c in range(sums_ref.shape[0])], axis=0)
-    for start, out in ((0, fine_ref), (24, coarse_ref)):
-        total = jnp.concatenate([rows[start : start + 12], rows[start + 12 : start + 24]], axis=1)
-        heads = out.shape[0]
-        for b in range(out.shape[1]):
-            out[:, b, :] = total[b * heads : (b + 1) * heads]
+def table_sum_kernel(kept_ref, other_ref, out_ref):
+    total = kept_ref[...].astype(f32) + other_ref[...].astype(f32)
+    total = jnp.concatenate([total[0:12], total[12:24]], axis=1)
+    heads = out_ref.shape[0]
+    for b in range(out_ref.shape[1]):
+        out_ref[:, b, :] = total[b * heads : (b + 1) * heads]
 
 
 def fine_kernel(
@@ -358,7 +371,7 @@
         r2_ref[rows, :] = scale
         active, slope = gelu_pair(mm(renormed, up_ref[...]))
         slope_ref[rows, :] = slope.astype(bf16)
-        result = first + mm(active.astype(bf16), down_ref[...])
+        result = first + mm_nt(active.astype(bf16), down_ref[...])
         res_ref[rows, :] = result.astype(bf16)
         windows.append(result)
     slon_ref[...] = pack([quadrant(windows, q, 3) for q in range(3)], 112)
@@ -428,61 +441,75 @@
     everything = parts_ref[...]
     moved = mm(one_hot(split_ref[...], 576), everything).astype(bf16)
     dlon_ref[...] = moved[0:112]
-    dlat_ref[...] = moved[112:224]
-    ddiag_ref[...] = moved[224:272]
-    dloc_ref[...] = moved[272:608]
-
-
-def fine_back_kernel(
-    dlon_ref, dlat_ref, ddiag_ref, dloc_ref, back_ref,
-    q_ref, k_ref, v_ref, probs_ref, n2_ref, r2_ref, slope_ref,
-    proj_ref, up_ref, down_ref, base_ref, slot_ref, coarse_table_ref,
-    grad_ref, dq_ref, dk_ref, dv_ref, table_ref,
-    source, score_ref, rows_ref,
-):
-    source[0:112] = dlon_ref[...]
-    source[112:224] = dlat_ref[...]
-    source[224:272] = ddiag_ref[...]
-    source[272:608] = dloc_ref[...]
+    dloc_ref[...] = moved[112:448]
+    dlat_ref[...] = moved[448:560]
+    ddiag_ref[...] = moved[560:608]
+
+
+def band_back(band, source, back_ref, saved, weights, outs, score_ref):
+    q_ref, k_ref, v_ref, probs_ref, n2_ref, r2_ref, slope_ref = saved
+    proj_ref, up_ref, down_ref = weights
+    grad_ref, dq_ref, dk_ref, dv_ref = outs
     everything = source[...]
-    for w in range(4):
+    for across in range(2):
+        w = band * 2 + across
         rows = pl.ds(w * WIN, WIN)
-        grad = mm(one_hot(back_ref[rows, :], 608), everything)
-        inner = mm_nt(grad.astype(bf16), down_ref[...]) * slope_ref[rows, :].astype(f32)
+        here = pl.ds(across * WIN, WIN)
+        grad = mm(one_hot(back_ref[rows, :], everything.shape[0]), everything)
+        inner = mm(grad.astype(bf16), down_ref[...]) * slope_ref[rows, :].astype(f32)
         grad = grad + norm_back(
             mm_nt(inner.astype(bf16), up_ref[...]), n2_ref[rows, :].astype(f32), r2_ref[rows, :]
         )
-        grad_ref[rows, :] = grad
+        grad_ref[here, :] = grad
         mix_grad = mm_nt(grad.astype(bf16), proj_ref[...]).astype(bf16)
         dq, dk, dv = attend_back(
             q_ref[rows, :], k_ref[rows, :], v_ref[rows, :], mix_grad,
-            probs_ref, w * 6 * WIN,
-            score_ref.at[pl.ds(w // 2 * 6 * WIN, 6 * WIN)], w % 2 == 1,
+            probs_ref, w * 6 * WIN, score_ref, across == 1,
         )
-        dq_ref[rows, :] = dq.astype(bf16)
-        dk_ref[rows, :] = dk.astype(bf16)
-        dv_ref[rows, :] = dv.astype(bf16)
-    tables = [table_grad(score_ref, base_ref, slot_ref, rows_ref), coarse_table_ref[...]]
-    rows = jnp.concatenate([part.astype(f32) for part in tables], axis=0)
-    count = table_ref.shape[1]
-    for chunk in range(table_ref.shape[0]):
-        table_ref[chunk] = rows[chunk * count : (chunk + 1) * count].astype(bf16)
-
-
-def qkv_back_kernel(
-    grad_ref, dq_ref, dk_ref, dv_ref, n1_ref, r1_ref, qkv_ref, clon_ref, clat_ref, cdiag_ref,
-    res_ref, slon_ref, slat_ref, sdiag_ref,
+        dq_ref[here, :] = dq.astype(bf16)
+        dk_ref[here, :] = dk.astype(bf16)
+        dv_ref[here, :] = dv.astype(bf16)
+
+
+def first_band_kernel(dlon_ref, dloc_ref, back_ref, *refs):
+    *refs, source = refs
+    source[0:112] = dlon_ref[...]
+    source[112:448] = dloc_ref[...]
+    band_back(0, source, back_ref, refs[:7], refs[7:10], refs[10:14], refs[14])
+
+
+def second_band_kernel(
+    dlon_ref, dloc_ref, dlat_ref, ddiag_ref, back_ref, first_ref, base_ref, slot_ref, *refs
 ):
+    *refs, source, score_ref, rows_ref = refs
+    source[0:112] = dlon_ref[...]
+    source[112:448] = dloc_ref[...]
+    source[448:560] = dlat_ref[...]
+    source[560:608] = ddiag_ref[...]
+    half = 6 * WIN
+    score_ref[pl.ds(0, half), :] = first_ref[...]
+    band_back(
+        1, source, back_ref, refs[:7], refs[7:10], refs[10:14], score_ref.at[pl.ds(half, half)]
+    )
+    refs[14][...] = table_grad(score_ref, base_ref, slot_ref, rows_ref)
+
+
+def qkv_back_kernel(*refs):
+    bands, refs = (refs[:4], refs[4:8]), refs[8:]
+    n1_ref, r1_ref, qkv_ref, clon_ref, clat_ref, cdiag_ref = refs[:6]
+    res_ref, slon_ref, slat_ref, sdiag_ref = refs[6:]
     w_qkv = qkv_ref[...]
     windows = []
     for w in range(4):
+        grad_ref, dq_ref, dk_ref, dv_ref = bands[w // 2]
         rows = pl.ds(w * WIN, WIN)
+        here = pl.ds(w % 2 * WIN, WIN)
         normed_grad = (
-            mm_nt(dq_ref[rows, :], w_qkv[:, 0:192])
-            + mm_nt(dk_ref[rows, :], w_qkv[:, 192:384])
-            + mm_nt(dv_ref[rows, :], w_qkv[:, 384:576])
+            mm_nt(dq_ref[here, :], w_qkv[:, 0:192])
+            + mm_nt(dk_ref[here, :], w_qkv[:, 192:384])
+            + mm_nt(dv_ref[here, :], w_qkv[:, 384:576])
         )
-        result = grad_ref[rows, :] + norm_back(
+        result = grad_ref[here, :] + norm_back(
             normed_grad, n1_ref[rows, :].astype(f32), r1_ref[rows, :]
         )
         res_ref[rows, :] = result.astype(bf16)
@@ -558,18 +585,17 @@
     return move(on_lon, steps, 0), move(on_lat, 0, steps), move(on_both, steps, steps)
 
 
-def lon_total(value):
+def swap(value, step):
     count = lax.axis_size("lon")
-    if value.shape[0] == count:
-        parts = lax.all_to_all(value, "lon", 0, 0)
-        total = jnp.sum(parts.astype(f32), axis=0, keepdims=True).astype(bf16)
-        return lax.all_to_all(jnp.broadcast_to(total, value.shape), "lon", 0, 0)
-    step = 1
-    while step < count:
-        other = lax.ppermute(value, "lon", [(s, s ^ step) for s in range(count)])
-        value = (value.astype(f32) + other.astype(f32)).astype(bf16)
-        step *= 2
-    return value
+    return lax.ppermute(value, "lon", [(s, s ^ step) for s in range(count)])
+
+
+def add(mine, other):
+    return (mine.astype(f32) + other.astype(f32)).astype(bf16)
+
+
+def lon_steps():
+    return [1 << bit for bit in range(lax.axis_size("lon").bit_length() - 1)]
 
 
 def body(
@@ -577,6 +603,7 @@
     coarse_qkv, coarse_proj, coarse_up, coarse_down, coarse_bias, out_grad,
 ):
     lat_index = lax.axis_index("lat")
+    fine_down = fine_down.T
     flat = tokens.reshape(576, 192)
     column = lambda index: jnp.asarray(index).reshape(-1, 1)
     line = lambda index: jnp.asarray(index).reshape(1, -1)
@@ -588,7 +615,17 @@
     table_rows = ((12, 192, WIN), bf16)
     held = ((12, 2, 12, 16, WIN), bf16)
 
-    *sent, grad_here = run(edge_kernel, wide_edges + [quad], [], 1, (flat, out_grad))
+    *sent, grad_here = pl.pallas_call(
+        edge_kernel,
+        in_specs=[pl.BlockSpec(memory_space=pl.ANY)] * 2,
+        out_shape=[jax.ShapeDtypeStruct(*shape) for shape in wide_edges + [quad]],
+        scratch_shapes=[
+            pltpu.VMEM((576, 192), bf16),
+            pltpu.VMEM((6, 12, 2, 384), bf16),
+            pltpu.SemaphoreType.DMA((2,)),
+        ],
+        compiler_params=pltpu.CompilerParams(vmem_limit_bytes=56 * 1024 * 1024),
+    )(flat, out_grad.transpose(1, 2, 0, 3))
     first = send(sent, 1)
     (fine_table,) = run(
         bias_kernel, [scores], [held], 2,
@@ -632,26 +669,52 @@
     )
     c00, c01, c10, c11 = coarse[:4]
     arrived = send(coarse[4:7], -1)
+    dlon, dlat, ddiag = arrived
+    dlat, scored = lax.optimization_barrier((dlat, coarse[8]))
     (coarse_grad,) = run(
         coarse_table_kernel, [((24, 6 * ENTRIES), bf16)], [table_rows], 2,
-        (coarse[8], column(BASE), line(ROW_SLOT)),
-    )
-    chunks = 8 if lax.axis_size("lon") == 8 else 1
-    *passed, tables = run(
-        fine_back_kernel,
-        [((576, 192), f32)] + [tok] * 3 + [((chunks, 48 // chunks, 6 * ENTRIES), bf16)],
+        (scored, column(BASE), line(ROW_SLOT)),
+    )
+    steps = lon_steps()
+    other = swap(coarse_grad, steps[-1])
+    half_tok = ((288, 192), bf16)
+    half_outs = [((288, 192), f32)] + [half_tok] * 3
+    saved = (q, k, v, probs, n2, r2, slope, fine_proj, fine_up, fine_down)
+    *first_half, first_scores = run(
+        first_band_kernel,
+        half_outs + [((6 * WIN, WIN), f32)],
+        [((448, 192), bf16)],
+        4,
+        (dlon, coarse[7], column(BACK), *saved),
+    )
+    first_scores, other = lax.optimization_barrier((first_scores, other))
+    coarse_grad = add(coarse_grad, other)
+    other = swap(coarse_grad, steps[-2])
+    *second_half, fine_grad = run(
+        second_band_kernel,
+        half_outs + [((24, 6 * ENTRIES), bf16)],
         [((608, 192), bf16), scores, table_rows],
-        7,
+        5,
         (
-            *arrived, coarse[7], column(BACK), q, k, v, probs, n2, r2, slope,
-            fine_proj, fine_up, fine_down, column(BASE), line(ROW_SLOT), coarse_grad,
+            dlon, coarse[7], dlat, ddiag, column(BACK), first_scores,
+            column(BASE), line(ROW_SLOT), *saved,
         ),
     )
-    sums = lon_total(tables)
-    fine_back = run(
+    second_half[0], other = lax.optimization_barrier((second_half[0], other))
+    coarse_grad = add(coarse_grad, other)
+    for step in reversed(steps[:-2]):
+        coarse_sums = (coarse_grad, swap(coarse_grad, step))
+        coarse_grad = add(*coarse_sums)
+    other = swap(fine_grad, steps[0])
+    fine_back = list(run(
         qkv_back_kernel, [tok] + wide_edges, [], 2,
-        (*passed, n1, r1, fine_qkv, c10, c01, c00),
-    )
+        (*first_half, *second_half, n1, r1, fine_qkv, c10, c01, c00),
+    ))
+    fine_back[0], other = lax.optimization_barrier((fine_back[0], other))
+    fine_grad = add(fine_grad, other)
+    for step in steps[1:]:
+        fine_sums = (fine_grad, swap(fine_grad, step))
+        fine_grad = add(*fine_sums)
     arrived = send(fine_back[1:4], -1)
     d_tokens, coarse_result = run(
         last_kernel,
@@ -660,11 +723,10 @@
         1,
         (fine_back[0], *arrived, column(LEAVE), c11, column(RESULT)),
     )
-    fine_out, coarse_out = run(
-        table_sum_kernel,
-        [((HEADS_F, 2, 12 * ENTRIES), f32), ((HEADS_C, 1, 12 * ENTRIES), f32)],
-        [], 1, (sums,),
-    )
+    (coarse_out,) = run(
+        table_sum_kernel, [((HEADS_C, 1, 12 * ENTRIES), f32)], [], 1, coarse_sums
+    )
+    (fine_out,) = run(table_sum_kernel, [((HEADS_F, 2, 12 * ENTRIES), f32)], [], 1, fine_sums)
     return (
         coarse_result,
         d_tokens.reshape(tokens.shape),

time: 88.9 us -> 73.4 us (0.83); the launches traced: 87.5 us -> 73.1 us
  blocking collectives: 13.6 us -> 0 us
  local copies, waits for them, and re-layouts: 10.6 us -> 3.54 us
  waiting for transfers between devices: 6.55 us -> 11.7 us
  starting transfers between devices: 21.6 us -> 19.5 us
  Pallas kernels: 33.8 us -> 35.6 us
  other arithmetic: 0.38 us -> 1.82 us
    all_to_all x1 -> x0, blocking collectives: 13.6 us -> none  [lon_total(): parts = lax.all_to_all(value, 'lon', 0, 0)]
    ppermute x0 -> x6, waiting for transfers between devices: none -> 6.35 us  [swap(): return lax.ppermute(value, 'lon', [(s, s ^ step) for s in range(count)])]
    unnamed x69 -> x51, local copies, waits for them, and re-layouts: 9.66 us -> 3.32 us
    ppermute x0 -> x6, starting transfers between devices: none -> 5.67 us  [swap(): return lax.ppermute(value, 'lon', [(s, s ^ step) for s in range(count)])]
    all_to_all x1 -> x0, starting transfers between devices: 3.4 us -> none  [lon_total(): return lax.all_to_all(jnp.broadcast_to(total, value.shape), 'lon', 0, 0)]
    ppermute x4, starting transfers between devices: 8.07 us -> 6.09 us  [move(): return lax.ppermute(value, 'lon', pairs)]
    pallas_call x0 -> x1, Pallas kernels: none -> 1.85 us  [body(): pl.pallas_call(edge_kernel, in_specs=[pl.BlockSpec(memory_space=pl.ANY)]...]
    ppermute x4, starting transfers between devices: 4.31 us -> 2.69 us  [move(): return lax.ppermute(value, 'lat', pairs)]
  transfers between devices with their start and end apart: 13 -> 18, of which waited for: 4 -> 7; matrix products, arithmetic and copies ran while one was open for 2% -> 4% of each run, Pallas kernels for 9% -> 23%
where the time goes in v3:
time: 73.4 us; the launch traced here: 73.1 us
  Pallas kernels  35.6 us (49%)
  starting transfers between devices  19.5 us (27%)
  waiting for transfers between devices  11.7 us (16%)
  local copies, waits for them, and re-layouts  3.54 us (5%)
  other arithmetic  1.82 us (2%)
  between operations  1.05 us (1%)
    pallas_call x11, Pallas kernels, run(): pl.pallas_call(kernel, out_shape=shapes, scratch_shapes=[pltpu.VMEM(shape...  33.7 us
    ppermute x6, waiting for transfers between devices, swap(): return lax.ppermute(value, 'lon', [(s, s ^ step) for s in range(count)])  6.35 us
    ppermute x4, starting transfers between devices, move(): return lax.ppermute(value, 'lon', pairs)  6.09 us
    ppermute x6, starting transfers between devices, swap(): return lax.ppermute(value, 'lon', [(s, s ^ step) for s in range(count)])  5.67 us
    ppermute x4, starting transfers between devices, move(): return lax.ppermute(value, ('lon', 'lat'), pairs)  5.02 us
    ppermute x4, waiting for transfers between devices, move(): return lax.ppermute(value, ('lon', 'lat'), pairs)  3.39 us
    unnamed x51, local copies, waits for them, and re-layouts  3.32 us
    ppermute x4, starting transfers between devices, move(): return lax.ppermute(value, 'lat', pairs)  2.69 us
  transfers between devices with their start and end apart: 18, of which 7 were waited for; matrix products, arithmetic and copies ran while one was open for 4% of the time, Pallas kernels for 23%

profile of v3, /device:TPU:0, one launch (start us, length us, event | category | flops | bytes accessed | tf_op | source)
XLA Modules:
  0.0 73.1 jit_solution(2527932585829983162)
XLA Ops:
  0.6 1.9 %shard_map.237 = (bf16[208,192]{1,0:T(8,128)(2,1)}, bf16[208,192]{1,0:T(8,128)(2,1)}, bf16[144,192]{1,0:T(8,128)(2,1)}, bf16[96,192]{1,0:T(8,128)(2,1)}) custom-call(bf16[576,192]{1,0:T(8,128)(2,1)} %bitcast.12, bf16[6,12,2,384]{3,2,1,0:T(2,128)(2,1)} %bitcast.19), custom_call_target="tpu_custom_call" | custom-call | tf_op jit(solution)/shard_map/pallas_call | solution.py:618
  2.5 2.5 %collective-permute-start.2 = (bf16[144,192]{1,0:T(8,128)(2,1)}, bf16[144,192]{1,0:T(8,128)(2,1)S(1)}, u32[]{:S(2)}, u32[]{:S(2)}) collective-permute-start(bf16[144,192]{1,0:T(8,128)(2,1)} %get-tuple-element.69), channel_id=1, source_target_pairs={{0,5},{1,6},{2,7},{3,4},{4,9},{5,10},{6,11},{7,8},{8,13},{9,14},{1... | collective-permute-start | bytes 165896 | tf_op jit(solution)/shard_map/ppermute | solution.py:580
  4.9 1.5 %collective-permute-start = (bf16[208,192]{1,0:T(8,128)(2,1)}, bf16[208,192]{1,0:T(8,128)(2,1)S(1)}, u32[]{:S(2)}, u32[]{:S(2)}) collective-permute-start(bf16[208,192]{1,0:T(8,128)(2,1)} %get-tuple-element.67), channel_id=1, source_target_pairs={{0,4},{4,8},{8,12},{12,16},{16,20},{20,24},{24,28},{28,0},{1,5},{5... | collective-permute-start | bytes 239624 | tf_op jit(solution)/shard_map/ppermute | solution.py:571
  6.5 1.3 %collective-permute-start.1 = (bf16[208,192]{1,0:T(8,128)(2,1)}, bf16[208,192]{1,0:T(8,128)(2,1)S(1)}, u32[]{:S(2)}, u32[]{:S(2)}) collective-permute-start(bf16[208,192]{1,0:T(8,128)(2,1)} %get-tuple-element.68), channel_id=1, source_target_pairs={{0,1},{1,2},{2,3},{3,0},{4,5},{5,6},{6,7},{7,4},{8,9},{9,10},{10,1... | collective-permute-start | bytes 239624 | tf_op jit(solution)/shard_map/ppermute | solution.py:574
  7.8 0.7 broadcast_multiply_fusion
  8.5 0.1 mul.11
  8.6 0.7 broadcast_select_fusion
  9.3 0.1 fusion
  9.4 0.1 eq.32
  9.5 0.1 compare_select_fusion.mask_ref
  9.7 0.1 or_select_fusion.mask_ref
  9.8 0.9 %copy-done.9 = f32[2,6,3312]{2,0,1:T(2,128)S(1)} copy-done((f32[2,6,3312]{2,0,1:T(2,128)S(1)}, f32[2,6,3312]{2,0,1:T(2,128)}, u32[]{:S(2)}) %copy-start.9) | copy-done | bytes 159000
  10.7 0.9 %copy-done.20 = s32[144,1]{1,0:T(8,128)S(1)} copy-done((s32[144,1]{1,0:T(8,128)S(1)}, s32[144,1]{1,0:T(8,128)}, u32[]{:S(2)}) %copy-start.20) | copy-done | bytes 600
  11.6 0.7 copy-done.23
  12.3 2.2 %shard_map.238.bias_ref = f32[1728,144]{1,0:T(8,128)S(1)} custom-call(f32[6,2,3312]{2,1,0:T(2,128)S(1)} %bitcast.17, s32[1,144]{1,0:T(1,128)S(1)} %copy-done.23, s32[144,1]{1,0:T(8,128)S(1)} %copy-done.20), custom_call_target="tpu_custom_call" | custom-call | flops 2000000000 | bytes 1155456 | tf_op jit(solution)/shard_map/pallas_call | solution.py:556
  14.6 7.6 %shard_map.239 = (bf16[576,192]{1,0:T(8,128)(2,1)S(1)}, bf16[112,192]{1,0:T(8,128)(2,1)S(1)}, bf16[112,192]{1,0:T(8,128)(2,1)S(1)}, bf16[48,192]{1,0:T(8,128)(2,...) custom-call(bf16[576,192]{1,0:T(8,128)(2,1)S(1)} %bitcast.13, ...), custom_call_target="tpu_custom_call" | custom-call | flops 8000000000 | bytes 5966592 | tf_op jit(solution)/shard_map/pallas_call | solution.py:556
  22.3 1.6 %collective-permute-start.3 = (bf16[112,192]{1,0:T(8,128)(2,1)S(1)}, bf16[112,192]{1,0:T(8,128)(2,1)S(1)}, u32[]{:S(2)}, u32[]{:S(2)}) collective-permute-start(bf16[112,192]{1,0:T(8,128)(2,1)S(1)} %get-tuple-element.71), channel_id=1, source_target_pairs={{0,4},{4,8},{8,12},{12,16},{16,20},{20,24},{24,28},{28,0},{1,5},{5... | collective-permute-start | bytes 129032 | tf_op jit(solution)/shard_map/ppermute | solution.py:571
  23.8 0.5 collective-permute-start.5
  24.4 0.7 collective-permute-start.4
  25.1 2.2 %shard_map.240.bias_ref = f32[1728,144]{1,0:T(8,128)S(1)} custom-call(f32[12,1,3312]{2,1,0:T(1,128)S(1)} %bitcast.18, s32[1,144]{1,0:T(1,128)S(1)} %copy-done.24, s32[144,1]{1,0:T(8,128)S(1)} %copy-done.21), custom_call_target="tpu_custom_call" | custom-call | flops 2000000000 | bytes 1155456 | tf_op jit(solution)/shard_map/pallas_call | solution.py:556
  27.3 3.4 %collective-permute-done.5.diag_ref = bf16[48,192]{1,0:T(8,128)(2,1)S(1)} collective-permute-done((bf16[48,192]{1,0:T(8,128)(2,1)S(1)}, bf16[48,192]{1,0:T(8,128)(2,1)S(1)}, u32[]{:S(2)}, u32[]{:S(2)}) %collective-permute-start.5) | collective-permute-done | bytes 18464 | tf_op jit(solution)/shard_map/ppermute | solution.py:580
  30.8 8.5 %shard_map.241 = (bf16[96,192]{1,0:T(8,128)(2,1)S(1)}, bf16[96,192]{1,0:T(8,128)(2,1)S(1)}, bf16[96,192]{1,0:T(8,128)(2,1)S(1)}, bf16[96,192]{1,0:T(8,128)(2,1)S...) custom-call(bf16[576,192]{1,0:T(8,128)(2,1)S(1)} %get-tuple-element., ...), custom_call_target="tpu_custom_call" | custom-call | flops 8999999488 | bytes 7165568 | tf_op jit(solution)/shard_map/pallas_call | solution.py:556
  39.3 0.1 collective-permute-start.7
  39.3 1.6 %collective-permute-start.8 = (bf16[48,192]{1,0:T(8,128)(2,1)S(1)}, bf16[48,192]{1,0:T(8,128)(2,1)S(1)}, u32[]{:S(2)}, u32[]{:S(2)}) collective-permute-start(bf16[48,192]{1,0:T(8,128)(2,1)S(1)} %get-tuple-element.92), channel_id=1, source_target_pairs={{0,31},{1,28},{2,29},{3,30},{4,3},{5,0},{6,1},{7,2},{8,7},{9,4},{1... | collective-permute-start | bytes 55304 | tf_op jit(solution)/shard_map/ppermute | solution.py:580
  40.9 0.8 %collective-permute-start.6 = (bf16[112,192]{1,0:T(8,128)(2,1)S(1)}, bf16[112,192]{1,0:T(8,128)(2,1)S(1)}, u32[]{:S(2)}, u32[]{:S(2)}) collective-permute-start(bf16[112,192]{1,0:T(8,128)(2,1)S(1)} %get-tuple-element.76), channel_id=1, source_target_pairs={{0,28},{4,0},{8,4},{12,8},{16,12},{20,16},{24,20},{28,24},{1,29},{... | collective-permute-start | bytes 129032 | tf_op jit(solution)/shard_map/ppermute | solution.py:571
  41.7 1.4 %shard_map.243 = bf16[24,1656]{1,0:T(8,128)(2,1)S(1)} custom-call(f32[1728,144]{1,0:T(8,128)S(1)} %get-tuple-element.94.score_ref, s32[144,1]{1,0:T(8,128)S(1)} %copy-done.19, s32[1,144]{1,0:T(1,128)S(1)} %copy-done.22), custom_call_target="tpu_custom_call" | custom-call | flops 2000000000 | bytes 1075968 | tf_op jit(solution)/shard_map/pallas_call | solution.py:556
  43.1 0.6 collective-permute-start.9
  43.7 1.5 %collective-permute-done.6.dlon_ref = bf16[112,192]{1,0:T(8,128)(2,1)S(1)} collective-permute-done((bf16[112,192]{1,0:T(8,128)(2,1)S(1)}, bf16[112,192]{1,0:T(8,128)(2,1)S(1)}, u32[]{:S(2)}, u32[]{:S(2)}) %collective-permute-start.6) | collective-permute-done | bytes 43040 | tf_op jit(solution)/shard_map/ppermute | solution.py:571
  45.2 3.5 %shard_map.242 = (f32[288,192]{1,0:T(8,128)S(1)}, bf16[288,192]{1,0:T(8,128)(2,1)S(1)}, bf16[288,192]{1,0:T(8,128)(2,1)S(1)}, bf16[288,192]{1,0:T(8,128)(2,1)S(1)}, f32[864,144]{1,0:T(8,128)S(1)}) custom-call(bf16[112,192]{1,0:T(8,128)(2,1)S(1)} %collective-permute-done.6.dlon_ref, bf16[336,192]{1,0:T(8,128)(2,1)S(1)} %get-tuple-element.77.dloc_ref, ...), custom_call_target="tpu_custom_call" | custom-call | flops 4000000000 | bytes 4655616 | tf_op jit(solution)/shard_map/pallas_call | solution.py:556
  48.7 1.5 %collective-permute-done.9 = bf16[24,1656]{1,0:T(8,128)(2,1)S(1)} collective-permute-done((bf16[24,1656]{1,0:T(8,128)(2,1)S(1)}, bf16[24,1656]{1,0:T(8,128)(2,1)S(1)}, u32[]{:S(2)}, u32[]{:S(2)}) %collective-permute-start.9) | collective-permute-done | bytes 79520 | tf_op jit(solution)/shard_map/ppermute | solution.py:590
  50.2 0.1 collective-permute-start.10
  50.3 4.6 %shard_map.244 = (f32[288,192]{1,0:T(8,128)S(1)}, bf16[288,192]{1,0:T(8,128)(2,1)S(1)}, bf16[288,192]{1,0:T(8,128)(2,1)S(1)}, bf16[288,192]{1,0:T(8,128)(2,1)S(1)}, bf16[24,1656]{1,0:T(8,128)(2,1)S(1)}) custom-call(bf16[112,192]{1,0:T(8,128)(2,1)S(1)} %collective-permute-done.6.dlon_ref, bf16[336,192]{1,0:T(8,128)(2,1)S(1)} %get-tuple-element.77.dloc_ref, ...), custom_call_target="tpu_custom_call" | custom-call | flops 5000000000 | bytes 4797696 | tf_op jit(solution)/shard_map/pallas_call | solution.py:556
  54.9 0.9 %collective-permute-start.11 = (bf16[24,1656]{1,0:T(8,128)(2,1)S(1)}, bf16[24,1656]{1,0:T(8,128)(2,1)S(1)}, u32[]{:S(2)}, u32[]{:S(2)}) collective-permute-start(bf16[24,1656]{1,0:T(8,128)(2,1)S(1)} %get-tuple-element.108), channel_id=1, source_target_pairs={{0,4},{4,0},{8,12},{12,8},{16,20},{20,16},{24,28},{28,24},{1,5},{5... | collective-permute-start | bytes 238472 | tf_op jit(solution)/shard_map/ppermute | solution.py:590
  55.8 0.8 %shard_map.245 = (bf16[576,192]{1,0:T(8,128)(2,1)S(1)}, bf16[208,192]{1,0:T(8,128)(2,1)S(1)}, bf16[208,192]{1,0:T(8,128)(2,1)S(1)}, bf16[144,192]{1,0:T(8,128)(2,1)S(1)}) custom-call(f32[288,192]{1,0:T(8,128)S(1)} %get-tuple-element.85.refs_0_, bf16[288,192]{1,0:T(8,128)(2,1)S(1)} %get-tuple-element.86.refs_1_, ...), custom_call_target="tpu_custom_call" | custom-call | flops 2000000000 | bytes 2097408 | tf_op jit(solution)/shard_map/pallas_call | solution.py:556
  56.6 2.8 %collective-permute-done.11 = bf16[24,1656]{1,0:T(8,128)(2,1)S(1)} collective-permute-done((bf16[24,1656]{1,0:T(8,128)(2,1)S(1)}, bf16[24,1656]{1,0:T(8,128)(2,1)S(1)}, u32[]{:S(2)}, u32[]{:S(2)}) %collective-permute-start.11) | collective-permute-done | bytes 79520 | tf_op jit(solution)/shard_map/ppermute | solution.py:590
  59.4 2.1 %collective-permute-start.15 = (bf16[24,1656]{1,0:T(8,128)(2,1)S(1)}, bf16[24,1656]{1,0:T(8,128)(2,1)S(1)}, u32[]{:S(2)}, u32[]{:S(2)}) collective-permute-start(bf16[24,1656]{1,0:T(8,128)(2,1)S(1)} %add_convert_fusion.2), channel_id=1, source_target_pairs={{0,8},{4,12},{8,0},{12,4},{16,24},{20,28},{24,16},{28,20},{1,9},{5... | collective-permute-start | bytes 238472 | tf_op jit(solution)/shard_map/ppermute | solution.py:590
  61.5 0.5 collective-permute-start.14
  62.1 0.4 collective-permute-start.17
  62.5 2.2 %collective-permute-start.12 = (bf16[208,192]{1,0:T(8,128)(2,1)S(1)}, bf16[208,192]{1,0:T(8,128)(2,1)S(1)}, u32[]{:S(2)}, u32[]{:S(2)}) collective-permute-start(bf16[208,192]{1,0:T(8,128)(2,1)S(1)} %get-tuple-element.110), channel_id=1, source_target_pairs={{0,28},{4,0},{8,4},{12,8},{16,12},{20,16},{24,20},{28,24},{1,29},{... | collective-permute-start | bytes 239624 | tf_op jit(solution)/shard_map/ppermute | solution.py:571
  64.7 0.6 collective-permute-start.13
  65.3 1.7 %collective-permute-start.16 = (bf16[24,1656]{1,0:T(8,128)(2,1)S(1)}, bf16[24,1656]{1,0:T(8,128)(2,1)S(1)}, u32[]{:S(2)}, u32[]{:S(2)}) collective-permute-start(bf16[24,1656]{1,0:T(8,128)(2,1)S(1)} %add_convert_fusion.1.kept_ref), channel_id=1, source_target_pairs={{0,16},{4,20},{8,24},{12,28},{16,0},{20,4},{24,8},{28,12},{1,17},{... | collective-permute-start | bytes 238472 | tf_op jit(solution)/shard_map/ppermute | solution.py:590
  67.0 1.3 %collective-permute-done.17.other_ref = bf16[24,1656]{1,0:T(8,128)(2,1)S(1)} collective-permute-done((bf16[24,1656]{1,0:T(8,128)(2,1)S(1)}, bf16[24,1656]{1,0:T(8,128)(2,1)S(1)}, u32[]{:S(2)}, u32[]{:S(2)}) %collective-permute-start.17) | collective-permute-done | bytes 79520 | tf_op jit(solution)/shard_map/ppermute | solution.py:590
  68.3 0.8 %shard_map.248 = f32[12,1,3312]{2,1,0:T(1,128)} custom-call(bf16[24,1656]{1,0:T(8,128)(2,1)S(1)} %add_convert_fusion.kept_ref, bf16[24,1656]{1,0:T(8,128)(2,1)S(1)} %collective-permute-done.17.other_ref), custom_call_target="tpu_custom_call" | custom-call | flops 1000000000 | bytes 317952 | tf_op jit(solution)/shard_map/pallas_call | solution.py:556
  69.0 0.4 collective-permute-done.12.lon_ref
  69.5 1.3 %shard_map.246 = (bf16[576,192]{1,0:T(8,128)(2,1)}, bf16[2,6,12,384]{3,2,1,0:T(8,128)(2,1)S(1)}) custom-call(bf16[576,192]{1,0:T(8,128)(2,1)S(1)} %get-tuple-element.109.res_ref, bf16[208,192]{1,0:T(8,128)(2,1)S(1)} %collective-permute-done.12.lon_ref, bf16[208,192]{1,0:T(8,128)(2,1)S(1)} %collective-permute-done.13.lat_ref, ...), custom_call_target="tpu_custom_call" | custom-call | flops 1000000000 | bytes 807744 | tf_op jit(solution)/shard_map/pallas_call | solution.py:556
  70.8 0.7 copy.29
  71.5 0.8 %collective-permute-done.16.other_ref = bf16[24,1656]{1,0:T(8,128)(2,1)S(1)} collective-permute-done((bf16[24,1656]{1,0:T(8,128)(2,1)S(1)}, bf16[24,1656]{1,0:T(8,128)(2,1)S(1)}, u32[]{:S(2)}, u32[]{:S(2)}) %collective-permute-start.16) | collective-permute-done | bytes 79520 | tf_op jit(solution)/shard_map/ppermute | solution.py:590
  72.3 0.8 %shard_map.247 = f32[6,2,3312]{2,1,0:T(2,128)} custom-call(bf16[24,1656]{1,0:T(8,128)(2,1)S(1)} %add_convert_fusion.1.kept_ref, bf16[24,1656]{1,0:T(8,128)(2,1)S(1)} %collective-permute-done.16.other_ref), custom_call_target="tpu_custom_call" | custom-call | flops 1000000000 | bytes 317952 | tf_op jit(solution)/shard_map/pallas_call | solution.py:556
  (63 shorter events, 0.3 us)
Async XLA Ops:
  2.5 12.0 %collective-permute-start.2 = (bf16[144,192]{1,0:T(8,128)(2,1)}, bf16[144,192]{1,0:T(8,128)(2,1)S(1)}, u32[]{:S(2)}, u32[]{:S(2)}) collective-permute-start(bf16[144,192]{1,0:T(8,128)(2,1)} %get-tuple-element.69), channel_id=1, source_target_pairs={{0,5},{1,6},{2,7},{3,4},{4,9},{5,10},{6,11},{7,8},{8,13},{9,14},{1... | collective-permute-start | bytes 165896 | tf_op jit(solution)/shard_map/ppermute | solution.py:580
  4.9 9.6 %collective-permute-start = (bf16[208,192]{1,0:T(8,128)(2,1)}, bf16[208,192]{1,0:T(8,128)(2,1)S(1)}, u32[]{:S(2)}, u32[]{:S(2)}) collective-permute-start(bf16[208,192]{1,0:T(8,128)(2,1)} %get-tuple-element.67), channel_id=1, source_target_pairs={{0,4},{4,8},{8,12},{12,16},{16,20},{20,24},{24,28},{28,0},{1,5},{5... | collective-permute-start | bytes 239624 | tf_op jit(solution)/shard_map/ppermute | solution.py:571
  6.5 8.1 %collective-permute-start.1 = (bf16[208,192]{1,0:T(8,128)(2,1)}, bf16[208,192]{1,0:T(8,128)(2,1)S(1)}, u32[]{:S(2)}, u32[]{:S(2)}) collective-permute-start(bf16[208,192]{1,0:T(8,128)(2,1)} %get-tuple-element.68), channel_id=1, source_target_pairs={{0,1},{1,2},{2,3},{3,0},{4,5},{5,6},{6,7},{7,4},{8,9},{9,10},{10,1... | collective-permute-start | bytes 239624 | tf_op jit(solution)/shard_map/ppermute | solution.py:574
  9.8 0.9 %copy-start.9 = (f32[2,6,3312]{2,0,1:T(2,128)S(1)}, f32[2,6,3312]{2,0,1:T(2,128)}, u32[]{:S(2)}) copy-start(f32[2,6,3312]{2,0,1:T(2,128)} %param.30) | copy-start | bytes 476932
  10.7 0.9 %copy-start.20 = (s32[144,1]{1,0:T(8,128)S(1)}, s32[144,1]{1,0:T(8,128)}, u32[]{:S(2)}) copy-start(s32[144,1]{1,0:T(8,128)} %constant.84.slot_ref) | copy-start | bytes 1732
  11.6 0.7 copy-start.23
  12.2 2.3 %copy-start = (bf16[2,12,24,192]{3,2,1,0:T(8,128)(2,1)S(1)}, bf16[2,12,24,192]{3,2,1,0:T(8,128)(2,1)}, u32[]{:S(2)}) copy-start(bf16[2,12,24,192]{3,2,1,0:T(8,128)(2,1)} %param.24) | copy-start | bytes 663556
  12.2 2.3 %copy-start.6 = (bf16[192,768]{1,0:T(8,128)(2,1)S(1)}, bf16[192,768]{1,0:T(8,128)(2,1)}, u32[]{:S(2)}) copy-start(bf16[192,768]{1,0:T(8,128)(2,1)} %refs_8_.3) | copy-start | bytes 884740
  12.2 2.3 %copy-start.7 = (bf16[768,192]{0,1:T(8,128)(2,1)S(1)}, bf16[768,192]{0,1:T(8,128)(2,1)}, u32[]{:S(2)}) copy-start(bf16[768,192]{0,1:T(8,128)(2,1)} %param.29) | copy-start | bytes 884740
  12.3 2.3 %copy-start.8 = (bf16[192,576]{1,0:T(8,128)(2,1)S(1)}, bf16[192,576]{1,0:T(8,128)(2,1)}, u32[]{:S(2)}) copy-start(bf16[192,576]{1,0:T(8,128)(2,1)} %refs_10_.1) | copy-start | bytes 663556
  12.3 2.3 %copy-start.11 = (bf16[192,192]{1,0:T(8,128)(2,1)S(1)}, bf16[192,192]{1,0:T(8,128)(2,1)}, u32[]{:S(2)}) copy-start(bf16[192,192]{1,0:T(8,128)(2,1)} %refs_7_.3) | copy-start | bytes 221188
  12.3 2.3 %copy-start.17 = (s32[576,1]{1,0:T(8,128)S(1)}, s32[576,1]{1,0:T(8,128)}, u32[]{:S(2)}) copy-start(s32[576,1]{1,0:T(8,128)} %constant.82.arrive_ref) | copy-start | bytes 6916
  14.6 10.5 %copy-start.10 = (f32[1,12,3312]{2,0,1:T(1,128)S(1)}, f32[1,12,3312]{2,0,1:T(1,128)}, u32[]{:S(2)}) copy-start(f32[1,12,3312]{2,0,1:T(1,128)} %param.36) | copy-start | bytes 476932
  14.6 10.5 %copy-start.21 = (s32[144,1]{1,0:T(8,128)S(1)}, s32[144,1]{1,0:T(8,128)}, u32[]{:S(2)}) copy-start(s32[144,1]{1,0:T(8,128)} %constant.84.slot_ref) | copy-start | bytes 1732
  14.6 10.4 %copy-start.24 = (s32[1,144]{1,0:T(1,128)S(1)}, s32[1,144]{1,0:T(1,128)}, u32[]{:S(2)}) copy-start(s32[1,144]{1,0:T(1,128)} %constant.83.base_ref) | copy-start | bytes 1732
  22.3 8.4 %collective-permute-start.3 = (bf16[112,192]{1,0:T(8,128)(2,1)S(1)}, bf16[112,192]{1,0:T(8,128)(2,1)S(1)}, u32[]{:S(2)}, u32[]{:S(2)}) collective-permute-start(bf16[112,192]{1,0:T(8,128)(2,1)S(1)} %get-tuple-element.71), channel_id=1, source_target_pairs={{0,4},{4,8},{8,12},{12,16},{16,20},{20,24},{24,28},{28,0},{1,5},{5... | collective-permute-start | bytes 129032 | tf_op jit(solution)/shard_map/ppermute | solution.py:571
  23.8 6.8 %collective-permute-start.5 = (bf16[48,192]{1,0:T(8,128)(2,1)S(1)}, bf16[48,192]{1,0:T(8,128)(2,1)S(1)}, u32[]{:S(2)}, u32[]{:S(2)}) collective-permute-start(bf16[48,192]{1,0:T(8,128)(2,1)S(1)} %get-tuple-element.73), channel_id=1, source_target_pairs={{0,5},{1,6},{2,7},{3,4},{4,9},{5,10},{6,11},{7,8},{8,13},{9,14},{1... | collective-permute-start | bytes 55304 | tf_op jit(solution)/shard_map/ppermute | solution.py:580
  24.3 6.4 %copy-start.1 = (bf16[384,1536]{1,0:T(8,128)(2,1)S(1)}, bf16[384,1536]{1,0:T(8,128)(2,1)}, u32[]{:S(2)}) copy-start(bf16[384,1536]{1,0:T(8,128)(2,1)} %up_ref.3) | copy-start | bytes 3538948
  24.3 6.4 %copy-start.2 = (bf16[1536,384]{1,0:T(8,128)(2,1)S(1)}, bf16[1536,384]{1,0:T(8,128)(2,1)}, u32[]{:S(2)}) copy-start(bf16[1536,384]{1,0:T(8,128)(2,1)} %down_ref.1) | copy-start | bytes 3538948
  24.3 6.4 %copy-start.3 = (bf16[384,1152]{1,0:T(8,128)(2,1)S(1)}, bf16[384,1152]{1,0:T(8,128)(2,1)}, u32[]{:S(2)}) copy-start(bf16[384,1152]{1,0:T(8,128)(2,1)} %qkv_ref.3) | copy-start | bytes 2654212
  24.3 6.4 %copy-start.4 = (bf16[768,384]{1,0:T(8,128)(2,1)S(1)}, bf16[768,384]{1,0:T(8,128)(2,1)}, u32[]{:S(2)}) copy-start(bf16[768,384]{1,0:T(8,128)(2,1)} %reduce_ref.1) | copy-start | bytes 1769476
  24.3 6.4 %copy-start.5 = (bf16[384,384]{1,0:T(8,128)(2,1)S(1)}, bf16[384,384]{1,0:T(8,128)(2,1)}, u32[]{:S(2)}) copy-start(bf16[384,384]{1,0:T(8,128)(2,1)} %proj_ref.3) | copy-start | bytes 884740
  24.3 6.4 %copy-start.12 = (bf16[96,192]{1,0:T(8,128)(2,1)S(1)}, bf16[96,192]{1,0:T(8,128)(2,1)}, u32[]{:S(2)}) copy-start(bf16[96,192]{1,0:T(8,128)(2,1)} %get-tuple-element.75.gloc_ref) | copy-start | bytes 110596
  24.3 6.4 %copy-start.13 = (s32[608,1]{1,0:T(8,128)S(1)}, s32[608,1]{1,0:T(8,128)}, u32[]{:S(2)}) copy-start(s32[608,1]{1,0:T(8,128)} %constant.86.split_ref) | copy-start | bytes 7300
  24.3 6.4 %copy-start.16 = (s32[576,1]{1,0:T(8,128)S(1)}, s32[576,1]{1,0:T(8,128)}, u32[]{:S(2)}) copy-start(s32[576,1]{1,0:T(8,128)} %constant.85.merge_ref) | copy-start | bytes 6916
  24.4 6.3 %collective-permute-start.4 = (bf16[112,192]{1,0:T(8,128)(2,1)S(1)}, bf16[112,192]{1,0:T(8,128)(2,1)S(1)}, u32[]{:S(2)}, u32[]{:S(2)}) collective-permute-start(bf16[112,192]{1,0:T(8,128)(2,1)S(1)} %get-tuple-element.72), channel_id=1, source_target_pairs={{0,1},{1,2},{2,3},{3,0},{4,5},{5,6},{6,7},{7,4},{8,9},{9,10},{10,1... | collective-permute-start | bytes 129032 | tf_op jit(solution)/shard_map/ppermute | solution.py:574
  30.8 10.9 %copy-start.19 = (s32[144,1]{1,0:T(8,128)S(1)}, s32[144,1]{1,0:T(8,128)}, u32[]{:S(2)}) copy-start(s32[144,1]{1,0:T(8,128)} %constant.88.base_ref) | copy-start | bytes 1732
  30.8 10.9 %copy-start.22 = (s32[1,144]{1,0:T(1,128)S(1)}, s32[1,144]{1,0:T(1,128)}, u32[]{:S(2)}) copy-start(s32[1,144]{1,0:T(1,128)} %constant.89.slot_ref) | copy-start | bytes 1732
  39.3 2.4 %collective-permute-start.7 = (bf16[112,192]{1,0:T(8,128)(2,1)S(1)}, bf16[112,192]{1,0:T(8,128)(2,1)S(1)}, u32[]{:S(2)}, u32[]{:S(2)}) collective-permute-start(bf16[112,192]{1,0:T(8,128)(2,1)S(1)} %get-tuple-element.89), channel_id=1, source_target_pairs={{0,3},{1,0},{2,1},{3,2},{4,7},{5,4},{6,5},{7,6},{8,11},{9,8},{10,9... | collective-permute-start | bytes 129032 | tf_op jit(solution)/shard_map/ppermute | solution.py:574
  39.3 11.0 %collective-permute-start.8 = (bf16[48,192]{1,0:T(8,128)(2,1)S(1)}, bf16[48,192]{1,0:T(8,128)(2,1)S(1)}, u32[]{:S(2)}, u32[]{:S(2)}) collective-permute-start(bf16[48,192]{1,0:T(8,128)(2,1)S(1)} %get-tuple-element.92), channel_id=1, source_target_pairs={{0,31},{1,28},{2,29},{3,30},{4,3},{5,0},{6,1},{7,2},{8,7},{9,4},{1... | collective-permute-start | bytes 55304 | tf_op jit(solution)/shard_map/ppermute | solution.py:580
  40.9 4.3 %collective-permute-start.6 = (bf16[112,192]{1,0:T(8,128)(2,1)S(1)}, bf16[112,192]{1,0:T(8,128)(2,1)S(1)}, u32[]{:S(2)}, u32[]{:S(2)}) collective-permute-start(bf16[112,192]{1,0:T(8,128)(2,1)S(1)} %get-tuple-element.76), channel_id=1, source_target_pairs={{0,28},{4,0},{8,4},{12,8},{16,12},{20,16},{24,20},{28,24},{1,29},{... | collective-permute-start | bytes 129032 | tf_op jit(solution)/shard_map/ppermute | solution.py:571
  41.7 3.5 %copy-start.15 = (s32[576,1]{1,0:T(8,128)S(1)}, s32[576,1]{1,0:T(8,128)}, u32[]{:S(2)}) copy-start(s32[576,1]{1,0:T(8,128)} %constant.87.back_ref) | copy-start | bytes 6916
  43.1 7.1 %collective-permute-start.9 = (bf16[24,1656]{1,0:T(8,128)(2,1)S(1)}, bf16[24,1656]{1,0:T(8,128)(2,1)S(1)}, u32[]{:S(2)}, u32[]{:S(2)}) collective-permute-start(bf16[24,1656]{1,0:T(8,128)(2,1)S(1)} %shard_map.243), channel_id=1, source_target_pairs={{0,16},{4,20},{8,24},{12,28},{16,0},{20,4},{24,8},{28,12},{1,17},{... | collective-permute-start | bytes 238472 | tf_op jit(solution)/shard_map/ppermute | solution.py:590
  50.2 5.6 %collective-permute-start.10 = (bf16[24,1656]{1,0:T(8,128)(2,1)S(1)}, bf16[24,1656]{1,0:T(8,128)(2,1)S(1)}, u32[]{:S(2)}, u32[]{:S(2)}) collective-permute-start(bf16[24,1656]{1,0:T(8,128)(2,1)S(1)} %add_convert_fusion.3), channel_id=1, source_target_pairs={{0,8},{4,12},{8,0},{12,4},{16,24},{20,28},{24,16},{28,20},{1,9},{5... | collective-permute-start | bytes 238472 | tf_op jit(solution)/shard_map/ppermute | solution.py:590
  54.9 4.5 %collective-permute-start.11 = (bf16[24,1656]{1,0:T(8,128)(2,1)S(1)}, bf16[24,1656]{1,0:T(8,128)(2,1)S(1)}, u32[]{:S(2)}, u32[]{:S(2)}) collective-permute-start(bf16[24,1656]{1,0:T(8,128)(2,1)S(1)} %get-tuple-element.108), channel_id=1, source_target_pairs={{0,4},{4,0},{8,12},{12,8},{16,20},{20,16},{24,28},{28,24},{1,5},{5... | collective-permute-start | bytes 238472 | tf_op jit(solution)/shard_map/ppermute | solution.py:590
  59.4 5.9 %collective-permute-start.15 = (bf16[24,1656]{1,0:T(8,128)(2,1)S(1)}, bf16[24,1656]{1,0:T(8,128)(2,1)S(1)}, u32[]{:S(2)}, u32[]{:S(2)}) collective-permute-start(bf16[24,1656]{1,0:T(8,128)(2,1)S(1)} %add_convert_fusion.2), channel_id=1, source_target_pairs={{0,8},{4,12},{8,0},{12,4},{16,24},{20,28},{24,16},{28,20},{1,9},{5... | collective-permute-start | bytes 238472 | tf_op jit(solution)/shard_map/ppermute | solution.py:590
  61.5 7.5 %collective-permute-start.14 = (bf16[144,192]{1,0:T(8,128)(2,1)S(1)}, bf16[144,192]{1,0:T(8,128)(2,1)S(1)}, u32[]{:S(2)}, u32[]{:S(2)}) collective-permute-start(bf16[144,192]{1,0:T(8,128)(2,1)S(1)} %get-tuple-element.112), channel_id=1, source_target_pairs={{0,31},{1,28},{2,29},{3,30},{4,3},{5,0},{6,1},{7,2},{8,7},{9,4},{1... | collective-permute-start | bytes 165896 | tf_op jit(solution)/shard_map/ppermute | solution.py:580
  62.1 6.2 %collective-permute-start.17 = (bf16[24,1656]{1,0:T(8,128)(2,1)S(1)}, bf16[24,1656]{1,0:T(8,128)(2,1)S(1)}, u32[]{:S(2)}, u32[]{:S(2)}) collective-permute-start(bf16[24,1656]{1,0:T(8,128)(2,1)S(1)} %add_convert_fusion.kept_ref), channel_id=1, source_target_pairs={{0,4},{4,0},{8,12},{12,8},{16,20},{20,16},{24,28},{28,24},{1,5},{5... | collective-permute-start | bytes 238472 | tf_op jit(solution)/shard_map/ppermute | solution.py:590
  62.5 7.0 %collective-permute-start.12 = (bf16[208,192]{1,0:T(8,128)(2,1)S(1)}, bf16[208,192]{1,0:T(8,128)(2,1)S(1)}, u32[]{:S(2)}, u32[]{:S(2)}) collective-permute-start(bf16[208,192]{1,0:T(8,128)(2,1)S(1)} %get-tuple-element.110), channel_id=1, source_target_pairs={{0,28},{4,0},{8,4},{12,8},{16,12},{20,16},{24,20},{28,24},{1,29},{... | collective-permute-start | bytes 239624 | tf_op jit(solution)/shard_map/ppermute | solution.py:571
  64.7 4.8 %collective-permute-start.13 = (bf16[208,192]{1,0:T(8,128)(2,1)S(1)}, bf16[208,192]{1,0:T(8,128)(2,1)S(1)}, u32[]{:S(2)}, u32[]{:S(2)}) collective-permute-start(bf16[208,192]{1,0:T(8,128)(2,1)S(1)} %get-tuple-element.111), channel_id=1, source_target_pairs={{0,3},{1,0},{2,1},{3,2},{4,7},{5,4},{6,5},{7,6},{8,11},{9,8},{10,9... | collective-permute-start | bytes 239624 | tf_op jit(solution)/shard_map/ppermute | solution.py:574
  65.3 4.2 %copy-start.14 = (s32[576,1]{1,0:T(8,128)S(1)}, s32[576,1]{1,0:T(8,128)}, u32[]{:S(2)}) copy-start(s32[576,1]{1,0:T(8,128)} %constant.90.leave_ref) | copy-start | bytes 6916
  65.3 4.1 %copy-start.18 = (s32[144,1]{1,0:T(8,128)S(1)}, s32[144,1]{1,0:T(8,128)}, u32[]{:S(2)}) copy-start(s32[144,1]{1,0:T(8,128)} %constant.91.result_ref) | copy-start | bytes 1732
  65.3 7.0 %collective-permute-start.16 = (bf16[24,1656]{1,0:T(8,128)(2,1)S(1)}, bf16[24,1656]{1,0:T(8,128)(2,1)S(1)}, u32[]{:S(2)}, u32[]{:S(2)}) collective-permute-start(bf16[24,1656]{1,0:T(8,128)(2,1)S(1)} %add_convert_fusion.1.kept_ref), channel_id=1, source_target_pairs={{0,16},{4,20},{8,24},{12,28},{16,0},{20,4},{24,8},{28,12},{1,17},{... | collective-permute-start | bytes 238472 | tf_op jit(solution)/shard_map/ppermute | solution.py:590

commit v4 on v3

--- a/solution.py
+++ b/solution.py
@@ -80,19 +80,34 @@
                 else:
                     leave[natural] = 800 + in_quad(z, i, j)
     result = np.zeros(WIN, np.int32)
-    base = np.zeros(WIN, np.int32)
-    row_slot = np.zeros(WIN, np.int32)
     for z in range(2):
         for i in range(6):
             for j in range(12):
                 result[z * 72 + i * 12 + j] = (i // 3 * 2 + j // 6) * 48 + in_quad(z, i, j)
-                here = spot(z, i, j)
-                base[here] = (z * 6 + i) * SPAN + 11 - j
-                row_slot[here] = j * 16 + z * 6 + i
-    return arrive, merge, split, back, leave, result, base, row_slot
-
-
-ARRIVE, MERGE, SPLIT, BACK, LEAVE, RESULT, BASE, ROW_SLOT = index_maps()
+    return arrive, merge, split, back, leave, result
+
+
+ARRIVE, MERGE, SPLIT, BACK, LEAVE, RESULT = index_maps()
+
+
+def places(shape, axis):
+    t = lax.broadcasted_iota(jnp.int32, shape, axis)
+    quad = (t * 57) >> 11
+    t = t - quad * QUAD
+    level = (t * 57) >> 10
+    t = t - level * 18
+    row = (t * 43) >> 8
+    return level * 6 + (quad >> 1) * 3 + row, t - row * 6 + (quad & 1) * 6
+
+
+def entry_base(shape, axis):
+    row, column = places(shape, axis)
+    return row * SPAN + 11 - column
+
+
+def row_slot(shape, axis):
+    row, column = places(shape, axis)
+    return column * 16 + row
 
 
 def one_hot(column, width):
@@ -217,16 +232,17 @@
     ).astype(bf16)
 
 
-def table_grad(score_ref, base_ref, slot_ref, rows_ref):
+def table_grad(score_ref, rows_ref):
     regroup = jnp.where(
-        lax.broadcasted_iota(jnp.int32, (192, WIN), 0) == slot_ref[...], 1.0, 0.0
+        lax.broadcasted_iota(jnp.int32, (192, WIN), 0) == row_slot((1, WIN), 1), 1.0, 0.0
     ).astype(bf16)
     for h in range(12):
         moved = mm(regroup, score_ref[pl.ds(h * WIN, WIN), :].astype(bf16)).astype(bf16)
         rows_ref[:, pl.ds(h * 16, 16), :] = moved.reshape(12, 16, WIN)
     total = jnp.zeros((192, ENTRIES), f32)
+    base = entry_base((WIN, 1), 0)
     for column in range(12):
-        total += mm(rows_ref[column], one_hot(base_ref[...] + column, ENTRIES))
+        total += mm(rows_ref[column], one_hot(base + column, ENTRIES))
     swapped = mm(swap_rows(), total.astype(bf16))
     halves = [
         jnp.concatenate([swapped[a * 16 : a * 16 + 12] for a in range(start, start + 6)], axis=1)
@@ -251,17 +267,7 @@
     return [values[:, 0:192], values[:, 192:384]]
 
 
-def edge_kernel(
-    tokens_hbm, grad_hbm, slon_ref, slat_ref, sdiag_ref, gloc_ref, tokens_ref, grad_ref, done
-):
-    copies = [
-        pltpu.make_async_copy(tokens_hbm, tokens_ref, done.at[0]),
-        pltpu.make_async_copy(grad_hbm, grad_ref, done.at[1]),
-    ]
-    for copy in copies:
-        copy.start()
-    for copy in copies:
-        copy.wait()
+def edge_kernel(tokens_ref, grad_ref, slon_ref, slat_ref, sdiag_ref, gloc_ref):
     tokens = tokens_ref[...].astype(f32)
     grads = grad_ref[...].astype(f32)
 
@@ -290,7 +296,7 @@
     sdiag_ref[48:96], sdiag_ref[96:144] = halves(grad_quadrant(1, 1))
 
 
-def expand(table_ref, base_ref, slot_ref, out_ref, held):
+def expand(table_ref, out_ref, held):
     table = jnp.concatenate([table_ref[:, b, :] for b in range(table_ref.shape[1])], axis=0)
     filler = jnp.zeros((4, ENTRIES), f32)
     pieces = []
@@ -304,24 +310,25 @@
         [mm(swap, high).astype(bf16), mm(swap, low).astype(bf16)], axis=0
     )
     entry = lax.broadcasted_iota(jnp.int32, (ENTRIES, WIN), 0)
+    base = entry_base((1, WIN), 1)
     for column in range(12):
-        picker = jnp.where(entry == base_ref[...] + column, 1.0, 0.0).astype(bf16)
+        picker = jnp.where(entry == base + column, 1.0, 0.0).astype(bf16)
         picked = mm(table, picker).astype(bf16)
         held[:, 0, column] = picked[0:192].reshape(12, 16, WIN)
         held[:, 1, column] = picked[192:384].reshape(12, 16, WIN)
     spots = lax.broadcasted_iota(jnp.int32, (WIN, 384), 1)
     spots = jnp.where(spots >= 192, spots - 192, spots)
-    twice = jnp.where(spots == slot_ref[...], 1.0, 0.0).astype(bf16)
+    twice = jnp.where(spots == row_slot((WIN, 1), 0), 1.0, 0.0).astype(bf16)
     for h in range(12):
         out_ref[pl.ds(h * WIN, WIN), :] = mm(twice, held[h].reshape(384, WIN)) * LOG2E
 
 
-def bias_kernel(table_ref, base_ref, slot_ref, out_ref, held):
-    expand(table_ref, base_ref, slot_ref, out_ref, held)
-
-
-def coarse_table_kernel(score_ref, base_ref, slot_ref, table_ref, rows_ref):
-    table_ref[...] = table_grad(score_ref, base_ref, slot_ref, rows_ref)
+def bias_kernel(table_ref, out_ref, held):
+    expand(table_ref, out_ref, held)
+
+
+def coarse_table_kernel(score_ref, table_ref, rows_ref):
+    table_ref[...] = table_grad(score_ref, rows_ref)
 
 
 def table_sum_kernel(kept_ref, other_ref, out_ref):
@@ -332,13 +339,11 @@
         out_ref[:, b, :] = total[b * heads : (b + 1) * heads]
 
 
-def fine_kernel(
-    tokens_ref, lon_ref, lat_ref, diag_ref, arrive_ref, bias_ref, mask_ref,
-    qkv_ref, proj_ref, up_ref, down_ref,
-    res_ref, slon_ref, slat_ref, sdiag_ref,
-    q_ref, k_ref, v_ref, probs_ref, n1_ref, r1_ref, n2_ref, r2_ref, slope_ref,
-    source,
-):
+def fine_windows(numbers, refs):
+    tokens_ref, lon_ref, lat_ref, diag_ref, arrive_ref, bias_ref, mask_ref = refs[:7]
+    qkv_ref, proj_ref, up_ref, down_ref, res_ref = refs[7:12]
+    q_ref, k_ref, v_ref, probs_ref, n1_ref, r1_ref, n2_ref, r2_ref, slope_ref = refs[12:21]
+    source = refs[21]
     source[0:576] = tokens_ref[...]
     source[576:688] = lon_ref[0:112]
     source[688:800] = lat_ref[0:112]
@@ -346,9 +351,9 @@
     everything = source[...]
     w_qkv = qkv_ref[...]
     bases = []
-    for w in range(4):
-        rows = pl.ds(w * WIN, WIN)
-        base = mm(one_hot(arrive_ref[rows, :], 848), everything)
+    for slot, w in enumerate(numbers):
+        rows = pl.ds(slot * WIN, WIN)
+        base = mm(one_hot(arrive_ref[pl.ds(w * WIN, WIN), :], 848), everything)
         normed, scale = norm(base)
         normed = normed.astype(bf16)
         n1_ref[rows, :] = normed
@@ -357,14 +362,14 @@
         k_ref[rows, :] = mm(normed, w_qkv[:, 192:384]).astype(bf16)
         v_ref[rows, :] = mm(normed, w_qkv[:, 384:576]).astype(bf16)
         bases.append(base)
-    windows = []
-    for w in range(4):
-        rows = pl.ds(w * WIN, WIN)
+    windows = {}
+    for slot, w in enumerate(numbers):
+        rows = pl.ds(slot * WIN, WIN)
         mixture = attend(
             q_ref[rows, :], k_ref[rows, :], v_ref[rows, :],
-            bias_ref, w // 2 * 6 * WIN, mask_ref[w], probs_ref, w * 6 * WIN,
+            bias_ref, w // 2 * 6 * WIN, mask_ref[w], probs_ref, slot * 6 * WIN,
         ).astype(bf16)
-        first = bases[w] + mm(mixture, proj_ref[...])
+        first = bases[slot] + mm(mixture, proj_ref[...])
         renormed, scale = norm(first)
         renormed = renormed.astype(bf16)
         n2_ref[rows, :] = renormed
@@ -373,20 +378,31 @@
         slope_ref[rows, :] = slope.astype(bf16)
         result = first + mm_nt(active.astype(bf16), down_ref[...])
         res_ref[rows, :] = result.astype(bf16)
-        windows.append(result)
+        windows[w] = result
+    return windows
+
+
+def fine_edge_kernel(*refs):
+    slon_ref, slat_ref, sdiag_ref = refs[11:14]
+    windows = fine_windows((1, 2, 3), refs[:11] + refs[14:])
     slon_ref[...] = pack([quadrant(windows, q, 3) for q in range(3)], 112)
     slat_ref[...] = pack([quadrant(windows, 3, q) for q in range(3)], 112)
     sdiag_ref[...] = pack([quadrant(windows, 3, 3)], 48)
 
 
+def fine_inner_kernel(*refs):
+    fine_windows((0,), refs)
+
+
 def coarse_kernel(
-    res_ref, lon_ref, lat_ref, diag_ref, merge_ref, split_ref, bias_ref, mask_ref,
+    inner_ref, res_ref, lon_ref, lat_ref, diag_ref, merge_ref, split_ref, bias_ref, mask_ref,
     gloc_ref, glon_ref, glat_ref, gdiag_ref,
     reduce_ref, qkv_ref, proj_ref, up_ref, down_ref,
     c0, c1, c2, c3, dlon_ref, dlat_ref, ddiag_ref, dloc_ref, score_ref,
     source, probs_ref, parts_ref,
 ):
-    source[0:576] = res_ref[...]
+    source[0:144] = inner_ref[...]
+    source[144:576] = res_ref[...]
     source[576:688] = lon_ref[...]
     source[688:800] = lat_ref[...]
     source[800:848] = diag_ref[...]
@@ -446,16 +462,15 @@
     ddiag_ref[...] = moved[560:608]
 
 
-def band_back(band, source, back_ref, saved, weights, outs, score_ref):
-    q_ref, k_ref, v_ref, probs_ref, n2_ref, r2_ref, slope_ref = saved
+def band_back(parts, source, back_ref, weights, outs, score_ref):
     proj_ref, up_ref, down_ref = weights
     grad_ref, dq_ref, dk_ref, dv_ref = outs
     everything = source[...]
-    for across in range(2):
-        w = band * 2 + across
-        rows = pl.ds(w * WIN, WIN)
+    for across, (w, slot, saved) in enumerate(parts):
+        q_ref, k_ref, v_ref, probs_ref, n2_ref, r2_ref, slope_ref = saved
+        rows = pl.ds(slot * WIN, WIN)
         here = pl.ds(across * WIN, WIN)
-        grad = mm(one_hot(back_ref[rows, :], everything.shape[0]), everything)
+        grad = mm(one_hot(back_ref[pl.ds(w * WIN, WIN), :], everything.shape[0]), everything)
         inner = mm(grad.astype(bf16), down_ref[...]) * slope_ref[rows, :].astype(f32)
         grad = grad + norm_back(
             mm_nt(inner.astype(bf16), up_ref[...]), n2_ref[rows, :].astype(f32), r2_ref[rows, :]
@@ -464,7 +479,7 @@
         mix_grad = mm_nt(grad.astype(bf16), proj_ref[...]).astype(bf16)
         dq, dk, dv = attend_back(
             q_ref[rows, :], k_ref[rows, :], v_ref[rows, :], mix_grad,
-            probs_ref, w * 6 * WIN, score_ref, across == 1,
+            probs_ref, slot * 6 * WIN, score_ref, across == 1,
         )
         dq_ref[here, :] = dq.astype(bf16)
         dk_ref[here, :] = dk.astype(bf16)
@@ -475,11 +490,12 @@
     *refs, source = refs
     source[0:112] = dlon_ref[...]
     source[112:448] = dloc_ref[...]
-    band_back(0, source, back_ref, refs[:7], refs[7:10], refs[10:14], refs[14])
+    parts = ((0, 0, refs[:7]), (1, 0, refs[7:14]))
+    band_back(parts, source, back_ref, refs[14:17], refs[17:21], refs[21])
 
 
 def second_band_kernel(
-    dlon_ref, dloc_ref, dlat_ref, ddiag_ref, back_ref, first_ref, base_ref, slot_ref, *refs
+    dlon_ref, dloc_ref, dlat_ref, ddiag_ref, back_ref, first_ref, *refs
 ):
     *refs, source, score_ref, rows_ref = refs
     source[0:112] = dlon_ref[...]
@@ -488,16 +504,18 @@
     source[560:608] = ddiag_ref[...]
     half = 6 * WIN
     score_ref[pl.ds(0, half), :] = first_ref[...]
+    parts = ((2, 1, refs[:7]), (3, 2, refs[:7]))
     band_back(
-        1, source, back_ref, refs[:7], refs[7:10], refs[10:14], score_ref.at[pl.ds(half, half)]
-    )
-    refs[14][...] = table_grad(score_ref, base_ref, slot_ref, rows_ref)
+        parts, source, back_ref, refs[7:10], refs[10:14], score_ref.at[pl.ds(half, half)]
+    )
+    refs[14][...] = table_grad(score_ref, rows_ref)
 
 
 def qkv_back_kernel(*refs):
     bands, refs = (refs[:4], refs[4:8]), refs[8:]
-    n1_ref, r1_ref, qkv_ref, clon_ref, clat_ref, cdiag_ref = refs[:6]
-    res_ref, slon_ref, slat_ref, sdiag_ref = refs[6:]
+    norms = (refs[0:2], refs[2:4])
+    qkv_ref, clon_ref, clat_ref, cdiag_ref = refs[4:8]
+    res_ref, slon_ref, slat_ref, sdiag_ref = refs[8:]
     w_qkv = qkv_ref[...]
     windows = []
     for w in range(4):
@@ -509,8 +527,10 @@
             + mm_nt(dk_ref[here, :], w_qkv[:, 192:384])
             + mm_nt(dv_ref[here, :], w_qkv[:, 384:576])
         )
+        n1_ref, r1_ref = norms[min(w, 1)]
+        slot = pl.ds(max(w - 1, 0) * WIN, WIN)
         result = grad_ref[here, :] + norm_back(
-            normed_grad, n1_ref[rows, :].astype(f32), r1_ref[rows, :]
+            normed_grad, n1_ref[slot, :].astype(f32), r1_ref[slot, :]
         )
         res_ref[rows, :] = result.astype(bf16)
         windows.append(result)
@@ -606,7 +626,6 @@
     fine_down = fine_down.T
     flat = tokens.reshape(576, 192)
     column = lambda index: jnp.asarray(index).reshape(-1, 1)
-    line = lambda index: jnp.asarray(index).reshape(1, -1)
     tok = ((576, 192), bf16)
     edges = [((112, 192), bf16), ((112, 192), bf16), ((48, 192), bf16)]
     wide_edges = [((208, 192), bf16), ((208, 192), bf16), ((144, 192), bf16)]
@@ -615,26 +634,18 @@
     table_rows = ((12, 192, WIN), bf16)
     held = ((12, 2, 12, 16, WIN), bf16)
 
-    *sent, grad_here = pl.pallas_call(
-        edge_kernel,
-        in_specs=[pl.BlockSpec(memory_space=pl.ANY)] * 2,
-        out_shape=[jax.ShapeDtypeStruct(*shape) for shape in wide_edges + [quad]],
-        scratch_shapes=[
-            pltpu.VMEM((576, 192), bf16),
-            pltpu.VMEM((6, 12, 2, 384), bf16),
-            pltpu.SemaphoreType.DMA((2,)),
-        ],
-        compiler_params=pltpu.CompilerParams(vmem_limit_bytes=56 * 1024 * 1024),
-    )(flat, out_grad.transpose(1, 2, 0, 3))
+    *sent, grad_here = run(
+        edge_kernel, wide_edges + [quad], [], 1, (flat, out_grad.transpose(1, 2, 0, 3))
+    )
     first = send(sent, 1)
     (fine_table,) = run(
         bias_kernel, [scores], [held], 2,
-        (fine_bias.transpose(1, 0, 2), line(BASE), column(ROW_SLOT)),
-    )
-
-    labels = mask_ids.reshape(2, 2, 2, 3, 2, 2, 6)
-    top = jnp.zeros((2, 2, 1, 1, 1, 1), jnp.int32).at[0, 0].set(1)[None]
-    labels = labels * 2 + jnp.where(lat_index == 0, top, 0)
+        (fine_bias.transpose(1, 0, 2),),
+    )
+
+    row = lax.broadcasted_iota(jnp.int32, mask_ids.shape, 1) + lat_index * mask_ids.shape[1]
+    labels = mask_ids * 2 + jnp.where(row < 3, 1, 0)
+    labels = labels.reshape(2, 2, 2, 3, 2, 2, 6)
     labels = labels.transpose(1, 4, 2, 5, 0, 3, 6).reshape(4, WIN)
     fine_mask = jnp.where(labels[:, :, None] == labels[:, None, :], 0.0, -1e30).astype(f32)
     low_half = jnp.arange(WIN) < WIN // 2
@@ -642,20 +653,33 @@
         (low_half[:, None] == low_half[None, :]) | (lat_index != 0), 0.0, -1e30
     ).astype(f32)
 
-    fine = run(
-        fine_kernel,
-        [tok] + edges
-        + [tok] * 3
-        + [((24 * WIN, WIN), bf16), tok, ((576, 1), f32), tok, ((576, 1), f32), ((576, 768), bf16)],
-        [((848, 192), bf16)],
-        8,
-        (flat, *first, column(ARRIVE), fine_table, fine_mask, fine_qkv, fine_proj, fine_up, fine_down),
-    )
-    q, k, v, probs, n1, r1, n2, r2, slope = fine[4:]
-    arrived = send(fine[1:4], 1)
-    late_table, _ = lax.optimization_barrier((coarse_bias.transpose(1, 0, 2), fine[1]))
+    def saved_shapes(windows):
+        rows = windows * WIN
+        part = ((rows, 192), bf16)
+        scale = ((rows, 1), f32)
+        probs = ((6 * rows, WIN), bf16)
+        return [part] * 3 + [probs, part, scale, part, scale, ((rows, 768), bf16)]
+
+    inputs = (
+        flat, *first, column(ARRIVE), fine_table, fine_mask,
+        fine_qkv, fine_proj, fine_up, fine_down,
+    )
+    gathered = [((848, 192), bf16)]
+    outer = run(
+        fine_edge_kernel,
+        edges + [((3 * WIN, 192), bf16)] + saved_shapes(3),
+        gathered, 6, inputs,
+    )
+    arrived = send(outer[:3], 1)
+    flat_after, _ = lax.optimization_barrier((flat, outer[3]))
+    inner = run(
+        fine_inner_kernel,
+        [((WIN, 192), bf16)] + saved_shapes(1),
+        gathered, 2, (flat_after, *inputs[1:]),
+    )
+    late_table, _ = lax.optimization_barrier((coarse_bias.transpose(1, 0, 2), outer[3]))
     (coarse_table,) = run(
-        bias_kernel, [scores], [held], 2, (late_table, line(BASE), column(ROW_SLOT))
+        bias_kernel, [scores], [held], 2, (late_table,)
     )
     coarse = run(
         coarse_kernel,
@@ -663,7 +687,7 @@
         [((848, 192), bf16), ((12 * WIN, WIN), bf16), ((576, 192), bf16)],
         9,
         (
-            fine[0], *arrived, column(MERGE), column(SPLIT), coarse_table, coarse_mask, grad_here, *first,
+            inner[0], outer[3], *arrived, column(MERGE), column(SPLIT), coarse_table, coarse_mask, grad_here, *first,
             reduce_weight, coarse_qkv, coarse_proj, coarse_up, coarse_down,
         ),
     )
@@ -673,19 +697,23 @@
     dlat, scored = lax.optimization_barrier((dlat, coarse[8]))
     (coarse_grad,) = run(
         coarse_table_kernel, [((24, 6 * ENTRIES), bf16)], [table_rows], 2,
-        (scored, column(BASE), line(ROW_SLOT)),
+        (scored,),
     )
     steps = lon_steps()
     other = swap(coarse_grad, steps[-1])
     half_tok = ((288, 192), bf16)
     half_outs = [((288, 192), f32)] + [half_tok] * 3
-    saved = (q, k, v, probs, n2, r2, slope, fine_proj, fine_up, fine_down)
+    q, k, v, probs, n1, r1, n2, r2, slope = outer[4:]
+    outer_saved = (q, k, v, probs, n2, r2, slope)
+    q, k, v, probs, n1_inner, r1_inner, n2, r2, slope = inner[1:]
+    inner_saved = (q, k, v, probs, n2, r2, slope)
+    weights = (fine_proj, fine_up, fine_down)
     *first_half, first_scores = run(
         first_band_kernel,
         half_outs + [((6 * WIN, WIN), f32)],
         [((448, 192), bf16)],
         4,
-        (dlon, coarse[7], column(BACK), *saved),
+        (dlon, coarse[7], column(BACK), *inner_saved, *outer_saved, *weights),
     )
     first_scores, other = lax.optimization_barrier((first_scores, other))
     coarse_grad = add(coarse_grad, other)
@@ -697,7 +725,7 @@
         5,
         (
             dlon, coarse[7], dlat, ddiag, column(BACK), first_scores,
-            column(BASE), line(ROW_SLOT), *saved,
+            *outer_saved, *weights,
         ),
     )
     second_half[0], other = lax.optimization_barrier((second_half[0], other))
@@ -705,23 +733,23 @@
     for step in reversed(steps[:-2]):
         coarse_sums = (coarse_grad, swap(coarse_grad, step))
         coarse_grad = add(*coarse_sums)
-    other = swap(fine_grad, steps[0])
+    other = swap(fine_grad, steps[-1])
     fine_back = list(run(
         qkv_back_kernel, [tok] + wide_edges, [], 2,
-        (*first_half, *second_half, n1, r1, fine_qkv, c10, c01, c00),
+        (*first_half, *second_half, n1_inner, r1_inner, n1, r1, fine_qkv, c10, c01, c00),
     ))
-    fine_back[0], other = lax.optimization_barrier((fine_back[0], other))
+    alon, alat, adiag = send(fine_back[1:4], -1)
+    alat, other = lax.optimization_barrier((alat, other))
     fine_grad = add(fine_grad, other)
-    for step in steps[1:]:
+    for step in reversed(steps[:-1]):
         fine_sums = (fine_grad, swap(fine_grad, step))
         fine_grad = add(*fine_sums)
-    arrived = send(fine_back[1:4], -1)
     d_tokens, coarse_result = run(
         last_kernel,
         [tok, ((2, 6, 12, 384), bf16)],
         [((848, 192), bf16), ((192, 192), bf16)],
         1,
-        (fine_back[0], *arrived, column(LEAVE), c11, column(RESULT)),
+        (fine_back[0], alon, alat, adiag, column(LEAVE), c11, column(RESULT)),
     )
     (coarse_out,) = run(
         table_sum_kernel, [((HEADS_C, 1, 12 * ENTRIES), f32)], [], 1, coarse_sums

time: 73.4 us -> 73 us (level)
  starting transfers between devices: 19.5 us -> 22.9 us
  other arithmetic: 1.82 us -> 0.42 us
  waiting for transfers between devices: 11.7 us -> 10.6 us
    ppermute x4, starting transfers between devices: 5.02 us -> 7.67 us  [move(): return lax.ppermute(value, ('lon', 'lat'), pairs)]
    ppermute x4, waiting for transfers between devices: 3.39 us -> 0.77 us  [move(): return lax.ppermute(value, ('lon', 'lat'), pairs)]
    pallas_call x1 -> x0, Pallas kernels: 1.85 us -> none  [body(): pl.pallas_call(edge_kernel, in_specs=[pl.BlockSpec(memory_space=pl.ANY)]...]
    pallas_call x11 -> x13, Pallas kernels: 33.7 us -> 34.9 us  [run(): pl.pallas_call(kernel, out_shape=shapes, scratch_shapes=[pltpu.VMEM(shape...]
    ppermute x4, waiting for transfers between devices: 1.92 us -> 3.11 us  [move(): return lax.ppermute(value, 'lon', pairs)]
    ppermute x4, starting transfers between devices: 2.69 us -> 3.43 us  [move(): return lax.ppermute(value, 'lat', pairs)]
    unnamed x51 -> x43, local copies, waits for them, and re-layouts: 3.32 us -> 2.7 us
  transfers between devices with their start and end apart: 18 -> 18, of which waited for: 7 -> 7; matrix products, arithmetic and copies ran while one was open for 4% -> 2% of each run, Pallas kernels for 23% -> 27%
where the time goes in v4:
time: 73 us; the launch traced here: 72.8 us
  Pallas kernels  34.9 us (48%)
  starting transfers between devices  22.9 us (31%)
  waiting for transfers between devices  10.6 us (15%)
  local copies, waits for them, and re-layouts  2.93 us (4%)
  between operations  1.07 us (1%)
    pallas_call x13, Pallas kernels, run(): pl.pallas_call(kernel, out_shape=shapes, scratch_shapes=[pltpu.VMEM(shape...  34.9 us
    ppermute x4, starting transfers between devices, move(): return lax.ppermute(value, ('lon', 'lat'), pairs)  7.67 us
    ppermute x6, waiting for transfers between devices, swap(): return lax.ppermute(value, 'lon', [(s, s ^ step) for s in range(count)])  6.68 us
    ppermute x4, starting transfers between devices, move(): return lax.ppermute(value, 'lon', pairs)  6.12 us
    ppermute x6, starting transfers between devices, swap(): return lax.ppermute(value, 'lon', [(s, s ^ step) for s in range(count)])  5.64 us
    ppermute x4, starting transfers between devices, move(): return lax.ppermute(value, 'lat', pairs)  3.43 us
    ppermute x4, waiting for transfers between devices, move(): return lax.ppermute(value, 'lon', pairs)  3.11 us
    unnamed x43, local copies, waits for them, and re-layouts  2.7 us
  transfers between devices with their start and end apart: 18, of which 7 were waited for; matrix products, arithmetic and copies ran while one was open for 2% of the time, Pallas kernels for 27%

profile of v4, /device:TPU:0, one launch (start us, length us, event | category | flops | bytes accessed | tf_op | source)
XLA Modules:
  0.0 72.8 jit_solution(15204084078337761915)
XLA Ops:
  0.6 1.0 %copy-done.4 = bf16[2,12,24,192]{3,2,1,0:T(8,128)(2,1)S(1)} copy-done((bf16[2,12,24,192]{3,2,1,0:T(8,128)(2,1)S(1)}, bf16[2,12,24,192]{3,2,1,0:T(8,128)(2,1)}, u32[]{:S(2)}) %copy-start.4) | copy-done | bytes 221208
  1.6 0.9 %copy-done.12 = bf16[2,6,12,384]{3,0,2,1:T(2,128)(2,1)S(1)} copy-done((bf16[2,6,12,384]{3,0,2,1:T(2,128)(2,1)S(1)}, bf16[2,6,12,384]{3,0,2,1:T(2,128)(2,1)}, u32[]{:S(2)}) %copy-start.12) | copy-done | bytes 110616
  2.5 0.2 shard_map.219
  2.7 2.5 %collective-permute-start.2 = (bf16[144,192]{1,0:T(8,128)(2,1)S(1)}, bf16[144,192]{1,0:T(8,128)(2,1)S(1)}, u32[]{:S(2)}, u32[]{:S(2)}) collective-permute-start(bf16[144,192]{1,0:T(8,128)(2,1)S(1)} %get-tuple-element.68), channel_id=1, source_target_pairs={{0,5},{1,6},{2,7},{3,4},{4,9},{5,10},{6,11},{7,8},{8,13},{9,14},{1... | collective-permute-start | bytes 165896 | tf_op jit(solution)/shard_map/ppermute | solution.py:600
  5.2 1.5 %collective-permute-start = (bf16[208,192]{1,0:T(8,128)(2,1)S(1)}, bf16[208,192]{1,0:T(8,128)(2,1)S(1)}, u32[]{:S(2)}, u32[]{:S(2)}) collective-permute-start(bf16[208,192]{1,0:T(8,128)(2,1)S(1)} %get-tuple-element.66), channel_id=1, source_target_pairs={{0,4},{4,8},{8,12},{12,16},{16,20},{20,24},{24,28},{28,0},{1,5},{5... | collective-permute-start | bytes 239624 | tf_op jit(solution)/shard_map/ppermute | solution.py:591
  6.7 1.3 %collective-permute-start.1 = (bf16[208,192]{1,0:T(8,128)(2,1)S(1)}, bf16[208,192]{1,0:T(8,128)(2,1)S(1)}, u32[]{:S(2)}, u32[]{:S(2)}) collective-permute-start(bf16[208,192]{1,0:T(8,128)(2,1)S(1)} %get-tuple-element.67), channel_id=1, source_target_pairs={{0,1},{1,2},{2,3},{3,0},{4,5},{5,6},{6,7},{7,4},{8,9},{9,10},{10,1... | collective-permute-start | bytes 239624 | tf_op jit(solution)/shard_map/ppermute | solution.py:594
  8.0 0.1 multiply_add_fusion
  8.1 0.1 reshape.48
  8.3 0.1 eq.28
  8.4 0.1 compare_select_fusion.refs_6_
  8.5 0.1 or_select_fusion.mask_ref
  8.7 0.0 copy-start.18
  8.7 2.3 %shard_map.220.refs_5_ = f32[1728,144]{1,0:T(8,128)S(1)} custom-call(f32[6,2,3312]{2,1,0:T(2,128)S(1)} %bitcast.20), custom_call_target="tpu_custom_call" | custom-call | flops 2000000000 | bytes 1154304 | tf_op jit(solution)/shard_map/pallas_call | solution.py:576
  11.0 0.8 %collective-permute-done.2.refs_3_.gdiag_ref = bf16[144,192]{1,0:T(8,128)(2,1)S(1)} collective-permute-done((bf16[144,192]{1,0:T(8,128)(2,1)S(1)}, bf16[144,192]{1,0:T(8,128)(2,1)S(1)}, u32[]{:S(2)}, u32[]{:S(2)}) %collective-permute-start.2) | collective-permute-done | bytes 55328 | tf_op jit(solution)/shard_map/ppermute | solution.py:600
  11.8 2.0 %collective-permute-done.refs_1_.glon_ref = bf16[208,192]{1,0:T(8,128)(2,1)S(1)} collective-permute-done((bf16[208,192]{1,0:T(8,128)(2,1)S(1)}, bf16[208,192]{1,0:T(8,128)(2,1)S(1)}, u32[]{:S(2)}, u32[]{:S(2)}) %collective-permute-start) | collective-permute-done | bytes 79904 | tf_op jit(solution)/shard_map/ppermute | solution.py:591
  13.8 5.8 %shard_map.221 = (bf16[112,192]{1,0:T(8,128)(2,1)S(1)}, bf16[112,192]{1,0:T(8,128)(2,1)S(1)}, bf16[48,192]{1,0:T(8,128)(2,1)S(1)}, bf16[432,192]{1,0:T(8,128)(2,...) custom-call(bf16[576,192]{1,0:T(8,128)(2,1)S(1)} %bitcast.14, ...), custom_call_target="tpu_custom_call" | custom-call | flops 6000000000 | bytes 5163648 | tf_op jit(solution)/shard_map/pallas_call | solution.py:576
  19.6 0.1 collective-permute-start.5
  19.7 1.1 %collective-permute-start.3 = (bf16[112,192]{1,0:T(8,128)(2,1)S(1)}, bf16[112,192]{1,0:T(8,128)(2,1)S(1)}, u32[]{:S(2)}, u32[]{:S(2)}) collective-permute-start(bf16[112,192]{1,0:T(8,128)(2,1)S(1)} %get-tuple-element.72), channel_id=1, source_target_pairs={{0,4},{4,8},{8,12},{12,16},{16,20},{20,24},{24,28},{28,0},{1,5},{5... | collective-permute-start | bytes 129032 | tf_op jit(solution)/shard_map/ppermute | solution.py:591
  20.8 1.4 %collective-permute-start.4 = (bf16[112,192]{1,0:T(8,128)(2,1)S(1)}, bf16[112,192]{1,0:T(8,128)(2,1)S(1)}, u32[]{:S(2)}, u32[]{:S(2)}) collective-permute-start(bf16[112,192]{1,0:T(8,128)(2,1)S(1)} %get-tuple-element.73), channel_id=1, source_target_pairs={{0,1},{1,2},{2,3},{3,0},{4,5},{5,6},{6,7},{7,4},{8,9},{9,10},{10,1... | collective-permute-start | bytes 129032 | tf_op jit(solution)/shard_map/ppermute | solution.py:594
  22.1 2.3 %shard_map.223.bias_ref = f32[1728,144]{1,0:T(8,128)S(1)} custom-call(f32[12,1,3312]{2,1,0:T(1,128)S(1)} %bitcast.21), custom_call_target="tpu_custom_call" | custom-call | flops 2000000000 | bytes 1154304 | tf_op jit(solution)/shard_map/pallas_call | solution.py:576
  24.5 0.0 copy-start.14
  24.5 2.7 %shard_map.222 = (bf16[144,192]{1,0:T(8,128)(2,1)S(1)}, bf16[144,192]{1,0:T(8,128)(2,1)S(1)}, bf16[144,192]{1,0:T(8,128)(2,1)S(1)}, bf16[144,192]{1,0:T(8,128)(2...) custom-call(bf16[576,192]{1,0:T(8,128)(2,1)S(1)} %bitcast.15, ...), custom_call_target="tpu_custom_call" | custom-call | flops 2000000000 | bytes 3453312 | tf_op jit(solution)/shard_map/pallas_call | solution.py:576
  27.4 8.5 %shard_map.224 = (bf16[96,192]{1,0:T(8,128)(2,1)S(1)}, bf16[96,192]{1,0:T(8,128)(2,1)S(1)}, bf16[96,192]{1,0:T(8,128)(2,1)S(1)}, bf16[96,192]{1,0:T(8,128)(2,1)S...) custom-call(bf16[144,192]{1,0:T(8,128)(2,1)S(1)} %get-tuple-element., ...), custom_call_target="tpu_custom_call" | custom-call | flops 8999999488 | bytes 7165568 | tf_op jit(solution)/shard_map/pallas_call | solution.py:576
  35.8 0.4 collective-permute-start.7
  36.3 3.4 %collective-permute-start.8 = (bf16[48,192]{1,0:T(8,128)(2,1)S(1)}, bf16[48,192]{1,0:T(8,128)(2,1)S(1)}, u32[]{:S(2)}, u32[]{:S(2)}) collective-permute-start(bf16[48,192]{1,0:T(8,128)(2,1)S(1)} %get-tuple-element.100), channel_id=1, source_target_pairs={{0,31},{1,28},{2,29},{3,30},{4,3},{5,0},{6,1},{7,2},{8,7},{9,4},{1... | collective-permute-start | bytes 55304 | tf_op jit(solution)/shard_map/ppermute | solution.py:600
  39.7 1.6 %collective-permute-start.6 = (bf16[112,192]{1,0:T(8,128)(2,1)S(1)}, bf16[112,192]{1,0:T(8,128)(2,1)S(1)}, u32[]{:S(2)}, u32[]{:S(2)}) collective-permute-start(bf16[112,192]{1,0:T(8,128)(2,1)S(1)} %get-tuple-element.77), channel_id=1, source_target_pairs={{0,28},{4,0},{8,4},{12,8},{16,12},{20,16},{24,20},{28,24},{1,29},{... | collective-permute-start | bytes 129032 | tf_op jit(solution)/shard_map/ppermute | solution.py:591
  41.3 1.4 %shard_map.226 = bf16[24,1656]{1,0:T(8,128)(2,1)S(1)} custom-call(f32[1728,144]{1,0:T(8,128)S(1)} %get-tuple-element.102.score_ref), custom_call_target="tpu_custom_call" | custom-call | flops 2000000000 | bytes 1074816 | tf_op jit(solution)/shard_map/pallas_call | solution.py:576
  42.7 0.1 collective-permute-start.9
  42.7 1.1 %collective-permute-done.6.dlon_ref = bf16[112,192]{1,0:T(8,128)(2,1)S(1)} collective-permute-done((bf16[112,192]{1,0:T(8,128)(2,1)S(1)}, bf16[112,192]{1,0:T(8,128)(2,1)S(1)}, u32[]{:S(2)}, u32[]{:S(2)}) %collective-permute-start.6) | collective-permute-done | bytes 43040 | tf_op jit(solution)/shard_map/ppermute | solution.py:591
  43.9 3.5 %shard_map.225 = (f32[288,192]{1,0:T(8,128)S(1)}, bf16[288,192]{1,0:T(8,128)(2,1)S(1)}, bf16[288,192]{1,0:T(8,128)(2,1)S(1)}, bf16[288,192]{1,0:T(8,128)(2,1)S(1)}, f32[864,144]{1,0:T(8,128)S(1)}) custom-call(bf16[112,192]{1,0:T(8,128)(2,1)S(1)} %collective-permute-done.6.dlon_ref, bf16[336,192]{1,0:T(8,128)(2,1)S(1)} %get-tuple-element.78.dloc_ref, ...), custom_call_target="tpu_custom_call" | custom-call | flops 4000000000 | bytes 4655616 | tf_op jit(solution)/shard_map/pallas_call | solution.py:576
  47.4 1.8 %collective-permute-done.9 = bf16[24,1656]{1,0:T(8,128)(2,1)S(1)} collective-permute-done((bf16[24,1656]{1,0:T(8,128)(2,1)S(1)}, bf16[24,1656]{1,0:T(8,128)(2,1)S(1)}, u32[]{:S(2)}, u32[]{:S(2)}) %collective-permute-start.9) | collective-permute-done | bytes 79520 | tf_op jit(solution)/shard_map/ppermute | solution.py:610
  49.3 0.1 collective-permute-start.10
  49.4 4.6 %shard_map.227 = (f32[288,192]{1,0:T(8,128)S(1)}, bf16[288,192]{1,0:T(8,128)(2,1)S(1)}, bf16[288,192]{1,0:T(8,128)(2,1)S(1)}, bf16[288,192]{1,0:T(8,128)(2,1)S(1)}, bf16[24,1656]{1,0:T(8,128)(2,1)S(1)}) custom-call(bf16[112,192]{1,0:T(8,128)(2,1)S(1)} %collective-permute-done.6.dlon_ref, bf16[336,192]{1,0:T(8,128)(2,1)S(1)} %get-tuple-element.78.dloc_ref, ...), custom_call_target="tpu_custom_call" | custom-call | flops 5000000000 | bytes 4104768 | tf_op jit(solution)/shard_map/pallas_call | solution.py:576
  54.0 2.7 %collective-permute-start.13 = (bf16[24,1656]{1,0:T(8,128)(2,1)S(1)}, bf16[24,1656]{1,0:T(8,128)(2,1)S(1)}, u32[]{:S(2)}, u32[]{:S(2)}) collective-permute-start(bf16[24,1656]{1,0:T(8,128)(2,1)S(1)} %get-tuple-element.120), channel_id=1, source_target_pairs={{0,16},{4,20},{8,24},{12,28},{16,0},{20,4},{24,8},{28,12},{1,17},{... | collective-permute-start | bytes 238472 | tf_op jit(solution)/shard_map/ppermute | solution.py:610
  56.6 0.8 %shard_map.228 = (bf16[576,192]{1,0:T(8,128)(2,1)S(1)}, bf16[208,192]{1,0:T(8,128)(2,1)S(1)}, bf16[208,192]{1,0:T(8,128)(2,1)S(1)}, bf16[144,192]{1,0:T(8,128)(2,1)S(1)}) custom-call(f32[288,192]{1,0:T(8,128)S(1)} %get-tuple-element.93.refs_0_, bf16[288,192]{1,0:T(8,128)(2,1)S(1)} %get-tuple-element.94.refs_1_, ...), custom_call_target="tpu_custom_call" | custom-call | flops 2000000000 | bytes 2097408 | tf_op jit(solution)/shard_map/pallas_call | solution.py:576
  57.4 0.3 collective-permute-start.12
  57.7 1.8 %collective-permute-start.14 = (bf16[144,192]{1,0:T(8,128)(2,1)S(1)}, bf16[144,192]{1,0:T(8,128)(2,1)S(1)}, u32[]{:S(2)}, u32[]{:S(2)}) collective-permute-start(bf16[144,192]{1,0:T(8,128)(2,1)S(1)} %get-tuple-element.122), channel_id=1, source_target_pairs={{0,31},{1,28},{2,29},{3,30},{4,3},{5,0},{6,1},{7,2},{8,7},{9,4},{1... | collective-permute-start | bytes 165896 | tf_op jit(solution)/shard_map/ppermute | solution.py:600
  59.5 0.7 collective-permute-start.17
  60.2 1.9 %collective-permute-start.11 = (bf16[208,192]{1,0:T(8,128)(2,1)S(1)}, bf16[208,192]{1,0:T(8,128)(2,1)S(1)}, u32[]{:S(2)}, u32[]{:S(2)}) collective-permute-start(bf16[208,192]{1,0:T(8,128)(2,1)S(1)} %get-tuple-element.118), channel_id=1, source_target_pairs={{0,28},{4,0},{8,4},{12,8},{16,12},{20,16},{24,20},{28,24},{1,29},{... | collective-permute-start | bytes 239624 | tf_op jit(solution)/shard_map/ppermute | solution.py:591
  62.2 0.9 %collective-permute-start.15 = (bf16[24,1656]{1,0:T(8,128)(2,1)S(1)}, bf16[24,1656]{1,0:T(8,128)(2,1)S(1)}, u32[]{:S(2)}, u32[]{:S(2)}) collective-permute-start(bf16[24,1656]{1,0:T(8,128)(2,1)S(1)} %add_convert_fusion.2), channel_id=1, source_target_pairs={{0,8},{4,12},{8,0},{12,4},{16,24},{20,28},{24,16},{28,20},{1,9},{5... | collective-permute-start | bytes 238472 | tf_op jit(solution)/shard_map/ppermute | solution.py:610
  63.1 2.1 %collective-permute-done.17.other_ref = bf16[24,1656]{1,0:T(8,128)(2,1)S(1)} collective-permute-done((bf16[24,1656]{1,0:T(8,128)(2,1)S(1)}, bf16[24,1656]{1,0:T(8,128)(2,1)S(1)}, u32[]{:S(2)}, u32[]{:S(2)}) %collective-permute-start.17) | collective-permute-done | bytes 79520 | tf_op jit(solution)/shard_map/ppermute | solution.py:610
  65.2 0.8 %shard_map.231 = f32[12,1,3312]{2,1,0:T(1,128)} custom-call(bf16[24,1656]{1,0:T(8,128)(2,1)S(1)} %add_convert_fusion.kept_ref, bf16[24,1656]{1,0:T(8,128)(2,1)S(1)} %collective-permute-done.17.other_ref), custom_call_target="tpu_custom_call" | custom-call | flops 1000000000 | bytes 317952 | tf_op jit(solution)/shard_map/pallas_call | solution.py:576
  66.0 1.5 %collective-permute-done.15 = bf16[24,1656]{1,0:T(8,128)(2,1)S(1)} collective-permute-done((bf16[24,1656]{1,0:T(8,128)(2,1)S(1)}, bf16[24,1656]{1,0:T(8,128)(2,1)S(1)}, u32[]{:S(2)}, u32[]{:S(2)}) %collective-permute-start.15) | collective-permute-done | bytes 79520 | tf_op jit(solution)/shard_map/ppermute | solution.py:610
  67.5 1.2 %collective-permute-start.16 = (bf16[24,1656]{1,0:T(8,128)(2,1)S(1)}, bf16[24,1656]{1,0:T(8,128)(2,1)S(1)}, u32[]{:S(2)}, u32[]{:S(2)}) collective-permute-start(bf16[24,1656]{1,0:T(8,128)(2,1)S(1)} %add_convert_fusion.1.kept_ref), channel_id=1, source_target_pairs={{0,4},{4,0},{8,12},{12,8},{16,20},{20,16},{24,28},{28,24},{1,5},{5... | collective-permute-start | bytes 238472 | tf_op jit(solution)/shard_map/ppermute | solution.py:610
  68.7 1.3 %shard_map.229 = (bf16[576,192]{1,0:T(8,128)(2,1)}, bf16[2,6,12,384]{3,2,1,0:T(8,128)(2,1)S(1)}) custom-call(bf16[576,192]{1,0:T(8,128)(2,1)S(1)} %get-tuple-element.117.res_ref, bf16[208,192]{1,0:T(8,128)(2,1)S(1)} %collective-permute-done.11.lon_ref, bf16[208,192]{1,0:T(8,128)(2,1)S(1)} %collective-permute-done.12.lat_ref, ...), custom_call_target="tpu_custom_call" | custom-call | flops 1000000000 | bytes 807744 | tf_op jit(solution)/shard_map/pallas_call | solution.py:576
  70.1 0.7 %copy.27 = bf16[2,6,12,384]{3,0,2,1:T(2,128)(2,1)} copy(bf16[2,6,12,384]{3,2,1,0:T(8,128)(2,1)S(1)} %get-tuple-element.132) | data formatting | bytes 221184
  70.8 1.2 %collective-permute-done.16.other_ref = bf16[24,1656]{1,0:T(8,128)(2,1)S(1)} collective-permute-done((bf16[24,1656]{1,0:T(8,128)(2,1)S(1)}, bf16[24,1656]{1,0:T(8,128)(2,1)S(1)}, u32[]{:S(2)}, u32[]{:S(2)}) %collective-permute-start.16) | collective-permute-done | bytes 79520 | tf_op jit(solution)/shard_map/ppermute | solution.py:610
  72.0 0.8 %shard_map.230 = f32[6,2,3312]{2,1,0:T(2,128)} custom-call(bf16[24,1656]{1,0:T(8,128)(2,1)S(1)} %add_convert_fusion.1.kept_ref, bf16[24,1656]{1,0:T(8,128)(2,1)S(1)} %collective-permute-done.16.other_ref), custom_call_target="tpu_custom_call" | custom-call | flops 1000000000 | bytes 317952 | tf_op jit(solution)/shard_map/pallas_call | solution.py:576
  (56 shorter events, 0.3 us)
Async XLA Ops:
  0.6 1.0 %copy-start.4 = (bf16[2,12,24,192]{3,2,1,0:T(8,128)(2,1)S(1)}, bf16[2,12,24,192]{3,2,1,0:T(8,128)(2,1)}, u32[]{:S(2)}) copy-start(bf16[2,12,24,192]{3,2,1,0:T(8,128)(2,1)} %param.20) | copy-start | bytes 663556
  1.6 0.9 %copy-start.12 = (bf16[2,6,12,384]{3,0,2,1:T(2,128)(2,1)S(1)}, bf16[2,6,12,384]{3,0,2,1:T(2,128)(2,1)}, u32[]{:S(2)}) copy-start(bf16[2,6,12,384]{3,0,2,1:T(2,128)(2,1)} %param.33) | copy-start | bytes 331780
  2.5 5.5 %copy-start.20 = (s32[2,12,24]{2,0,1:T(2,128)S(1)}, s32[2,12,24]{2,0,1:T(2,128)}, u32[]{:S(2)}) copy-start(s32[2,12,24]{2,0,1:T(2,128)} %param.21) | copy-start | bytes 6916
  2.5 6.1 %copy-start.10 = (f32[2,6,3312]{2,0,1:T(2,128)S(1)}, f32[2,6,3312]{2,0,1:T(2,128)}, u32[]{:S(2)}) copy-start(f32[2,6,3312]{2,0,1:T(2,128)} %param.26) | copy-start | bytes 476932
  2.7 9.1 %collective-permute-start.2 = (bf16[144,192]{1,0:T(8,128)(2,1)S(1)}, bf16[144,192]{1,0:T(8,128)(2,1)S(1)}, u32[]{:S(2)}, u32[]{:S(2)}) collective-permute-start(bf16[144,192]{1,0:T(8,128)(2,1)S(1)} %get-tuple-element.68), channel_id=1, source_target_pairs={{0,5},{1,6},{2,7},{3,4},{4,9},{5,10},{6,11},{7,8},{8,13},{9,14},{1... | collective-permute-start | bytes 165896 | tf_op jit(solution)/shard_map/ppermute | solution.py:600
  5.2 8.6 %collective-permute-start = (bf16[208,192]{1,0:T(8,128)(2,1)S(1)}, bf16[208,192]{1,0:T(8,128)(2,1)S(1)}, u32[]{:S(2)}, u32[]{:S(2)}) collective-permute-start(bf16[208,192]{1,0:T(8,128)(2,1)S(1)} %get-tuple-element.66), channel_id=1, source_target_pairs={{0,4},{4,8},{8,12},{12,16},{16,20},{20,24},{24,28},{28,0},{1,5},{5... | collective-permute-start | bytes 239624 | tf_op jit(solution)/shard_map/ppermute | solution.py:591
  6.7 7.0 %collective-permute-start.1 = (bf16[208,192]{1,0:T(8,128)(2,1)S(1)}, bf16[208,192]{1,0:T(8,128)(2,1)S(1)}, u32[]{:S(2)}, u32[]{:S(2)}) collective-permute-start(bf16[208,192]{1,0:T(8,128)(2,1)S(1)} %get-tuple-element.67), channel_id=1, source_target_pairs={{0,1},{1,2},{2,3},{3,0},{4,5},{5,6},{6,7},{7,4},{8,9},{9,10},{10,1... | collective-permute-start | bytes 239624 | tf_op jit(solution)/shard_map/ppermute | solution.py:594
  8.6 5.1 %copy-start.5 = (bf16[2,12,24,192]{3,2,1,0:T(8,128)(2,1)S(1)}, bf16[2,12,24,192]{3,2,1,0:T(8,128)(2,1)}, u32[]{:S(2)}) copy-start(bf16[2,12,24,192]{3,2,1,0:T(8,128)(2,1)} %param.20) | copy-start | bytes 663556
  8.7 5.1 %copy-start.7 = (bf16[192,768]{1,0:T(8,128)(2,1)S(1)}, bf16[192,768]{1,0:T(8,128)(2,1)}, u32[]{:S(2)}) copy-start(bf16[192,768]{1,0:T(8,128)(2,1)} %refs_8_.5) | copy-start | bytes 884740
  8.7 5.1 %copy-start.8 = (bf16[768,192]{0,1:T(8,128)(2,1)S(1)}, bf16[768,192]{0,1:T(8,128)(2,1)}, u32[]{:S(2)}) copy-start(bf16[768,192]{0,1:T(8,128)(2,1)} %param.25) | copy-start | bytes 884740
  8.7 5.1 %copy-start.9 = (bf16[192,576]{1,0:T(8,128)(2,1)S(1)}, bf16[192,576]{1,0:T(8,128)(2,1)}, u32[]{:S(2)}) copy-start(bf16[192,576]{1,0:T(8,128)(2,1)} %refs_12_.1) | copy-start | bytes 663556
  8.7 5.1 %copy-start.13 = (bf16[192,192]{1,0:T(8,128)(2,1)S(1)}, bf16[192,192]{1,0:T(8,128)(2,1)}, u32[]{:S(2)}) copy-start(bf16[192,192]{1,0:T(8,128)(2,1)} %refs_7_.5) | copy-start | bytes 221188
  8.7 5.1 %copy-start.18 = (s32[576,1]{1,0:T(8,128)S(1)}, s32[576,1]{1,0:T(8,128)}, u32[]{:S(2)}) copy-start(s32[576,1]{1,0:T(8,128)} %constant.41.refs_4_) | copy-start | bytes 6916
  13.8 8.4 %copy-start.11 = (f32[1,12,3312]{2,0,1:T(1,128)S(1)}, f32[1,12,3312]{2,0,1:T(1,128)}, u32[]{:S(2)}) copy-start(f32[1,12,3312]{2,0,1:T(1,128)} %param.32) | copy-start | bytes 476932
  19.6 7.6 %collective-permute-start.5 = (bf16[48,192]{1,0:T(8,128)(2,1)S(1)}, bf16[48,192]{1,0:T(8,128)(2,1)S(1)}, u32[]{:S(2)}, u32[]{:S(2)}) collective-permute-start(bf16[48,192]{1,0:T(8,128)(2,1)S(1)} %get-tuple-element.74), channel_id=1, source_target_pairs={{0,5},{1,6},{2,7},{3,4},{4,9},{5,10},{6,11},{7,8},{8,13},{9,14},{1... | collective-permute-start | bytes 55304 | tf_op jit(solution)/shard_map/ppermute | solution.py:600
  19.7 7.6 %collective-permute-start.3 = (bf16[112,192]{1,0:T(8,128)(2,1)S(1)}, bf16[112,192]{1,0:T(8,128)(2,1)S(1)}, u32[]{:S(2)}, u32[]{:S(2)}) collective-permute-start(bf16[112,192]{1,0:T(8,128)(2,1)S(1)} %get-tuple-element.72), channel_id=1, source_target_pairs={{0,4},{4,8},{8,12},{12,16},{16,20},{20,24},{24,28},{28,0},{1,5},{5... | collective-permute-start | bytes 129032 | tf_op jit(solution)/shard_map/ppermute | solution.py:591
  20.8 6.5 %collective-permute-start.4 = (bf16[112,192]{1,0:T(8,128)(2,1)S(1)}, bf16[112,192]{1,0:T(8,128)(2,1)S(1)}, u32[]{:S(2)}, u32[]{:S(2)}) collective-permute-start(bf16[112,192]{1,0:T(8,128)(2,1)S(1)} %get-tuple-element.73), channel_id=1, source_target_pairs={{0,1},{1,2},{2,3},{3,0},{4,5},{5,6},{6,7},{7,4},{8,9},{9,10},{10,1... | collective-permute-start | bytes 129032 | tf_op jit(solution)/shard_map/ppermute | solution.py:594
  24.4 2.9 %copy-start = (bf16[384,1536]{1,0:T(8,128)(2,1)S(1)}, bf16[384,1536]{1,0:T(8,128)(2,1)}, u32[]{:S(2)}) copy-start(bf16[384,1536]{1,0:T(8,128)(2,1)} %up_ref.1) | copy-start | bytes 3538948
  24.4 2.9 %copy-start.1 = (bf16[1536,384]{1,0:T(8,128)(2,1)S(1)}, bf16[1536,384]{1,0:T(8,128)(2,1)}, u32[]{:S(2)}) copy-start(bf16[1536,384]{1,0:T(8,128)(2,1)} %down_ref.1) | copy-start | bytes 3538948
  24.5 2.8 %copy-start.2 = (bf16[384,1152]{1,0:T(8,128)(2,1)S(1)}, bf16[384,1152]{1,0:T(8,128)(2,1)}, u32[]{:S(2)}) copy-start(bf16[384,1152]{1,0:T(8,128)(2,1)} %qkv_ref.1) | copy-start | bytes 2654212
  24.5 2.8 %copy-start.3 = (bf16[768,384]{1,0:T(8,128)(2,1)S(1)}, bf16[768,384]{1,0:T(8,128)(2,1)}, u32[]{:S(2)}) copy-start(bf16[768,384]{1,0:T(8,128)(2,1)} %reduce_ref.1) | copy-start | bytes 1769476
  24.5 2.8 %copy-start.6 = (bf16[384,384]{1,0:T(8,128)(2,1)S(1)}, bf16[384,384]{1,0:T(8,128)(2,1)}, u32[]{:S(2)}) copy-start(bf16[384,384]{1,0:T(8,128)(2,1)} %proj_ref.1) | copy-start | bytes 884740
  24.5 2.8 %copy-start.14 = (s32[608,1]{1,0:T(8,128)S(1)}, s32[608,1]{1,0:T(8,128)}, u32[]{:S(2)}) copy-start(s32[608,1]{1,0:T(8,128)} %constant.43.split_ref) | copy-start | bytes 7300
  24.5 2.8 %copy-start.17 = (s32[576,1]{1,0:T(8,128)S(1)}, s32[576,1]{1,0:T(8,128)}, u32[]{:S(2)}) copy-start(s32[576,1]{1,0:T(8,128)} %constant.42.merge_ref) | copy-start | bytes 6916
  35.8 5.4 %collective-permute-start.7 = (bf16[112,192]{1,0:T(8,128)(2,1)S(1)}, bf16[112,192]{1,0:T(8,128)(2,1)S(1)}, u32[]{:S(2)}, u32[]{:S(2)}) collective-permute-start(bf16[112,192]{1,0:T(8,128)(2,1)S(1)} %get-tuple-element.97), channel_id=1, source_target_pairs={{0,3},{1,0},{2,1},{3,2},{4,7},{5,4},{6,5},{7,6},{8,11},{9,8},{10,9... | collective-permute-start | bytes 129032 | tf_op jit(solution)/shard_map/ppermute | solution.py:594
  36.3 13.1 %collective-permute-start.8 = (bf16[48,192]{1,0:T(8,128)(2,1)S(1)}, bf16[48,192]{1,0:T(8,128)(2,1)S(1)}, u32[]{:S(2)}, u32[]{:S(2)}) collective-permute-start(bf16[48,192]{1,0:T(8,128)(2,1)S(1)} %get-tuple-element.100), channel_id=1, source_target_pairs={{0,31},{1,28},{2,29},{3,30},{4,3},{5,0},{6,1},{7,2},{8,7},{9,4},{1... | collective-permute-start | bytes 55304 | tf_op jit(solution)/shard_map/ppermute | solution.py:600
  39.7 4.2 %collective-permute-start.6 = (bf16[112,192]{1,0:T(8,128)(2,1)S(1)}, bf16[112,192]{1,0:T(8,128)(2,1)S(1)}, u32[]{:S(2)}, u32[]{:S(2)}) collective-permute-start(bf16[112,192]{1,0:T(8,128)(2,1)S(1)} %get-tuple-element.77), channel_id=1, source_target_pairs={{0,28},{4,0},{8,4},{12,8},{16,12},{20,16},{24,20},{28,24},{1,29},{... | collective-permute-start | bytes 129032 | tf_op jit(solution)/shard_map/ppermute | solution.py:591
  41.3 2.6 %copy-start.16 = (s32[576,1]{1,0:T(8,128)S(1)}, s32[576,1]{1,0:T(8,128)}, u32[]{:S(2)}) copy-start(s32[576,1]{1,0:T(8,128)} %constant.44.back_ref) | copy-start | bytes 6916
  42.7 6.6 %collective-permute-start.9 = (bf16[24,1656]{1,0:T(8,128)(2,1)S(1)}, bf16[24,1656]{1,0:T(8,128)(2,1)S(1)}, u32[]{:S(2)}, u32[]{:S(2)}) collective-permute-start(bf16[24,1656]{1,0:T(8,128)(2,1)S(1)} %shard_map.226), channel_id=1, source_target_pairs={{0,16},{4,20},{8,24},{12,28},{16,0},{20,4},{24,8},{28,12},{1,17},{... | collective-permute-start | bytes 238472 | tf_op jit(solution)/shard_map/ppermute | solution.py:610
  49.3 7.4 %collective-permute-start.10 = (bf16[24,1656]{1,0:T(8,128)(2,1)S(1)}, bf16[24,1656]{1,0:T(8,128)(2,1)S(1)}, u32[]{:S(2)}, u32[]{:S(2)}) collective-permute-start(bf16[24,1656]{1,0:T(8,128)(2,1)S(1)} %add_convert_fusion.3), channel_id=1, source_target_pairs={{0,8},{4,12},{8,0},{12,4},{16,24},{20,28},{24,16},{28,20},{1,9},{5... | collective-permute-start | bytes 238472 | tf_op jit(solution)/shard_map/ppermute | solution.py:610
  54.0 8.1 %collective-permute-start.13 = (bf16[24,1656]{1,0:T(8,128)(2,1)S(1)}, bf16[24,1656]{1,0:T(8,128)(2,1)S(1)}, u32[]{:S(2)}, u32[]{:S(2)}) collective-permute-start(bf16[24,1656]{1,0:T(8,128)(2,1)S(1)} %get-tuple-element.120), channel_id=1, source_target_pairs={{0,16},{4,20},{8,24},{12,28},{16,0},{20,4},{24,8},{28,12},{1,17},{... | collective-permute-start | bytes 238472 | tf_op jit(solution)/shard_map/ppermute | solution.py:610
  57.4 4.7 %collective-permute-start.12 = (bf16[208,192]{1,0:T(8,128)(2,1)S(1)}, bf16[208,192]{1,0:T(8,128)(2,1)S(1)}, u32[]{:S(2)}, u32[]{:S(2)}) collective-permute-start(bf16[208,192]{1,0:T(8,128)(2,1)S(1)} %get-tuple-element.119), channel_id=1, source_target_pairs={{0,3},{1,0},{2,1},{3,2},{4,7},{5,4},{6,5},{7,6},{8,11},{9,8},{10,9... | collective-permute-start | bytes 239624 | tf_op jit(solution)/shard_map/ppermute | solution.py:594
  57.7 11.0 %collective-permute-start.14 = (bf16[144,192]{1,0:T(8,128)(2,1)S(1)}, bf16[144,192]{1,0:T(8,128)(2,1)S(1)}, u32[]{:S(2)}, u32[]{:S(2)}) collective-permute-start(bf16[144,192]{1,0:T(8,128)(2,1)S(1)} %get-tuple-element.122), channel_id=1, source_target_pairs={{0,31},{1,28},{2,29},{3,30},{4,3},{5,0},{6,1},{7,2},{8,7},{9,4},{1... | collective-permute-start | bytes 165896 | tf_op jit(solution)/shard_map/ppermute | solution.py:600
  59.5 5.8 %collective-permute-start.17 = (bf16[24,1656]{1,0:T(8,128)(2,1)S(1)}, bf16[24,1656]{1,0:T(8,128)(2,1)S(1)}, u32[]{:S(2)}, u32[]{:S(2)}) collective-permute-start(bf16[24,1656]{1,0:T(8,128)(2,1)S(1)} %add_convert_fusion.kept_ref), channel_id=1, source_target_pairs={{0,4},{4,0},{8,12},{12,8},{16,20},{20,16},{24,28},{28,24},{1,5},{5... | collective-permute-start | bytes 238472 | tf_op jit(solution)/shard_map/ppermute | solution.py:610
  60.2 8.6 %collective-permute-start.11 = (bf16[208,192]{1,0:T(8,128)(2,1)S(1)}, bf16[208,192]{1,0:T(8,128)(2,1)S(1)}, u32[]{:S(2)}, u32[]{:S(2)}) collective-permute-start(bf16[208,192]{1,0:T(8,128)(2,1)S(1)} %get-tuple-element.118), channel_id=1, source_target_pairs={{0,28},{4,0},{8,4},{12,8},{16,12},{20,16},{24,20},{28,24},{1,29},{... | collective-permute-start | bytes 239624 | tf_op jit(solution)/shard_map/ppermute | solution.py:591
  62.1 6.6 %copy-start.15 = (s32[576,1]{1,0:T(8,128)S(1)}, s32[576,1]{1,0:T(8,128)}, u32[]{:S(2)}) copy-start(s32[576,1]{1,0:T(8,128)} %constant.45.leave_ref) | copy-start | bytes 6916
  62.2 6.6 %copy-start.19 = (s32[144,1]{1,0:T(8,128)S(1)}, s32[144,1]{1,0:T(8,128)}, u32[]{:S(2)}) copy-start(s32[144,1]{1,0:T(8,128)} %constant.46.result_ref) | copy-start | bytes 1732
  62.2 5.3 %collective-permute-start.15 = (bf16[24,1656]{1,0:T(8,128)(2,1)S(1)}, bf16[24,1656]{1,0:T(8,128)(2,1)S(1)}, u32[]{:S(2)}, u32[]{:S(2)}) collective-permute-start(bf16[24,1656]{1,0:T(8,128)(2,1)S(1)} %add_convert_fusion.2), channel_id=1, source_target_pairs={{0,8},{4,12},{8,0},{12,4},{16,24},{20,28},{24,16},{28,20},{1,9},{5... | collective-permute-start | bytes 238472 | tf_op jit(solution)/shard_map/ppermute | solution.py:610
  67.5 4.5 %collective-permute-start.16 = (bf16[24,1656]{1,0:T(8,128)(2,1)S(1)}, bf16[24,1656]{1,0:T(8,128)(2,1)S(1)}, u32[]{:S(2)}, u32[]{:S(2)}) collective-permute-start(bf16[24,1656]{1,0:T(8,128)(2,1)S(1)} %add_convert_fusion.1.kept_ref), channel_id=1, source_target_pairs={{0,4},{4,0},{8,12},{12,8},{16,20},{20,16},{24,28},{28,24},{1,5},{5... | collective-permute-start | bytes 238472 | tf_op jit(solution)/shard_map/ppermute | solution.py:610

commit v5 on v4

--- a/solution.py
+++ b/solution.py
@@ -258,13 +258,39 @@
     return jnp.concatenate(pieces, axis=0).astype(bf16)
 
 
+def dense(pieces, rows, coarse=None):
+    count = sum(piece.shape[0] for piece in pieces)
+    if rows > count:
+        pieces = pieces + [jnp.zeros((rows - count, 192), f32)]
+    tokens = jnp.concatenate(pieces, axis=0)
+    half = rows // 2
+    side = jnp.concatenate([tokens[0:half, 128:192], tokens[half:rows, 128:192]], axis=1)
+    filler = jnp.zeros((4, 128), f32)
+    out = [tokens[:, 0:128], side]
+    if coarse is None:
+        out += [filler, filler]
+    else:
+        for start in range(0, 384, 128):
+            out += [coarse[:, start : start + 128], filler]
+    return jnp.concatenate(out, axis=0).astype(bf16)
+
+
+def tokens_of(ref, rows):
+    values = ref[...].astype(f32)
+    side = values[rows : rows + rows // 2]
+    side = jnp.concatenate([side[:, 0:64], side[:, 64:128]], axis=0)
+    return jnp.concatenate([values[0:rows], side], axis=1).astype(bf16)
+
+
+def coarse_of(ref, rows):
+    values = ref[...].astype(f32)
+    starts = [rows + rows // 2 + 40 * part for part in range(3)]
+    return jnp.concatenate([values[start : start + QUAD] for start in starts], axis=1)
+
+
 def quadrant(windows, qi, qj):
     part = (qi % 2 * 2 + qj % 2) * QUAD
     return windows[qi // 2 * 2 + qj // 2][part : part + QUAD]
-
-
-def halves(values):
-    return [values[:, 0:192], values[:, 192:384]]
 
 
 def edge_kernel(tokens_ref, grad_ref, slon_ref, slat_ref, sdiag_ref, gloc_ref):
@@ -285,15 +311,12 @@
             for z in range(2)
             for row in range(3)
         ]
-        return pack(pieces, 48)
-
-    slon_ref[0:112] = pack([token_quadrant(q * 3, 18) for q in range(3)], 112)
-    slat_ref[0:112] = pack([token_quadrant(9, q * 6) for q in range(3)], 112)
-    sdiag_ref[0:48] = pack([token_quadrant(9, 18)], 48)
-    gloc_ref[0:48], gloc_ref[48:96] = halves(grad_quadrant(0, 0))
-    slon_ref[112:160], slon_ref[160:208] = halves(grad_quadrant(0, 1))
-    slat_ref[112:160], slat_ref[160:208] = halves(grad_quadrant(1, 0))
-    sdiag_ref[48:96], sdiag_ref[96:144] = halves(grad_quadrant(1, 1))
+        return jnp.concatenate(pieces, axis=0)
+
+    slon_ref[...] = dense([token_quadrant(q * 3, 18) for q in range(3)], 112, grad_quadrant(0, 1))
+    slat_ref[...] = dense([token_quadrant(9, q * 6) for q in range(3)], 112, grad_quadrant(1, 0))
+    sdiag_ref[...] = dense([token_quadrant(9, 18)], 48, grad_quadrant(1, 1))
+    gloc_ref[...] = pack([grad_quadrant(0, 0)], 48)
 
 
 def expand(table_ref, out_ref, held):
@@ -331,12 +354,16 @@
     table_ref[...] = table_grad(score_ref, rows_ref)
 
 
-def table_sum_kernel(kept_ref, other_ref, out_ref):
-    total = kept_ref[...].astype(f32) + other_ref[...].astype(f32)
-    total = jnp.concatenate([total[0:12], total[12:24]], axis=1)
-    heads = out_ref.shape[0]
-    for b in range(out_ref.shape[1]):
-        out_ref[:, b, :] = total[b * heads : (b + 1) * heads]
+def table_sum_kernel(fine_kept, fine_other, coarse_kept, coarse_other, fine_ref, coarse_ref):
+    for kept, other, out_ref in (
+        (fine_kept, fine_other, fine_ref),
+        (coarse_kept, coarse_other, coarse_ref),
+    ):
+        total = kept[...].astype(f32) + other[...].astype(f32)
+        total = jnp.concatenate([total[0:12], total[12:24]], axis=1)
+        heads = out_ref.shape[0]
+        for b in range(out_ref.shape[1]):
+            out_ref[:, b, :] = total[b * heads : (b + 1) * heads]
 
 
 def fine_windows(numbers, refs):
@@ -345,9 +372,9 @@
     q_ref, k_ref, v_ref, probs_ref, n1_ref, r1_ref, n2_ref, r2_ref, slope_ref = refs[12:21]
     source = refs[21]
     source[0:576] = tokens_ref[...]
-    source[576:688] = lon_ref[0:112]
-    source[688:800] = lat_ref[0:112]
-    source[800:848] = diag_ref[0:48]
+    source[576:688] = tokens_of(lon_ref, 112)
+    source[688:800] = tokens_of(lat_ref, 112)
+    source[800:848] = tokens_of(diag_ref, 48)
     everything = source[...]
     w_qkv = qkv_ref[...]
     bases = []
@@ -385,9 +412,9 @@
 def fine_edge_kernel(*refs):
     slon_ref, slat_ref, sdiag_ref = refs[11:14]
     windows = fine_windows((1, 2, 3), refs[:11] + refs[14:])
-    slon_ref[...] = pack([quadrant(windows, q, 3) for q in range(3)], 112)
-    slat_ref[...] = pack([quadrant(windows, 3, q) for q in range(3)], 112)
-    sdiag_ref[...] = pack([quadrant(windows, 3, 3)], 48)
+    slon_ref[...] = dense([quadrant(windows, q, 3) for q in range(3)], 112)
+    slat_ref[...] = dense([quadrant(windows, 3, q) for q in range(3)], 112)
+    sdiag_ref[...] = dense([quadrant(windows, 3, 3)], 48)
 
 
 def fine_inner_kernel(*refs):
@@ -403,9 +430,9 @@
 ):
     source[0:144] = inner_ref[...]
     source[144:576] = res_ref[...]
-    source[576:688] = lon_ref[...]
-    source[688:800] = lat_ref[...]
-    source[800:848] = diag_ref[...]
+    source[576:688] = tokens_of(lon_ref, 112)
+    source[688:800] = tokens_of(lat_ref, 112)
+    source[800:848] = tokens_of(diag_ref, 48)
     everything = source[...]
     parts = [mm(one_hot(merge_ref[pl.ds(k * WIN, WIN), :], 848), everything) for k in range(4)]
     mean = sum(jnp.sum(part, axis=-1, keepdims=True) for part in parts) * (1.0 / 768)
@@ -427,14 +454,17 @@
     active, slope = gelu_pair(mm(renormed, up_ref[...]))
     result = first + mm(active.astype(bf16), down_ref[...])
     for index, out in enumerate((c0, c1, c2, c3)):
-        piece = pack([result[index * QUAD : (index + 1) * QUAD]], 48)
-        out[0:48], out[48:96] = halves(piece)
-
-    pieces = []
-    for ref, start in ((gdiag_ref, 48), (glat_ref, 112), (glon_ref, 112), (gloc_ref, 0)):
-        both = [ref[start : start + 48], ref[start + 48 : start + 96]]
-        pieces.append(jnp.concatenate([half.astype(f32)[:QUAD] for half in both], axis=1))
-    grad = jnp.concatenate(pieces, axis=0)
+        out[...] = pack([result[index * QUAD : (index + 1) * QUAD]], 48)
+
+    grad = jnp.concatenate(
+        [
+            coarse_of(gdiag_ref, 48),
+            coarse_of(glat_ref, 112),
+            coarse_of(glon_ref, 112),
+            gloc_ref[...].astype(f32)[:QUAD],
+        ],
+        axis=0,
+    )
     inner = mm_nt(grad.astype(bf16), down_ref[...]) * slope
     grad = grad + norm_back(mm_nt(inner.astype(bf16), up_ref[...]), renormed.astype(f32), scale2)
     mix_grad = mm_nt(grad.astype(bf16), proj_ref[...]).astype(bf16)
@@ -455,11 +485,11 @@
         part = (grads[k] - mean - parts[k].astype(f32) * along) * merge_scale
         parts_ref[pl.ds(k * WIN, WIN), :] = part.astype(bf16)
     everything = parts_ref[...]
-    moved = mm(one_hot(split_ref[...], 576), everything).astype(bf16)
-    dlon_ref[...] = moved[0:112]
-    dloc_ref[...] = moved[112:448]
-    dlat_ref[...] = moved[448:560]
-    ddiag_ref[...] = moved[560:608]
+    moved = mm(one_hot(split_ref[...], 576), everything)
+    dlon_ref[...] = dense([moved[0:112]], 112)
+    dloc_ref[...] = moved[112:448].astype(bf16)
+    dlat_ref[...] = dense([moved[448:560]], 112)
+    ddiag_ref[...] = dense([moved[560:608]], 48)
 
 
 def band_back(parts, source, back_ref, weights, outs, score_ref):
@@ -488,7 +518,7 @@
 
 def first_band_kernel(dlon_ref, dloc_ref, back_ref, *refs):
     *refs, source = refs
-    source[0:112] = dlon_ref[...]
+    source[0:112] = tokens_of(dlon_ref, 112)
     source[112:448] = dloc_ref[...]
     parts = ((0, 0, refs[:7]), (1, 0, refs[7:14]))
     band_back(parts, source, back_ref, refs[14:17], refs[17:21], refs[21])
@@ -498,10 +528,10 @@
     dlon_ref, dloc_ref, dlat_ref, ddiag_ref, back_ref, first_ref, *refs
 ):
     *refs, source, score_ref, rows_ref = refs
-    source[0:112] = dlon_ref[...]
+    source[0:112] = tokens_of(dlon_ref, 112)
     source[112:448] = dloc_ref[...]
-    source[448:560] = dlat_ref[...]
-    source[560:608] = ddiag_ref[...]
+    source[448:560] = tokens_of(dlat_ref, 112)
+    source[560:608] = tokens_of(ddiag_ref, 48)
     half = 6 * WIN
     score_ref[pl.ds(0, half), :] = first_ref[...]
     parts = ((2, 1, refs[:7]), (3, 2, refs[:7]))
@@ -534,12 +564,12 @@
         )
         res_ref[rows, :] = result.astype(bf16)
         windows.append(result)
-    slon_ref[0:112] = pack([quadrant(windows, q, 0) for q in range(1, 4)], 112)
-    slat_ref[0:112] = pack([quadrant(windows, 0, q) for q in range(1, 4)], 112)
-    sdiag_ref[0:48] = pack([quadrant(windows, 0, 0)], 48)
-    slon_ref[112:208] = clon_ref[...]
-    slat_ref[112:208] = clat_ref[...]
-    sdiag_ref[48:144] = cdiag_ref[...]
+    clon, clat, cdiag = [
+        ref[...].astype(f32)[:QUAD] for ref in (clon_ref, clat_ref, cdiag_ref)
+    ]
+    slon_ref[...] = dense([quadrant(windows, q, 0) for q in range(1, 4)], 112, clon)
+    slat_ref[...] = dense([quadrant(windows, 0, q) for q in range(1, 4)], 112, clat)
+    sdiag_ref[...] = dense([quadrant(windows, 0, 0)], 48, cdiag)
 
 
 def last_kernel(
@@ -547,22 +577,18 @@
     tokens_ref, coarse_ref, source, coarse_source,
 ):
     source[0:576] = res_ref[...]
-    source[576:688] = lon_ref[0:112]
-    source[688:800] = lat_ref[0:112]
-    source[800:848] = diag_ref[0:48]
+    source[576:688] = tokens_of(lon_ref, 112)
+    source[688:800] = tokens_of(lat_ref, 112)
+    source[800:848] = tokens_of(diag_ref, 48)
     everything = source[...]
     for w in range(4):
         rows = pl.ds(w * WIN, WIN)
         tokens_ref[rows, :] = mm(one_hot(leave_ref[rows, :], 848), everything).astype(bf16)
-    picks = one_hot(result_ref[...], 192)
-    moved = []
-    for half in (0, 48):
-        coarse_source[0:48] = cloc_ref[half : half + 48]
-        coarse_source[48:96] = lon_ref[112 + half : 160 + half]
-        coarse_source[96:144] = lat_ref[112 + half : 160 + half]
-        coarse_source[144:192] = diag_ref[48 + half : 96 + half]
-        moved.append(mm(picks, coarse_source[...]))
-    moved = jnp.concatenate(moved, axis=1)
+    coarse_source[0:48] = cloc_ref[...]
+    coarse_source[48:96] = pack([coarse_of(lon_ref, 112)], 48)
+    coarse_source[96:144] = pack([coarse_of(lat_ref, 112)], 48)
+    coarse_source[144:192] = pack([coarse_of(diag_ref, 48)], 48)
+    moved = mm(one_hot(result_ref[...], 192), coarse_source[...])
     for z in range(2):
         for row in range(6):
             start = z * 72 + row * 12
@@ -627,9 +653,9 @@
     flat = tokens.reshape(576, 192)
     column = lambda index: jnp.asarray(index).reshape(-1, 1)
     tok = ((576, 192), bf16)
-    edges = [((112, 192), bf16), ((112, 192), bf16), ((48, 192), bf16)]
-    wide_edges = [((208, 192), bf16), ((208, 192), bf16), ((144, 192), bf16)]
-    quad = ((96, 192), bf16)
+    edges = [((176, 128), bf16), ((176, 128), bf16), ((80, 128), bf16)]
+    wide_edges = [((288, 128), bf16), ((288, 128), bf16), ((192, 128), bf16)]
+    quad = ((48, 384), bf16)
     scores = ((12 * WIN, WIN), f32)
     table_rows = ((12, 192, WIN), bf16)
     held = ((12, 2, 12, 16, WIN), bf16)
@@ -747,14 +773,15 @@
     d_tokens, coarse_result = run(
         last_kernel,
         [tok, ((2, 6, 12, 384), bf16)],
-        [((848, 192), bf16), ((192, 192), bf16)],
+        [((848, 192), bf16), ((192, 384), bf16)],
         1,
         (fine_back[0], alon, alat, adiag, column(LEAVE), c11, column(RESULT)),
     )
-    (coarse_out,) = run(
-        table_sum_kernel, [((HEADS_C, 1, 12 * ENTRIES), f32)], [], 1, coarse_sums
-    )
-    (fine_out,) = run(table_sum_kernel, [((HEADS_F, 2, 12 * ENTRIES), f32)], [], 1, fine_sums)
+    fine_out, coarse_out = run(
+        table_sum_kernel,
+        [((HEADS_F, 2, 12 * ENTRIES), f32), ((HEADS_C, 1, 12 * ENTRIES), f32)],
+        [], 1, (*fine_sums, *coarse_sums),
+    )
     return (
         coarse_result,
         d_tokens.reshape(tokens.shape),

time: 73 us -> 71.6 us (0.981)
  starting transfers between devices: 22.9 us -> 21.4 us
    ppermute x6, starting transfers between devices: 5.64 us -> 4.31 us  [swap(): return lax.ppermute(value, 'lon', [(s, s ^ step) for s in range(count)])]
    ppermute x6, waiting for transfers between devices: 6.68 us -> 7.77 us  [swap(): return lax.ppermute(value, 'lon', [(s, s ^ step) for s in range(count)])]
    pallas_call x13 -> x12, Pallas kernels: 34.9 us -> 34.6 us  [run(): pl.pallas_call(kernel, out_shape=shapes, scratch_shapes=[pltpu.VMEM(shape...]
  transfers between devices with their start and end apart: 18 -> 18, of which waited for: 7 -> 9; matrix products, arithmetic and copies ran while one was open for 2% -> 2% of each run, Pallas kernels for 27% -> 27%
where the time goes in v5:
time: 71.6 us; the launch traced here: 71.4 us
  Pallas kernels  34.6 us (48%)
  starting transfers between devices  21.4 us (30%)
  waiting for transfers between devices  11 us (15%)
  local copies, waits for them, and re-layouts  2.93 us (4%)
  between operations  1.03 us (1%)
    pallas_call x12, Pallas kernels, run(): pl.pallas_call(kernel, out_shape=shapes, scratch_shapes=[pltpu.VMEM(shape...  34.6 us
    ppermute x6, waiting for transfers between devices, swap(): return lax.ppermute(value, 'lon', [(s, s ^ step) for s in range(count)])  7.77 us
    ppermute x4, starting transfers between devices, move(): return lax.ppermute(value, ('lon', 'lat'), pairs)  7.25 us
    ppermute x4, starting transfers between devices, move(): return lax.ppermute(value, 'lon', pairs)  6.18 us
    ppermute x6, starting transfers between devices, swap(): return lax.ppermute(value, 'lon', [(s, s ^ step) for s in range(count)])  4.31 us
    ppermute x4, starting transfers between devices, move(): return lax.ppermute(value, 'lat', pairs)  3.63 us
    ppermute x4, waiting for transfers between devices, move(): return lax.ppermute(value, 'lon', pairs)  2.85 us
    unnamed x43, local copies, waits for them, and re-layouts  2.69 us
  transfers between devices with their start and end apart: 18, of which 9 were waited for; matrix products, arithmetic and copies ran while one was open for 2% of the time, Pallas kernels for 27%

profile of v5, /device:TPU:0, one launch (start us, length us, event | category | flops | bytes accessed | tf_op | source)
XLA Modules:
  0.0 71.4 jit_solution(14630829336214086932)
XLA Ops:
  0.6 1.0 %copy-done.4 = bf16[2,12,24,192]{3,2,1,0:T(8,128)(2,1)S(1)} copy-done((bf16[2,12,24,192]{3,2,1,0:T(8,128)(2,1)S(1)}, bf16[2,12,24,192]{3,2,1,0:T(8,128)(2,1)}, u32[]{:S(2)}) %copy-start.4) | copy-done | bytes 221208
  1.6 0.9 %copy-done.12 = bf16[2,6,12,384]{3,0,2,1:T(2,128)(2,1)S(1)} copy-done((bf16[2,6,12,384]{3,0,2,1:T(2,128)(2,1)S(1)}, bf16[2,6,12,384]{3,0,2,1:T(2,128)(2,1)}, u32[]{:S(2)}) %copy-start.12) | copy-done | bytes 110616
  2.5 0.2 shard_map.219
  2.7 2.5 %collective-permute-start.2 = (bf16[192,128]{1,0:T(8,128)(2,1)S(1)}, bf16[192,128]{1,0:T(8,128)(2,1)S(1)}, u32[]{:S(2)}, u32[]{:S(2)}) collective-permute-start(bf16[192,128]{1,0:T(8,128)(2,1)S(1)} %get-tuple-element.70), channel_id=1, source_target_pairs={{0,5},{1,6},{2,7},{3,4},{4,9},{5,10},{6,11},{7,8},{8,13},{9,14},{1... | collective-permute-start | bytes 147464 | tf_op jit(solution)/shard_map/ppermute | solution.py:626
  5.1 1.5 %collective-permute-start = (bf16[288,128]{1,0:T(8,128)(2,1)S(1)}, bf16[288,128]{1,0:T(8,128)(2,1)S(1)}, u32[]{:S(2)}, u32[]{:S(2)}) collective-permute-start(bf16[288,128]{1,0:T(8,128)(2,1)S(1)} %get-tuple-element.68), channel_id=1, source_target_pairs={{0,4},{4,8},{8,12},{12,16},{16,20},{20,24},{24,28},{28,0},{1,5},{5... | collective-permute-start | bytes 221192 | tf_op jit(solution)/shard_map/ppermute | solution.py:617
  6.6 1.3 %collective-permute-start.1 = (bf16[288,128]{1,0:T(8,128)(2,1)S(1)}, bf16[288,128]{1,0:T(8,128)(2,1)S(1)}, u32[]{:S(2)}, u32[]{:S(2)}) collective-permute-start(bf16[288,128]{1,0:T(8,128)(2,1)S(1)} %get-tuple-element.69), channel_id=1, source_target_pairs={{0,1},{1,2},{2,3},{3,0},{4,5},{5,6},{6,7},{7,4},{8,9},{9,10},{10,1... | collective-permute-start | bytes 221192 | tf_op jit(solution)/shard_map/ppermute | solution.py:620
  8.0 0.1 multiply_add_fusion
  8.1 0.1 reshape.48
  8.2 0.1 eq.28
  8.3 0.1 compare_select_fusion.refs_6_
  8.5 0.1 or_select_fusion.mask_ref
  8.7 0.0 copy-start.18
  8.7 2.3 %shard_map.220.refs_5_ = f32[1728,144]{1,0:T(8,128)S(1)} custom-call(f32[6,2,3312]{2,1,0:T(2,128)S(1)} %bitcast.20), custom_call_target="tpu_custom_call" | custom-call | flops 2000000000 | bytes 1154304 | tf_op jit(solution)/shard_map/pallas_call | solution.py:602
  11.0 0.4 collective-permute-done.2.refs_3_.gdiag_ref
  11.3 1.1 %collective-permute-done.refs_1_.glon_ref = bf16[288,128]{1,0:T(8,128)(2,1)S(1)} collective-permute-done((bf16[288,128]{1,0:T(8,128)(2,1)S(1)}, bf16[288,128]{1,0:T(8,128)(2,1)S(1)}, u32[]{:S(2)}, u32[]{:S(2)}) %collective-permute-start) | collective-permute-done | bytes 73760 | tf_op jit(solution)/shard_map/ppermute | solution.py:617
  12.5 5.9 %shard_map.221 = (bf16[176,128]{1,0:T(8,128)(2,1)S(1)}, bf16[176,128]{1,0:T(8,128)(2,1)S(1)}, bf16[80,128]{1,0:T(8,128)(2,1)S(1)}, bf16[432,192]{1,0:T(8,128)(2,...) custom-call(bf16[576,192]{1,0:T(8,128)(2,1)S(1)} %bitcast.14, ...), custom_call_target="tpu_custom_call" | custom-call | flops 6000000000 | bytes 5151360 | tf_op jit(solution)/shard_map/pallas_call | solution.py:602
  18.4 0.1 collective-permute-start.5
  18.4 1.5 %collective-permute-start.3 = (bf16[176,128]{1,0:T(8,128)(2,1)S(1)}, bf16[176,128]{1,0:T(8,128)(2,1)S(1)}, u32[]{:S(2)}, u32[]{:S(2)}) collective-permute-start(bf16[176,128]{1,0:T(8,128)(2,1)S(1)} %get-tuple-element.74), channel_id=1, source_target_pairs={{0,4},{4,8},{8,12},{12,16},{16,20},{20,24},{24,28},{28,0},{1,5},{5... | collective-permute-start | bytes 135176 | tf_op jit(solution)/shard_map/ppermute | solution.py:617
  19.9 1.0 %collective-permute-start.4 = (bf16[176,128]{1,0:T(8,128)(2,1)S(1)}, bf16[176,128]{1,0:T(8,128)(2,1)S(1)}, u32[]{:S(2)}, u32[]{:S(2)}) collective-permute-start(bf16[176,128]{1,0:T(8,128)(2,1)S(1)} %get-tuple-element.75), channel_id=1, source_target_pairs={{0,1},{1,2},{2,3},{3,0},{4,5},{5,6},{6,7},{7,4},{8,9},{9,10},{10,1... | collective-permute-start | bytes 135176 | tf_op jit(solution)/shard_map/ppermute | solution.py:620
  21.0 2.3 %shard_map.223.bias_ref = f32[1728,144]{1,0:T(8,128)S(1)} custom-call(f32[12,1,3312]{2,1,0:T(1,128)S(1)} %bitcast.21), custom_call_target="tpu_custom_call" | custom-call | flops 2000000000 | bytes 1154304 | tf_op jit(solution)/shard_map/pallas_call | solution.py:602
  23.3 2.7 %shard_map.222 = (bf16[144,192]{1,0:T(8,128)(2,1)S(1)}, bf16[144,192]{1,0:T(8,128)(2,1)S(1)}, bf16[144,192]{1,0:T(8,128)(2,1)S(1)}, bf16[144,192]{1,0:T(8,128)(2...) custom-call(bf16[576,192]{1,0:T(8,128)(2,1)S(1)} %bitcast.15, ...), custom_call_target="tpu_custom_call" | custom-call | flops 2000000000 | bytes 3434880 | tf_op jit(solution)/shard_map/pallas_call | solution.py:602
  26.2 8.6 %shard_map.224 = (bf16[48,384]{1,0:T(8,128)(2,1)S(1)}, bf16[48,384]{1,0:T(8,128)(2,1)S(1)}, bf16[48,384]{1,0:T(8,128)(2,1)S(1)}, bf16[48,384]{1,0:T(8,128)(2,1)S...) custom-call(bf16[144,192]{1,0:T(8,128)(2,1)S(1)} %get-tuple-element., ...), custom_call_target="tpu_custom_call" | custom-call | flops 8999999488 | bytes 7159424 | tf_op jit(solution)/shard_map/pallas_call | solution.py:602
  34.8 0.8 %collective-permute-start.7 = (bf16[176,128]{1,0:T(8,128)(2,1)S(1)}, bf16[176,128]{1,0:T(8,128)(2,1)S(1)}, u32[]{:S(2)}, u32[]{:S(2)}) collective-permute-start(bf16[176,128]{1,0:T(8,128)(2,1)S(1)} %get-tuple-element.99), channel_id=1, source_target_pairs={{0,3},{1,0},{2,1},{3,2},{4,7},{5,4},{6,5},{7,6},{8,11},{9,8},{10,9... | collective-permute-start | bytes 135176 | tf_op jit(solution)/shard_map/ppermute | solution.py:620
  35.6 3.1 %collective-permute-start.8 = (bf16[80,128]{1,0:T(8,128)(2,1)S(1)}, bf16[80,128]{1,0:T(8,128)(2,1)S(1)}, u32[]{:S(2)}, u32[]{:S(2)}) collective-permute-start(bf16[80,128]{1,0:T(8,128)(2,1)S(1)} %get-tuple-element.102), channel_id=1, source_target_pairs={{0,31},{1,28},{2,29},{3,30},{4,3},{5,0},{6,1},{7,2},{8,7},{9,4},{1... | collective-permute-start | bytes 61448 | tf_op jit(solution)/shard_map/ppermute | solution.py:626
  38.7 1.6 %collective-permute-start.6 = (bf16[176,128]{1,0:T(8,128)(2,1)S(1)}, bf16[176,128]{1,0:T(8,128)(2,1)S(1)}, u32[]{:S(2)}, u32[]{:S(2)}) collective-permute-start(bf16[176,128]{1,0:T(8,128)(2,1)S(1)} %get-tuple-element.79), channel_id=1, source_target_pairs={{0,28},{4,0},{8,4},{12,8},{16,12},{20,16},{24,20},{28,24},{1,29},{... | collective-permute-start | bytes 135176 | tf_op jit(solution)/shard_map/ppermute | solution.py:617
  40.3 1.4 %shard_map.226 = bf16[24,1656]{1,0:T(8,128)(2,1)S(1)} custom-call(f32[1728,144]{1,0:T(8,128)S(1)} %get-tuple-element.104.score_ref), custom_call_target="tpu_custom_call" | custom-call | flops 2000000000 | bytes 1074816 | tf_op jit(solution)/shard_map/pallas_call | solution.py:602
  41.7 0.1 collective-permute-start.9
  41.8 0.9 %collective-permute-done.6.dlon_ref = bf16[176,128]{1,0:T(8,128)(2,1)S(1)} collective-permute-done((bf16[176,128]{1,0:T(8,128)(2,1)S(1)}, bf16[176,128]{1,0:T(8,128)(2,1)S(1)}, u32[]{:S(2)}, u32[]{:S(2)}) %collective-permute-start.6) | collective-permute-done | bytes 45088 | tf_op jit(solution)/shard_map/ppermute | solution.py:617
  42.8 3.6 %shard_map.225 = (f32[288,192]{1,0:T(8,128)S(1)}, bf16[288,192]{1,0:T(8,128)(2,1)S(1)}, bf16[288,192]{1,0:T(8,128)(2,1)S(1)}, bf16[288,192]{1,0:T(8,128)(2,1)S(1)}, f32[864,144]{1,0:T(8,128)S(1)}) custom-call(bf16[176,128]{1,0:T(8,128)(2,1)S(1)} %collective-permute-done.6.dlon_ref, bf16[336,192]{1,0:T(8,128)(2,1)S(1)} %get-tuple-element.80.dloc_ref, ...), custom_call_target="tpu_custom_call" | custom-call | flops 4000000000 | bytes 4657664 | tf_op jit(solution)/shard_map/pallas_call | solution.py:602
  46.4 1.7 %collective-permute-done.9 = bf16[24,1656]{1,0:T(8,128)(2,1)S(1)} collective-permute-done((bf16[24,1656]{1,0:T(8,128)(2,1)S(1)}, bf16[24,1656]{1,0:T(8,128)(2,1)S(1)}, u32[]{:S(2)}, u32[]{:S(2)}) %collective-permute-start.9) | collective-permute-done | bytes 79520 | tf_op jit(solution)/shard_map/ppermute | solution.py:636
  48.1 0.1 collective-permute-start.10
  48.2 4.7 %shard_map.227 = (f32[288,192]{1,0:T(8,128)S(1)}, bf16[288,192]{1,0:T(8,128)(2,1)S(1)}, bf16[288,192]{1,0:T(8,128)(2,1)S(1)}, bf16[288,192]{1,0:T(8,128)(2,1)S(1)}, bf16[24,1656]{1,0:T(8,128)(2,1)S(1)}) custom-call(bf16[176,128]{1,0:T(8,128)(2,1)S(1)} %collective-permute-done.6.dlon_ref, bf16[336,192]{1,0:T(8,128)(2,1)S(1)} %get-tuple-element.80.dloc_ref, ...), custom_call_target="tpu_custom_call" | custom-call | flops 5000000000 | bytes 4110912 | tf_op jit(solution)/shard_map/pallas_call | solution.py:602
  52.9 2.7 %collective-permute-start.13 = (bf16[24,1656]{1,0:T(8,128)(2,1)S(1)}, bf16[24,1656]{1,0:T(8,128)(2,1)S(1)}, u32[]{:S(2)}, u32[]{:S(2)}) collective-permute-start(bf16[24,1656]{1,0:T(8,128)(2,1)S(1)} %get-tuple-element.122), channel_id=1, source_target_pairs={{0,16},{4,20},{8,24},{12,28},{16,0},{20,4},{24,8},{28,12},{1,17},{... | collective-permute-start | bytes 238472 | tf_op jit(solution)/shard_map/ppermute | solution.py:636
  55.5 0.8 %shard_map.228 = (bf16[576,192]{1,0:T(8,128)(2,1)S(1)}, bf16[288,128]{1,0:T(8,128)(2,1)S(1)}, bf16[288,128]{1,0:T(8,128)(2,1)S(1)}, bf16[192,128]{1,0:T(8,128)(2,1)S(1)}) custom-call(f32[288,192]{1,0:T(8,128)S(1)} %get-tuple-element.95.refs_0_, bf16[288,192]{1,0:T(8,128)(2,1)S(1)} %get-tuple-element.96.refs_1_, ...), custom_call_target="tpu_custom_call" | custom-call | flops 2000000000 | bytes 2078976 | tf_op jit(solution)/shard_map/pallas_call | solution.py:602
  56.4 0.5 collective-permute-start.12
  56.9 3.1 %collective-permute-done.13 = bf16[24,1656]{1,0:T(8,128)(2,1)S(1)} collective-permute-done((bf16[24,1656]{1,0:T(8,128)(2,1)S(1)}, bf16[24,1656]{1,0:T(8,128)(2,1)S(1)}, u32[]{:S(2)}, u32[]{:S(2)}) %collective-permute-start.13) | collective-permute-done | bytes 79520 | tf_op jit(solution)/shard_map/ppermute | solution.py:636
  60.0 0.4 collective-permute-start.15
  60.4 1.6 %collective-permute-start.14 = (bf16[192,128]{1,0:T(8,128)(2,1)S(1)}, bf16[192,128]{1,0:T(8,128)(2,1)S(1)}, u32[]{:S(2)}, u32[]{:S(2)}) collective-permute-start(bf16[192,128]{1,0:T(8,128)(2,1)S(1)} %get-tuple-element.124), channel_id=1, source_target_pairs={{0,31},{1,28},{2,29},{3,30},{4,3},{5,0},{6,1},{7,2},{8,7},{9,4},{1... | collective-permute-start | bytes 147464 | tf_op jit(solution)/shard_map/ppermute | solution.py:626
  62.0 1.5 %collective-permute-start.11 = (bf16[288,128]{1,0:T(8,128)(2,1)S(1)}, bf16[288,128]{1,0:T(8,128)(2,1)S(1)}, u32[]{:S(2)}, u32[]{:S(2)}) collective-permute-start(bf16[288,128]{1,0:T(8,128)(2,1)S(1)} %get-tuple-element.120), channel_id=1, source_target_pairs={{0,28},{4,0},{8,4},{12,8},{16,12},{20,16},{24,20},{28,24},{1,29},{... | collective-permute-start | bytes 221192 | tf_op jit(solution)/shard_map/ppermute | solution.py:617
  63.5 0.5 collective-permute-start.17
  64.0 1.1 %collective-permute-done.15 = bf16[24,1656]{1,0:T(8,128)(2,1)S(1)} collective-permute-done((bf16[24,1656]{1,0:T(8,128)(2,1)S(1)}, bf16[24,1656]{1,0:T(8,128)(2,1)S(1)}, u32[]{:S(2)}, u32[]{:S(2)}) %collective-permute-start.15) | collective-permute-done | bytes 79520 | tf_op jit(solution)/shard_map/ppermute | solution.py:636
  65.2 0.6 collective-permute-start.16
  65.8 0.8 %collective-permute-done.11.lon_ref = bf16[288,128]{1,0:T(8,128)(2,1)S(1)} collective-permute-done((bf16[288,128]{1,0:T(8,128)(2,1)S(1)}, bf16[288,128]{1,0:T(8,128)(2,1)S(1)}, u32[]{:S(2)}, u32[]{:S(2)}) %collective-permute-start.11) | collective-permute-done | bytes 73760 | tf_op jit(solution)/shard_map/ppermute | solution.py:617
  66.7 1.3 %shard_map.229 = (bf16[576,192]{1,0:T(8,128)(2,1)}, bf16[2,6,12,384]{3,2,1,0:T(8,128)(2,1)S(1)}) custom-call(bf16[576,192]{1,0:T(8,128)(2,1)S(1)} %get-tuple-element.119.res_ref, bf16[288,128]{1,0:T(8,128)(2,1)S(1)} %collective-permute-done.11.lon_ref, bf16[288,128]{1,0:T(8,128)(2,1)S(1)} %collective-permute-done.12.lat_ref, ...), custom_call_target="tpu_custom_call" | custom-call | flops 1000000000 | bytes 789312 | tf_op jit(solution)/shard_map/pallas_call | solution.py:602
  68.0 0.7 %copy.27 = bf16[2,6,12,384]{3,0,2,1:T(2,128)(2,1)} copy(bf16[2,6,12,384]{3,2,1,0:T(8,128)(2,1)S(1)} %get-tuple-element.136) | data formatting | bytes 221184
  68.7 0.1 collective-permute-done.17.coarse_other
  68.8 1.8 %collective-permute-done.16.fine_other = bf16[24,1656]{1,0:T(8,128)(2,1)S(1)} collective-permute-done((bf16[24,1656]{1,0:T(8,128)(2,1)S(1)}, bf16[24,1656]{1,0:T(8,128)(2,1)S(1)}, u32[]{:S(2)}, u32[]{:S(2)}) %collective-permute-start.16) | collective-permute-done | bytes 79520 | tf_op jit(solution)/shard_map/ppermute | solution.py:636
  70.6 0.8 %shard_map.230 = (f32[6,2,3312]{2,1,0:T(2,128)}, f32[12,1,3312]{2,1,0:T(1,128)}) custom-call(bf16[24,1656]{1,0:T(8,128)(2,1)S(1)} %add_convert_fusion.1.fine_kept, bf16[24,1656]{1,0:T(8,128)(2,1)S(1)} %collective-permute-done.16.fine_other, bf16[24,1656]{1,0:T(8,128)(2,1)S(1)} %add_convert_fusion.coarse_kept, ...), custom_call_target="tpu_custom_call" | custom-call | flops 1000000000 | bytes 635904 | tf_op jit(solution)/shard_map/pallas_call | solution.py:602
  (55 shorter events, 0.3 us)
Async XLA Ops:
  0.6 1.0 %copy-start.4 = (bf16[2,12,24,192]{3,2,1,0:T(8,128)(2,1)S(1)}, bf16[2,12,24,192]{3,2,1,0:T(8,128)(2,1)}, u32[]{:S(2)}) copy-start(bf16[2,12,24,192]{3,2,1,0:T(8,128)(2,1)} %param.20) | copy-start | bytes 663556
  1.6 0.9 %copy-start.12 = (bf16[2,6,12,384]{3,0,2,1:T(2,128)(2,1)S(1)}, bf16[2,6,12,384]{3,0,2,1:T(2,128)(2,1)}, u32[]{:S(2)}) copy-start(bf16[2,6,12,384]{3,0,2,1:T(2,128)(2,1)} %param.33) | copy-start | bytes 331780
  2.5 5.5 %copy-start.20 = (s32[2,12,24]{2,0,1:T(2,128)S(1)}, s32[2,12,24]{2,0,1:T(2,128)}, u32[]{:S(2)}) copy-start(s32[2,12,24]{2,0,1:T(2,128)} %param.21) | copy-start | bytes 6916
  2.5 6.1 %copy-start.10 = (f32[2,6,3312]{2,0,1:T(2,128)S(1)}, f32[2,6,3312]{2,0,1:T(2,128)}, u32[]{:S(2)}) copy-start(f32[2,6,3312]{2,0,1:T(2,128)} %param.26) | copy-start | bytes 476932
  2.7 8.7 %collective-permute-start.2 = (bf16[192,128]{1,0:T(8,128)(2,1)S(1)}, bf16[192,128]{1,0:T(8,128)(2,1)S(1)}, u32[]{:S(2)}, u32[]{:S(2)}) collective-permute-start(bf16[192,128]{1,0:T(8,128)(2,1)S(1)} %get-tuple-element.70), channel_id=1, source_target_pairs={{0,5},{1,6},{2,7},{3,4},{4,9},{5,10},{6,11},{7,8},{8,13},{9,14},{1... | collective-permute-start | bytes 147464 | tf_op jit(solution)/shard_map/ppermute | solution.py:626
  5.1 7.3 %collective-permute-start = (bf16[288,128]{1,0:T(8,128)(2,1)S(1)}, bf16[288,128]{1,0:T(8,128)(2,1)S(1)}, u32[]{:S(2)}, u32[]{:S(2)}) collective-permute-start(bf16[288,128]{1,0:T(8,128)(2,1)S(1)} %get-tuple-element.68), channel_id=1, source_target_pairs={{0,4},{4,8},{8,12},{12,16},{16,20},{20,24},{24,28},{28,0},{1,5},{5... | collective-permute-start | bytes 221192 | tf_op jit(solution)/shard_map/ppermute | solution.py:617
  6.6 5.7 %collective-permute-start.1 = (bf16[288,128]{1,0:T(8,128)(2,1)S(1)}, bf16[288,128]{1,0:T(8,128)(2,1)S(1)}, u32[]{:S(2)}, u32[]{:S(2)}) collective-permute-start(bf16[288,128]{1,0:T(8,128)(2,1)S(1)} %get-tuple-element.69), channel_id=1, source_target_pairs={{0,1},{1,2},{2,3},{3,0},{4,5},{5,6},{6,7},{7,4},{8,9},{9,10},{10,1... | collective-permute-start | bytes 221192 | tf_op jit(solution)/shard_map/ppermute | solution.py:620
  8.6 3.8 %copy-start.5 = (bf16[2,12,24,192]{3,2,1,0:T(8,128)(2,1)S(1)}, bf16[2,12,24,192]{3,2,1,0:T(8,128)(2,1)}, u32[]{:S(2)}) copy-start(bf16[2,12,24,192]{3,2,1,0:T(8,128)(2,1)} %param.20) | copy-start | bytes 663556
  8.6 3.8 %copy-start.7 = (bf16[192,768]{1,0:T(8,128)(2,1)S(1)}, bf16[192,768]{1,0:T(8,128)(2,1)}, u32[]{:S(2)}) copy-start(bf16[192,768]{1,0:T(8,128)(2,1)} %refs_8_.5) | copy-start | bytes 884740
  8.6 3.8 %copy-start.8 = (bf16[768,192]{0,1:T(8,128)(2,1)S(1)}, bf16[768,192]{0,1:T(8,128)(2,1)}, u32[]{:S(2)}) copy-start(bf16[768,192]{0,1:T(8,128)(2,1)} %param.25) | copy-start | bytes 884740
  8.6 3.8 %copy-start.9 = (bf16[192,576]{1,0:T(8,128)(2,1)S(1)}, bf16[192,576]{1,0:T(8,128)(2,1)}, u32[]{:S(2)}) copy-start(bf16[192,576]{1,0:T(8,128)(2,1)} %refs_12_.1) | copy-start | bytes 663556
  8.6 3.8 %copy-start.13 = (bf16[192,192]{1,0:T(8,128)(2,1)S(1)}, bf16[192,192]{1,0:T(8,128)(2,1)}, u32[]{:S(2)}) copy-start(bf16[192,192]{1,0:T(8,128)(2,1)} %refs_7_.5) | copy-start | bytes 221188
  8.7 3.8 %copy-start.18 = (s32[576,1]{1,0:T(8,128)S(1)}, s32[576,1]{1,0:T(8,128)}, u32[]{:S(2)}) copy-start(s32[576,1]{1,0:T(8,128)} %constant.41.refs_4_) | copy-start | bytes 6916
  12.4 8.5 %copy-start.11 = (f32[1,12,3312]{2,0,1:T(1,128)S(1)}, f32[1,12,3312]{2,0,1:T(1,128)}, u32[]{:S(2)}) copy-start(f32[1,12,3312]{2,0,1:T(1,128)} %param.32) | copy-start | bytes 476932
  18.4 7.7 %collective-permute-start.5 = (bf16[80,128]{1,0:T(8,128)(2,1)S(1)}, bf16[80,128]{1,0:T(8,128)(2,1)S(1)}, u32[]{:S(2)}, u32[]{:S(2)}) collective-permute-start(bf16[80,128]{1,0:T(8,128)(2,1)S(1)} %get-tuple-element.76), channel_id=1, source_target_pairs={{0,5},{1,6},{2,7},{3,4},{4,9},{5,10},{6,11},{7,8},{8,13},{9,14},{1... | collective-permute-start | bytes 61448 | tf_op jit(solution)/shard_map/ppermute | solution.py:626
  18.4 7.7 %collective-permute-start.3 = (bf16[176,128]{1,0:T(8,128)(2,1)S(1)}, bf16[176,128]{1,0:T(8,128)(2,1)S(1)}, u32[]{:S(2)}, u32[]{:S(2)}) collective-permute-start(bf16[176,128]{1,0:T(8,128)(2,1)S(1)} %get-tuple-element.74), channel_id=1, source_target_pairs={{0,4},{4,8},{8,12},{12,16},{16,20},{20,24},{24,28},{28,0},{1,5},{5... | collective-permute-start | bytes 135176 | tf_op jit(solution)/shard_map/ppermute | solution.py:617
  19.9 6.2 %collective-permute-start.4 = (bf16[176,128]{1,0:T(8,128)(2,1)S(1)}, bf16[176,128]{1,0:T(8,128)(2,1)S(1)}, u32[]{:S(2)}, u32[]{:S(2)}) collective-permute-start(bf16[176,128]{1,0:T(8,128)(2,1)S(1)} %get-tuple-element.75), channel_id=1, source_target_pairs={{0,1},{1,2},{2,3},{3,0},{4,5},{5,6},{6,7},{7,4},{8,9},{9,10},{10,1... | collective-permute-start | bytes 135176 | tf_op jit(solution)/shard_map/ppermute | solution.py:620
  23.3 2.9 %copy-start = (bf16[384,1536]{1,0:T(8,128)(2,1)S(1)}, bf16[384,1536]{1,0:T(8,128)(2,1)}, u32[]{:S(2)}) copy-start(bf16[384,1536]{1,0:T(8,128)(2,1)} %up_ref.1) | copy-start | bytes 3538948
  23.3 2.9 %copy-start.1 = (bf16[1536,384]{1,0:T(8,128)(2,1)S(1)}, bf16[1536,384]{1,0:T(8,128)(2,1)}, u32[]{:S(2)}) copy-start(bf16[1536,384]{1,0:T(8,128)(2,1)} %down_ref.1) | copy-start | bytes 3538948
  23.3 2.9 %copy-start.2 = (bf16[384,1152]{1,0:T(8,128)(2,1)S(1)}, bf16[384,1152]{1,0:T(8,128)(2,1)}, u32[]{:S(2)}) copy-start(bf16[384,1152]{1,0:T(8,128)(2,1)} %qkv_ref.1) | copy-start | bytes 2654212
  23.3 2.8 %copy-start.3 = (bf16[768,384]{1,0:T(8,128)(2,1)S(1)}, bf16[768,384]{1,0:T(8,128)(2,1)}, u32[]{:S(2)}) copy-start(bf16[768,384]{1,0:T(8,128)(2,1)} %reduce_ref.1) | copy-start | bytes 1769476
  23.3 2.8 %copy-start.6 = (bf16[384,384]{1,0:T(8,128)(2,1)S(1)}, bf16[384,384]{1,0:T(8,128)(2,1)}, u32[]{:S(2)}) copy-start(bf16[384,384]{1,0:T(8,128)(2,1)} %proj_ref.1) | copy-start | bytes 884740
  23.3 2.8 %copy-start.14 = (s32[608,1]{1,0:T(8,128)S(1)}, s32[608,1]{1,0:T(8,128)}, u32[]{:S(2)}) copy-start(s32[608,1]{1,0:T(8,128)} %constant.43.split_ref) | copy-start | bytes 7300
  23.3 2.8 %copy-start.17 = (s32[576,1]{1,0:T(8,128)S(1)}, s32[576,1]{1,0:T(8,128)}, u32[]{:S(2)}) copy-start(s32[576,1]{1,0:T(8,128)} %constant.42.merge_ref) | copy-start | bytes 6916
  34.8 5.5 %collective-permute-start.7 = (bf16[176,128]{1,0:T(8,128)(2,1)S(1)}, bf16[176,128]{1,0:T(8,128)(2,1)S(1)}, u32[]{:S(2)}, u32[]{:S(2)}) collective-permute-start(bf16[176,128]{1,0:T(8,128)(2,1)S(1)} %get-tuple-element.99), channel_id=1, source_target_pairs={{0,3},{1,0},{2,1},{3,2},{4,7},{5,4},{6,5},{7,6},{8,11},{9,8},{10,9... | collective-permute-start | bytes 135176 | tf_op jit(solution)/shard_map/ppermute | solution.py:620
  35.6 12.6 %collective-permute-start.8 = (bf16[80,128]{1,0:T(8,128)(2,1)S(1)}, bf16[80,128]{1,0:T(8,128)(2,1)S(1)}, u32[]{:S(2)}, u32[]{:S(2)}) collective-permute-start(bf16[80,128]{1,0:T(8,128)(2,1)S(1)} %get-tuple-element.102), channel_id=1, source_target_pairs={{0,31},{1,28},{2,29},{3,30},{4,3},{5,0},{6,1},{7,2},{8,7},{9,4},{1... | collective-permute-start | bytes 61448 | tf_op jit(solution)/shard_map/ppermute | solution.py:626
  38.7 4.0 %collective-permute-start.6 = (bf16[176,128]{1,0:T(8,128)(2,1)S(1)}, bf16[176,128]{1,0:T(8,128)(2,1)S(1)}, u32[]{:S(2)}, u32[]{:S(2)}) collective-permute-start(bf16[176,128]{1,0:T(8,128)(2,1)S(1)} %get-tuple-element.79), channel_id=1, source_target_pairs={{0,28},{4,0},{8,4},{12,8},{16,12},{20,16},{24,20},{28,24},{1,29},{... | collective-permute-start | bytes 135176 | tf_op jit(solution)/shard_map/ppermute | solution.py:617
  40.3 2.4 %copy-start.16 = (s32[576,1]{1,0:T(8,128)S(1)}, s32[576,1]{1,0:T(8,128)}, u32[]{:S(2)}) copy-start(s32[576,1]{1,0:T(8,128)} %constant.44.back_ref) | copy-start | bytes 6916
  41.7 6.4 %collective-permute-start.9 = (bf16[24,1656]{1,0:T(8,128)(2,1)S(1)}, bf16[24,1656]{1,0:T(8,128)(2,1)S(1)}, u32[]{:S(2)}, u32[]{:S(2)}) collective-permute-start(bf16[24,1656]{1,0:T(8,128)(2,1)S(1)} %shard_map.226), channel_id=1, source_target_pairs={{0,16},{4,20},{8,24},{12,28},{16,0},{20,4},{24,8},{28,12},{1,17},{... | collective-permute-start | bytes 238472 | tf_op jit(solution)/shard_map/ppermute | solution.py:636
  48.1 7.4 %collective-permute-start.10 = (bf16[24,1656]{1,0:T(8,128)(2,1)S(1)}, bf16[24,1656]{1,0:T(8,128)(2,1)S(1)}, u32[]{:S(2)}, u32[]{:S(2)}) collective-permute-start(bf16[24,1656]{1,0:T(8,128)(2,1)S(1)} %add_convert_fusion.3), channel_id=1, source_target_pairs={{0,8},{4,12},{8,0},{12,4},{16,24},{20,28},{24,16},{28,20},{1,9},{5... | collective-permute-start | bytes 238472 | tf_op jit(solution)/shard_map/ppermute | solution.py:636
  52.9 7.1 %collective-permute-start.13 = (bf16[24,1656]{1,0:T(8,128)(2,1)S(1)}, bf16[24,1656]{1,0:T(8,128)(2,1)S(1)}, u32[]{:S(2)}, u32[]{:S(2)}) collective-permute-start(bf16[24,1656]{1,0:T(8,128)(2,1)S(1)} %get-tuple-element.122), channel_id=1, source_target_pairs={{0,16},{4,20},{8,24},{12,28},{16,0},{20,4},{24,8},{28,12},{1,17},{... | collective-permute-start | bytes 238472 | tf_op jit(solution)/shard_map/ppermute | solution.py:636
  55.5 11.1 %copy-start.15 = (s32[576,1]{1,0:T(8,128)S(1)}, s32[576,1]{1,0:T(8,128)}, u32[]{:S(2)}) copy-start(s32[576,1]{1,0:T(8,128)} %constant.45.leave_ref) | copy-start | bytes 6916
  55.5 11.1 %copy-start.19 = (s32[144,1]{1,0:T(8,128)S(1)}, s32[144,1]{1,0:T(8,128)}, u32[]{:S(2)}) copy-start(s32[144,1]{1,0:T(8,128)} %constant.46.result_ref) | copy-start | bytes 1732
  56.4 3.6 %collective-permute-start.12 = (bf16[288,128]{1,0:T(8,128)(2,1)S(1)}, bf16[288,128]{1,0:T(8,128)(2,1)S(1)}, u32[]{:S(2)}, u32[]{:S(2)}) collective-permute-start(bf16[288,128]{1,0:T(8,128)(2,1)S(1)} %get-tuple-element.121), channel_id=1, source_target_pairs={{0,3},{1,0},{2,1},{3,2},{4,7},{5,4},{6,5},{7,6},{8,11},{9,8},{10,9... | collective-permute-start | bytes 221192 | tf_op jit(solution)/shard_map/ppermute | solution.py:620
  60.0 5.1 %collective-permute-start.15 = (bf16[24,1656]{1,0:T(8,128)(2,1)S(1)}, bf16[24,1656]{1,0:T(8,128)(2,1)S(1)}, u32[]{:S(2)}, u32[]{:S(2)}) collective-permute-start(bf16[24,1656]{1,0:T(8,128)(2,1)S(1)} %add_convert_fusion.2), channel_id=1, source_target_pairs={{0,8},{4,12},{8,0},{12,4},{16,24},{20,28},{24,16},{28,20},{1,9},{5... | collective-permute-start | bytes 238472 | tf_op jit(solution)/shard_map/ppermute | solution.py:636
  60.4 5.4 %collective-permute-start.14 = (bf16[192,128]{1,0:T(8,128)(2,1)S(1)}, bf16[192,128]{1,0:T(8,128)(2,1)S(1)}, u32[]{:S(2)}, u32[]{:S(2)}) collective-permute-start(bf16[192,128]{1,0:T(8,128)(2,1)S(1)} %get-tuple-element.124), channel_id=1, source_target_pairs={{0,31},{1,28},{2,29},{3,30},{4,3},{5,0},{6,1},{7,2},{8,7},{9,4},{1... | collective-permute-start | bytes 147464 | tf_op jit(solution)/shard_map/ppermute | solution.py:626
  62.0 4.6 %collective-permute-start.11 = (bf16[288,128]{1,0:T(8,128)(2,1)S(1)}, bf16[288,128]{1,0:T(8,128)(2,1)S(1)}, u32[]{:S(2)}, u32[]{:S(2)}) collective-permute-start(bf16[288,128]{1,0:T(8,128)(2,1)S(1)} %get-tuple-element.120), channel_id=1, source_target_pairs={{0,28},{4,0},{8,4},{12,8},{16,12},{20,16},{24,20},{28,24},{1,29},{... | collective-permute-start | bytes 221192 | tf_op jit(solution)/shard_map/ppermute | solution.py:617
  63.5 5.3 %collective-permute-start.17 = (bf16[24,1656]{1,0:T(8,128)(2,1)S(1)}, bf16[24,1656]{1,0:T(8,128)(2,1)S(1)}, u32[]{:S(2)}, u32[]{:S(2)}) collective-permute-start(bf16[24,1656]{1,0:T(8,128)(2,1)S(1)} %add_convert_fusion.coarse_kept), channel_id=1, source_target_pairs={{0,4},{4,0},{8,12},{12,8},{16,20},{20,16},{24,28},{28,24},{1,5},{5... | collective-permute-start | bytes 238472 | tf_op jit(solution)/shard_map/ppermute | solution.py:636
  65.2 5.4 %collective-permute-start.16 = (bf16[24,1656]{1,0:T(8,128)(2,1)S(1)}, bf16[24,1656]{1,0:T(8,128)(2,1)S(1)}, u32[]{:S(2)}, u32[]{:S(2)}) collective-permute-start(bf16[24,1656]{1,0:T(8,128)(2,1)S(1)} %add_convert_fusion.1.fine_kept), channel_id=1, source_target_pairs={{0,4},{4,0},{8,12},{12,8},{16,20},{20,16},{24,28},{28,24},{1,5},{5... | collective-permute-start | bytes 238472 | tf_op jit(solution)/shard_map/ppermute | solution.py:636

commit v6 on v5

--- a/solution.py
+++ b/solution.py
@@ -293,9 +293,8 @@
     return windows[qi // 2 * 2 + qj // 2][part : part + QUAD]
 
 
-def edge_kernel(tokens_ref, grad_ref, slon_ref, slat_ref, sdiag_ref, gloc_ref):
+def edge_kernel(tokens_ref, slon_ref, slat_ref, sdiag_ref):
     tokens = tokens_ref[...].astype(f32)
-    grads = grad_ref[...].astype(f32)
 
     def token_quadrant(row, start):
         pieces = []
@@ -305,18 +304,9 @@
                 pieces.append(tokens[place : place + 6])
         return jnp.concatenate(pieces, axis=0)
 
-    def grad_quadrant(hi, hj):
-        pieces = [
-            grads[hi * 3 + row, hj * 6 : hj * 6 + 6, z]
-            for z in range(2)
-            for row in range(3)
-        ]
-        return jnp.concatenate(pieces, axis=0)
-
-    slon_ref[...] = dense([token_quadrant(q * 3, 18) for q in range(3)], 112, grad_quadrant(0, 1))
-    slat_ref[...] = dense([token_quadrant(9, q * 6) for q in range(3)], 112, grad_quadrant(1, 0))
-    sdiag_ref[...] = dense([token_quadrant(9, 18)], 48, grad_quadrant(1, 1))
-    gloc_ref[...] = pack([grad_quadrant(0, 0)], 48)
+    slon_ref[...] = dense([token_quadrant(q * 3, 18) for q in range(3)], 112)
+    slat_ref[...] = dense([token_quadrant(9, q * 6) for q in range(3)], 112)
+    sdiag_ref[...] = dense([token_quadrant(9, 18)], 48)
 
 
 def expand(table_ref, out_ref, held):
@@ -409,12 +399,21 @@
     return windows
 
 
-def fine_edge_kernel(*refs):
-    slon_ref, slat_ref, sdiag_ref = refs[11:14]
-    windows = fine_windows((1, 2, 3), refs[:11] + refs[14:])
-    slon_ref[...] = dense([quadrant(windows, q, 3) for q in range(3)], 112)
-    slat_ref[...] = dense([quadrant(windows, 3, q) for q in range(3)], 112)
-    sdiag_ref[...] = dense([quadrant(windows, 3, 3)], 48)
+def fine_edge_kernel(grad_ref, *refs):
+    slon_ref, slat_ref, sdiag_ref, gloc_ref = refs[11:15]
+    windows = fine_windows((1, 2, 3), refs[:11] + refs[15:])
+    grads = grad_ref[...].astype(f32)
+
+    def grad_quadrant(hi, hj):
+        pieces = [
+            grads[hi * 3 + row, hj * 6 : hj * 6 + 6, z] for z in range(2) for row in range(3)
+        ]
+        return jnp.concatenate(pieces, axis=0)
+
+    slon_ref[...] = dense([quadrant(windows, q, 3) for q in range(3)], 112, grad_quadrant(0, 1))
+    slat_ref[...] = dense([quadrant(windows, 3, q) for q in range(3)], 112, grad_quadrant(1, 0))
+    sdiag_ref[...] = dense([quadrant(windows, 3, 3)], 48, grad_quadrant(1, 1))
+    gloc_ref[...] = pack([grad_quadrant(0, 0)], 48)
 
 
 def fine_inner_kernel(*refs):
@@ -423,7 +422,7 @@
 
 def coarse_kernel(
     inner_ref, res_ref, lon_ref, lat_ref, diag_ref, merge_ref, split_ref, bias_ref, mask_ref,
-    gloc_ref, glon_ref, glat_ref, gdiag_ref,
+    gloc_ref,
     reduce_ref, qkv_ref, proj_ref, up_ref, down_ref,
     c0, c1, c2, c3, dlon_ref, dlat_ref, ddiag_ref, dloc_ref, score_ref,
     source, probs_ref, parts_ref,
@@ -458,9 +457,9 @@
 
     grad = jnp.concatenate(
         [
-            coarse_of(gdiag_ref, 48),
-            coarse_of(glat_ref, 112),
-            coarse_of(glon_ref, 112),
+            coarse_of(diag_ref, 48),
+            coarse_of(lat_ref, 112),
+            coarse_of(lon_ref, 112),
             gloc_ref[...].astype(f32)[:QUAD],
         ],
         axis=0,
@@ -660,10 +659,7 @@
     table_rows = ((12, 192, WIN), bf16)
     held = ((12, 2, 12, 16, WIN), bf16)
 
-    *sent, grad_here = run(
-        edge_kernel, wide_edges + [quad], [], 1, (flat, out_grad.transpose(1, 2, 0, 3))
-    )
-    first = send(sent, 1)
+    first = send(run(edge_kernel, edges, [], 1, (flat,)), 1)
     (fine_table,) = run(
         bias_kernel, [scores], [held], 2,
         (fine_bias.transpose(1, 0, 2),),
@@ -693,17 +689,17 @@
     gathered = [((848, 192), bf16)]
     outer = run(
         fine_edge_kernel,
-        edges + [((3 * WIN, 192), bf16)] + saved_shapes(3),
-        gathered, 6, inputs,
+        wide_edges + [quad, ((3 * WIN, 192), bf16)] + saved_shapes(3),
+        gathered, 6, (out_grad.transpose(1, 2, 0, 3), *inputs),
     )
     arrived = send(outer[:3], 1)
-    flat_after, _ = lax.optimization_barrier((flat, outer[3]))
+    flat_after, _ = lax.optimization_barrier((flat, outer[4]))
     inner = run(
         fine_inner_kernel,
         [((WIN, 192), bf16)] + saved_shapes(1),
         gathered, 2, (flat_after, *inputs[1:]),
     )
-    late_table, _ = lax.optimization_barrier((coarse_bias.transpose(1, 0, 2), outer[3]))
+    late_table, _ = lax.optimization_barrier((coarse_bias.transpose(1, 0, 2), outer[4]))
     (coarse_table,) = run(
         bias_kernel, [scores], [held], 2, (late_table,)
     )
@@ -713,7 +709,7 @@
         [((848, 192), bf16), ((12 * WIN, WIN), bf16), ((576, 192), bf16)],
         9,
         (
-            inner[0], outer[3], *arrived, column(MERGE), column(SPLIT), coarse_table, coarse_mask, grad_here, *first,
+            inner[0], outer[4], *arrived, column(MERGE), column(SPLIT), coarse_table, coarse_mask, outer[3],
             reduce_weight, coarse_qkv, coarse_proj, coarse_up, coarse_down,
         ),
     )
@@ -726,10 +722,10 @@
         (scored,),
     )
     steps = lon_steps()
-    other = swap(coarse_grad, steps[-1])
+    other = swap(coarse_grad, steps[0])
     half_tok = ((288, 192), bf16)
     half_outs = [((288, 192), f32)] + [half_tok] * 3
-    q, k, v, probs, n1, r1, n2, r2, slope = outer[4:]
+    q, k, v, probs, n1, r1, n2, r2, slope = outer[5:]
     outer_saved = (q, k, v, probs, n2, r2, slope)
     q, k, v, probs, n1_inner, r1_inner, n2, r2, slope = inner[1:]
     inner_saved = (q, k, v, probs, n2, r2, slope)
@@ -743,7 +739,7 @@
     )
     first_scores, other = lax.optimization_barrier((first_scores, other))
     coarse_grad = add(coarse_grad, other)
-    other = swap(coarse_grad, steps[-2])
+    other = swap(coarse_grad, steps[-1])
     *second_half, fine_grad = run(
         second_band_kernel,
         half_outs + [((24, 6 * ENTRIES), bf16)],
@@ -756,7 +752,7 @@
     )
     second_half[0], other = lax.optimization_barrier((second_half[0], other))
     coarse_grad = add(coarse_grad, other)
-    for step in reversed(steps[:-2]):
+    for step in steps[1:-1]:
         coarse_sums = (coarse_grad, swap(coarse_grad, step))
         coarse_grad = add(*coarse_sums)
     other = swap(fine_grad, steps[-1])
@@ -765,7 +761,7 @@
         (*first_half, *second_half, n1_inner, r1_inner, n1, r1, fine_qkv, c10, c01, c00),
     ))
     alon, alat, adiag = send(fine_back[1:4], -1)
-    alat, other = lax.optimization_barrier((alat, other))
+    alat, adiag, other = lax.optimization_barrier((alat, adiag, other))
     fine_grad = add(fine_grad, other)
     for step in reversed(steps[:-1]):
         fine_sums = (fine_grad, swap(fine_grad, step))

time: 71.6 us -> 71.4 us (level)
  starting transfers between devices: 21.4 us -> 24.7 us
  waiting for transfers between devices: 11 us -> 8.39 us
  local copies, waits for them, and re-layouts: 2.93 us -> 2.04 us
    ppermute x6, waiting for transfers between devices: 7.77 us -> 2.86 us  [swap(): return lax.ppermute(value, 'lon', [(s, s ^ step) for s in range(count)])]
    ppermute x4, starting transfers between devices: 7.25 us -> 10 us  [move(): return lax.ppermute(value, ('lon', 'lat'), pairs)]
    ppermute x4, starting transfers between devices: 6.18 us -> 8.42 us  [move(): return lax.ppermute(value, 'lon', pairs)]
    ppermute x4, waiting for transfers between devices: 0.38 us -> 2.27 us  [move(): return lax.ppermute(value, ('lon', 'lat'), pairs)]
    ppermute x4, starting transfers between devices: 3.63 us -> 2.57 us  [move(): return lax.ppermute(value, 'lat', pairs)]
    unnamed x43, local copies, waits for them, and re-layouts: 2.69 us -> 1.8 us
where the time goes in v6:
time: 71.4 us; the launch traced here: 71.2 us
  Pallas kernels  34.6 us (48%)
  starting transfers between devices  24.7 us (35%)
  waiting for transfers between devices  8.39 us (12%)
  local copies, waits for them, and re-layouts  2.04 us (3%)
  between operations  1.02 us (1%)
    pallas_call x12, Pallas kernels, run(): pl.pallas_call(kernel, out_shape=shapes, scratch_shapes=[pltpu.VMEM(shape...  34.6 us
    ppermute x4, starting transfers between devices, move(): return lax.ppermute(value, ('lon', 'lat'), pairs)  10 us
    ppermute x4, starting transfers between devices, move(): return lax.ppermute(value, 'lon', pairs)  8.42 us
    ppermute x6, starting transfers between devices, swap(): return lax.ppermute(value, 'lon', [(s, s ^ step) for s in range(count)])  3.75 us
    ppermute x4, waiting for transfers between devices, move(): return lax.ppermute(value, 'lon', pairs)  3.25 us
    ppermute x6, waiting for transfers between devices, swap(): return lax.ppermute(value, 'lon', [(s, s ^ step) for s in range(count)])  2.86 us
    ppermute x4, starting transfers between devices, move(): return lax.ppermute(value, 'lat', pairs)  2.57 us
    ppermute x4, waiting for transfers between devices, move(): return lax.ppermute(value, ('lon', 'lat'), pairs)  2.27 us
  transfers between devices with their start and end apart: 18, of which 9 were waited for; matrix products, arithmetic and copies ran while one was open for 2% of the time, Pallas kernels for 27%

profile of v6, /device:TPU:0, one launch (start us, length us, event | category | flops | bytes accessed | tf_op | source)
XLA Modules:
  0.0 71.2 jit_solution(7277389126147547477)
XLA Ops:
  0.6 1.0 %copy-done.4 = bf16[2,12,24,192]{3,2,1,0:T(8,128)(2,1)S(1)} copy-done((bf16[2,12,24,192]{3,2,1,0:T(8,128)(2,1)S(1)}, bf16[2,12,24,192]{3,2,1,0:T(8,128)(2,1)}, u32[]{:S(2)}) %copy-start.4) | copy-done | bytes 221208
  1.6 0.1 shard_map.219
  1.7 2.5 %collective-permute-start.2 = (bf16[80,128]{1,0:T(8,128)(2,1)S(1)}, bf16[80,128]{1,0:T(8,128)(2,1)S(1)}, u32[]{:S(2)}, u32[]{:S(2)}) collective-permute-start(bf16[80,128]{1,0:T(8,128)(2,1)S(1)} %get-tuple-element.71), channel_id=1, source_target_pairs={{0,5},{1,6},{2,7},{3,4},{4,9},{5,10},{6,11},{7,8},{8,13},{9,14},{1... | collective-permute-start | bytes 61448 | tf_op jit(solution)/shard_map/ppermute | solution.py:625
  4.2 1.5 %collective-permute-start = (bf16[176,128]{1,0:T(8,128)(2,1)S(1)}, bf16[176,128]{1,0:T(8,128)(2,1)S(1)}, u32[]{:S(2)}, u32[]{:S(2)}) collective-permute-start(bf16[176,128]{1,0:T(8,128)(2,1)S(1)} %get-tuple-element.69), channel_id=1, source_target_pairs={{0,4},{4,8},{8,12},{12,16},{16,20},{20,24},{24,28},{28,0},{1,5},{5... | collective-permute-start | bytes 135176 | tf_op jit(solution)/shard_map/ppermute | solution.py:616
  5.7 1.3 %collective-permute-start.1 = (bf16[176,128]{1,0:T(8,128)(2,1)S(1)}, bf16[176,128]{1,0:T(8,128)(2,1)S(1)}, u32[]{:S(2)}, u32[]{:S(2)}) collective-permute-start(bf16[176,128]{1,0:T(8,128)(2,1)S(1)} %get-tuple-element.70), channel_id=1, source_target_pairs={{0,1},{1,2},{2,3},{3,0},{4,5},{5,6},{6,7},{7,4},{8,9},{9,10},{10,1... | collective-permute-start | bytes 135176 | tf_op jit(solution)/shard_map/ppermute | solution.py:619
  7.0 0.1 multiply_add_fusion
  7.1 0.1 reshape.48
  7.2 0.1 eq.28
  7.4 0.1 compare_select_fusion.refs_6_
  7.5 0.1 or_select_fusion.mask_ref
  7.7 0.0 copy-start.18
  7.7 2.3 %shard_map.220.refs_5_ = f32[1728,144]{1,0:T(8,128)S(1)} custom-call(f32[6,2,3312]{2,1,0:T(2,128)S(1)} %bitcast.20), custom_call_target="tpu_custom_call" | custom-call | flops 2000000000 | bytes 1154304 | tf_op jit(solution)/shard_map/pallas_call | solution.py:601
  10.0 0.9 %collective-permute-done.refs_1_ = bf16[176,128]{1,0:T(8,128)(2,1)S(1)} collective-permute-done((bf16[176,128]{1,0:T(8,128)(2,1)S(1)}, bf16[176,128]{1,0:T(8,128)(2,1)S(1)}, u32[]{:S(2)}, u32[]{:S(2)}) %collective-permute-start) | collective-permute-done | bytes 45088 | tf_op jit(solution)/shard_map/ppermute | solution.py:616
  11.0 6.0 %shard_map.221 = (bf16[288,128]{1,0:T(8,128)(2,1)S(1)}, bf16[288,128]{1,0:T(8,128)(2,1)S(1)}, bf16[192,128]{1,0:T(8,128)(2,1)S(1)}, bf16[48,384]{1,0:T(8,128)(2,...) custom-call(bf16[6,12,2,384]{3,2,1,0:T(2,128)(2,1)S(1)} %bitcast.22,, ...), custom_call_target="tpu_custom_call" | custom-call | flops 6000000000 | bytes 5298816 | tf_op jit(solution)/shard_map/pallas_call | solution.py:601
  17.0 0.6 collective-permute-start.5
  17.5 1.5 %collective-permute-start.3 = (bf16[288,128]{1,0:T(8,128)(2,1)S(1)}, bf16[288,128]{1,0:T(8,128)(2,1)S(1)}, u32[]{:S(2)}, u32[]{:S(2)}) collective-permute-start(bf16[288,128]{1,0:T(8,128)(2,1)S(1)} %get-tuple-element.75), channel_id=1, source_target_pairs={{0,4},{4,8},{8,12},{12,16},{16,20},{20,24},{24,28},{28,0},{1,5},{5... | collective-permute-start | bytes 221192 | tf_op jit(solution)/shard_map/ppermute | solution.py:616
  19.1 0.1 collective-permute-start.4
  19.2 2.3 %shard_map.223.bias_ref = f32[1728,144]{1,0:T(8,128)S(1)} custom-call(f32[12,1,3312]{2,1,0:T(1,128)S(1)} %bitcast.21), custom_call_target="tpu_custom_call" | custom-call | flops 2000000000 | bytes 1154304 | tf_op jit(solution)/shard_map/pallas_call | solution.py:601
  21.5 0.0 copy-start.14
  21.5 0.0 copy-start.17
  21.5 2.7 %shard_map.222 = (bf16[144,192]{1,0:T(8,128)(2,1)S(1)}, bf16[144,192]{1,0:T(8,128)(2,1)S(1)}, bf16[144,192]{1,0:T(8,128)(2,1)S(1)}, bf16[144,192]{1,0:T(8,128)(2...) custom-call(bf16[576,192]{1,0:T(8,128)(2,1)S(1)} %bitcast.15, ...), custom_call_target="tpu_custom_call" | custom-call | flops 2000000000 | bytes 3348864 | tf_op jit(solution)/shard_map/pallas_call | solution.py:601
  24.3 0.3 collective-permute-done.5.diag_ref
  24.6 0.9 %collective-permute-done.3.lon_ref = bf16[288,128]{1,0:T(8,128)(2,1)S(1)} collective-permute-done((bf16[288,128]{1,0:T(8,128)(2,1)S(1)}, bf16[288,128]{1,0:T(8,128)(2,1)S(1)}, u32[]{:S(2)}, u32[]{:S(2)}) %collective-permute-start.3) | collective-permute-done | bytes 73760 | tf_op jit(solution)/shard_map/ppermute | solution.py:616
  25.6 8.6 %shard_map.224 = (bf16[48,384]{1,0:T(8,128)(2,1)S(1)}, bf16[48,384]{1,0:T(8,128)(2,1)S(1)}, bf16[48,384]{1,0:T(8,128)(2,1)S(1)}, bf16[48,384]{1,0:T(8,128)(2,1)S...) custom-call(bf16[144,192]{1,0:T(8,128)(2,1)S(1)} %get-tuple-element., ...), custom_call_target="tpu_custom_call" | custom-call | flops 8999999488 | bytes 7048832 | tf_op jit(solution)/shard_map/pallas_call | solution.py:601
  34.2 1.1 %collective-permute-start.7 = (bf16[176,128]{1,0:T(8,128)(2,1)S(1)}, bf16[176,128]{1,0:T(8,128)(2,1)S(1)}, u32[]{:S(2)}, u32[]{:S(2)}) collective-permute-start(bf16[176,128]{1,0:T(8,128)(2,1)S(1)} %get-tuple-element.100), channel_id=1, source_target_pairs={{0,3},{1,0},{2,1},{3,2},{4,7},{5,4},{6,5},{7,6},{8,11},{9,8},{10,9... | collective-permute-start | bytes 135176 | tf_op jit(solution)/shard_map/ppermute | solution.py:619
  35.3 2.1 %collective-permute-start.8 = (bf16[80,128]{1,0:T(8,128)(2,1)S(1)}, bf16[80,128]{1,0:T(8,128)(2,1)S(1)}, u32[]{:S(2)}, u32[]{:S(2)}) collective-permute-start(bf16[80,128]{1,0:T(8,128)(2,1)S(1)} %get-tuple-element.103), channel_id=1, source_target_pairs={{0,31},{1,28},{2,29},{3,30},{4,3},{5,0},{6,1},{7,2},{8,7},{9,4},{1... | collective-permute-start | bytes 61448 | tf_op jit(solution)/shard_map/ppermute | solution.py:625
  37.4 1.5 %collective-permute-start.6 = (bf16[176,128]{1,0:T(8,128)(2,1)S(1)}, bf16[176,128]{1,0:T(8,128)(2,1)S(1)}, u32[]{:S(2)}, u32[]{:S(2)}) collective-permute-start(bf16[176,128]{1,0:T(8,128)(2,1)S(1)} %get-tuple-element.80), channel_id=1, source_target_pairs={{0,28},{4,0},{8,4},{12,8},{16,12},{20,16},{24,20},{28,24},{1,29},{... | collective-permute-start | bytes 135176 | tf_op jit(solution)/shard_map/ppermute | solution.py:616
  38.9 1.4 %shard_map.226 = bf16[24,1656]{1,0:T(8,128)(2,1)S(1)} custom-call(f32[1728,144]{1,0:T(8,128)S(1)} %get-tuple-element.105.score_ref), custom_call_target="tpu_custom_call" | custom-call | flops 2000000000 | bytes 1074816 | tf_op jit(solution)/shard_map/pallas_call | solution.py:601
  40.3 0.5 collective-permute-start.9
  40.9 0.7 collective-permute-done.6.dlon_ref
  41.6 3.6 %shard_map.225 = (f32[288,192]{1,0:T(8,128)S(1)}, bf16[288,192]{1,0:T(8,128)(2,1)S(1)}, bf16[288,192]{1,0:T(8,128)(2,1)S(1)}, bf16[288,192]{1,0:T(8,128)(2,1)S(1)}, f32[864,144]{1,0:T(8,128)S(1)}) custom-call(bf16[176,128]{1,0:T(8,128)(2,1)S(1)} %collective-permute-done.6.dlon_ref, bf16[336,192]{1,0:T(8,128)(2,1)S(1)} %get-tuple-element.81.dloc_ref, ...), custom_call_target="tpu_custom_call" | custom-call | flops 4000000000 | bytes 4657664 | tf_op jit(solution)/shard_map/pallas_call | solution.py:601
  45.2 0.9 %collective-permute-start.10 = (bf16[24,1656]{1,0:T(8,128)(2,1)S(1)}, bf16[24,1656]{1,0:T(8,128)(2,1)S(1)}, u32[]{:S(2)}, u32[]{:S(2)}) collective-permute-start(bf16[24,1656]{1,0:T(8,128)(2,1)S(1)} %add_convert_fusion.3), channel_id=1, source_target_pairs={{0,16},{4,20},{8,24},{12,28},{16,0},{20,4},{24,8},{28,12},{1,17},{... | collective-permute-start | bytes 238472 | tf_op jit(solution)/shard_map/ppermute | solution.py:635
  46.1 4.7 %shard_map.227 = (f32[288,192]{1,0:T(8,128)S(1)}, bf16[288,192]{1,0:T(8,128)(2,1)S(1)}, bf16[288,192]{1,0:T(8,128)(2,1)S(1)}, bf16[288,192]{1,0:T(8,128)(2,1)S(1)}, bf16[24,1656]{1,0:T(8,128)(2,1)S(1)}) custom-call(bf16[176,128]{1,0:T(8,128)(2,1)S(1)} %collective-permute-done.6.dlon_ref, bf16[336,192]{1,0:T(8,128)(2,1)S(1)} %get-tuple-element.81.dloc_ref, ...), custom_call_target="tpu_custom_call" | custom-call | flops 5000000000 | bytes 4110912 | tf_op jit(solution)/shard_map/pallas_call | solution.py:601
  50.7 2.2 %collective-permute-start.14 = (bf16[24,1656]{1,0:T(8,128)(2,1)S(1)}, bf16[24,1656]{1,0:T(8,128)(2,1)S(1)}, u32[]{:S(2)}, u32[]{:S(2)}) collective-permute-start(bf16[24,1656]{1,0:T(8,128)(2,1)S(1)} %get-tuple-element.124), channel_id=1, source_target_pairs={{0,16},{4,20},{8,24},{12,28},{16,0},{20,4},{24,8},{28,12},{1,17},{... | collective-permute-start | bytes 238472 | tf_op jit(solution)/shard_map/ppermute | solution.py:635
  52.9 0.8 %shard_map.228 = (bf16[576,192]{1,0:T(8,128)(2,1)S(1)}, bf16[288,128]{1,0:T(8,128)(2,1)S(1)}, bf16[288,128]{1,0:T(8,128)(2,1)S(1)}, bf16[192,128]{1,0:T(8,128)(2,1)S(1)}) custom-call(f32[288,192]{1,0:T(8,128)S(1)} %get-tuple-element.96.refs_0_, bf16[288,192]{1,0:T(8,128)(2,1)S(1)} %get-tuple-element.97.refs_1_, ...), custom_call_target="tpu_custom_call" | custom-call | flops 2000000000 | bytes 2078976 | tf_op jit(solution)/shard_map/pallas_call | solution.py:601
  53.8 0.1 collective-permute-start.12
  53.9 4.8 %collective-permute-start.13 = (bf16[192,128]{1,0:T(8,128)(2,1)S(1)}, bf16[192,128]{1,0:T(8,128)(2,1)S(1)}, u32[]{:S(2)}, u32[]{:S(2)}) collective-permute-start(bf16[192,128]{1,0:T(8,128)(2,1)S(1)} %get-tuple-element.123), channel_id=1, source_target_pairs={{0,31},{1,28},{2,29},{3,30},{4,3},{5,0},{6,1},{7,2},{8,7},{9,4},{1... | collective-permute-start | bytes 147464 | tf_op jit(solution)/shard_map/ppermute | solution.py:625
  58.7 1.9 %collective-permute-done.13.diag_ref = bf16[192,128]{1,0:T(8,128)(2,1)S(1)} collective-permute-done((bf16[192,128]{1,0:T(8,128)(2,1)S(1)}, bf16[192,128]{1,0:T(8,128)(2,1)S(1)}, u32[]{:S(2)}, u32[]{:S(2)}) %collective-permute-start.13) | collective-permute-done | bytes 49184 | tf_op jit(solution)/shard_map/ppermute | solution.py:625
  60.7 0.1 collective-permute-start.15
  60.8 3.8 %collective-permute-start.11 = (bf16[288,128]{1,0:T(8,128)(2,1)S(1)}, bf16[288,128]{1,0:T(8,128)(2,1)S(1)}, u32[]{:S(2)}, u32[]{:S(2)}) collective-permute-start(bf16[288,128]{1,0:T(8,128)(2,1)S(1)} %get-tuple-element.121), channel_id=1, source_target_pairs={{0,28},{4,0},{8,4},{12,8},{16,12},{20,16},{24,20},{28,24},{1,29},{... | collective-permute-start | bytes 221192 | tf_op jit(solution)/shard_map/ppermute | solution.py:616
  64.6 1.2 %collective-permute-done.15 = bf16[24,1656]{1,0:T(8,128)(2,1)S(1)} collective-permute-done((bf16[24,1656]{1,0:T(8,128)(2,1)S(1)}, bf16[24,1656]{1,0:T(8,128)(2,1)S(1)}, u32[]{:S(2)}, u32[]{:S(2)}) %collective-permute-start.15) | collective-permute-done | bytes 79520 | tf_op jit(solution)/shard_map/ppermute | solution.py:635
  65.8 0.1 collective-permute-start.16
  65.9 0.7 %collective-permute-done.11.lon_ref = bf16[288,128]{1,0:T(8,128)(2,1)S(1)} collective-permute-done((bf16[288,128]{1,0:T(8,128)(2,1)S(1)}, bf16[288,128]{1,0:T(8,128)(2,1)S(1)}, u32[]{:S(2)}, u32[]{:S(2)}) %collective-permute-start.11) | collective-permute-done | bytes 73760 | tf_op jit(solution)/shard_map/ppermute | solution.py:616
  66.7 1.3 %shard_map.229 = (bf16[576,192]{1,0:T(8,128)(2,1)}, bf16[2,6,12,384]{3,2,1,0:T(8,128)(2,1)S(1)}) custom-call(bf16[576,192]{1,0:T(8,128)(2,1)S(1)} %get-tuple-element.120.res_ref, bf16[288,128]{1,0:T(8,128)(2,1)S(1)} %collective-permute-done.11.lon_ref, bf16[288,128]{1,0:T(8,128)(2,1)S(1)} %collective-permute-done.12.lat_ref, ...), custom_call_target="tpu_custom_call" | custom-call | flops 1000000000 | bytes 789312 | tf_op jit(solution)/shard_map/pallas_call | solution.py:601
  68.0 0.7 %copy.27 = bf16[2,6,12,384]{3,0,2,1:T(2,128)(2,1)} copy(bf16[2,6,12,384]{3,2,1,0:T(8,128)(2,1)S(1)} %get-tuple-element.138) | data formatting | bytes 221184
  68.7 0.8 %collective-permute-done.17.coarse_other = bf16[24,1656]{1,0:T(8,128)(2,1)S(1)} collective-permute-done((bf16[24,1656]{1,0:T(8,128)(2,1)S(1)}, bf16[24,1656]{1,0:T(8,128)(2,1)S(1)}, u32[]{:S(2)}, u32[]{:S(2)}) %collective-permute-start.17) | collective-permute-done | bytes 79520 | tf_op jit(solution)/shard_map/ppermute | solution.py:635
  69.6 0.8 %collective-permute-done.16.fine_other = bf16[24,1656]{1,0:T(8,128)(2,1)S(1)} collective-permute-done((bf16[24,1656]{1,0:T(8,128)(2,1)S(1)}, bf16[24,1656]{1,0:T(8,128)(2,1)S(1)}, u32[]{:S(2)}, u32[]{:S(2)}) %collective-permute-start.16) | collective-permute-done | bytes 79520 | tf_op jit(solution)/shard_map/ppermute | solution.py:635
  70.4 0.8 %shard_map.230 = (f32[6,2,3312]{2,1,0:T(2,128)}, f32[12,1,3312]{2,1,0:T(1,128)}) custom-call(bf16[24,1656]{1,0:T(8,128)(2,1)S(1)} %add_convert_fusion.1.fine_kept, bf16[24,1656]{1,0:T(8,128)(2,1)S(1)} %collective-permute-done.16.fine_other, bf16[24,1656]{1,0:T(8,128)(2,1)S(1)} %add_convert_fusion.coarse_kept, ...), custom_call_target="tpu_custom_call" | custom-call | flops 1000000000 | bytes 635904 | tf_op jit(solution)/shard_map/pallas_call | solution.py:601
  (55 shorter events, 0.3 us)
Async XLA Ops:
  0.6 1.0 %copy-start.4 = (bf16[2,12,24,192]{3,2,1,0:T(8,128)(2,1)S(1)}, bf16[2,12,24,192]{3,2,1,0:T(8,128)(2,1)}, u32[]{:S(2)}) copy-start(bf16[2,12,24,192]{3,2,1,0:T(8,128)(2,1)} %param.20) | copy-start | bytes 663556
  1.6 5.4 %copy-start.20 = (s32[2,12,24]{2,0,1:T(2,128)S(1)}, s32[2,12,24]{2,0,1:T(2,128)}, u32[]{:S(2)}) copy-start(s32[2,12,24]{2,0,1:T(2,128)} %param.21) | copy-start | bytes 6916
  1.6 6.0 %copy-start.10 = (f32[2,6,3312]{2,0,1:T(2,128)S(1)}, f32[2,6,3312]{2,0,1:T(2,128)}, u32[]{:S(2)}) copy-start(f32[2,6,3312]{2,0,1:T(2,128)} %param.26) | copy-start | bytes 476932
  1.7 8.3 %collective-permute-start.2 = (bf16[80,128]{1,0:T(8,128)(2,1)S(1)}, bf16[80,128]{1,0:T(8,128)(2,1)S(1)}, u32[]{:S(2)}, u32[]{:S(2)}) collective-permute-start(bf16[80,128]{1,0:T(8,128)(2,1)S(1)} %get-tuple-element.71), channel_id=1, source_target_pairs={{0,5},{1,6},{2,7},{3,4},{4,9},{5,10},{6,11},{7,8},{8,13},{9,14},{1... | collective-permute-start | bytes 61448 | tf_op jit(solution)/shard_map/ppermute | solution.py:625
  4.2 6.7 %collective-permute-start = (bf16[176,128]{1,0:T(8,128)(2,1)S(1)}, bf16[176,128]{1,0:T(8,128)(2,1)S(1)}, u32[]{:S(2)}, u32[]{:S(2)}) collective-permute-start(bf16[176,128]{1,0:T(8,128)(2,1)S(1)} %get-tuple-element.69), channel_id=1, source_target_pairs={{0,4},{4,8},{8,12},{12,16},{16,20},{20,24},{24,28},{28,0},{1,5},{5... | collective-permute-start | bytes 135176 | tf_op jit(solution)/shard_map/ppermute | solution.py:616
  5.7 5.2 %collective-permute-start.1 = (bf16[176,128]{1,0:T(8,128)(2,1)S(1)}, bf16[176,128]{1,0:T(8,128)(2,1)S(1)}, u32[]{:S(2)}, u32[]{:S(2)}) collective-permute-start(bf16[176,128]{1,0:T(8,128)(2,1)S(1)} %get-tuple-element.70), channel_id=1, source_target_pairs={{0,1},{1,2},{2,3},{3,0},{4,5},{5,6},{6,7},{7,4},{8,9},{9,10},{10,1... | collective-permute-start | bytes 135176 | tf_op jit(solution)/shard_map/ppermute | solution.py:619
  7.6 3.3 %copy-start.5 = (bf16[2,12,24,192]{3,2,1,0:T(8,128)(2,1)S(1)}, bf16[2,12,24,192]{3,2,1,0:T(8,128)(2,1)}, u32[]{:S(2)}) copy-start(bf16[2,12,24,192]{3,2,1,0:T(8,128)(2,1)} %param.20) | copy-start | bytes 663556
  7.6 3.3 %copy-start.7 = (bf16[192,768]{1,0:T(8,128)(2,1)S(1)}, bf16[192,768]{1,0:T(8,128)(2,1)}, u32[]{:S(2)}) copy-start(bf16[192,768]{1,0:T(8,128)(2,1)} %refs_8_.5) | copy-start | bytes 884740
  7.7 3.3 %copy-start.8 = (bf16[768,192]{0,1:T(8,128)(2,1)S(1)}, bf16[768,192]{0,1:T(8,128)(2,1)}, u32[]{:S(2)}) copy-start(bf16[768,192]{0,1:T(8,128)(2,1)} %param.25) | copy-start | bytes 884740
  7.7 3.3 %copy-start.9 = (bf16[192,576]{1,0:T(8,128)(2,1)S(1)}, bf16[192,576]{1,0:T(8,128)(2,1)}, u32[]{:S(2)}) copy-start(bf16[192,576]{1,0:T(8,128)(2,1)} %refs_12_.1) | copy-start | bytes 663556
  7.7 3.3 %copy-start.12 = (bf16[2,6,12,384]{3,0,2,1:T(2,128)(2,1)S(1)}, bf16[2,6,12,384]{3,0,2,1:T(2,128)(2,1)}, u32[]{:S(2)}) copy-start(bf16[2,6,12,384]{3,0,2,1:T(2,128)(2,1)} %param.33) | copy-start | bytes 331780
  7.7 3.3 %copy-start.13 = (bf16[192,192]{1,0:T(8,128)(2,1)S(1)}, bf16[192,192]{1,0:T(8,128)(2,1)}, u32[]{:S(2)}) copy-start(bf16[192,192]{1,0:T(8,128)(2,1)} %refs_7_.5) | copy-start | bytes 221188
  7.7 3.3 %copy-start.18 = (s32[576,1]{1,0:T(8,128)S(1)}, s32[576,1]{1,0:T(8,128)}, u32[]{:S(2)}) copy-start(s32[576,1]{1,0:T(8,128)} %constant.41.refs_4_) | copy-start | bytes 6916
  11.0 8.2 %copy-start.11 = (f32[1,12,3312]{2,0,1:T(1,128)S(1)}, f32[1,12,3312]{2,0,1:T(1,128)}, u32[]{:S(2)}) copy-start(f32[1,12,3312]{2,0,1:T(1,128)} %param.32) | copy-start | bytes 476932
  17.0 7.7 %collective-permute-start.5 = (bf16[192,128]{1,0:T(8,128)(2,1)S(1)}, bf16[192,128]{1,0:T(8,128)(2,1)S(1)}, u32[]{:S(2)}, u32[]{:S(2)}) collective-permute-start(bf16[192,128]{1,0:T(8,128)(2,1)S(1)} %get-tuple-element.77), channel_id=1, source_target_pairs={{0,5},{1,6},{2,7},{3,4},{4,9},{5,10},{6,11},{7,8},{8,13},{9,14},{1... | collective-permute-start | bytes 147464 | tf_op jit(solution)/shard_map/ppermute | solution.py:625
  17.5 8.0 %collective-permute-start.3 = (bf16[288,128]{1,0:T(8,128)(2,1)S(1)}, bf16[288,128]{1,0:T(8,128)(2,1)S(1)}, u32[]{:S(2)}, u32[]{:S(2)}) collective-permute-start(bf16[288,128]{1,0:T(8,128)(2,1)S(1)} %get-tuple-element.75), channel_id=1, source_target_pairs={{0,4},{4,8},{8,12},{12,16},{16,20},{20,24},{24,28},{28,0},{1,5},{5... | collective-permute-start | bytes 221192 | tf_op jit(solution)/shard_map/ppermute | solution.py:616
  19.1 6.5 %collective-permute-start.4 = (bf16[288,128]{1,0:T(8,128)(2,1)S(1)}, bf16[288,128]{1,0:T(8,128)(2,1)S(1)}, u32[]{:S(2)}, u32[]{:S(2)}) collective-permute-start(bf16[288,128]{1,0:T(8,128)(2,1)S(1)} %get-tuple-element.76), channel_id=1, source_target_pairs={{0,1},{1,2},{2,3},{3,0},{4,5},{5,6},{6,7},{7,4},{8,9},{9,10},{10,1... | collective-permute-start | bytes 221192 | tf_op jit(solution)/shard_map/ppermute | solution.py:619
  21.5 4.1 %copy-start = (bf16[384,1536]{1,0:T(8,128)(2,1)S(1)}, bf16[384,1536]{1,0:T(8,128)(2,1)}, u32[]{:S(2)}) copy-start(bf16[384,1536]{1,0:T(8,128)(2,1)} %up_ref.1) | copy-start | bytes 3538948
  21.5 4.1 %copy-start.1 = (bf16[1536,384]{1,0:T(8,128)(2,1)S(1)}, bf16[1536,384]{1,0:T(8,128)(2,1)}, u32[]{:S(2)}) copy-start(bf16[1536,384]{1,0:T(8,128)(2,1)} %down_ref.1) | copy-start | bytes 3538948
  21.5 4.1 %copy-start.2 = (bf16[384,1152]{1,0:T(8,128)(2,1)S(1)}, bf16[384,1152]{1,0:T(8,128)(2,1)}, u32[]{:S(2)}) copy-start(bf16[384,1152]{1,0:T(8,128)(2,1)} %qkv_ref.1) | copy-start | bytes 2654212
  21.5 4.1 %copy-start.3 = (bf16[768,384]{1,0:T(8,128)(2,1)S(1)}, bf16[768,384]{1,0:T(8,128)(2,1)}, u32[]{:S(2)}) copy-start(bf16[768,384]{1,0:T(8,128)(2,1)} %reduce_ref.1) | copy-start | bytes 1769476
  21.5 4.1 %copy-start.6 = (bf16[384,384]{1,0:T(8,128)(2,1)S(1)}, bf16[384,384]{1,0:T(8,128)(2,1)}, u32[]{:S(2)}) copy-start(bf16[384,384]{1,0:T(8,128)(2,1)} %proj_ref.1) | copy-start | bytes 884740
  21.5 4.1 %copy-start.14 = (s32[608,1]{1,0:T(8,128)S(1)}, s32[608,1]{1,0:T(8,128)}, u32[]{:S(2)}) copy-start(s32[608,1]{1,0:T(8,128)} %constant.43.split_ref) | copy-start | bytes 7300
  21.5 4.1 %copy-start.17 = (s32[576,1]{1,0:T(8,128)S(1)}, s32[576,1]{1,0:T(8,128)}, u32[]{:S(2)}) copy-start(s32[576,1]{1,0:T(8,128)} %constant.42.merge_ref) | copy-start | bytes 6916
  34.2 4.7 %collective-permute-start.7 = (bf16[176,128]{1,0:T(8,128)(2,1)S(1)}, bf16[176,128]{1,0:T(8,128)(2,1)S(1)}, u32[]{:S(2)}, u32[]{:S(2)}) collective-permute-start(bf16[176,128]{1,0:T(8,128)(2,1)S(1)} %get-tuple-element.100), channel_id=1, source_target_pairs={{0,3},{1,0},{2,1},{3,2},{4,7},{5,4},{6,5},{7,6},{8,11},{9,8},{10,9... | collective-permute-start | bytes 135176 | tf_op jit(solution)/shard_map/ppermute | solution.py:619
  35.3 10.8 %collective-permute-start.8 = (bf16[80,128]{1,0:T(8,128)(2,1)S(1)}, bf16[80,128]{1,0:T(8,128)(2,1)S(1)}, u32[]{:S(2)}, u32[]{:S(2)}) collective-permute-start(bf16[80,128]{1,0:T(8,128)(2,1)S(1)} %get-tuple-element.103), channel_id=1, source_target_pairs={{0,31},{1,28},{2,29},{3,30},{4,3},{5,0},{6,1},{7,2},{8,7},{9,4},{1... | collective-permute-start | bytes 61448 | tf_op jit(solution)/shard_map/ppermute | solution.py:625
  37.4 4.2 %collective-permute-start.6 = (bf16[176,128]{1,0:T(8,128)(2,1)S(1)}, bf16[176,128]{1,0:T(8,128)(2,1)S(1)}, u32[]{:S(2)}, u32[]{:S(2)}) collective-permute-start(bf16[176,128]{1,0:T(8,128)(2,1)S(1)} %get-tuple-element.80), channel_id=1, source_target_pairs={{0,28},{4,0},{8,4},{12,8},{16,12},{20,16},{24,20},{28,24},{1,29},{... | collective-permute-start | bytes 135176 | tf_op jit(solution)/shard_map/ppermute | solution.py:616
  38.9 2.6 %copy-start.16 = (s32[576,1]{1,0:T(8,128)S(1)}, s32[576,1]{1,0:T(8,128)}, u32[]{:S(2)}) copy-start(s32[576,1]{1,0:T(8,128)} %constant.44.back_ref) | copy-start | bytes 6916
  40.3 4.8 %collective-permute-start.9 = (bf16[24,1656]{1,0:T(8,128)(2,1)S(1)}, bf16[24,1656]{1,0:T(8,128)(2,1)S(1)}, u32[]{:S(2)}, u32[]{:S(2)}) collective-permute-start(bf16[24,1656]{1,0:T(8,128)(2,1)S(1)} %shard_map.226), channel_id=1, source_target_pairs={{0,4},{4,0},{8,12},{12,8},{16,20},{20,16},{24,28},{28,24},{1,5},{5... | collective-permute-start | bytes 238472 | tf_op jit(solution)/shard_map/ppermute | solution.py:635
  45.2 7.7 %collective-permute-start.10 = (bf16[24,1656]{1,0:T(8,128)(2,1)S(1)}, bf16[24,1656]{1,0:T(8,128)(2,1)S(1)}, u32[]{:S(2)}, u32[]{:S(2)}) collective-permute-start(bf16[24,1656]{1,0:T(8,128)(2,1)S(1)} %add_convert_fusion.3), channel_id=1, source_target_pairs={{0,16},{4,20},{8,24},{12,28},{16,0},{20,4},{24,8},{28,12},{1,17},{... | collective-permute-start | bytes 238472 | tf_op jit(solution)/shard_map/ppermute | solution.py:635
  50.7 8.0 %collective-permute-start.14 = (bf16[24,1656]{1,0:T(8,128)(2,1)S(1)}, bf16[24,1656]{1,0:T(8,128)(2,1)S(1)}, u32[]{:S(2)}, u32[]{:S(2)}) collective-permute-start(bf16[24,1656]{1,0:T(8,128)(2,1)S(1)} %get-tuple-element.124), channel_id=1, source_target_pairs={{0,16},{4,20},{8,24},{12,28},{16,0},{20,4},{24,8},{28,12},{1,17},{... | collective-permute-start | bytes 238472 | tf_op jit(solution)/shard_map/ppermute | solution.py:635
  52.9 13.7 %copy-start.15 = (s32[576,1]{1,0:T(8,128)S(1)}, s32[576,1]{1,0:T(8,128)}, u32[]{:S(2)}) copy-start(s32[576,1]{1,0:T(8,128)} %constant.45.leave_ref) | copy-start | bytes 6916
  52.9 13.7 %copy-start.19 = (s32[144,1]{1,0:T(8,128)S(1)}, s32[144,1]{1,0:T(8,128)}, u32[]{:S(2)}) copy-start(s32[144,1]{1,0:T(8,128)} %constant.46.result_ref) | copy-start | bytes 1732
  53.8 6.9 %collective-permute-start.12 = (bf16[288,128]{1,0:T(8,128)(2,1)S(1)}, bf16[288,128]{1,0:T(8,128)(2,1)S(1)}, u32[]{:S(2)}, u32[]{:S(2)}) collective-permute-start(bf16[288,128]{1,0:T(8,128)(2,1)S(1)} %get-tuple-element.122), channel_id=1, source_target_pairs={{0,3},{1,0},{2,1},{3,2},{4,7},{5,4},{6,5},{7,6},{8,11},{9,8},{10,9... | collective-permute-start | bytes 221192 | tf_op jit(solution)/shard_map/ppermute | solution.py:619
  53.9 6.8 %collective-permute-start.13 = (bf16[192,128]{1,0:T(8,128)(2,1)S(1)}, bf16[192,128]{1,0:T(8,128)(2,1)S(1)}, u32[]{:S(2)}, u32[]{:S(2)}) collective-permute-start(bf16[192,128]{1,0:T(8,128)(2,1)S(1)} %get-tuple-element.123), channel_id=1, source_target_pairs={{0,31},{1,28},{2,29},{3,30},{4,3},{5,0},{6,1},{7,2},{8,7},{9,4},{1... | collective-permute-start | bytes 147464 | tf_op jit(solution)/shard_map/ppermute | solution.py:625
  60.7 5.1 %collective-permute-start.15 = (bf16[24,1656]{1,0:T(8,128)(2,1)S(1)}, bf16[24,1656]{1,0:T(8,128)(2,1)S(1)}, u32[]{:S(2)}, u32[]{:S(2)}) collective-permute-start(bf16[24,1656]{1,0:T(8,128)(2,1)S(1)} %add_convert_fusion.2), channel_id=1, source_target_pairs={{0,8},{4,12},{8,0},{12,4},{16,24},{20,28},{24,16},{28,20},{1,9},{5... | collective-permute-start | bytes 238472 | tf_op jit(solution)/shard_map/ppermute | solution.py:635
  60.8 5.8 %collective-permute-start.11 = (bf16[288,128]{1,0:T(8,128)(2,1)S(1)}, bf16[288,128]{1,0:T(8,128)(2,1)S(1)}, u32[]{:S(2)}, u32[]{:S(2)}) collective-permute-start(bf16[288,128]{1,0:T(8,128)(2,1)S(1)} %get-tuple-element.121), channel_id=1, source_target_pairs={{0,28},{4,0},{8,4},{12,8},{16,12},{20,16},{24,20},{28,24},{1,29},{... | collective-permute-start | bytes 221192 | tf_op jit(solution)/shard_map/ppermute | solution.py:616
  64.6 5.0 %collective-permute-start.17 = (bf16[24,1656]{1,0:T(8,128)(2,1)S(1)}, bf16[24,1656]{1,0:T(8,128)(2,1)S(1)}, u32[]{:S(2)}, u32[]{:S(2)}) collective-permute-start(bf16[24,1656]{1,0:T(8,128)(2,1)S(1)} %add_convert_fusion.coarse_kept), channel_id=1, source_target_pairs={{0,8},{4,12},{8,0},{12,4},{16,24},{20,28},{24,16},{28,20},{1,9},{5... | collective-permute-start | bytes 238472 | tf_op jit(solution)/shard_map/ppermute | solution.py:635
  65.8 4.6 %collective-permute-start.16 = (bf16[24,1656]{1,0:T(8,128)(2,1)S(1)}, bf16[24,1656]{1,0:T(8,128)(2,1)S(1)}, u32[]{:S(2)}, u32[]{:S(2)}) collective-permute-start(bf16[24,1656]{1,0:T(8,128)(2,1)S(1)} %add_convert_fusion.1.fine_kept), channel_id=1, source_target_pairs={{0,4},{4,0},{8,12},{12,8},{16,20},{20,16},{24,28},{28,24},{1,5},{5... | collective-permute-start | bytes 238472 | tf_op jit(solution)/shard_map/ppermute | solution.py:635

commit v7 on v6

--- a/solution.py
+++ b/solution.py
@@ -722,7 +722,7 @@
         (scored,),
     )
     steps = lon_steps()
-    other = swap(coarse_grad, steps[0])
+    other = swap(coarse_grad, steps[1])
     half_tok = ((288, 192), bf16)
     half_outs = [((288, 192), f32)] + [half_tok] * 3
     q, k, v, probs, n1, r1, n2, r2, slope = outer[5:]
@@ -752,10 +752,10 @@
     )
     second_half[0], other = lax.optimization_barrier((second_half[0], other))
     coarse_grad = add(coarse_grad, other)
-    for step in steps[1:-1]:
+    for step in (*steps[2:-1], steps[0]):
         coarse_sums = (coarse_grad, swap(coarse_grad, step))
         coarse_grad = add(*coarse_sums)
-    other = swap(fine_grad, steps[-1])
+    other = swap(fine_grad, steps[0])
     fine_back = list(run(
         qkv_back_kernel, [tok] + wide_edges, [], 2,
         (*first_half, *second_half, n1_inner, r1_inner, n1, r1, fine_qkv, c10, c01, c00),
@@ -763,7 +763,7 @@
     alon, alat, adiag = send(fine_back[1:4], -1)
     alat, adiag, other = lax.optimization_barrier((alat, adiag, other))
     fine_grad = add(fine_grad, other)
-    for step in reversed(steps[:-1]):
+    for step in steps[1:]:
         fine_sums = (fine_grad, swap(fine_grad, step))
         fine_grad = add(*fine_sums)
     d_tokens, coarse_result = run(

time: 71.4 us -> 71.3 us (level)
  waiting for transfers between devices: 8.39 us -> 10.4 us
  starting transfers between devices: 24.7 us -> 22.7 us
    ppermute x4, starting transfers between devices: 10 us -> 8.23 us  [move(): return lax.ppermute(value, ('lon', 'lat'), pairs)]
    ppermute x6, waiting for transfers between devices: 2.86 us -> 4.57 us  [swap(): return lax.ppermute(value, 'lon', [(s, s ^ step) for s in range(count)])]
    ppermute x4, starting transfers between devices: 8.42 us -> 6.84 us  [move(): return lax.ppermute(value, 'lon', pairs)]
    ppermute x6, starting transfers between devices: 3.75 us -> 4.76 us  [swap(): return lax.ppermute(value, 'lon', [(s, s ^ step) for s in range(count)])]
  transfers between devices with their start and end apart: 18 -> 18, of which waited for: 9 -> 10; matrix products, arithmetic and copies ran while one was open for 2% -> 2% of each run, Pallas kernels for 27% -> 27%
where the time goes in v7:
time: 71.3 us; the launch traced here: 71.1 us
  Pallas kernels  34.6 us (49%)
  starting transfers between devices  22.7 us (32%)
  waiting for transfers between devices  10.4 us (15%)
  local copies, waits for them, and re-layouts  2.04 us (3%)
  between operations  1 us (1%)
    pallas_call x12, Pallas kernels, run(): pl.pallas_call(kernel, out_shape=shapes, scratch_shapes=[pltpu.VMEM(shape...  34.6 us
    ppermute x4, starting transfers between devices, move(): return lax.ppermute(value, ('lon', 'lat'), pairs)  8.23 us
    ppermute x4, starting transfers between devices, move(): return lax.ppermute(value, 'lon', pairs)  6.84 us
    ppermute x6, starting transfers between devices, swap(): return lax.ppermute(value, 'lon', [(s, s ^ step) for s in range(count)])  4.76 us
    ppermute x6, waiting for transfers between devices, swap(): return lax.ppermute(value, 'lon', [(s, s ^ step) for s in range(count)])  4.57 us
    ppermute x4, waiting for transfers between devices, move(): return lax.ppermute(value, 'lon', pairs)  3.71 us
    ppermute x4, starting transfers between devices, move(): return lax.ppermute(value, 'lat', pairs)  2.87 us
    ppermute x4, waiting for transfers between devices, move(): return lax.ppermute(value, ('lon', 'lat'), pairs)  2.08 us
  transfers between devices with their start and end apart: 18, of which 10 were waited for; matrix products, arithmetic and copies ran while one was open for 2% of the time, Pallas kernels for 27%

profile of v7, /device:TPU:0, one launch (start us, length us, event | category | flops | bytes accessed | tf_op | source)
XLA Modules:
  0.0 71.1 jit_solution(789042730701748377)
XLA Ops:
  0.6 1.0 %copy-done.4 = bf16[2,12,24,192]{3,2,1,0:T(8,128)(2,1)S(1)} copy-done((bf16[2,12,24,192]{3,2,1,0:T(8,128)(2,1)S(1)}, bf16[2,12,24,192]{3,2,1,0:T(8,128)(2,1)}, u32[]{:S(2)}) %copy-start.4) | copy-done | bytes 221208
  1.6 0.1 shard_map.219
  1.7 2.5 %collective-permute-start.2 = (bf16[80,128]{1,0:T(8,128)(2,1)S(1)}, bf16[80,128]{1,0:T(8,128)(2,1)S(1)}, u32[]{:S(2)}, u32[]{:S(2)}) collective-permute-start(bf16[80,128]{1,0:T(8,128)(2,1)S(1)} %get-tuple-element.71), channel_id=1, source_target_pairs={{0,5},{1,6},{2,7},{3,4},{4,9},{5,10},{6,11},{7,8},{8,13},{9,14},{1... | collective-permute-start | bytes 61448 | tf_op jit(solution)/shard_map/ppermute | solution.py:625
  4.2 1.5 %collective-permute-start = (bf16[176,128]{1,0:T(8,128)(2,1)S(1)}, bf16[176,128]{1,0:T(8,128)(2,1)S(1)}, u32[]{:S(2)}, u32[]{:S(2)}) collective-permute-start(bf16[176,128]{1,0:T(8,128)(2,1)S(1)} %get-tuple-element.69), channel_id=1, source_target_pairs={{0,4},{4,8},{8,12},{12,16},{16,20},{20,24},{24,28},{28,0},{1,5},{5... | collective-permute-start | bytes 135176 | tf_op jit(solution)/shard_map/ppermute | solution.py:616
  5.7 1.3 %collective-permute-start.1 = (bf16[176,128]{1,0:T(8,128)(2,1)S(1)}, bf16[176,128]{1,0:T(8,128)(2,1)S(1)}, u32[]{:S(2)}, u32[]{:S(2)}) collective-permute-start(bf16[176,128]{1,0:T(8,128)(2,1)S(1)} %get-tuple-element.70), channel_id=1, source_target_pairs={{0,1},{1,2},{2,3},{3,0},{4,5},{5,6},{6,7},{7,4},{8,9},{9,10},{10,1... | collective-permute-start | bytes 135176 | tf_op jit(solution)/shard_map/ppermute | solution.py:619
  7.0 0.1 multiply_add_fusion
  7.1 0.1 reshape.48
  7.2 0.1 eq.28
  7.4 0.1 compare_select_fusion.refs_6_
  7.5 0.1 or_select_fusion.mask_ref
  7.7 0.0 copy-start.18
  7.7 2.3 %shard_map.220.refs_5_ = f32[1728,144]{1,0:T(8,128)S(1)} custom-call(f32[6,2,3312]{2,1,0:T(2,128)S(1)} %bitcast.20), custom_call_target="tpu_custom_call" | custom-call | flops 2000000000 | bytes 1154304 | tf_op jit(solution)/shard_map/pallas_call | solution.py:601
  10.0 0.9 %collective-permute-done.refs_1_ = bf16[176,128]{1,0:T(8,128)(2,1)S(1)} collective-permute-done((bf16[176,128]{1,0:T(8,128)(2,1)S(1)}, bf16[176,128]{1,0:T(8,128)(2,1)S(1)}, u32[]{:S(2)}, u32[]{:S(2)}) %collective-permute-start) | collective-permute-done | bytes 45088 | tf_op jit(solution)/shard_map/ppermute | solution.py:616
  11.0 6.0 %shard_map.221 = (bf16[288,128]{1,0:T(8,128)(2,1)S(1)}, bf16[288,128]{1,0:T(8,128)(2,1)S(1)}, bf16[192,128]{1,0:T(8,128)(2,1)S(1)}, bf16[48,384]{1,0:T(8,128)(2,...) custom-call(bf16[6,12,2,384]{3,2,1,0:T(2,128)(2,1)S(1)} %bitcast.22,, ...), custom_call_target="tpu_custom_call" | custom-call | flops 6000000000 | bytes 5298816 | tf_op jit(solution)/shard_map/pallas_call | solution.py:601
  17.0 0.6 collective-permute-start.5
  17.5 1.5 %collective-permute-start.3 = (bf16[288,128]{1,0:T(8,128)(2,1)S(1)}, bf16[288,128]{1,0:T(8,128)(2,1)S(1)}, u32[]{:S(2)}, u32[]{:S(2)}) collective-permute-start(bf16[288,128]{1,0:T(8,128)(2,1)S(1)} %get-tuple-element.75), channel_id=1, source_target_pairs={{0,4},{4,8},{8,12},{12,16},{16,20},{20,24},{24,28},{28,0},{1,5},{5... | collective-permute-start | bytes 221192 | tf_op jit(solution)/shard_map/ppermute | solution.py:616
  19.1 0.1 collective-permute-start.4
  19.2 2.3 %shard_map.223.bias_ref = f32[1728,144]{1,0:T(8,128)S(1)} custom-call(f32[12,1,3312]{2,1,0:T(1,128)S(1)} %bitcast.21), custom_call_target="tpu_custom_call" | custom-call | flops 2000000000 | bytes 1154304 | tf_op jit(solution)/shard_map/pallas_call | solution.py:601
  21.5 0.0 copy-start.17
  21.5 2.7 %shard_map.222 = (bf16[144,192]{1,0:T(8,128)(2,1)S(1)}, bf16[144,192]{1,0:T(8,128)(2,1)S(1)}, bf16[144,192]{1,0:T(8,128)(2,1)S(1)}, bf16[144,192]{1,0:T(8,128)(2...) custom-call(bf16[576,192]{1,0:T(8,128)(2,1)S(1)} %bitcast.15, ...), custom_call_target="tpu_custom_call" | custom-call | flops 2000000000 | bytes 3348864 | tf_op jit(solution)/shard_map/pallas_call | solution.py:601
  24.3 0.3 collective-permute-done.5.diag_ref
  24.6 0.9 %collective-permute-done.3.lon_ref = bf16[288,128]{1,0:T(8,128)(2,1)S(1)} collective-permute-done((bf16[288,128]{1,0:T(8,128)(2,1)S(1)}, bf16[288,128]{1,0:T(8,128)(2,1)S(1)}, u32[]{:S(2)}, u32[]{:S(2)}) %collective-permute-start.3) | collective-permute-done | bytes 73760 | tf_op jit(solution)/shard_map/ppermute | solution.py:616
  25.6 8.6 %shard_map.224 = (bf16[48,384]{1,0:T(8,128)(2,1)S(1)}, bf16[48,384]{1,0:T(8,128)(2,1)S(1)}, bf16[48,384]{1,0:T(8,128)(2,1)S(1)}, bf16[48,384]{1,0:T(8,128)(2,1)S...) custom-call(bf16[144,192]{1,0:T(8,128)(2,1)S(1)} %get-tuple-element., ...), custom_call_target="tpu_custom_call" | custom-call | flops 8999999488 | bytes 7048832 | tf_op jit(solution)/shard_map/pallas_call | solution.py:601
  34.2 1.1 %collective-permute-start.7 = (bf16[176,128]{1,0:T(8,128)(2,1)S(1)}, bf16[176,128]{1,0:T(8,128)(2,1)S(1)}, u32[]{:S(2)}, u32[]{:S(2)}) collective-permute-start(bf16[176,128]{1,0:T(8,128)(2,1)S(1)} %get-tuple-element.100), channel_id=1, source_target_pairs={{0,3},{1,0},{2,1},{3,2},{4,7},{5,4},{6,5},{7,6},{8,11},{9,8},{10,9... | collective-permute-start | bytes 135176 | tf_op jit(solution)/shard_map/ppermute | solution.py:619
  35.3 2.1 %collective-permute-start.8 = (bf16[80,128]{1,0:T(8,128)(2,1)S(1)}, bf16[80,128]{1,0:T(8,128)(2,1)S(1)}, u32[]{:S(2)}, u32[]{:S(2)}) collective-permute-start(bf16[80,128]{1,0:T(8,128)(2,1)S(1)} %get-tuple-element.103), channel_id=1, source_target_pairs={{0,31},{1,28},{2,29},{3,30},{4,3},{5,0},{6,1},{7,2},{8,7},{9,4},{1... | collective-permute-start | bytes 61448 | tf_op jit(solution)/shard_map/ppermute | solution.py:625
  37.4 1.5 %collective-permute-start.6 = (bf16[176,128]{1,0:T(8,128)(2,1)S(1)}, bf16[176,128]{1,0:T(8,128)(2,1)S(1)}, u32[]{:S(2)}, u32[]{:S(2)}) collective-permute-start(bf16[176,128]{1,0:T(8,128)(2,1)S(1)} %get-tuple-element.80), channel_id=1, source_target_pairs={{0,28},{4,0},{8,4},{12,8},{16,12},{20,16},{24,20},{28,24},{1,29},{... | collective-permute-start | bytes 135176 | tf_op jit(solution)/shard_map/ppermute | solution.py:616
  38.9 1.4 %shard_map.226 = bf16[24,1656]{1,0:T(8,128)(2,1)S(1)} custom-call(f32[1728,144]{1,0:T(8,128)S(1)} %get-tuple-element.105.score_ref), custom_call_target="tpu_custom_call" | custom-call | flops 2000000000 | bytes 1074816 | tf_op jit(solution)/shard_map/pallas_call | solution.py:601
  40.3 0.2 collective-permute-start.9
  40.5 1.0 %collective-permute-done.6.dlon_ref = bf16[176,128]{1,0:T(8,128)(2,1)S(1)} collective-permute-done((bf16[176,128]{1,0:T(8,128)(2,1)S(1)}, bf16[176,128]{1,0:T(8,128)(2,1)S(1)}, u32[]{:S(2)}, u32[]{:S(2)}) %collective-permute-start.6) | collective-permute-done | bytes 45088 | tf_op jit(solution)/shard_map/ppermute | solution.py:616
  41.6 3.6 %shard_map.225 = (f32[288,192]{1,0:T(8,128)S(1)}, bf16[288,192]{1,0:T(8,128)(2,1)S(1)}, bf16[288,192]{1,0:T(8,128)(2,1)S(1)}, bf16[288,192]{1,0:T(8,128)(2,1)S(1)}, f32[864,144]{1,0:T(8,128)S(1)}) custom-call(bf16[176,128]{1,0:T(8,128)(2,1)S(1)} %collective-permute-done.6.dlon_ref, bf16[336,192]{1,0:T(8,128)(2,1)S(1)} %get-tuple-element.81.dloc_ref, ...), custom_call_target="tpu_custom_call" | custom-call | flops 4000000000 | bytes 4657664 | tf_op jit(solution)/shard_map/pallas_call | solution.py:601
  45.2 0.9 %collective-permute-start.10 = (bf16[24,1656]{1,0:T(8,128)(2,1)S(1)}, bf16[24,1656]{1,0:T(8,128)(2,1)S(1)}, u32[]{:S(2)}, u32[]{:S(2)}) collective-permute-start(bf16[24,1656]{1,0:T(8,128)(2,1)S(1)} %add_convert_fusion.3), channel_id=1, source_target_pairs={{0,16},{4,20},{8,24},{12,28},{16,0},{20,4},{24,8},{28,12},{1,17},{... | collective-permute-start | bytes 238472 | tf_op jit(solution)/shard_map/ppermute | solution.py:635
  46.1 4.7 %shard_map.227 = (f32[288,192]{1,0:T(8,128)S(1)}, bf16[288,192]{1,0:T(8,128)(2,1)S(1)}, bf16[288,192]{1,0:T(8,128)(2,1)S(1)}, bf16[288,192]{1,0:T(8,128)(2,1)S(1)}, bf16[24,1656]{1,0:T(8,128)(2,1)S(1)}) custom-call(bf16[176,128]{1,0:T(8,128)(2,1)S(1)} %collective-permute-done.6.dlon_ref, bf16[336,192]{1,0:T(8,128)(2,1)S(1)} %get-tuple-element.81.dloc_ref, ...), custom_call_target="tpu_custom_call" | custom-call | flops 5000000000 | bytes 4110912 | tf_op jit(solution)/shard_map/pallas_call | solution.py:601
  50.7 0.9 %collective-permute-start.14 = (bf16[24,1656]{1,0:T(8,128)(2,1)S(1)}, bf16[24,1656]{1,0:T(8,128)(2,1)S(1)}, u32[]{:S(2)}, u32[]{:S(2)}) collective-permute-start(bf16[24,1656]{1,0:T(8,128)(2,1)S(1)} %get-tuple-element.124), channel_id=1, source_target_pairs={{0,4},{4,0},{8,12},{12,8},{16,20},{20,16},{24,28},{28,24},{1,5},{5... | collective-permute-start | bytes 238472 | tf_op jit(solution)/shard_map/ppermute | solution.py:635
  51.6 0.4 collective-permute-done.10
  52.0 0.8 %shard_map.228 = (bf16[576,192]{1,0:T(8,128)(2,1)S(1)}, bf16[288,128]{1,0:T(8,128)(2,1)S(1)}, bf16[288,128]{1,0:T(8,128)(2,1)S(1)}, bf16[192,128]{1,0:T(8,128)(2,1)S(1)}) custom-call(f32[288,192]{1,0:T(8,128)S(1)} %get-tuple-element.96.refs_0_, bf16[288,192]{1,0:T(8,128)(2,1)S(1)} %get-tuple-element.97.refs_1_, ...), custom_call_target="tpu_custom_call" | custom-call | flops 2000000000 | bytes 2078976 | tf_op jit(solution)/shard_map/pallas_call | solution.py:601
  52.9 0.4 collective-permute-start.12
  53.3 3.1 %collective-permute-start.13 = (bf16[192,128]{1,0:T(8,128)(2,1)S(1)}, bf16[192,128]{1,0:T(8,128)(2,1)S(1)}, u32[]{:S(2)}, u32[]{:S(2)}) collective-permute-start(bf16[192,128]{1,0:T(8,128)(2,1)S(1)} %get-tuple-element.123), channel_id=1, source_target_pairs={{0,31},{1,28},{2,29},{3,30},{4,3},{5,0},{6,1},{7,2},{8,7},{9,4},{1... | collective-permute-start | bytes 147464 | tf_op jit(solution)/shard_map/ppermute | solution.py:625
  56.4 1.7 %collective-permute-done.13.diag_ref = bf16[192,128]{1,0:T(8,128)(2,1)S(1)} collective-permute-done((bf16[192,128]{1,0:T(8,128)(2,1)S(1)}, bf16[192,128]{1,0:T(8,128)(2,1)S(1)}, u32[]{:S(2)}, u32[]{:S(2)}) %collective-permute-start.13) | collective-permute-done | bytes 49184 | tf_op jit(solution)/shard_map/ppermute | solution.py:625
  58.1 1.8 %collective-permute-start.15 = (bf16[24,1656]{1,0:T(8,128)(2,1)S(1)}, bf16[24,1656]{1,0:T(8,128)(2,1)S(1)}, u32[]{:S(2)}, u32[]{:S(2)}) collective-permute-start(bf16[24,1656]{1,0:T(8,128)(2,1)S(1)} %add_convert_fusion.2), channel_id=1, source_target_pairs={{0,8},{4,12},{8,0},{12,4},{16,24},{20,28},{24,16},{28,20},{1,9},{5... | collective-permute-start | bytes 238472 | tf_op jit(solution)/shard_map/ppermute | solution.py:635
  60.0 2.2 %collective-permute-start.11 = (bf16[288,128]{1,0:T(8,128)(2,1)S(1)}, bf16[288,128]{1,0:T(8,128)(2,1)S(1)}, u32[]{:S(2)}, u32[]{:S(2)}) collective-permute-start(bf16[288,128]{1,0:T(8,128)(2,1)S(1)} %get-tuple-element.121), channel_id=1, source_target_pairs={{0,28},{4,0},{8,4},{12,8},{16,12},{20,16},{24,20},{28,24},{1,29},{... | collective-permute-start | bytes 221192 | tf_op jit(solution)/shard_map/ppermute | solution.py:616
  62.2 1.0 %collective-permute-done.15 = bf16[24,1656]{1,0:T(8,128)(2,1)S(1)} collective-permute-done((bf16[24,1656]{1,0:T(8,128)(2,1)S(1)}, bf16[24,1656]{1,0:T(8,128)(2,1)S(1)}, u32[]{:S(2)}, u32[]{:S(2)}) %collective-permute-start.15) | collective-permute-done | bytes 79520 | tf_op jit(solution)/shard_map/ppermute | solution.py:635
  63.2 1.0 %collective-permute-start.16 = (bf16[24,1656]{1,0:T(8,128)(2,1)S(1)}, bf16[24,1656]{1,0:T(8,128)(2,1)S(1)}, u32[]{:S(2)}, u32[]{:S(2)}) collective-permute-start(bf16[24,1656]{1,0:T(8,128)(2,1)S(1)} %add_convert_fusion.1.fine_kept), channel_id=1, source_target_pairs={{0,16},{4,20},{8,24},{12,28},{16,0},{20,4},{24,8},{28,12},{1,17},{... | collective-permute-start | bytes 238472 | tf_op jit(solution)/shard_map/ppermute | solution.py:635
  64.2 0.8 %collective-permute-done.11.lon_ref = bf16[288,128]{1,0:T(8,128)(2,1)S(1)} collective-permute-done((bf16[288,128]{1,0:T(8,128)(2,1)S(1)}, bf16[288,128]{1,0:T(8,128)(2,1)S(1)}, u32[]{:S(2)}, u32[]{:S(2)}) %collective-permute-start.11) | collective-permute-done | bytes 73760 | tf_op jit(solution)/shard_map/ppermute | solution.py:616
  65.1 1.3 %shard_map.229 = (bf16[576,192]{1,0:T(8,128)(2,1)}, bf16[2,6,12,384]{3,2,1,0:T(8,128)(2,1)S(1)}) custom-call(bf16[576,192]{1,0:T(8,128)(2,1)S(1)} %get-tuple-element.120.res_ref, bf16[288,128]{1,0:T(8,128)(2,1)S(1)} %collective-permute-done.11.lon_ref, bf16[288,128]{1,0:T(8,128)(2,1)S(1)} %collective-permute-done.12.lat_ref, ...), custom_call_target="tpu_custom_call" | custom-call | flops 1000000000 | bytes 789312 | tf_op jit(solution)/shard_map/pallas_call | solution.py:601
  66.4 0.7 %copy.27 = bf16[2,6,12,384]{3,0,2,1:T(2,128)(2,1)} copy(bf16[2,6,12,384]{3,2,1,0:T(8,128)(2,1)S(1)} %get-tuple-element.138) | data formatting | bytes 221184
  67.2 0.2 collective-permute-done.17.coarse_other
  67.4 2.9 %collective-permute-done.16.fine_other = bf16[24,1656]{1,0:T(8,128)(2,1)S(1)} collective-permute-done((bf16[24,1656]{1,0:T(8,128)(2,1)S(1)}, bf16[24,1656]{1,0:T(8,128)(2,1)S(1)}, u32[]{:S(2)}, u32[]{:S(2)}) %collective-permute-start.16) | collective-permute-done | bytes 79520 | tf_op jit(solution)/shard_map/ppermute | solution.py:635
  70.3 0.8 %shard_map.230 = (f32[6,2,3312]{2,1,0:T(2,128)}, f32[12,1,3312]{2,1,0:T(1,128)}) custom-call(bf16[24,1656]{1,0:T(8,128)(2,1)S(1)} %add_convert_fusion.1.fine_kept, bf16[24,1656]{1,0:T(8,128)(2,1)S(1)} %collective-permute-done.16.fine_other, bf16[24,1656]{1,0:T(8,128)(2,1)S(1)} %add_convert_fusion.coarse_kept, ...), custom_call_target="tpu_custom_call" | custom-call | flops 1000000000 | bytes 635904 | tf_op jit(solution)/shard_map/pallas_call | solution.py:601
  (55 shorter events, 0.3 us)
Async XLA Ops:
  0.6 1.0 %copy-start.4 = (bf16[2,12,24,192]{3,2,1,0:T(8,128)(2,1)S(1)}, bf16[2,12,24,192]{3,2,1,0:T(8,128)(2,1)}, u32[]{:S(2)}) copy-start(bf16[2,12,24,192]{3,2,1,0:T(8,128)(2,1)} %param.20) | copy-start | bytes 663556
  1.6 5.4 %copy-start.20 = (s32[2,12,24]{2,0,1:T(2,128)S(1)}, s32[2,12,24]{2,0,1:T(2,128)}, u32[]{:S(2)}) copy-start(s32[2,12,24]{2,0,1:T(2,128)} %param.21) | copy-start | bytes 6916
  1.6 6.0 %copy-start.10 = (f32[2,6,3312]{2,0,1:T(2,128)S(1)}, f32[2,6,3312]{2,0,1:T(2,128)}, u32[]{:S(2)}) copy-start(f32[2,6,3312]{2,0,1:T(2,128)} %param.26) | copy-start | bytes 476932
  1.7 8.3 %collective-permute-start.2 = (bf16[80,128]{1,0:T(8,128)(2,1)S(1)}, bf16[80,128]{1,0:T(8,128)(2,1)S(1)}, u32[]{:S(2)}, u32[]{:S(2)}) collective-permute-start(bf16[80,128]{1,0:T(8,128)(2,1)S(1)} %get-tuple-element.71), channel_id=1, source_target_pairs={{0,5},{1,6},{2,7},{3,4},{4,9},{5,10},{6,11},{7,8},{8,13},{9,14},{1... | collective-permute-start | bytes 61448 | tf_op jit(solution)/shard_map/ppermute | solution.py:625
  4.2 6.7 %collective-permute-start = (bf16[176,128]{1,0:T(8,128)(2,1)S(1)}, bf16[176,128]{1,0:T(8,128)(2,1)S(1)}, u32[]{:S(2)}, u32[]{:S(2)}) collective-permute-start(bf16[176,128]{1,0:T(8,128)(2,1)S(1)} %get-tuple-element.69), channel_id=1, source_target_pairs={{0,4},{4,8},{8,12},{12,16},{16,20},{20,24},{24,28},{28,0},{1,5},{5... | collective-permute-start | bytes 135176 | tf_op jit(solution)/shard_map/ppermute | solution.py:616
  5.7 5.2 %collective-permute-start.1 = (bf16[176,128]{1,0:T(8,128)(2,1)S(1)}, bf16[176,128]{1,0:T(8,128)(2,1)S(1)}, u32[]{:S(2)}, u32[]{:S(2)}) collective-permute-start(bf16[176,128]{1,0:T(8,128)(2,1)S(1)} %get-tuple-element.70), channel_id=1, source_target_pairs={{0,1},{1,2},{2,3},{3,0},{4,5},{5,6},{6,7},{7,4},{8,9},{9,10},{10,1... | collective-permute-start | bytes 135176 | tf_op jit(solution)/shard_map/ppermute | solution.py:619
  7.6 3.3 %copy-start.5 = (bf16[2,12,24,192]{3,2,1,0:T(8,128)(2,1)S(1)}, bf16[2,12,24,192]{3,2,1,0:T(8,128)(2,1)}, u32[]{:S(2)}) copy-start(bf16[2,12,24,192]{3,2,1,0:T(8,128)(2,1)} %param.20) | copy-start | bytes 663556
  7.6 3.3 %copy-start.7 = (bf16[192,768]{1,0:T(8,128)(2,1)S(1)}, bf16[192,768]{1,0:T(8,128)(2,1)}, u32[]{:S(2)}) copy-start(bf16[192,768]{1,0:T(8,128)(2,1)} %refs_8_.5) | copy-start | bytes 884740
  7.7 3.3 %copy-start.8 = (bf16[768,192]{0,1:T(8,128)(2,1)S(1)}, bf16[768,192]{0,1:T(8,128)(2,1)}, u32[]{:S(2)}) copy-start(bf16[768,192]{0,1:T(8,128)(2,1)} %param.25) | copy-start | bytes 884740
  7.7 3.3 %copy-start.9 = (bf16[192,576]{1,0:T(8,128)(2,1)S(1)}, bf16[192,576]{1,0:T(8,128)(2,1)}, u32[]{:S(2)}) copy-start(bf16[192,576]{1,0:T(8,128)(2,1)} %refs_12_.1) | copy-start | bytes 663556
  7.7 3.3 %copy-start.12 = (bf16[2,6,12,384]{3,0,2,1:T(2,128)(2,1)S(1)}, bf16[2,6,12,384]{3,0,2,1:T(2,128)(2,1)}, u32[]{:S(2)}) copy-start(bf16[2,6,12,384]{3,0,2,1:T(2,128)(2,1)} %param.33) | copy-start | bytes 331780
  7.7 3.3 %copy-start.13 = (bf16[192,192]{1,0:T(8,128)(2,1)S(1)}, bf16[192,192]{1,0:T(8,128)(2,1)}, u32[]{:S(2)}) copy-start(bf16[192,192]{1,0:T(8,128)(2,1)} %refs_7_.5) | copy-start | bytes 221188
  7.7 3.3 %copy-start.18 = (s32[576,1]{1,0:T(8,128)S(1)}, s32[576,1]{1,0:T(8,128)}, u32[]{:S(2)}) copy-start(s32[576,1]{1,0:T(8,128)} %constant.41.refs_4_) | copy-start | bytes 6916
  11.0 8.2 %copy-start.11 = (f32[1,12,3312]{2,0,1:T(1,128)S(1)}, f32[1,12,3312]{2,0,1:T(1,128)}, u32[]{:S(2)}) copy-start(f32[1,12,3312]{2,0,1:T(1,128)} %param.32) | copy-start | bytes 476932
  17.0 7.7 %collective-permute-start.5 = (bf16[192,128]{1,0:T(8,128)(2,1)S(1)}, bf16[192,128]{1,0:T(8,128)(2,1)S(1)}, u32[]{:S(2)}, u32[]{:S(2)}) collective-permute-start(bf16[192,128]{1,0:T(8,128)(2,1)S(1)} %get-tuple-element.77), channel_id=1, source_target_pairs={{0,5},{1,6},{2,7},{3,4},{4,9},{5,10},{6,11},{7,8},{8,13},{9,14},{1... | collective-permute-start | bytes 147464 | tf_op jit(solution)/shard_map/ppermute | solution.py:625
  17.5 8.0 %collective-permute-start.3 = (bf16[288,128]{1,0:T(8,128)(2,1)S(1)}, bf16[288,128]{1,0:T(8,128)(2,1)S(1)}, u32[]{:S(2)}, u32[]{:S(2)}) collective-permute-start(bf16[288,128]{1,0:T(8,128)(2,1)S(1)} %get-tuple-element.75), channel_id=1, source_target_pairs={{0,4},{4,8},{8,12},{12,16},{16,20},{20,24},{24,28},{28,0},{1,5},{5... | collective-permute-start | bytes 221192 | tf_op jit(solution)/shard_map/ppermute | solution.py:616
  19.1 6.5 %collective-permute-start.4 = (bf16[288,128]{1,0:T(8,128)(2,1)S(1)}, bf16[288,128]{1,0:T(8,128)(2,1)S(1)}, u32[]{:S(2)}, u32[]{:S(2)}) collective-permute-start(bf16[288,128]{1,0:T(8,128)(2,1)S(1)} %get-tuple-element.76), channel_id=1, source_target_pairs={{0,1},{1,2},{2,3},{3,0},{4,5},{5,6},{6,7},{7,4},{8,9},{9,10},{10,1... | collective-permute-start | bytes 221192 | tf_op jit(solution)/shard_map/ppermute | solution.py:619
  21.5 4.1 %copy-start = (bf16[384,1536]{1,0:T(8,128)(2,1)S(1)}, bf16[384,1536]{1,0:T(8,128)(2,1)}, u32[]{:S(2)}) copy-start(bf16[384,1536]{1,0:T(8,128)(2,1)} %up_ref.1) | copy-start | bytes 3538948
  21.5 4.1 %copy-start.1 = (bf16[1536,384]{1,0:T(8,128)(2,1)S(1)}, bf16[1536,384]{1,0:T(8,128)(2,1)}, u32[]{:S(2)}) copy-start(bf16[1536,384]{1,0:T(8,128)(2,1)} %down_ref.1) | copy-start | bytes 3538948
  21.5 4.1 %copy-start.2 = (bf16[384,1152]{1,0:T(8,128)(2,1)S(1)}, bf16[384,1152]{1,0:T(8,128)(2,1)}, u32[]{:S(2)}) copy-start(bf16[384,1152]{1,0:T(8,128)(2,1)} %qkv_ref.1) | copy-start | bytes 2654212
  21.5 4.1 %copy-start.3 = (bf16[768,384]{1,0:T(8,128)(2,1)S(1)}, bf16[768,384]{1,0:T(8,128)(2,1)}, u32[]{:S(2)}) copy-start(bf16[768,384]{1,0:T(8,128)(2,1)} %reduce_ref.1) | copy-start | bytes 1769476
  21.5 4.1 %copy-start.6 = (bf16[384,384]{1,0:T(8,128)(2,1)S(1)}, bf16[384,384]{1,0:T(8,128)(2,1)}, u32[]{:S(2)}) copy-start(bf16[384,384]{1,0:T(8,128)(2,1)} %proj_ref.1) | copy-start | bytes 884740
  21.5 4.1 %copy-start.14 = (s32[608,1]{1,0:T(8,128)S(1)}, s32[608,1]{1,0:T(8,128)}, u32[]{:S(2)}) copy-start(s32[608,1]{1,0:T(8,128)} %constant.43.split_ref) | copy-start | bytes 7300
  21.5 4.1 %copy-start.17 = (s32[576,1]{1,0:T(8,128)S(1)}, s32[576,1]{1,0:T(8,128)}, u32[]{:S(2)}) copy-start(s32[576,1]{1,0:T(8,128)} %constant.42.merge_ref) | copy-start | bytes 6916
  34.2 4.7 %collective-permute-start.7 = (bf16[176,128]{1,0:T(8,128)(2,1)S(1)}, bf16[176,128]{1,0:T(8,128)(2,1)S(1)}, u32[]{:S(2)}, u32[]{:S(2)}) collective-permute-start(bf16[176,128]{1,0:T(8,128)(2,1)S(1)} %get-tuple-element.100), channel_id=1, source_target_pairs={{0,3},{1,0},{2,1},{3,2},{4,7},{5,4},{6,5},{7,6},{8,11},{9,8},{10,9... | collective-permute-start | bytes 135176 | tf_op jit(solution)/shard_map/ppermute | solution.py:619
  35.3 10.8 %collective-permute-start.8 = (bf16[80,128]{1,0:T(8,128)(2,1)S(1)}, bf16[80,128]{1,0:T(8,128)(2,1)S(1)}, u32[]{:S(2)}, u32[]{:S(2)}) collective-permute-start(bf16[80,128]{1,0:T(8,128)(2,1)S(1)} %get-tuple-element.103), channel_id=1, source_target_pairs={{0,31},{1,28},{2,29},{3,30},{4,3},{5,0},{6,1},{7,2},{8,7},{9,4},{1... | collective-permute-start | bytes 61448 | tf_op jit(solution)/shard_map/ppermute | solution.py:625
  37.4 4.2 %collective-permute-start.6 = (bf16[176,128]{1,0:T(8,128)(2,1)S(1)}, bf16[176,128]{1,0:T(8,128)(2,1)S(1)}, u32[]{:S(2)}, u32[]{:S(2)}) collective-permute-start(bf16[176,128]{1,0:T(8,128)(2,1)S(1)} %get-tuple-element.80), channel_id=1, source_target_pairs={{0,28},{4,0},{8,4},{12,8},{16,12},{20,16},{24,20},{28,24},{1,29},{... | collective-permute-start | bytes 135176 | tf_op jit(solution)/shard_map/ppermute | solution.py:616
  38.9 2.6 %copy-start.16 = (s32[576,1]{1,0:T(8,128)S(1)}, s32[576,1]{1,0:T(8,128)}, u32[]{:S(2)}) copy-start(s32[576,1]{1,0:T(8,128)} %constant.44.back_ref) | copy-start | bytes 6916
  40.3 4.8 %collective-permute-start.9 = (bf16[24,1656]{1,0:T(8,128)(2,1)S(1)}, bf16[24,1656]{1,0:T(8,128)(2,1)S(1)}, u32[]{:S(2)}, u32[]{:S(2)}) collective-permute-start(bf16[24,1656]{1,0:T(8,128)(2,1)S(1)} %shard_map.226), channel_id=1, source_target_pairs={{0,8},{4,12},{8,0},{12,4},{16,24},{20,28},{24,16},{28,20},{1,9},{5... | collective-permute-start | bytes 238472 | tf_op jit(solution)/shard_map/ppermute | solution.py:635
  45.2 6.8 %collective-permute-start.10 = (bf16[24,1656]{1,0:T(8,128)(2,1)S(1)}, bf16[24,1656]{1,0:T(8,128)(2,1)S(1)}, u32[]{:S(2)}, u32[]{:S(2)}) collective-permute-start(bf16[24,1656]{1,0:T(8,128)(2,1)S(1)} %add_convert_fusion.3), channel_id=1, source_target_pairs={{0,16},{4,20},{8,24},{12,28},{16,0},{20,4},{24,8},{28,12},{1,17},{... | collective-permute-start | bytes 238472 | tf_op jit(solution)/shard_map/ppermute | solution.py:635
  50.7 5.6 %collective-permute-start.14 = (bf16[24,1656]{1,0:T(8,128)(2,1)S(1)}, bf16[24,1656]{1,0:T(8,128)(2,1)S(1)}, u32[]{:S(2)}, u32[]{:S(2)}) collective-permute-start(bf16[24,1656]{1,0:T(8,128)(2,1)S(1)} %get-tuple-element.124), channel_id=1, source_target_pairs={{0,4},{4,0},{8,12},{12,8},{16,20},{20,16},{24,28},{28,24},{1,5},{5... | collective-permute-start | bytes 238472 | tf_op jit(solution)/shard_map/ppermute | solution.py:635
  52.0 13.0 %copy-start.15 = (s32[576,1]{1,0:T(8,128)S(1)}, s32[576,1]{1,0:T(8,128)}, u32[]{:S(2)}) copy-start(s32[576,1]{1,0:T(8,128)} %constant.45.leave_ref) | copy-start | bytes 6916
  52.0 13.0 %copy-start.19 = (s32[144,1]{1,0:T(8,128)S(1)}, s32[144,1]{1,0:T(8,128)}, u32[]{:S(2)}) copy-start(s32[144,1]{1,0:T(8,128)} %constant.46.result_ref) | copy-start | bytes 1732
  52.9 5.2 %collective-permute-start.12 = (bf16[288,128]{1,0:T(8,128)(2,1)S(1)}, bf16[288,128]{1,0:T(8,128)(2,1)S(1)}, u32[]{:S(2)}, u32[]{:S(2)}) collective-permute-start(bf16[288,128]{1,0:T(8,128)(2,1)S(1)} %get-tuple-element.122), channel_id=1, source_target_pairs={{0,3},{1,0},{2,1},{3,2},{4,7},{5,4},{6,5},{7,6},{8,11},{9,8},{10,9... | collective-permute-start | bytes 221192 | tf_op jit(solution)/shard_map/ppermute | solution.py:619
  53.3 4.8 %collective-permute-start.13 = (bf16[192,128]{1,0:T(8,128)(2,1)S(1)}, bf16[192,128]{1,0:T(8,128)(2,1)S(1)}, u32[]{:S(2)}, u32[]{:S(2)}) collective-permute-start(bf16[192,128]{1,0:T(8,128)(2,1)S(1)} %get-tuple-element.123), channel_id=1, source_target_pairs={{0,31},{1,28},{2,29},{3,30},{4,3},{5,0},{6,1},{7,2},{8,7},{9,4},{1... | collective-permute-start | bytes 147464 | tf_op jit(solution)/shard_map/ppermute | solution.py:625
  58.1 5.0 %collective-permute-start.15 = (bf16[24,1656]{1,0:T(8,128)(2,1)S(1)}, bf16[24,1656]{1,0:T(8,128)(2,1)S(1)}, u32[]{:S(2)}, u32[]{:S(2)}) collective-permute-start(bf16[24,1656]{1,0:T(8,128)(2,1)S(1)} %add_convert_fusion.2), channel_id=1, source_target_pairs={{0,8},{4,12},{8,0},{12,4},{16,24},{20,28},{24,16},{28,20},{1,9},{5... | collective-permute-start | bytes 238472 | tf_op jit(solution)/shard_map/ppermute | solution.py:635
  60.0 5.1 %collective-permute-start.11 = (bf16[288,128]{1,0:T(8,128)(2,1)S(1)}, bf16[288,128]{1,0:T(8,128)(2,1)S(1)}, u32[]{:S(2)}, u32[]{:S(2)}) collective-permute-start(bf16[288,128]{1,0:T(8,128)(2,1)S(1)} %get-tuple-element.121), channel_id=1, source_target_pairs={{0,28},{4,0},{8,4},{12,8},{16,12},{20,16},{24,20},{28,24},{1,29},{... | collective-permute-start | bytes 221192 | tf_op jit(solution)/shard_map/ppermute | solution.py:616
  62.2 5.2 %collective-permute-start.17 = (bf16[24,1656]{1,0:T(8,128)(2,1)S(1)}, bf16[24,1656]{1,0:T(8,128)(2,1)S(1)}, u32[]{:S(2)}, u32[]{:S(2)}) collective-permute-start(bf16[24,1656]{1,0:T(8,128)(2,1)S(1)} %add_convert_fusion.coarse_kept), channel_id=1, source_target_pairs={{0,4},{4,0},{8,12},{12,8},{16,20},{20,16},{24,28},{28,24},{1,5},{5... | collective-permute-start | bytes 238472 | tf_op jit(solution)/shard_map/ppermute | solution.py:635
  63.2 7.1 %collective-permute-start.16 = (bf16[24,1656]{1,0:T(8,128)(2,1)S(1)}, bf16[24,1656]{1,0:T(8,128)(2,1)S(1)}, u32[]{:S(2)}, u32[]{:S(2)}) collective-permute-start(bf16[24,1656]{1,0:T(8,128)(2,1)S(1)} %add_convert_fusion.1.fine_kept), channel_id=1, source_target_pairs={{0,16},{4,20},{8,24},{12,28},{16,0},{20,4},{24,8},{28,12},{1,17},{... | collective-permute-start | bytes 238472 | tf_op jit(solution)/shard_map/ppermute | solution.py:635

commit v8 on v7

--- a/solution.py
+++ b/solution.py
@@ -761,7 +761,7 @@
         (*first_half, *second_half, n1_inner, r1_inner, n1, r1, fine_qkv, c10, c01, c00),
     ))
     alon, alat, adiag = send(fine_back[1:4], -1)
-    alat, adiag, other = lax.optimization_barrier((alat, adiag, other))
+    alat, other = lax.optimization_barrier((alat, other))
     fine_grad = add(fine_grad, other)
     for step in steps[1:]:
         fine_sums = (fine_grad, swap(fine_grad, step))

time: 71.3 us -> 70 us (0.982)
  waiting for transfers between devices: 10.4 us -> 9.62 us
    ppermute x6, starting transfers between devices: 4.76 us -> 7.1 us  [swap(): return lax.ppermute(value, 'lon', [(s, s ^ step) for s in range(count)])]
    ppermute x4, waiting for transfers between devices: 2.08 us -> 0.34 us  [move(): return lax.ppermute(value, ('lon', 'lat'), pairs)]
    ppermute x4, starting transfers between devices: 8.23 us -> 6.67 us  [move(): return lax.ppermute(value, ('lon', 'lat'), pairs)]
    ppermute x4, starting transfers between devices: 6.84 us -> 5.57 us  [move(): return lax.ppermute(value, 'lon', pairs)]
    ppermute x4, waiting for transfers between devices: 3.71 us -> 4.88 us  [move(): return lax.ppermute(value, 'lon', pairs)]
  transfers between devices with their start and end apart: 18 -> 18, of which waited for: 10 -> 8; matrix products, arithmetic and copies ran while one was open for 2% -> 2% of each run, Pallas kernels for 27% -> 27%
where the time goes in v8:
time: 70 us; the launch traced here: 69.9 us
  Pallas kernels  34.6 us (49%)
  starting transfers between devices  22.2 us (32%)
  waiting for transfers between devices  9.62 us (14%)
  local copies, waits for them, and re-layouts  2.04 us (3%)
  between operations  1.01 us (1%)
    pallas_call x12, Pallas kernels, run(): pl.pallas_call(kernel, out_shape=shapes, scratch_shapes=[pltpu.VMEM(shape...  34.6 us
    ppermute x6, starting transfers between devices, swap(): return lax.ppermute(value, 'lon', [(s, s ^ step) for s in range(count)])  7.1 us
    ppermute x4, starting transfers between devices, move(): return lax.ppermute(value, ('lon', 'lat'), pairs)  6.67 us
    ppermute x4, starting transfers between devices, move(): return lax.ppermute(value, 'lon', pairs)  5.57 us
    ppermute x4, waiting for transfers between devices, move(): return lax.ppermute(value, 'lon', pairs)  4.88 us
    ppermute x6, waiting for transfers between devices, swap(): return lax.ppermute(value, 'lon', [(s, s ^ step) for s in range(count)])  4.39 us
    ppermute x4, starting transfers between devices, move(): return lax.ppermute(value, 'lat', pairs)  2.87 us
    unnamed x43, local copies, waits for them, and re-layouts  1.8 us
  transfers between devices with their start and end apart: 18, of which 8 were waited for; matrix products, arithmetic and copies ran while one was open for 2% of the time, Pallas kernels for 27%

profile of v8, /device:TPU:0, one launch (start us, length us, event | category | flops | bytes accessed | tf_op | source)
XLA Modules:
  0.0 69.9 jit_solution(15275184000162127448)
XLA Ops:
  0.6 1.0 %copy-done.4 = bf16[2,12,24,192]{3,2,1,0:T(8,128)(2,1)S(1)} copy-done((bf16[2,12,24,192]{3,2,1,0:T(8,128)(2,1)S(1)}, bf16[2,12,24,192]{3,2,1,0:T(8,128)(2,1)}, u32[]{:S(2)}) %copy-start.4) | copy-done | bytes 221208
  1.6 0.1 shard_map.219
  1.7 2.5 %collective-permute-start.2 = (bf16[80,128]{1,0:T(8,128)(2,1)S(1)}, bf16[80,128]{1,0:T(8,128)(2,1)S(1)}, u32[]{:S(2)}, u32[]{:S(2)}) collective-permute-start(bf16[80,128]{1,0:T(8,128)(2,1)S(1)} %get-tuple-element.70), channel_id=1, source_target_pairs={{0,5},{1,6},{2,7},{3,4},{4,9},{5,10},{6,11},{7,8},{8,13},{9,14},{1... | collective-permute-start | bytes 61448 | tf_op jit(solution)/shard_map/ppermute | solution.py:625
  4.2 1.5 %collective-permute-start = (bf16[176,128]{1,0:T(8,128)(2,1)S(1)}, bf16[176,128]{1,0:T(8,128)(2,1)S(1)}, u32[]{:S(2)}, u32[]{:S(2)}) collective-permute-start(bf16[176,128]{1,0:T(8,128)(2,1)S(1)} %get-tuple-element.68), channel_id=1, source_target_pairs={{0,4},{4,8},{8,12},{12,16},{16,20},{20,24},{24,28},{28,0},{1,5},{5... | collective-permute-start | bytes 135176 | tf_op jit(solution)/shard_map/ppermute | solution.py:616
  5.7 1.3 %collective-permute-start.1 = (bf16[176,128]{1,0:T(8,128)(2,1)S(1)}, bf16[176,128]{1,0:T(8,128)(2,1)S(1)}, u32[]{:S(2)}, u32[]{:S(2)}) collective-permute-start(bf16[176,128]{1,0:T(8,128)(2,1)S(1)} %get-tuple-element.69), channel_id=1, source_target_pairs={{0,1},{1,2},{2,3},{3,0},{4,5},{5,6},{6,7},{7,4},{8,9},{9,10},{10,1... | collective-permute-start | bytes 135176 | tf_op jit(solution)/shard_map/ppermute | solution.py:619
  7.0 0.1 multiply_add_fusion
  7.1 0.1 reshape.48
  7.2 0.1 eq.28
  7.4 0.1 compare_select_fusion.refs_6_
  7.5 0.1 or_select_fusion.mask_ref
  7.7 0.0 copy-start.18
  7.7 2.3 %shard_map.220.refs_5_ = f32[1728,144]{1,0:T(8,128)S(1)} custom-call(f32[6,2,3312]{2,1,0:T(2,128)S(1)} %bitcast.20), custom_call_target="tpu_custom_call" | custom-call | flops 2000000000 | bytes 1154304 | tf_op jit(solution)/shard_map/pallas_call | solution.py:601
  10.0 0.9 %collective-permute-done.refs_1_ = bf16[176,128]{1,0:T(8,128)(2,1)S(1)} collective-permute-done((bf16[176,128]{1,0:T(8,128)(2,1)S(1)}, bf16[176,128]{1,0:T(8,128)(2,1)S(1)}, u32[]{:S(2)}, u32[]{:S(2)}) %collective-permute-start) | collective-permute-done | bytes 45088 | tf_op jit(solution)/shard_map/ppermute | solution.py:616
  11.0 6.0 %shard_map.221 = (bf16[288,128]{1,0:T(8,128)(2,1)S(1)}, bf16[288,128]{1,0:T(8,128)(2,1)S(1)}, bf16[192,128]{1,0:T(8,128)(2,1)S(1)}, bf16[48,384]{1,0:T(8,128)(2,...) custom-call(bf16[6,12,2,384]{3,2,1,0:T(2,128)(2,1)S(1)} %bitcast.22,, ...), custom_call_target="tpu_custom_call" | custom-call | flops 6000000000 | bytes 5298816 | tf_op jit(solution)/shard_map/pallas_call | solution.py:601
  17.0 0.6 collective-permute-start.5
  17.5 1.5 %collective-permute-start.3 = (bf16[288,128]{1,0:T(8,128)(2,1)S(1)}, bf16[288,128]{1,0:T(8,128)(2,1)S(1)}, u32[]{:S(2)}, u32[]{:S(2)}) collective-permute-start(bf16[288,128]{1,0:T(8,128)(2,1)S(1)} %get-tuple-element.74), channel_id=1, source_target_pairs={{0,4},{4,8},{8,12},{12,16},{16,20},{20,24},{24,28},{28,0},{1,5},{5... | collective-permute-start | bytes 221192 | tf_op jit(solution)/shard_map/ppermute | solution.py:616
  19.1 0.1 collective-permute-start.4
  19.2 2.3 %shard_map.223.bias_ref = f32[1728,144]{1,0:T(8,128)S(1)} custom-call(f32[12,1,3312]{2,1,0:T(1,128)S(1)} %bitcast.21), custom_call_target="tpu_custom_call" | custom-call | flops 2000000000 | bytes 1154304 | tf_op jit(solution)/shard_map/pallas_call | solution.py:601
  21.5 0.0 copy-start.14
  21.5 0.0 copy-start.17
  21.5 2.7 %shard_map.222 = (bf16[144,192]{1,0:T(8,128)(2,1)S(1)}, bf16[144,192]{1,0:T(8,128)(2,1)S(1)}, bf16[144,192]{1,0:T(8,128)(2,1)S(1)}, bf16[144,192]{1,0:T(8,128)(2...) custom-call(bf16[576,192]{1,0:T(8,128)(2,1)S(1)} %bitcast.15, ...), custom_call_target="tpu_custom_call" | custom-call | flops 2000000000 | bytes 3348864 | tf_op jit(solution)/shard_map/pallas_call | solution.py:601
  24.3 0.3 collective-permute-done.5.diag_ref
  24.6 0.9 %collective-permute-done.3.lon_ref = bf16[288,128]{1,0:T(8,128)(2,1)S(1)} collective-permute-done((bf16[288,128]{1,0:T(8,128)(2,1)S(1)}, bf16[288,128]{1,0:T(8,128)(2,1)S(1)}, u32[]{:S(2)}, u32[]{:S(2)}) %collective-permute-start.3) | collective-permute-done | bytes 73760 | tf_op jit(solution)/shard_map/ppermute | solution.py:616
  25.6 8.6 %shard_map.224 = (bf16[48,384]{1,0:T(8,128)(2,1)S(1)}, bf16[48,384]{1,0:T(8,128)(2,1)S(1)}, bf16[48,384]{1,0:T(8,128)(2,1)S(1)}, bf16[48,384]{1,0:T(8,128)(2,1)S...) custom-call(bf16[144,192]{1,0:T(8,128)(2,1)S(1)} %get-tuple-element., ...), custom_call_target="tpu_custom_call" | custom-call | flops 8999999488 | bytes 7048832 | tf_op jit(solution)/shard_map/pallas_call | solution.py:601
  34.2 1.1 %collective-permute-start.7 = (bf16[176,128]{1,0:T(8,128)(2,1)S(1)}, bf16[176,128]{1,0:T(8,128)(2,1)S(1)}, u32[]{:S(2)}, u32[]{:S(2)}) collective-permute-start(bf16[176,128]{1,0:T(8,128)(2,1)S(1)} %get-tuple-element.99), channel_id=1, source_target_pairs={{0,3},{1,0},{2,1},{3,2},{4,7},{5,4},{6,5},{7,6},{8,11},{9,8},{10,9... | collective-permute-start | bytes 135176 | tf_op jit(solution)/shard_map/ppermute | solution.py:619
  35.3 2.1 %collective-permute-start.8 = (bf16[80,128]{1,0:T(8,128)(2,1)S(1)}, bf16[80,128]{1,0:T(8,128)(2,1)S(1)}, u32[]{:S(2)}, u32[]{:S(2)}) collective-permute-start(bf16[80,128]{1,0:T(8,128)(2,1)S(1)} %get-tuple-element.102), channel_id=1, source_target_pairs={{0,31},{1,28},{2,29},{3,30},{4,3},{5,0},{6,1},{7,2},{8,7},{9,4},{1... | collective-permute-start | bytes 61448 | tf_op jit(solution)/shard_map/ppermute | solution.py:625
  37.4 1.5 %collective-permute-start.6 = (bf16[176,128]{1,0:T(8,128)(2,1)S(1)}, bf16[176,128]{1,0:T(8,128)(2,1)S(1)}, u32[]{:S(2)}, u32[]{:S(2)}) collective-permute-start(bf16[176,128]{1,0:T(8,128)(2,1)S(1)} %get-tuple-element.79), channel_id=1, source_target_pairs={{0,28},{4,0},{8,4},{12,8},{16,12},{20,16},{24,20},{28,24},{1,29},{... | collective-permute-start | bytes 135176 | tf_op jit(solution)/shard_map/ppermute | solution.py:616
  38.9 1.4 %shard_map.226 = bf16[24,1656]{1,0:T(8,128)(2,1)S(1)} custom-call(f32[1728,144]{1,0:T(8,128)S(1)} %get-tuple-element.104.score_ref), custom_call_target="tpu_custom_call" | custom-call | flops 2000000000 | bytes 1074816 | tf_op jit(solution)/shard_map/pallas_call | solution.py:601
  40.3 0.2 collective-permute-start.9
  40.5 1.0 %collective-permute-done.6.dlon_ref = bf16[176,128]{1,0:T(8,128)(2,1)S(1)} collective-permute-done((bf16[176,128]{1,0:T(8,128)(2,1)S(1)}, bf16[176,128]{1,0:T(8,128)(2,1)S(1)}, u32[]{:S(2)}, u32[]{:S(2)}) %collective-permute-start.6) | collective-permute-done | bytes 45088 | tf_op jit(solution)/shard_map/ppermute | solution.py:616
  41.6 3.6 %shard_map.225 = (f32[288,192]{1,0:T(8,128)S(1)}, bf16[288,192]{1,0:T(8,128)(2,1)S(1)}, bf16[288,192]{1,0:T(8,128)(2,1)S(1)}, bf16[288,192]{1,0:T(8,128)(2,1)S(1)}, f32[864,144]{1,0:T(8,128)S(1)}) custom-call(bf16[176,128]{1,0:T(8,128)(2,1)S(1)} %collective-permute-done.6.dlon_ref, bf16[336,192]{1,0:T(8,128)(2,1)S(1)} %get-tuple-element.80.dloc_ref, ...), custom_call_target="tpu_custom_call" | custom-call | flops 4000000000 | bytes 4657664 | tf_op jit(solution)/shard_map/pallas_call | solution.py:601
  45.2 0.9 %collective-permute-start.10 = (bf16[24,1656]{1,0:T(8,128)(2,1)S(1)}, bf16[24,1656]{1,0:T(8,128)(2,1)S(1)}, u32[]{:S(2)}, u32[]{:S(2)}) collective-permute-start(bf16[24,1656]{1,0:T(8,128)(2,1)S(1)} %add_convert_fusion.3), channel_id=1, source_target_pairs={{0,16},{4,20},{8,24},{12,28},{16,0},{20,4},{24,8},{28,12},{1,17},{... | collective-permute-start | bytes 238472 | tf_op jit(solution)/shard_map/ppermute | solution.py:635
  46.1 4.7 %shard_map.227 = (f32[288,192]{1,0:T(8,128)S(1)}, bf16[288,192]{1,0:T(8,128)(2,1)S(1)}, bf16[288,192]{1,0:T(8,128)(2,1)S(1)}, bf16[288,192]{1,0:T(8,128)(2,1)S(1)}, bf16[24,1656]{1,0:T(8,128)(2,1)S(1)}) custom-call(bf16[176,128]{1,0:T(8,128)(2,1)S(1)} %collective-permute-done.6.dlon_ref, bf16[336,192]{1,0:T(8,128)(2,1)S(1)} %get-tuple-element.80.dloc_ref, ...), custom_call_target="tpu_custom_call" | custom-call | flops 5000000000 | bytes 4110912 | tf_op jit(solution)/shard_map/pallas_call | solution.py:601
  50.7 0.9 %collective-permute-start.13 = (bf16[24,1656]{1,0:T(8,128)(2,1)S(1)}, bf16[24,1656]{1,0:T(8,128)(2,1)S(1)}, u32[]{:S(2)}, u32[]{:S(2)}) collective-permute-start(bf16[24,1656]{1,0:T(8,128)(2,1)S(1)} %get-tuple-element.122), channel_id=1, source_target_pairs={{0,4},{4,0},{8,12},{12,8},{16,20},{20,16},{24,28},{28,24},{1,5},{5... | collective-permute-start | bytes 238472 | tf_op jit(solution)/shard_map/ppermute | solution.py:635
  51.6 0.4 collective-permute-done.10
  52.0 0.8 %shard_map.228 = (bf16[576,192]{1,0:T(8,128)(2,1)S(1)}, bf16[288,128]{1,0:T(8,128)(2,1)S(1)}, bf16[288,128]{1,0:T(8,128)(2,1)S(1)}, bf16[192,128]{1,0:T(8,128)(2,1)S(1)}) custom-call(f32[288,192]{1,0:T(8,128)S(1)} %get-tuple-element.95.refs_0_, bf16[288,192]{1,0:T(8,128)(2,1)S(1)} %get-tuple-element.96.refs_1_, ...), custom_call_target="tpu_custom_call" | custom-call | flops 2000000000 | bytes 2078976 | tf_op jit(solution)/shard_map/pallas_call | solution.py:601
  52.9 0.4 collective-permute-start.12
  53.3 2.0 %collective-permute-done.13 = bf16[24,1656]{1,0:T(8,128)(2,1)S(1)} collective-permute-done((bf16[24,1656]{1,0:T(8,128)(2,1)S(1)}, bf16[24,1656]{1,0:T(8,128)(2,1)S(1)}, u32[]{:S(2)}, u32[]{:S(2)}) %collective-permute-start.13) | collective-permute-done | bytes 79520 | tf_op jit(solution)/shard_map/ppermute | solution.py:635
  55.4 3.0 %collective-permute-start.15 = (bf16[24,1656]{1,0:T(8,128)(2,1)S(1)}, bf16[24,1656]{1,0:T(8,128)(2,1)S(1)}, u32[]{:S(2)}, u32[]{:S(2)}) collective-permute-start(bf16[24,1656]{1,0:T(8,128)(2,1)S(1)} %add_convert_fusion.2), channel_id=1, source_target_pairs={{0,8},{4,12},{8,0},{12,4},{16,24},{20,28},{24,16},{28,20},{1,9},{5... | collective-permute-start | bytes 238472 | tf_op jit(solution)/shard_map/ppermute | solution.py:635
  58.4 1.5 %collective-permute-start.14 = (bf16[192,128]{1,0:T(8,128)(2,1)S(1)}, bf16[192,128]{1,0:T(8,128)(2,1)S(1)}, u32[]{:S(2)}, u32[]{:S(2)}) collective-permute-start(bf16[192,128]{1,0:T(8,128)(2,1)S(1)} %get-tuple-element.124), channel_id=1, source_target_pairs={{0,31},{1,28},{2,29},{3,30},{4,3},{5,0},{6,1},{7,2},{8,7},{9,4},{1... | collective-permute-start | bytes 147464 | tf_op jit(solution)/shard_map/ppermute | solution.py:625
  59.9 1.0 %collective-permute-start.11 = (bf16[288,128]{1,0:T(8,128)(2,1)S(1)}, bf16[288,128]{1,0:T(8,128)(2,1)S(1)}, u32[]{:S(2)}, u32[]{:S(2)}) collective-permute-start(bf16[288,128]{1,0:T(8,128)(2,1)S(1)} %get-tuple-element.120), channel_id=1, source_target_pairs={{0,28},{4,0},{8,4},{12,8},{16,12},{20,16},{24,20},{28,24},{1,29},{... | collective-permute-start | bytes 221192 | tf_op jit(solution)/shard_map/ppermute | solution.py:616
  60.9 1.1 %collective-permute-start.17 = (bf16[24,1656]{1,0:T(8,128)(2,1)S(1)}, bf16[24,1656]{1,0:T(8,128)(2,1)S(1)}, u32[]{:S(2)}, u32[]{:S(2)}) collective-permute-start(bf16[24,1656]{1,0:T(8,128)(2,1)S(1)} %add_convert_fusion.coarse_kept), channel_id=1, source_target_pairs={{0,4},{4,0},{8,12},{12,8},{16,20},{20,16},{24,28},{28,24},{1,5},{5... | collective-permute-start | bytes 238472 | tf_op jit(solution)/shard_map/ppermute | solution.py:635
  62.0 1.1 %collective-permute-start.16 = (bf16[24,1656]{1,0:T(8,128)(2,1)S(1)}, bf16[24,1656]{1,0:T(8,128)(2,1)S(1)}, u32[]{:S(2)}, u32[]{:S(2)}) collective-permute-start(bf16[24,1656]{1,0:T(8,128)(2,1)S(1)} %add_convert_fusion.1.fine_kept), channel_id=1, source_target_pairs={{0,16},{4,20},{8,24},{12,28},{16,0},{20,4},{24,8},{28,12},{1,17},{... | collective-permute-start | bytes 238472 | tf_op jit(solution)/shard_map/ppermute | solution.py:635
  63.1 2.0 %collective-permute-done.11.lon_ref = bf16[288,128]{1,0:T(8,128)(2,1)S(1)} collective-permute-done((bf16[288,128]{1,0:T(8,128)(2,1)S(1)}, bf16[288,128]{1,0:T(8,128)(2,1)S(1)}, u32[]{:S(2)}, u32[]{:S(2)}) %collective-permute-start.11) | collective-permute-done | bytes 73760 | tf_op jit(solution)/shard_map/ppermute | solution.py:616
  65.1 1.3 %shard_map.229 = (bf16[576,192]{1,0:T(8,128)(2,1)}, bf16[2,6,12,384]{3,2,1,0:T(8,128)(2,1)S(1)}) custom-call(bf16[576,192]{1,0:T(8,128)(2,1)S(1)} %get-tuple-element.119.res_ref, bf16[288,128]{1,0:T(8,128)(2,1)S(1)} %collective-permute-done.11.lon_ref, bf16[288,128]{1,0:T(8,128)(2,1)S(1)} %collective-permute-done.12.lat_ref, ...), custom_call_target="tpu_custom_call" | custom-call | flops 1000000000 | bytes 789312 | tf_op jit(solution)/shard_map/pallas_call | solution.py:601
  66.4 0.7 %copy.27 = bf16[2,6,12,384]{3,0,2,1:T(2,128)(2,1)} copy(bf16[2,6,12,384]{3,2,1,0:T(8,128)(2,1)S(1)} %get-tuple-element.136) | data formatting | bytes 221184
  67.2 1.9 %collective-permute-done.16.fine_other = bf16[24,1656]{1,0:T(8,128)(2,1)S(1)} collective-permute-done((bf16[24,1656]{1,0:T(8,128)(2,1)S(1)}, bf16[24,1656]{1,0:T(8,128)(2,1)S(1)}, u32[]{:S(2)}, u32[]{:S(2)}) %collective-permute-start.16) | collective-permute-done | bytes 79520 | tf_op jit(solution)/shard_map/ppermute | solution.py:635
  69.1 0.8 %shard_map.230 = (f32[6,2,3312]{2,1,0:T(2,128)}, f32[12,1,3312]{2,1,0:T(1,128)}) custom-call(bf16[24,1656]{1,0:T(8,128)(2,1)S(1)} %add_convert_fusion.1.fine_kept, bf16[24,1656]{1,0:T(8,128)(2,1)S(1)} %collective-permute-done.16.fine_other, bf16[24,1656]{1,0:T(8,128)(2,1)S(1)} %add_convert_fusion.coarse_kept, ...), custom_call_target="tpu_custom_call" | custom-call | flops 1000000000 | bytes 635904 | tf_op jit(solution)/shard_map/pallas_call | solution.py:601
  (55 shorter events, 0.3 us)
Async XLA Ops:
  0.6 1.0 %copy-start.4 = (bf16[2,12,24,192]{3,2,1,0:T(8,128)(2,1)S(1)}, bf16[2,12,24,192]{3,2,1,0:T(8,128)(2,1)}, u32[]{:S(2)}) copy-start(bf16[2,12,24,192]{3,2,1,0:T(8,128)(2,1)} %param.20) | copy-start | bytes 663556
  1.6 5.4 %copy-start.20 = (s32[2,12,24]{2,0,1:T(2,128)S(1)}, s32[2,12,24]{2,0,1:T(2,128)}, u32[]{:S(2)}) copy-start(s32[2,12,24]{2,0,1:T(2,128)} %param.21) | copy-start | bytes 6916
  1.6 6.0 %copy-start.10 = (f32[2,6,3312]{2,0,1:T(2,128)S(1)}, f32[2,6,3312]{2,0,1:T(2,128)}, u32[]{:S(2)}) copy-start(f32[2,6,3312]{2,0,1:T(2,128)} %param.26) | copy-start | bytes 476932
  1.7 8.3 %collective-permute-start.2 = (bf16[80,128]{1,0:T(8,128)(2,1)S(1)}, bf16[80,128]{1,0:T(8,128)(2,1)S(1)}, u32[]{:S(2)}, u32[]{:S(2)}) collective-permute-start(bf16[80,128]{1,0:T(8,128)(2,1)S(1)} %get-tuple-element.70), channel_id=1, source_target_pairs={{0,5},{1,6},{2,7},{3,4},{4,9},{5,10},{6,11},{7,8},{8,13},{9,14},{1... | collective-permute-start | bytes 61448 | tf_op jit(solution)/shard_map/ppermute | solution.py:625
  4.2 6.7 %collective-permute-start = (bf16[176,128]{1,0:T(8,128)(2,1)S(1)}, bf16[176,128]{1,0:T(8,128)(2,1)S(1)}, u32[]{:S(2)}, u32[]{:S(2)}) collective-permute-start(bf16[176,128]{1,0:T(8,128)(2,1)S(1)} %get-tuple-element.68), channel_id=1, source_target_pairs={{0,4},{4,8},{8,12},{12,16},{16,20},{20,24},{24,28},{28,0},{1,5},{5... | collective-permute-start | bytes 135176 | tf_op jit(solution)/shard_map/ppermute | solution.py:616
  5.7 5.2 %collective-permute-start.1 = (bf16[176,128]{1,0:T(8,128)(2,1)S(1)}, bf16[176,128]{1,0:T(8,128)(2,1)S(1)}, u32[]{:S(2)}, u32[]{:S(2)}) collective-permute-start(bf16[176,128]{1,0:T(8,128)(2,1)S(1)} %get-tuple-element.69), channel_id=1, source_target_pairs={{0,1},{1,2},{2,3},{3,0},{4,5},{5,6},{6,7},{7,4},{8,9},{9,10},{10,1... | collective-permute-start | bytes 135176 | tf_op jit(solution)/shard_map/ppermute | solution.py:619
  7.6 3.3 %copy-start.5 = (bf16[2,12,24,192]{3,2,1,0:T(8,128)(2,1)S(1)}, bf16[2,12,24,192]{3,2,1,0:T(8,128)(2,1)}, u32[]{:S(2)}) copy-start(bf16[2,12,24,192]{3,2,1,0:T(8,128)(2,1)} %param.20) | copy-start | bytes 663556
  7.6 3.3 %copy-start.7 = (bf16[192,768]{1,0:T(8,128)(2,1)S(1)}, bf16[192,768]{1,0:T(8,128)(2,1)}, u32[]{:S(2)}) copy-start(bf16[192,768]{1,0:T(8,128)(2,1)} %refs_8_.5) | copy-start | bytes 884740
  7.7 3.3 %copy-start.8 = (bf16[768,192]{0,1:T(8,128)(2,1)S(1)}, bf16[768,192]{0,1:T(8,128)(2,1)}, u32[]{:S(2)}) copy-start(bf16[768,192]{0,1:T(8,128)(2,1)} %param.25) | copy-start | bytes 884740
  7.7 3.3 %copy-start.9 = (bf16[192,576]{1,0:T(8,128)(2,1)S(1)}, bf16[192,576]{1,0:T(8,128)(2,1)}, u32[]{:S(2)}) copy-start(bf16[192,576]{1,0:T(8,128)(2,1)} %refs_12_.1) | copy-start | bytes 663556
  7.7 3.3 %copy-start.12 = (bf16[2,6,12,384]{3,0,2,1:T(2,128)(2,1)S(1)}, bf16[2,6,12,384]{3,0,2,1:T(2,128)(2,1)}, u32[]{:S(2)}) copy-start(bf16[2,6,12,384]{3,0,2,1:T(2,128)(2,1)} %param.33) | copy-start | bytes 331780
  7.7 3.3 %copy-start.13 = (bf16[192,192]{1,0:T(8,128)(2,1)S(1)}, bf16[192,192]{1,0:T(8,128)(2,1)}, u32[]{:S(2)}) copy-start(bf16[192,192]{1,0:T(8,128)(2,1)} %refs_7_.5) | copy-start | bytes 221188
  7.7 3.3 %copy-start.18 = (s32[576,1]{1,0:T(8,128)S(1)}, s32[576,1]{1,0:T(8,128)}, u32[]{:S(2)}) copy-start(s32[576,1]{1,0:T(8,128)} %constant.41.refs_4_) | copy-start | bytes 6916
  11.0 8.2 %copy-start.11 = (f32[1,12,3312]{2,0,1:T(1,128)S(1)}, f32[1,12,3312]{2,0,1:T(1,128)}, u32[]{:S(2)}) copy-start(f32[1,12,3312]{2,0,1:T(1,128)} %param.32) | copy-start | bytes 476932
  17.0 7.7 %collective-permute-start.5 = (bf16[192,128]{1,0:T(8,128)(2,1)S(1)}, bf16[192,128]{1,0:T(8,128)(2,1)S(1)}, u32[]{:S(2)}, u32[]{:S(2)}) collective-permute-start(bf16[192,128]{1,0:T(8,128)(2,1)S(1)} %get-tuple-element.76), channel_id=1, source_target_pairs={{0,5},{1,6},{2,7},{3,4},{4,9},{5,10},{6,11},{7,8},{8,13},{9,14},{1... | collective-permute-start | bytes 147464 | tf_op jit(solution)/shard_map/ppermute | solution.py:625
  17.5 8.0 %collective-permute-start.3 = (bf16[288,128]{1,0:T(8,128)(2,1)S(1)}, bf16[288,128]{1,0:T(8,128)(2,1)S(1)}, u32[]{:S(2)}, u32[]{:S(2)}) collective-permute-start(bf16[288,128]{1,0:T(8,128)(2,1)S(1)} %get-tuple-element.74), channel_id=1, source_target_pairs={{0,4},{4,8},{8,12},{12,16},{16,20},{20,24},{24,28},{28,0},{1,5},{5... | collective-permute-start | bytes 221192 | tf_op jit(solution)/shard_map/ppermute | solution.py:616
  19.1 6.5 %collective-permute-start.4 = (bf16[288,128]{1,0:T(8,128)(2,1)S(1)}, bf16[288,128]{1,0:T(8,128)(2,1)S(1)}, u32[]{:S(2)}, u32[]{:S(2)}) collective-permute-start(bf16[288,128]{1,0:T(8,128)(2,1)S(1)} %get-tuple-element.75), channel_id=1, source_target_pairs={{0,1},{1,2},{2,3},{3,0},{4,5},{5,6},{6,7},{7,4},{8,9},{9,10},{10,1... | collective-permute-start | bytes 221192 | tf_op jit(solution)/shard_map/ppermute | solution.py:619
  21.5 4.1 %copy-start = (bf16[384,1536]{1,0:T(8,128)(2,1)S(1)}, bf16[384,1536]{1,0:T(8,128)(2,1)}, u32[]{:S(2)}) copy-start(bf16[384,1536]{1,0:T(8,128)(2,1)} %up_ref.1) | copy-start | bytes 3538948
  21.5 4.1 %copy-start.1 = (bf16[1536,384]{1,0:T(8,128)(2,1)S(1)}, bf16[1536,384]{1,0:T(8,128)(2,1)}, u32[]{:S(2)}) copy-start(bf16[1536,384]{1,0:T(8,128)(2,1)} %down_ref.1) | copy-start | bytes 3538948
  21.5 4.1 %copy-start.2 = (bf16[384,1152]{1,0:T(8,128)(2,1)S(1)}, bf16[384,1152]{1,0:T(8,128)(2,1)}, u32[]{:S(2)}) copy-start(bf16[384,1152]{1,0:T(8,128)(2,1)} %qkv_ref.1) | copy-start | bytes 2654212
  21.5 4.1 %copy-start.3 = (bf16[768,384]{1,0:T(8,128)(2,1)S(1)}, bf16[768,384]{1,0:T(8,128)(2,1)}, u32[]{:S(2)}) copy-start(bf16[768,384]{1,0:T(8,128)(2,1)} %reduce_ref.1) | copy-start | bytes 1769476
  21.5 4.1 %copy-start.6 = (bf16[384,384]{1,0:T(8,128)(2,1)S(1)}, bf16[384,384]{1,0:T(8,128)(2,1)}, u32[]{:S(2)}) copy-start(bf16[384,384]{1,0:T(8,128)(2,1)} %proj_ref.1) | copy-start | bytes 884740
  21.5 4.1 %copy-start.14 = (s32[608,1]{1,0:T(8,128)S(1)}, s32[608,1]{1,0:T(8,128)}, u32[]{:S(2)}) copy-start(s32[608,1]{1,0:T(8,128)} %constant.43.split_ref) | copy-start | bytes 7300
  21.5 4.1 %copy-start.17 = (s32[576,1]{1,0:T(8,128)S(1)}, s32[576,1]{1,0:T(8,128)}, u32[]{:S(2)}) copy-start(s32[576,1]{1,0:T(8,128)} %constant.42.merge_ref) | copy-start | bytes 6916
  34.2 4.7 %collective-permute-start.7 = (bf16[176,128]{1,0:T(8,128)(2,1)S(1)}, bf16[176,128]{1,0:T(8,128)(2,1)S(1)}, u32[]{:S(2)}, u32[]{:S(2)}) collective-permute-start(bf16[176,128]{1,0:T(8,128)(2,1)S(1)} %get-tuple-element.99), channel_id=1, source_target_pairs={{0,3},{1,0},{2,1},{3,2},{4,7},{5,4},{6,5},{7,6},{8,11},{9,8},{10,9... | collective-permute-start | bytes 135176 | tf_op jit(solution)/shard_map/ppermute | solution.py:619
  35.3 10.8 %collective-permute-start.8 = (bf16[80,128]{1,0:T(8,128)(2,1)S(1)}, bf16[80,128]{1,0:T(8,128)(2,1)S(1)}, u32[]{:S(2)}, u32[]{:S(2)}) collective-permute-start(bf16[80,128]{1,0:T(8,128)(2,1)S(1)} %get-tuple-element.102), channel_id=1, source_target_pairs={{0,31},{1,28},{2,29},{3,30},{4,3},{5,0},{6,1},{7,2},{8,7},{9,4},{1... | collective-permute-start | bytes 61448 | tf_op jit(solution)/shard_map/ppermute | solution.py:625
  37.4 4.2 %collective-permute-start.6 = (bf16[176,128]{1,0:T(8,128)(2,1)S(1)}, bf16[176,128]{1,0:T(8,128)(2,1)S(1)}, u32[]{:S(2)}, u32[]{:S(2)}) collective-permute-start(bf16[176,128]{1,0:T(8,128)(2,1)S(1)} %get-tuple-element.79), channel_id=1, source_target_pairs={{0,28},{4,0},{8,4},{12,8},{16,12},{20,16},{24,20},{28,24},{1,29},{... | collective-permute-start | bytes 135176 | tf_op jit(solution)/shard_map/ppermute | solution.py:616
  38.9 2.6 %copy-start.16 = (s32[576,1]{1,0:T(8,128)S(1)}, s32[576,1]{1,0:T(8,128)}, u32[]{:S(2)}) copy-start(s32[576,1]{1,0:T(8,128)} %constant.44.back_ref) | copy-start | bytes 6916
  40.3 4.8 %collective-permute-start.9 = (bf16[24,1656]{1,0:T(8,128)(2,1)S(1)}, bf16[24,1656]{1,0:T(8,128)(2,1)S(1)}, u32[]{:S(2)}, u32[]{:S(2)}) collective-permute-start(bf16[24,1656]{1,0:T(8,128)(2,1)S(1)} %shard_map.226), channel_id=1, source_target_pairs={{0,8},{4,12},{8,0},{12,4},{16,24},{20,28},{24,16},{28,20},{1,9},{5... | collective-permute-start | bytes 238472 | tf_op jit(solution)/shard_map/ppermute | solution.py:635
  45.2 6.8 %collective-permute-start.10 = (bf16[24,1656]{1,0:T(8,128)(2,1)S(1)}, bf16[24,1656]{1,0:T(8,128)(2,1)S(1)}, u32[]{:S(2)}, u32[]{:S(2)}) collective-permute-start(bf16[24,1656]{1,0:T(8,128)(2,1)S(1)} %add_convert_fusion.3), channel_id=1, source_target_pairs={{0,16},{4,20},{8,24},{12,28},{16,0},{20,4},{24,8},{28,12},{1,17},{... | collective-permute-start | bytes 238472 | tf_op jit(solution)/shard_map/ppermute | solution.py:635
  50.7 4.6 %collective-permute-start.13 = (bf16[24,1656]{1,0:T(8,128)(2,1)S(1)}, bf16[24,1656]{1,0:T(8,128)(2,1)S(1)}, u32[]{:S(2)}, u32[]{:S(2)}) collective-permute-start(bf16[24,1656]{1,0:T(8,128)(2,1)S(1)} %get-tuple-element.122), channel_id=1, source_target_pairs={{0,4},{4,0},{8,12},{12,8},{16,20},{20,16},{24,28},{28,24},{1,5},{5... | collective-permute-start | bytes 238472 | tf_op jit(solution)/shard_map/ppermute | solution.py:635
  52.0 13.0 %copy-start.15 = (s32[576,1]{1,0:T(8,128)S(1)}, s32[576,1]{1,0:T(8,128)}, u32[]{:S(2)}) copy-start(s32[576,1]{1,0:T(8,128)} %constant.45.leave_ref) | copy-start | bytes 6916
  52.0 13.0 %copy-start.19 = (s32[144,1]{1,0:T(8,128)S(1)}, s32[144,1]{1,0:T(8,128)}, u32[]{:S(2)}) copy-start(s32[144,1]{1,0:T(8,128)} %constant.46.result_ref) | copy-start | bytes 1732
  52.9 2.4 %collective-permute-start.12 = (bf16[288,128]{1,0:T(8,128)(2,1)S(1)}, bf16[288,128]{1,0:T(8,128)(2,1)S(1)}, u32[]{:S(2)}, u32[]{:S(2)}) collective-permute-start(bf16[288,128]{1,0:T(8,128)(2,1)S(1)} %get-tuple-element.121), channel_id=1, source_target_pairs={{0,3},{1,0},{2,1},{3,2},{4,7},{5,4},{6,5},{7,6},{8,11},{9,8},{10,9... | collective-permute-start | bytes 221192 | tf_op jit(solution)/shard_map/ppermute | solution.py:619
  55.4 6.6 %collective-permute-start.15 = (bf16[24,1656]{1,0:T(8,128)(2,1)S(1)}, bf16[24,1656]{1,0:T(8,128)(2,1)S(1)}, u32[]{:S(2)}, u32[]{:S(2)}) collective-permute-start(bf16[24,1656]{1,0:T(8,128)(2,1)S(1)} %add_convert_fusion.2), channel_id=1, source_target_pairs={{0,8},{4,12},{8,0},{12,4},{16,24},{20,28},{24,16},{28,20},{1,9},{5... | collective-permute-start | bytes 238472 | tf_op jit(solution)/shard_map/ppermute | solution.py:635
  58.4 4.7 %collective-permute-start.14 = (bf16[192,128]{1,0:T(8,128)(2,1)S(1)}, bf16[192,128]{1,0:T(8,128)(2,1)S(1)}, u32[]{:S(2)}, u32[]{:S(2)}) collective-permute-start(bf16[192,128]{1,0:T(8,128)(2,1)S(1)} %get-tuple-element.124), channel_id=1, source_target_pairs={{0,31},{1,28},{2,29},{3,30},{4,3},{5,0},{6,1},{7,2},{8,7},{9,4},{1... | collective-permute-start | bytes 147464 | tf_op jit(solution)/shard_map/ppermute | solution.py:625
  59.9 5.2 %collective-permute-start.11 = (bf16[288,128]{1,0:T(8,128)(2,1)S(1)}, bf16[288,128]{1,0:T(8,128)(2,1)S(1)}, u32[]{:S(2)}, u32[]{:S(2)}) collective-permute-start(bf16[288,128]{1,0:T(8,128)(2,1)S(1)} %get-tuple-element.120), channel_id=1, source_target_pairs={{0,28},{4,0},{8,4},{12,8},{16,12},{20,16},{24,20},{28,24},{1,29},{... | collective-permute-start | bytes 221192 | tf_op jit(solution)/shard_map/ppermute | solution.py:616
  60.9 6.3 %collective-permute-start.17 = (bf16[24,1656]{1,0:T(8,128)(2,1)S(1)}, bf16[24,1656]{1,0:T(8,128)(2,1)S(1)}, u32[]{:S(2)}, u32[]{:S(2)}) collective-permute-start(bf16[24,1656]{1,0:T(8,128)(2,1)S(1)} %add_convert_fusion.coarse_kept), channel_id=1, source_target_pairs={{0,4},{4,0},{8,12},{12,8},{16,20},{20,16},{24,28},{28,24},{1,5},{5... | collective-permute-start | bytes 238472 | tf_op jit(solution)/shard_map/ppermute | solution.py:635
  62.0 7.1 %collective-permute-start.16 = (bf16[24,1656]{1,0:T(8,128)(2,1)S(1)}, bf16[24,1656]{1,0:T(8,128)(2,1)S(1)}, u32[]{:S(2)}, u32[]{:S(2)}) collective-permute-start(bf16[24,1656]{1,0:T(8,128)(2,1)S(1)} %add_convert_fusion.1.fine_kept), channel_id=1, source_target_pairs={{0,16},{4,20},{8,24},{12,28},{16,0},{20,4},{24,8},{28,12},{1,17},{... | collective-permute-start | bytes 238472 | tf_op jit(solution)/shard_map/ppermute | solution.py:635

commit v9 on v8

--- a/solution.py
+++ b/solution.py
@@ -752,9 +752,6 @@
     )
     second_half[0], other = lax.optimization_barrier((second_half[0], other))
     coarse_grad = add(coarse_grad, other)
-    for step in (*steps[2:-1], steps[0]):
-        coarse_sums = (coarse_grad, swap(coarse_grad, step))
-        coarse_grad = add(*coarse_sums)
     other = swap(fine_grad, steps[0])
     fine_back = list(run(
         qkv_back_kernel, [tok] + wide_edges, [], 2,
@@ -766,6 +763,11 @@
     for step in steps[1:]:
         fine_sums = (fine_grad, swap(fine_grad, step))
         fine_grad = add(*fine_sums)
+    coarse_grad, ready = lax.optimization_barrier((coarse_grad, fine_sums[0]))
+    fine_sums = (ready, fine_sums[1])
+    for step in (*steps[2:-1], steps[0]):
+        coarse_sums = (coarse_grad, swap(coarse_grad, step))
+        coarse_grad = add(*coarse_sums)
     d_tokens, coarse_result = run(
         last_kernel,
         [tok, ((2, 6, 12, 384), bf16)],

time: 70 us -> 69.7 us (level)
  transfers between devices with their start and end apart: 18 -> 18, of which waited for: 8 -> 9; matrix products, arithmetic and copies ran while one was open for 2% -> 2% of each run, Pallas kernels for 27% -> 27%
where the time goes in v9:
time: 69.7 us; the launch traced here: 69.6 us
  Pallas kernels  34.6 us (50%)
  starting transfers between devices  22.5 us (32%)
  waiting for transfers between devices  8.94 us (13%)
  local copies, waits for them, and re-layouts  2.04 us (3%)
  between operations  1.01 us (1%)
    pallas_call x12, Pallas kernels, run(): pl.pallas_call(kernel, out_shape=shapes, scratch_shapes=[pltpu.VMEM(shape...  34.6 us
    ppermute x6, starting transfers between devices, swap(): return lax.ppermute(value, 'lon', [(s, s ^ step) for s in range(count)])  7.45 us
    ppermute x4, starting transfers between devices, move(): return lax.ppermute(value, ('lon', 'lat'), pairs)  6.67 us
    ppermute x4, starting transfers between devices, move(): return lax.ppermute(value, 'lon', pairs)  5.57 us
    ppermute x6, waiting for transfers between devices, swap(): return lax.ppermute(value, 'lon', [(s, s ^ step) for s in range(count)])  4.36 us
    ppermute x4, waiting for transfers between devices, move(): return lax.ppermute(value, 'lon', pairs)  4.23 us
    ppermute x4, starting transfers between devices, move(): return lax.ppermute(value, 'lat', pairs)  2.87 us
    unnamed x43, local copies, waits for them, and re-layouts  1.8 us
  transfers between devices with their start and end apart: 18, of which 9 were waited for; matrix products, arithmetic and copies ran while one was open for 2% of the time, Pallas kernels for 27%

profile of v9, /device:TPU:0, one launch (start us, length us, event | category | flops | bytes accessed | tf_op | source)
XLA Modules:
  0.0 69.6 jit_solution(8340465412805367752)
XLA Ops:
  0.6 1.0 %copy-done.4 = bf16[2,12,24,192]{3,2,1,0:T(8,128)(2,1)S(1)} copy-done((bf16[2,12,24,192]{3,2,1,0:T(8,128)(2,1)S(1)}, bf16[2,12,24,192]{3,2,1,0:T(8,128)(2,1)}, u32[]{:S(2)}) %copy-start.4) | copy-done | bytes 221208
  1.6 0.1 shard_map.219
  1.7 2.5 %collective-permute-start.2 = (bf16[80,128]{1,0:T(8,128)(2,1)S(1)}, bf16[80,128]{1,0:T(8,128)(2,1)S(1)}, u32[]{:S(2)}, u32[]{:S(2)}) collective-permute-start(bf16[80,128]{1,0:T(8,128)(2,1)S(1)} %get-tuple-element.72), channel_id=1, source_target_pairs={{0,5},{1,6},{2,7},{3,4},{4,9},{5,10},{6,11},{7,8},{8,13},{9,14},{1... | collective-permute-start | bytes 61448 | tf_op jit(solution)/shard_map/ppermute | solution.py:625
  4.2 1.5 %collective-permute-start = (bf16[176,128]{1,0:T(8,128)(2,1)S(1)}, bf16[176,128]{1,0:T(8,128)(2,1)S(1)}, u32[]{:S(2)}, u32[]{:S(2)}) collective-permute-start(bf16[176,128]{1,0:T(8,128)(2,1)S(1)} %get-tuple-element.70), channel_id=1, source_target_pairs={{0,4},{4,8},{8,12},{12,16},{16,20},{20,24},{24,28},{28,0},{1,5},{5... | collective-permute-start | bytes 135176 | tf_op jit(solution)/shard_map/ppermute | solution.py:616
  5.7 1.3 %collective-permute-start.1 = (bf16[176,128]{1,0:T(8,128)(2,1)S(1)}, bf16[176,128]{1,0:T(8,128)(2,1)S(1)}, u32[]{:S(2)}, u32[]{:S(2)}) collective-permute-start(bf16[176,128]{1,0:T(8,128)(2,1)S(1)} %get-tuple-element.71), channel_id=1, source_target_pairs={{0,1},{1,2},{2,3},{3,0},{4,5},{5,6},{6,7},{7,4},{8,9},{9,10},{10,1... | collective-permute-start | bytes 135176 | tf_op jit(solution)/shard_map/ppermute | solution.py:619
  7.0 0.1 multiply_add_fusion
  7.1 0.1 reshape.48
  7.2 0.1 eq.28
  7.4 0.1 compare_select_fusion.refs_6_
  7.5 0.1 or_select_fusion.mask_ref
  7.7 0.0 copy-start.18
  7.7 2.3 %shard_map.220.refs_5_ = f32[1728,144]{1,0:T(8,128)S(1)} custom-call(f32[6,2,3312]{2,1,0:T(2,128)S(1)} %bitcast.20), custom_call_target="tpu_custom_call" | custom-call | flops 2000000000 | bytes 1154304 | tf_op jit(solution)/shard_map/pallas_call | solution.py:601
  10.0 0.9 %collective-permute-done.refs_1_ = bf16[176,128]{1,0:T(8,128)(2,1)S(1)} collective-permute-done((bf16[176,128]{1,0:T(8,128)(2,1)S(1)}, bf16[176,128]{1,0:T(8,128)(2,1)S(1)}, u32[]{:S(2)}, u32[]{:S(2)}) %collective-permute-start) | collective-permute-done | bytes 45088 | tf_op jit(solution)/shard_map/ppermute | solution.py:616
  11.0 6.0 %shard_map.221 = (bf16[288,128]{1,0:T(8,128)(2,1)S(1)}, bf16[288,128]{1,0:T(8,128)(2,1)S(1)}, bf16[192,128]{1,0:T(8,128)(2,1)S(1)}, bf16[48,384]{1,0:T(8,128)(2,...) custom-call(bf16[6,12,2,384]{3,2,1,0:T(2,128)(2,1)S(1)} %bitcast.22,, ...), custom_call_target="tpu_custom_call" | custom-call | flops 6000000000 | bytes 5298816 | tf_op jit(solution)/shard_map/pallas_call | solution.py:601
  17.0 0.6 collective-permute-start.5
  17.5 1.5 %collective-permute-start.3 = (bf16[288,128]{1,0:T(8,128)(2,1)S(1)}, bf16[288,128]{1,0:T(8,128)(2,1)S(1)}, u32[]{:S(2)}, u32[]{:S(2)}) collective-permute-start(bf16[288,128]{1,0:T(8,128)(2,1)S(1)} %get-tuple-element.76), channel_id=1, source_target_pairs={{0,4},{4,8},{8,12},{12,16},{16,20},{20,24},{24,28},{28,0},{1,5},{5... | collective-permute-start | bytes 221192 | tf_op jit(solution)/shard_map/ppermute | solution.py:616
  19.1 0.1 collective-permute-start.4
  19.2 2.3 %shard_map.223.bias_ref = f32[1728,144]{1,0:T(8,128)S(1)} custom-call(f32[12,1,3312]{2,1,0:T(1,128)S(1)} %bitcast.21), custom_call_target="tpu_custom_call" | custom-call | flops 2000000000 | bytes 1154304 | tf_op jit(solution)/shard_map/pallas_call | solution.py:601
  21.5 2.7 %shard_map.222 = (bf16[144,192]{1,0:T(8,128)(2,1)S(1)}, bf16[144,192]{1,0:T(8,128)(2,1)S(1)}, bf16[144,192]{1,0:T(8,128)(2,1)S(1)}, bf16[144,192]{1,0:T(8,128)(2...) custom-call(bf16[576,192]{1,0:T(8,128)(2,1)S(1)} %bitcast.15, ...), custom_call_target="tpu_custom_call" | custom-call | flops 2000000000 | bytes 3348864 | tf_op jit(solution)/shard_map/pallas_call | solution.py:601
  24.3 0.3 collective-permute-done.5.diag_ref
  24.6 0.9 %collective-permute-done.3.lon_ref = bf16[288,128]{1,0:T(8,128)(2,1)S(1)} collective-permute-done((bf16[288,128]{1,0:T(8,128)(2,1)S(1)}, bf16[288,128]{1,0:T(8,128)(2,1)S(1)}, u32[]{:S(2)}, u32[]{:S(2)}) %collective-permute-start.3) | collective-permute-done | bytes 73760 | tf_op jit(solution)/shard_map/ppermute | solution.py:616
  25.6 8.6 %shard_map.224 = (bf16[48,384]{1,0:T(8,128)(2,1)S(1)}, bf16[48,384]{1,0:T(8,128)(2,1)S(1)}, bf16[48,384]{1,0:T(8,128)(2,1)S(1)}, bf16[48,384]{1,0:T(8,128)(2,1)S...) custom-call(bf16[144,192]{1,0:T(8,128)(2,1)S(1)} %get-tuple-element., ...), custom_call_target="tpu_custom_call" | custom-call | flops 8999999488 | bytes 7048832 | tf_op jit(solution)/shard_map/pallas_call | solution.py:601
  34.2 1.1 %collective-permute-start.7 = (bf16[176,128]{1,0:T(8,128)(2,1)S(1)}, bf16[176,128]{1,0:T(8,128)(2,1)S(1)}, u32[]{:S(2)}, u32[]{:S(2)}) collective-permute-start(bf16[176,128]{1,0:T(8,128)(2,1)S(1)} %get-tuple-element.101), channel_id=1, source_target_pairs={{0,3},{1,0},{2,1},{3,2},{4,7},{5,4},{6,5},{7,6},{8,11},{9,8},{10,9... | collective-permute-start | bytes 135176 | tf_op jit(solution)/shard_map/ppermute | solution.py:619
  35.3 2.1 %collective-permute-start.8 = (bf16[80,128]{1,0:T(8,128)(2,1)S(1)}, bf16[80,128]{1,0:T(8,128)(2,1)S(1)}, u32[]{:S(2)}, u32[]{:S(2)}) collective-permute-start(bf16[80,128]{1,0:T(8,128)(2,1)S(1)} %get-tuple-element.104), channel_id=1, source_target_pairs={{0,31},{1,28},{2,29},{3,30},{4,3},{5,0},{6,1},{7,2},{8,7},{9,4},{1... | collective-permute-start | bytes 61448 | tf_op jit(solution)/shard_map/ppermute | solution.py:625
  37.4 1.5 %collective-permute-start.6 = (bf16[176,128]{1,0:T(8,128)(2,1)S(1)}, bf16[176,128]{1,0:T(8,128)(2,1)S(1)}, u32[]{:S(2)}, u32[]{:S(2)}) collective-permute-start(bf16[176,128]{1,0:T(8,128)(2,1)S(1)} %get-tuple-element.81), channel_id=1, source_target_pairs={{0,28},{4,0},{8,4},{12,8},{16,12},{20,16},{24,20},{28,24},{1,29},{... | collective-permute-start | bytes 135176 | tf_op jit(solution)/shard_map/ppermute | solution.py:616
  38.9 1.4 %shard_map.226 = bf16[24,1656]{1,0:T(8,128)(2,1)S(1)} custom-call(f32[1728,144]{1,0:T(8,128)S(1)} %get-tuple-element.106.score_ref), custom_call_target="tpu_custom_call" | custom-call | flops 2000000000 | bytes 1074816 | tf_op jit(solution)/shard_map/pallas_call | solution.py:601
  40.3 0.2 collective-permute-start.9
  40.5 1.0 %collective-permute-done.6.dlon_ref = bf16[176,128]{1,0:T(8,128)(2,1)S(1)} collective-permute-done((bf16[176,128]{1,0:T(8,128)(2,1)S(1)}, bf16[176,128]{1,0:T(8,128)(2,1)S(1)}, u32[]{:S(2)}, u32[]{:S(2)}) %collective-permute-start.6) | collective-permute-done | bytes 45088 | tf_op jit(solution)/shard_map/ppermute | solution.py:616
  41.6 3.6 %shard_map.225 = (f32[288,192]{1,0:T(8,128)S(1)}, bf16[288,192]{1,0:T(8,128)(2,1)S(1)}, bf16[288,192]{1,0:T(8,128)(2,1)S(1)}, bf16[288,192]{1,0:T(8,128)(2,1)S(1)}, f32[864,144]{1,0:T(8,128)S(1)}) custom-call(bf16[176,128]{1,0:T(8,128)(2,1)S(1)} %collective-permute-done.6.dlon_ref, bf16[336,192]{1,0:T(8,128)(2,1)S(1)} %get-tuple-element.82.dloc_ref, ...), custom_call_target="tpu_custom_call" | custom-call | flops 4000000000 | bytes 4657664 | tf_op jit(solution)/shard_map/pallas_call | solution.py:601
  45.2 0.9 %collective-permute-start.10 = (bf16[24,1656]{1,0:T(8,128)(2,1)S(1)}, bf16[24,1656]{1,0:T(8,128)(2,1)S(1)}, u32[]{:S(2)}, u32[]{:S(2)}) collective-permute-start(bf16[24,1656]{1,0:T(8,128)(2,1)S(1)} %add_convert_fusion.3), channel_id=1, source_target_pairs={{0,16},{4,20},{8,24},{12,28},{16,0},{20,4},{24,8},{28,12},{1,17},{... | collective-permute-start | bytes 238472 | tf_op jit(solution)/shard_map/ppermute | solution.py:635
  46.1 4.7 %shard_map.227 = (f32[288,192]{1,0:T(8,128)S(1)}, bf16[288,192]{1,0:T(8,128)(2,1)S(1)}, bf16[288,192]{1,0:T(8,128)(2,1)S(1)}, bf16[288,192]{1,0:T(8,128)(2,1)S(1)}, bf16[24,1656]{1,0:T(8,128)(2,1)S(1)}) custom-call(bf16[176,128]{1,0:T(8,128)(2,1)S(1)} %collective-permute-done.6.dlon_ref, bf16[336,192]{1,0:T(8,128)(2,1)S(1)} %get-tuple-element.82.dloc_ref, ...), custom_call_target="tpu_custom_call" | custom-call | flops 5000000000 | bytes 4110912 | tf_op jit(solution)/shard_map/pallas_call | solution.py:601
  50.7 0.9 %collective-permute-start.13 = (bf16[24,1656]{1,0:T(8,128)(2,1)S(1)}, bf16[24,1656]{1,0:T(8,128)(2,1)S(1)}, u32[]{:S(2)}, u32[]{:S(2)}) collective-permute-start(bf16[24,1656]{1,0:T(8,128)(2,1)S(1)} %get-tuple-element.124), channel_id=1, source_target_pairs={{0,4},{4,0},{8,12},{12,8},{16,20},{20,16},{24,28},{28,24},{1,5},{5... | collective-permute-start | bytes 238472 | tf_op jit(solution)/shard_map/ppermute | solution.py:635
  51.6 0.4 collective-permute-done.10
  52.0 0.8 %shard_map.228 = (bf16[576,192]{1,0:T(8,128)(2,1)S(1)}, bf16[288,128]{1,0:T(8,128)(2,1)S(1)}, bf16[288,128]{1,0:T(8,128)(2,1)S(1)}, bf16[192,128]{1,0:T(8,128)(2,1)S(1)}) custom-call(f32[288,192]{1,0:T(8,128)S(1)} %get-tuple-element.97.refs_0_, bf16[288,192]{1,0:T(8,128)(2,1)S(1)} %get-tuple-element.98.refs_1_, ...), custom_call_target="tpu_custom_call" | custom-call | flops 2000000000 | bytes 2078976 | tf_op jit(solution)/shard_map/pallas_call | solution.py:601
  52.9 0.4 collective-permute-start.12
  53.3 2.0 %collective-permute-done.13 = bf16[24,1656]{1,0:T(8,128)(2,1)S(1)} collective-permute-done((bf16[24,1656]{1,0:T(8,128)(2,1)S(1)}, bf16[24,1656]{1,0:T(8,128)(2,1)S(1)}, u32[]{:S(2)}, u32[]{:S(2)}) %collective-permute-start.13) | collective-permute-done | bytes 79520 | tf_op jit(solution)/shard_map/ppermute | solution.py:635
  55.4 3.0 %collective-permute-start.15 = (bf16[24,1656]{1,0:T(8,128)(2,1)S(1)}, bf16[24,1656]{1,0:T(8,128)(2,1)S(1)}, u32[]{:S(2)}, u32[]{:S(2)}) collective-permute-start(bf16[24,1656]{1,0:T(8,128)(2,1)S(1)} %add_convert_fusion.1), channel_id=1, source_target_pairs={{0,8},{4,12},{8,0},{12,4},{16,24},{20,28},{24,16},{28,20},{1,9},{5... | collective-permute-start | bytes 238472 | tf_op jit(solution)/shard_map/ppermute | solution.py:635
  58.4 1.5 %collective-permute-start.14 = (bf16[192,128]{1,0:T(8,128)(2,1)S(1)}, bf16[192,128]{1,0:T(8,128)(2,1)S(1)}, u32[]{:S(2)}, u32[]{:S(2)}) collective-permute-start(bf16[192,128]{1,0:T(8,128)(2,1)S(1)} %get-tuple-element.126), channel_id=1, source_target_pairs={{0,31},{1,28},{2,29},{3,30},{4,3},{5,0},{6,1},{7,2},{8,7},{9,4},{1... | collective-permute-start | bytes 147464 | tf_op jit(solution)/shard_map/ppermute | solution.py:625
  59.9 1.0 %collective-permute-start.11 = (bf16[288,128]{1,0:T(8,128)(2,1)S(1)}, bf16[288,128]{1,0:T(8,128)(2,1)S(1)}, u32[]{:S(2)}, u32[]{:S(2)}) collective-permute-start(bf16[288,128]{1,0:T(8,128)(2,1)S(1)} %get-tuple-element.122), channel_id=1, source_target_pairs={{0,28},{4,0},{8,4},{12,8},{16,12},{20,16},{24,20},{28,24},{1,29},{... | collective-permute-start | bytes 221192 | tf_op jit(solution)/shard_map/ppermute | solution.py:616
  60.9 0.3 collective-permute-done.15
  61.1 1.6 %collective-permute-start.16 = (bf16[24,1656]{1,0:T(8,128)(2,1)S(1)}, bf16[24,1656]{1,0:T(8,128)(2,1)S(1)}, u32[]{:S(2)}, u32[]{:S(2)}) collective-permute-start(bf16[24,1656]{1,0:T(8,128)(2,1)S(1)} %add_convert_fusion.fine_kept), channel_id=1, source_target_pairs={{0,16},{4,20},{8,24},{12,28},{16,0},{20,4},{24,8},{28,12},{1,17},{... | collective-permute-start | bytes 238472 | tf_op jit(solution)/shard_map/ppermute | solution.py:635
  62.7 1.0 %collective-permute-start.17 = (bf16[24,1656]{1,0:T(8,128)(2,1)S(1)}, bf16[24,1656]{1,0:T(8,128)(2,1)S(1)}, u32[]{:S(2)}, u32[]{:S(2)}) collective-permute-start(bf16[24,1656]{1,0:T(8,128)(2,1)S(1)} %add_convert_fusion.2.coarse_kept), channel_id=1, source_target_pairs={{0,4},{4,0},{8,12},{12,8},{16,20},{20,16},{24,28},{28,24},{1,5},{5... | collective-permute-start | bytes 238472 | tf_op jit(solution)/shard_map/ppermute | solution.py:635
  63.7 1.4 %collective-permute-done.11.lon_ref = bf16[288,128]{1,0:T(8,128)(2,1)S(1)} collective-permute-done((bf16[288,128]{1,0:T(8,128)(2,1)S(1)}, bf16[288,128]{1,0:T(8,128)(2,1)S(1)}, u32[]{:S(2)}, u32[]{:S(2)}) %collective-permute-start.11) | collective-permute-done | bytes 73760 | tf_op jit(solution)/shard_map/ppermute | solution.py:616
  65.0 1.3 %shard_map.229 = (bf16[576,192]{1,0:T(8,128)(2,1)}, bf16[2,6,12,384]{3,2,1,0:T(8,128)(2,1)S(1)}) custom-call(bf16[576,192]{1,0:T(8,128)(2,1)S(1)} %get-tuple-element.121.res_ref, bf16[288,128]{1,0:T(8,128)(2,1)S(1)} %collective-permute-done.11.lon_ref, bf16[288,128]{1,0:T(8,128)(2,1)S(1)} %collective-permute-done.12.lat_ref, ...), custom_call_target="tpu_custom_call" | custom-call | flops 1000000000 | bytes 789312 | tf_op jit(solution)/shard_map/pallas_call | solution.py:601
  66.4 0.7 %copy.27 = bf16[2,6,12,384]{3,0,2,1:T(2,128)(2,1)} copy(bf16[2,6,12,384]{3,2,1,0:T(8,128)(2,1)S(1)} %get-tuple-element.140) | data formatting | bytes 221184
  67.1 0.0 collective-permute-done.17.coarse_other
  67.1 1.6 %collective-permute-done.16.fine_other = bf16[24,1656]{1,0:T(8,128)(2,1)S(1)} collective-permute-done((bf16[24,1656]{1,0:T(8,128)(2,1)S(1)}, bf16[24,1656]{1,0:T(8,128)(2,1)S(1)}, u32[]{:S(2)}, u32[]{:S(2)}) %collective-permute-start.16) | collective-permute-done | bytes 79520 | tf_op jit(solution)/shard_map/ppermute | solution.py:635
  68.7 0.8 %shard_map.230 = (f32[6,2,3312]{2,1,0:T(2,128)}, f32[12,1,3312]{2,1,0:T(1,128)}) custom-call(bf16[24,1656]{1,0:T(8,128)(2,1)S(1)} %add_convert_fusion.fine_kept, bf16[24,1656]{1,0:T(8,128)(2,1)S(1)} %collective-permute-done.16.fine_other, bf16[24,1656]{1,0:T(8,128)(2,1)S(1)} %add_convert_fusion.2.coarse_kept, ...), custom_call_target="tpu_custom_call" | custom-call | flops 1000000000 | bytes 635904 | tf_op jit(solution)/shard_map/pallas_call | solution.py:601
  (55 shorter events, 0.3 us)
Async XLA Ops:
  0.6 1.0 %copy-start.4 = (bf16[2,12,24,192]{3,2,1,0:T(8,128)(2,1)S(1)}, bf16[2,12,24,192]{3,2,1,0:T(8,128)(2,1)}, u32[]{:S(2)}) copy-start(bf16[2,12,24,192]{3,2,1,0:T(8,128)(2,1)} %param.20) | copy-start | bytes 663556
  1.6 5.4 %copy-start.20 = (s32[2,12,24]{2,0,1:T(2,128)S(1)}, s32[2,12,24]{2,0,1:T(2,128)}, u32[]{:S(2)}) copy-start(s32[2,12,24]{2,0,1:T(2,128)} %param.21) | copy-start | bytes 6916
  1.6 6.0 %copy-start.10 = (f32[2,6,3312]{2,0,1:T(2,128)S(1)}, f32[2,6,3312]{2,0,1:T(2,128)}, u32[]{:S(2)}) copy-start(f32[2,6,3312]{2,0,1:T(2,128)} %param.26) | copy-start | bytes 476932
  1.7 8.3 %collective-permute-start.2 = (bf16[80,128]{1,0:T(8,128)(2,1)S(1)}, bf16[80,128]{1,0:T(8,128)(2,1)S(1)}, u32[]{:S(2)}, u32[]{:S(2)}) collective-permute-start(bf16[80,128]{1,0:T(8,128)(2,1)S(1)} %get-tuple-element.72), channel_id=1, source_target_pairs={{0,5},{1,6},{2,7},{3,4},{4,9},{5,10},{6,11},{7,8},{8,13},{9,14},{1... | collective-permute-start | bytes 61448 | tf_op jit(solution)/shard_map/ppermute | solution.py:625
  4.2 6.7 %collective-permute-start = (bf16[176,128]{1,0:T(8,128)(2,1)S(1)}, bf16[176,128]{1,0:T(8,128)(2,1)S(1)}, u32[]{:S(2)}, u32[]{:S(2)}) collective-permute-start(bf16[176,128]{1,0:T(8,128)(2,1)S(1)} %get-tuple-element.70), channel_id=1, source_target_pairs={{0,4},{4,8},{8,12},{12,16},{16,20},{20,24},{24,28},{28,0},{1,5},{5... | collective-permute-start | bytes 135176 | tf_op jit(solution)/shard_map/ppermute | solution.py:616
  5.7 5.2 %collective-permute-start.1 = (bf16[176,128]{1,0:T(8,128)(2,1)S(1)}, bf16[176,128]{1,0:T(8,128)(2,1)S(1)}, u32[]{:S(2)}, u32[]{:S(2)}) collective-permute-start(bf16[176,128]{1,0:T(8,128)(2,1)S(1)} %get-tuple-element.71), channel_id=1, source_target_pairs={{0,1},{1,2},{2,3},{3,0},{4,5},{5,6},{6,7},{7,4},{8,9},{9,10},{10,1... | collective-permute-start | bytes 135176 | tf_op jit(solution)/shard_map/ppermute | solution.py:619
  7.6 3.3 %copy-start.5 = (bf16[2,12,24,192]{3,2,1,0:T(8,128)(2,1)S(1)}, bf16[2,12,24,192]{3,2,1,0:T(8,128)(2,1)}, u32[]{:S(2)}) copy-start(bf16[2,12,24,192]{3,2,1,0:T(8,128)(2,1)} %param.20) | copy-start | bytes 663556
  7.6 3.3 %copy-start.7 = (bf16[192,768]{1,0:T(8,128)(2,1)S(1)}, bf16[192,768]{1,0:T(8,128)(2,1)}, u32[]{:S(2)}) copy-start(bf16[192,768]{1,0:T(8,128)(2,1)} %refs_8_.5) | copy-start | bytes 884740
  7.7 3.3 %copy-start.8 = (bf16[768,192]{0,1:T(8,128)(2,1)S(1)}, bf16[768,192]{0,1:T(8,128)(2,1)}, u32[]{:S(2)}) copy-start(bf16[768,192]{0,1:T(8,128)(2,1)} %param.25) | copy-start | bytes 884740
  7.7 3.3 %copy-start.9 = (bf16[192,576]{1,0:T(8,128)(2,1)S(1)}, bf16[192,576]{1,0:T(8,128)(2,1)}, u32[]{:S(2)}) copy-start(bf16[192,576]{1,0:T(8,128)(2,1)} %refs_12_.1) | copy-start | bytes 663556
  7.7 3.3 %copy-start.12 = (bf16[2,6,12,384]{3,0,2,1:T(2,128)(2,1)S(1)}, bf16[2,6,12,384]{3,0,2,1:T(2,128)(2,1)}, u32[]{:S(2)}) copy-start(bf16[2,6,12,384]{3,0,2,1:T(2,128)(2,1)} %param.33) | copy-start | bytes 331780
  7.7 3.3 %copy-start.13 = (bf16[192,192]{1,0:T(8,128)(2,1)S(1)}, bf16[192,192]{1,0:T(8,128)(2,1)}, u32[]{:S(2)}) copy-start(bf16[192,192]{1,0:T(8,128)(2,1)} %refs_7_.5) | copy-start | bytes 221188
  7.7 3.3 %copy-start.18 = (s32[576,1]{1,0:T(8,128)S(1)}, s32[576,1]{1,0:T(8,128)}, u32[]{:S(2)}) copy-start(s32[576,1]{1,0:T(8,128)} %constant.41.refs_4_) | copy-start | bytes 6916
  11.0 8.2 %copy-start.11 = (f32[1,12,3312]{2,0,1:T(1,128)S(1)}, f32[1,12,3312]{2,0,1:T(1,128)}, u32[]{:S(2)}) copy-start(f32[1,12,3312]{2,0,1:T(1,128)} %param.32) | copy-start | bytes 476932
  17.0 7.7 %collective-permute-start.5 = (bf16[192,128]{1,0:T(8,128)(2,1)S(1)}, bf16[192,128]{1,0:T(8,128)(2,1)S(1)}, u32[]{:S(2)}, u32[]{:S(2)}) collective-permute-start(bf16[192,128]{1,0:T(8,128)(2,1)S(1)} %get-tuple-element.78), channel_id=1, source_target_pairs={{0,5},{1,6},{2,7},{3,4},{4,9},{5,10},{6,11},{7,8},{8,13},{9,14},{1... | collective-permute-start | bytes 147464 | tf_op jit(solution)/shard_map/ppermute | solution.py:625
  17.5 8.0 %collective-permute-start.3 = (bf16[288,128]{1,0:T(8,128)(2,1)S(1)}, bf16[288,128]{1,0:T(8,128)(2,1)S(1)}, u32[]{:S(2)}, u32[]{:S(2)}) collective-permute-start(bf16[288,128]{1,0:T(8,128)(2,1)S(1)} %get-tuple-element.76), channel_id=1, source_target_pairs={{0,4},{4,8},{8,12},{12,16},{16,20},{20,24},{24,28},{28,0},{1,5},{5... | collective-permute-start | bytes 221192 | tf_op jit(solution)/shard_map/ppermute | solution.py:616
  19.1 6.5 %collective-permute-start.4 = (bf16[288,128]{1,0:T(8,128)(2,1)S(1)}, bf16[288,128]{1,0:T(8,128)(2,1)S(1)}, u32[]{:S(2)}, u32[]{:S(2)}) collective-permute-start(bf16[288,128]{1,0:T(8,128)(2,1)S(1)} %get-tuple-element.77), channel_id=1, source_target_pairs={{0,1},{1,2},{2,3},{3,0},{4,5},{5,6},{6,7},{7,4},{8,9},{9,10},{10,1... | collective-permute-start | bytes 221192 | tf_op jit(solution)/shard_map/ppermute | solution.py:619
  21.5 4.1 %copy-start = (bf16[384,1536]{1,0:T(8,128)(2,1)S(1)}, bf16[384,1536]{1,0:T(8,128)(2,1)}, u32[]{:S(2)}) copy-start(bf16[384,1536]{1,0:T(8,128)(2,1)} %up_ref.1) | copy-start | bytes 3538948
  21.5 4.1 %copy-start.1 = (bf16[1536,384]{1,0:T(8,128)(2,1)S(1)}, bf16[1536,384]{1,0:T(8,128)(2,1)}, u32[]{:S(2)}) copy-start(bf16[1536,384]{1,0:T(8,128)(2,1)} %down_ref.1) | copy-start | bytes 3538948
  21.5 4.1 %copy-start.2 = (bf16[384,1152]{1,0:T(8,128)(2,1)S(1)}, bf16[384,1152]{1,0:T(8,128)(2,1)}, u32[]{:S(2)}) copy-start(bf16[384,1152]{1,0:T(8,128)(2,1)} %qkv_ref.1) | copy-start | bytes 2654212
  21.5 4.1 %copy-start.3 = (bf16[768,384]{1,0:T(8,128)(2,1)S(1)}, bf16[768,384]{1,0:T(8,128)(2,1)}, u32[]{:S(2)}) copy-start(bf16[768,384]{1,0:T(8,128)(2,1)} %reduce_ref.1) | copy-start | bytes 1769476
  21.5 4.1 %copy-start.6 = (bf16[384,384]{1,0:T(8,128)(2,1)S(1)}, bf16[384,384]{1,0:T(8,128)(2,1)}, u32[]{:S(2)}) copy-start(bf16[384,384]{1,0:T(8,128)(2,1)} %proj_ref.1) | copy-start | bytes 884740
  21.5 4.1 %copy-start.14 = (s32[608,1]{1,0:T(8,128)S(1)}, s32[608,1]{1,0:T(8,128)}, u32[]{:S(2)}) copy-start(s32[608,1]{1,0:T(8,128)} %constant.43.split_ref) | copy-start | bytes 7300
  21.5 4.1 %copy-start.17 = (s32[576,1]{1,0:T(8,128)S(1)}, s32[576,1]{1,0:T(8,128)}, u32[]{:S(2)}) copy-start(s32[576,1]{1,0:T(8,128)} %constant.42.merge_ref) | copy-start | bytes 6916
  34.2 4.7 %collective-permute-start.7 = (bf16[176,128]{1,0:T(8,128)(2,1)S(1)}, bf16[176,128]{1,0:T(8,128)(2,1)S(1)}, u32[]{:S(2)}, u32[]{:S(2)}) collective-permute-start(bf16[176,128]{1,0:T(8,128)(2,1)S(1)} %get-tuple-element.101), channel_id=1, source_target_pairs={{0,3},{1,0},{2,1},{3,2},{4,7},{5,4},{6,5},{7,6},{8,11},{9,8},{10,9... | collective-permute-start | bytes 135176 | tf_op jit(solution)/shard_map/ppermute | solution.py:619
  35.3 10.8 %collective-permute-start.8 = (bf16[80,128]{1,0:T(8,128)(2,1)S(1)}, bf16[80,128]{1,0:T(8,128)(2,1)S(1)}, u32[]{:S(2)}, u32[]{:S(2)}) collective-permute-start(bf16[80,128]{1,0:T(8,128)(2,1)S(1)} %get-tuple-element.104), channel_id=1, source_target_pairs={{0,31},{1,28},{2,29},{3,30},{4,3},{5,0},{6,1},{7,2},{8,7},{9,4},{1... | collective-permute-start | bytes 61448 | tf_op jit(solution)/shard_map/ppermute | solution.py:625
  37.4 4.2 %collective-permute-start.6 = (bf16[176,128]{1,0:T(8,128)(2,1)S(1)}, bf16[176,128]{1,0:T(8,128)(2,1)S(1)}, u32[]{:S(2)}, u32[]{:S(2)}) collective-permute-start(bf16[176,128]{1,0:T(8,128)(2,1)S(1)} %get-tuple-element.81), channel_id=1, source_target_pairs={{0,28},{4,0},{8,4},{12,8},{16,12},{20,16},{24,20},{28,24},{1,29},{... | collective-permute-start | bytes 135176 | tf_op jit(solution)/shard_map/ppermute | solution.py:616
  38.9 2.6 %copy-start.16 = (s32[576,1]{1,0:T(8,128)S(1)}, s32[576,1]{1,0:T(8,128)}, u32[]{:S(2)}) copy-start(s32[576,1]{1,0:T(8,128)} %constant.44.back_ref) | copy-start | bytes 6916
  40.3 4.8 %collective-permute-start.9 = (bf16[24,1656]{1,0:T(8,128)(2,1)S(1)}, bf16[24,1656]{1,0:T(8,128)(2,1)S(1)}, u32[]{:S(2)}, u32[]{:S(2)}) collective-permute-start(bf16[24,1656]{1,0:T(8,128)(2,1)S(1)} %shard_map.226), channel_id=1, source_target_pairs={{0,8},{4,12},{8,0},{12,4},{16,24},{20,28},{24,16},{28,20},{1,9},{5... | collective-permute-start | bytes 238472 | tf_op jit(solution)/shard_map/ppermute | solution.py:635
  45.2 6.8 %collective-permute-start.10 = (bf16[24,1656]{1,0:T(8,128)(2,1)S(1)}, bf16[24,1656]{1,0:T(8,128)(2,1)S(1)}, u32[]{:S(2)}, u32[]{:S(2)}) collective-permute-start(bf16[24,1656]{1,0:T(8,128)(2,1)S(1)} %add_convert_fusion.3), channel_id=1, source_target_pairs={{0,16},{4,20},{8,24},{12,28},{16,0},{20,4},{24,8},{28,12},{1,17},{... | collective-permute-start | bytes 238472 | tf_op jit(solution)/shard_map/ppermute | solution.py:635
  50.7 4.6 %collective-permute-start.13 = (bf16[24,1656]{1,0:T(8,128)(2,1)S(1)}, bf16[24,1656]{1,0:T(8,128)(2,1)S(1)}, u32[]{:S(2)}, u32[]{:S(2)}) collective-permute-start(bf16[24,1656]{1,0:T(8,128)(2,1)S(1)} %get-tuple-element.124), channel_id=1, source_target_pairs={{0,4},{4,0},{8,12},{12,8},{16,20},{20,16},{24,28},{28,24},{1,5},{5... | collective-permute-start | bytes 238472 | tf_op jit(solution)/shard_map/ppermute | solution.py:635
  52.0 13.0 %copy-start.15 = (s32[576,1]{1,0:T(8,128)S(1)}, s32[576,1]{1,0:T(8,128)}, u32[]{:S(2)}) copy-start(s32[576,1]{1,0:T(8,128)} %constant.45.leave_ref) | copy-start | bytes 6916
  52.0 13.0 %copy-start.19 = (s32[144,1]{1,0:T(8,128)S(1)}, s32[144,1]{1,0:T(8,128)}, u32[]{:S(2)}) copy-start(s32[144,1]{1,0:T(8,128)} %constant.46.result_ref) | copy-start | bytes 1732
  52.9 2.4 %collective-permute-start.12 = (bf16[288,128]{1,0:T(8,128)(2,1)S(1)}, bf16[288,128]{1,0:T(8,128)(2,1)S(1)}, u32[]{:S(2)}, u32[]{:S(2)}) collective-permute-start(bf16[288,128]{1,0:T(8,128)(2,1)S(1)} %get-tuple-element.123), channel_id=1, source_target_pairs={{0,3},{1,0},{2,1},{3,2},{4,7},{5,4},{6,5},{7,6},{8,11},{9,8},{10,9... | collective-permute-start | bytes 221192 | tf_op jit(solution)/shard_map/ppermute | solution.py:619
  55.4 5.8 %collective-permute-start.15 = (bf16[24,1656]{1,0:T(8,128)(2,1)S(1)}, bf16[24,1656]{1,0:T(8,128)(2,1)S(1)}, u32[]{:S(2)}, u32[]{:S(2)}) collective-permute-start(bf16[24,1656]{1,0:T(8,128)(2,1)S(1)} %add_convert_fusion.1), channel_id=1, source_target_pairs={{0,8},{4,12},{8,0},{12,4},{16,24},{20,28},{24,16},{28,20},{1,9},{5... | collective-permute-start | bytes 238472 | tf_op jit(solution)/shard_map/ppermute | solution.py:635
  58.4 5.3 %collective-permute-start.14 = (bf16[192,128]{1,0:T(8,128)(2,1)S(1)}, bf16[192,128]{1,0:T(8,128)(2,1)S(1)}, u32[]{:S(2)}, u32[]{:S(2)}) collective-permute-start(bf16[192,128]{1,0:T(8,128)(2,1)S(1)} %get-tuple-element.126), channel_id=1, source_target_pairs={{0,31},{1,28},{2,29},{3,30},{4,3},{5,0},{6,1},{7,2},{8,7},{9,4},{1... | collective-permute-start | bytes 147464 | tf_op jit(solution)/shard_map/ppermute | solution.py:625
  59.9 5.1 %collective-permute-start.11 = (bf16[288,128]{1,0:T(8,128)(2,1)S(1)}, bf16[288,128]{1,0:T(8,128)(2,1)S(1)}, u32[]{:S(2)}, u32[]{:S(2)}) collective-permute-start(bf16[288,128]{1,0:T(8,128)(2,1)S(1)} %get-tuple-element.122), channel_id=1, source_target_pairs={{0,28},{4,0},{8,4},{12,8},{16,12},{20,16},{24,20},{28,24},{1,29},{... | collective-permute-start | bytes 221192 | tf_op jit(solution)/shard_map/ppermute | solution.py:616
  61.1 7.6 %collective-permute-start.16 = (bf16[24,1656]{1,0:T(8,128)(2,1)S(1)}, bf16[24,1656]{1,0:T(8,128)(2,1)S(1)}, u32[]{:S(2)}, u32[]{:S(2)}) collective-permute-start(bf16[24,1656]{1,0:T(8,128)(2,1)S(1)} %add_convert_fusion.fine_kept), channel_id=1, source_target_pairs={{0,16},{4,20},{8,24},{12,28},{16,0},{20,4},{24,8},{28,12},{1,17},{... | collective-permute-start | bytes 238472 | tf_op jit(solution)/shard_map/ppermute | solution.py:635
  62.7 4.4 %collective-permute-start.17 = (bf16[24,1656]{1,0:T(8,128)(2,1)S(1)}, bf16[24,1656]{1,0:T(8,128)(2,1)S(1)}, u32[]{:S(2)}, u32[]{:S(2)}) collective-permute-start(bf16[24,1656]{1,0:T(8,128)(2,1)S(1)} %add_convert_fusion.2.coarse_kept), channel_id=1, source_target_pairs={{0,4},{4,0},{8,12},{12,8},{16,20},{20,16},{24,28},{28,24},{1,5},{5... | collective-permute-start | bytes 238472 | tf_op jit(solution)/shard_map/ppermute | solution.py:635
